TPU v7x, 32 devices: a whole 2x2x4 slice. The times are simulated.
32 devices in a mesh: patch: 16 (over z, x, core), tp: 2 (over y).
Axes of the slice: x: 2, y: 2, z: 4, core: 2. Of those that a mesh axis runs over, the one named last changes fastest.
Arguments:
- hidden_states: bfloat16 [2, 2048, 3072], P(None, 'patch'), may hold values from -6 to 6
- modulation: float32 [3, 2, 3072], replicated, may hold values from -4 to 4
- qkv_weight: bfloat16 [3072, 3, 3072], P(None, None, 'tp'), may hold values from -0.109375 to 0.109375
- out_weight: bfloat16 [3072, 3072], P('tp'), may hold values from -0.109375 to 0.109375
- qk_gain: float32 [2, 128], replicated, may hold values from 0.8 to 2
- stale_kv: bfloat16 [2, 2, 2048, 3072], P(None, None, 'patch', 'tp'), may hold values from -400 to 400, as said below
Outputs:
- mixed: bfloat16 [2, 2048, 3072], P(None, 'patch', 'tp')
- fresh_kv: bfloat16 [2, 2, 2048, 3072], P(None, None, 'patch', 'tp')
Inputs may be any that keep to these rules, and one draw needn't show every extreme that they name: `stale_kv`: keys and values of the previous step, of every token of every clip.
All inputs are finite; a program needn't handle non-finite values.
Results may differ from a plain program's by a relative error of at most 0.012.
The roundings to bfloat16 on the way count: a program that leaves them out, or rounds other values in their place, can miss the bound.
Values may be sent and summed in bfloat16 or wider, within the bound.
No kernel may reach another device: no remote copies, remote signals or barrier semaphores. Data moves between devices by JAX's collectives and lax.ppermute only.
A program may use at most 192 MiB of HBM per device.

v0:
```python
import jax
import jax.numpy as jnp
from jax import lax
from jax.sharding import PartitionSpec as P

HEAD = 128


def head_norm(values_in, gain_row, heads_here):
    shaped = values_in.reshape(values_in.shape[0], values_in.shape[1], heads_here, HEAD)
    square_mean = jnp.mean(shaped * shaped, axis=-1, keepdims=True)
    return (shaped * lax.rsqrt(square_mean + 1e-06) * gain_row).astype(jnp.bfloat16)


def per_device(hidden_states, modulation, qkv_weight, out_weight, qk_gain, stale_kv):
    clip_count, row_count, width_all = hidden_states.shape
    heads_here = qkv_weight.shape[2] // HEAD
    inputs = hidden_states.astype(jnp.float32)
    feature_mean = jnp.mean(inputs, axis=-1, keepdims=True)
    centered = inputs - feature_mean
    feature_var = jnp.mean(centered * centered, axis=-1, keepdims=True)
    normed = (
        centered * lax.rsqrt(feature_var + 1e-06) * (1.0 + modulation[1][:, None, :])
        + modulation[0][:, None, :]
    ).astype(jnp.bfloat16)
    projected = jnp.einsum("ctd,dkh->kcth", normed, qkv_weight, preferred_element_type=jnp.float32)
    queries = head_norm(projected[0], qk_gain[0], heads_here)
    keys_new = head_norm(projected[1], qk_gain[1], heads_here)
    values_new = projected[2].astype(jnp.bfloat16).reshape(clip_count, row_count, heads_here, HEAD)
    fresh_kv = jnp.stack(
        [keys_new.reshape(clip_count, row_count, -1), values_new.reshape(clip_count, row_count, -1)]
    )
    inv_scale = HEAD ** (-0.5)
    local_scores = (
        jnp.einsum("cqhd,ckhd->chqk", queries, keys_new, preferred_element_type=jnp.float32)
        * inv_scale
    )
    start_max = jnp.max(local_scores, axis=-1)
    local_expo = jnp.exp(local_scores - start_max[..., None])
    start_sum = jnp.sum(local_expo, axis=-1)
    start_acc = jnp.einsum(
        "chqk,ckhd->chqd",
        local_expo.astype(jnp.bfloat16),
        values_new,
        preferred_element_type=jnp.float32,
    )
    own_first = lax.axis_index("patch") * row_count
    gathered = lax.all_gather(stale_kv, "patch", axis=2, tiled=True)
    count = gathered.shape[2]
    tile_keys = gathered[0].reshape(clip_count, count, heads_here, HEAD)
    tile_values = gathered[1].reshape(clip_count, count, heads_here, HEAD)
    scores = (
        jnp.einsum("cqhd,ckhd->chqk", queries, tile_keys, preferred_element_type=jnp.float32)
        * inv_scale
    )
    positions = jnp.arange(count, dtype=jnp.int32)
    own_rows = (positions >= own_first) & (positions < own_first + row_count)
    scores = jnp.where(own_rows[None, None, None, :], -1e30, scores)
    new_max = jnp.maximum(start_max, jnp.max(scores, axis=-1))
    rescale = jnp.exp(start_max - new_max)
    expo = jnp.exp(scores - new_max[..., None])
    new_sum = start_sum * rescale + jnp.sum(expo, axis=-1)
    new_weighted = start_acc * rescale[..., None] + jnp.einsum(
        "chqk,ckhd->chqd",
        expo.astype(jnp.bfloat16),
        tile_values,
        preferred_element_type=jnp.float32,
    )
    attended = (new_weighted / new_sum[..., None]).astype(jnp.bfloat16)
    attended = jnp.transpose(attended, (0, 2, 1, 3)).reshape(
        clip_count, row_count, heads_here * HEAD
    )
    product = jnp.einsum("cth,hd->ctd", attended, out_weight, preferred_element_type=jnp.float32)
    col_count = width_all // lax.axis_size("tp")
    col_first = lax.axis_index("tp") * col_count
    summed_part = lax.psum_scatter(
        product.astype(jnp.bfloat16), "tp", scatter_dimension=2, tiled=True
    ).astype(jnp.float32)
    input_part = lax.dynamic_slice_in_dim(inputs, col_first, col_count, 2)
    gate_part = lax.dynamic_slice_in_dim(modulation[2], col_first, col_count, 1)
    mixed = (input_part + gate_part[:, None, :] * summed_part).astype(jnp.bfloat16)
    return (mixed, fresh_kv)


def solution(mesh):
    in_specs = (
        P(None, "patch", None),
        P(),
        P(None, None, "tp"),
        P("tp", None),
        P(),
        P(None, None, "patch", "tp"),
    )
    out_specs = (P(None, "patch", "tp"), P(None, None, "patch", "tp"))
    return jax.shard_map(
        per_device, mesh=mesh, in_specs=in_specs, out_specs=out_specs, check_vma=False
    )
```

profile of v0, /device:TPU:0, one launch (start us, length us, event | category | flops | bytes accessed | tf_op | source)
XLA Modules:
  0.0 252.8 jit_solution(1920414705987995419)
XLA Ops:
  7.2 0.0 all-gather.2.cloned.1.call-start
  7.2 2.6 %copy.22 = bf16[2,2,128,1536]{2,3,1,0:T(8,128)(2,1)} copy(bf16[2,2,128,1536]{3,2,1,0:T(8,128)(2,1)} %param.11) | data formatting | bytes 3145728 | tf_op args[5]
  9.8 0.0 copy-start
  9.8 0.0 all-gather.2.cloned.1.call-update
  9.8 0.0 reduce-scatter.2.cloned.1.call-start
  9.9 1.3 copy-done
  11.2 0.0 copy-start.8
  11.2 0.3 convert_reduce_fusion
  11.5 0.6 multiply_reduce_fusion
  12.1 0.0 copy-done.8
  12.1 13.5 %fusion.16 = f32[3,2,128,1536]{3,2,0,1:T(8,128)S(1)} fusion(bf16[3072,3,1536]{2,0,1:T(8,128)(2,1)} %param.8, bf16[2,128,3072]{2,1,0:T(8,128)(2,1)S(1)} %copy-done, f32[2,3072]{1,0:T(2,128)S(1)} %get-tuple-element.13, f32[2,3072]{1,0:T(2,128)S(1)} %get-tuple-element.14, f32[2,128]{1,0:T(2,128)S(1)} %add_rsqrt_fusion.2, f32[2,128]{1,0:T(2,128)S(1)} %broadcast_multiply_fusion), kind=kOutput, calls=%fused_computation.15 | convolution fusion | flops 7252475904 | bytes 34654208 | tf_op jit(solution)/shard_map/ctd,dkh->kcth/dot_general | solution.py:26
  25.6 0.0 copy-start.4
  25.6 1.3 slice.42
  26.9 1.3 copy-done.4
  28.2 1.0 slice.51
  29.2 1.9 copy.17
  31.0 0.0 copy-start.1
  31.1 0.1 multiply_reduce_fusion.1
  31.2 1.5 mul.143
  32.7 0.0 copy-done.1
  32.7 0.0 copy-start.9
  32.7 1.9 copy.26
  34.6 0.0 copy-done.9
  34.6 3.6 %multiply_convert_fusion = (bf16[1,2,128,1536]{3,2,0,1:T(8,128)(2,1)}, f32[1,2,128,1536]{3,2,0,1:T(8,128)}) fusion(f32[1,2,128,1536]{3,2,0,1:T(8,128)S(1)} %copy.26, f32[1536]{0:T(1024)S(1)} %broadcast_bitcast_fusion, f32[3,2,128,1536]{3,2,0,1:T(8,128)} %copy-done.4), kind=kLoop, calls=%fused_computation.26 | loop fusion | flops 1179648 | bytes 7084032 | tf_op jit(solution)/shard_map/convert_element_type | solution.py:12
  38.2 1.9 copy.16
  40.2 2.3 copy.20
  42.5 0.0 copy-start.2
  42.5 0.1 multiply_reduce_fusion.2
  42.7 1.3 copy-done.2
  43.9 0.6 fusion.41
  44.6 0.0 copy-start.5
  44.6 1.1 copy-done.5
  45.7 0.3 fusion.27
  46.0 103.7 %all-gather.2.cloned.1.call-done = bf16[2,2,2048,1536]{2,3,1,0:T(8,128)(2,1)} async-done(((bf16[2,2,128,1536]{2,3,1,0:T(8,128)(2,1)}), bf16[2,2,2048,1536]{2,3,1,0:T(8,128)(2,1)}) %all-gather.2.cloned.1.call-update) | async-done | bytes 25165840 | tf_op jit(solution)/shard_map/all_gather | solution.py:48
  149.7 17.7 %fusion.39 = (bf16[1,2,2048,1536]{2,3,1,0:T(8,128)(2,1)}, bf16[1,2,2048,1536]{2,3,1,0:T(8,128)(2,1)}) fusion(bf16[2,2,2048,1536]{2,3,1,0:T(8,128)(2,1)} %all-gather.2.cloned.1.call-done), kind=kLoop, calls=%fused_computation.63 | loop fusion | bytes 50331648 | tf_op jit(solution)/shard_map/slice | solution.py:50
  167.4 13.5 %fusion.2 = (f32[2,12,128]{2,1,0:T(8,128)S(1)}, f32[2,12,128,2048]{3,2,1,0:T(8,128)}) fusion(pred[2048]{0:T(1024)(128)(4,1)S(1)} %fusion.34, bf16[2,2048,12,128]{1,3,2,0:T(8,128)(2,1)} %bitcast.62, f32[2,128,12,128]{1,3,2,0:T(8,128)S(1)} %bitcast.65, f32[128]{0:T(128)S(1)} %get-tuple-element.16, f32[2,128,12]{1,2,0:T(8,128)S(1)} %add_rsqrt_fusion.1), kind=kOutput, calls=%fused_computation.4 | convolution fusion | flops 1630663680 | bytes 39348736 | tf_op jit(solution)/shard_map/cqhd,ckhd->chqk/dot_general | solution.py:53
  180.9 11.1 %fusion.3 = f32[2,12,128]{2,1,0:T(8,128)S(1)} fusion(f32[2,12,128,2048]{3,2,1,0:T(8,128)} %get-tuple-element.20, f32[2,12,128]{2,1,0:T(8,128)S(1)} %max.18, pred[2048]{0:T(1024)(128)(4,1)S(1)} %fusion.34), kind=kLoop, calls=%fused_computation.5 | loop fusion | flops 25162752 | bytes 25192448 | tf_op jit(solution)/shard_map/reduce_sum | solution.py:62
  192.0 0.0 copy-start.6
  192.0 16.4 %fusion.5 = f32[2,12,128,128]{2,3,1,0:T(8,128)} fusion(bf16[2,2048,12,128]{1,3,2,0:T(8,128)(2,1)} %bitcast.68, f32[2,12,128,2048]{3,2,1,0:T(8,128)} %get-tuple-element.20, f32[2,12,128]{2,1,0:T(8,128)S(1)} %max.18, pred[2048]{0:T(1024)(128)(4,1)S(1)} %fusion.34), kind=kOutput, calls=%fused_computation.7 | convolution fusion | flops 1635778560 | bytes 39335936 | tf_op jit(solution)/shard_map/chqk,ckhd->chqd/dot_general | solution.py:63
  208.4 0.0 copy-done.6
  208.5 2.2 fusion.22
  210.6 7.4 %fusion.13 = bf16[2,128,3072]{2,1,0:T(8,128)(2,1)} fusion(bf16[2,128,1536]{1,2,0:T(8,128)(2,1)S(1)} %bitcast.70, bf16[1536,3072]{1,0:T(8,128)(2,1)} %param.9), kind=kOutput, calls=%fused_computation.14 | convolution fusion | flops 2416705536 | bytes 11796480 | tf_op jit(solution)/shard_map/cth,hd->ctd/dot_general | solution.py:73
  218.1 0.0 reduce-scatter.2.cloned.1.call-update
  218.1 0.0 copy-start.3
  218.1 0.0 copy-start.7
  218.1 2.0 convert_element_type.42
  220.1 0.0 copy-done.3
  220.1 0.0 copy-done.7
  220.1 0.1 pad_maximum_fusion
  220.3 1.2 copy.27
  221.5 21.6 %reduce-scatter.2.cloned.1.call-done = bf16[2,128,1536]{2,1,0:T(8,128)(2,1)} async-done(((bf16[2,128,3072]{2,1,0:T(8,128)(2,1)}), bf16[2,128,1536]{2,1,0:T(8,128)(2,1)}) %reduce-scatter.2.cloned.1.call-update) | async-done | bytes 786448 | tf_op jit(solution)/shard_map/reduce_scatter | solution.py:76
  243.2 2.7 %add_convert_fusion.1 = bf16[2,128,1536]{2,1,0:T(8,128)(2,1)} fusion(bf16[2,128,1536]{2,1,0:T(8,128)(2,1)} %reduce-scatter.2.cloned.1.call-done, f32[2,128,3072]{2,1,0:T(8,128)} %convert_element_type.42, s32[]{:T(128)S(6)} %select_n.8, f32[2,1536]{1,0:T(2,128)S(1)} %dynamic-slice_bitcast_fusion), kind=kLoop, calls=%fused_computation.27 | loop fusion | flops 1572864 | bytes 3158020 | tf_op jit(solution)/shard_map/convert_element_type | solution.py:81
  (11 shorter events, 0.1 us)
Async XLA Ops:
  7.2 142.6 %all-gather.2.cloned.1.call-start = ((), (), s32[]{:S(2)}) async-start(), calls=%async_computation.1 | async-start | bytes 26738688 | tf_op jit(solution)/shard_map/all_gather | solution.py:48
  9.8 1.4 copy-start
  9.8 233.4 %reduce-scatter.2.cloned.1.call-start = ((), (), s32[]{:S(2)}) async-start(), calls=%async_computation.2 | async-start | bytes 2359296 | tf_op jit(solution)/shard_map/reduce_scatter | solution.py:76
  11.2 0.9 copy-start.8
  25.6 2.6 %copy-start.4 = (f32[3,2,128,1536]{3,2,0,1:T(8,128)}, f32[3,2,128,1536]{3,2,0,1:T(8,128)S(1)}, u32[]{:S(2)}) copy-start(f32[3,2,128,1536]{3,2,0,1:T(8,128)S(1)} %fusion.16) | copy-start | bytes 14155780
  31.0 1.6 copy-start.1
  32.7 1.9 copy-start.9
  42.5 1.4 copy-start.2
  44.6 1.1 copy-start.5
  192.0 16.4 %copy-start.6 = (f32[2,12,128,128]{2,3,1,0:T(8,128)S(1)}, f32[2,12,128,128]{2,3,1,0:T(8,128)}, u32[]{:S(2)}) copy-start(f32[2,12,128,128]{2,3,1,0:T(8,128)} %copy-done.5) | copy-start | bytes 4718596
  218.1 2.1 copy-start.3
  218.1 2.0 copy-start.7
Sparse Core Ops, SparseCore 0:
  10.1 139.5 all-gather.1
  218.2 24.9 reduce-scatter.1
where the time goes:
time: 253 us
  waiting for transfers between devices  125 us (49%)
  matrix products  53.6 us (21%)
  local copies, waits for them, and re-layouts  38.4 us (15%)
  other arithmetic  21.1 us (8%)
  between operations  14.2 us (6%)
    all_gather x1, waiting for transfers between devices, per_device(): gathered = lax.all_gather(stale_kv, 'patch', axis=2, tiled=True)  104 us
    reduce_scatter x1, waiting for transfers between devices, per_device(): lax.psum_scatter(product.astype(jnp.bfloat16), 'tp', scatter_dimension=2,...  21.6 us
    slice x1, local copies, waits for them, and re-layouts, per_device(): tile_keys = gathered[0].reshape(clip_count, count, heads_here, HEAD)  17.7 us
    dot_general x1, matrix products, per_device(): jnp.einsum('chqk,ckhd->chqd', expo.astype(jnp.bfloat16), tile_values, pre...  16.4 us
    dot_general x1, matrix products, per_device(): jnp.einsum('ctd,dkh->kcth', normed, qkv_weight, preferred_element_type=jn...  13.5 us
    dot_general x1, matrix products, per_device(): jnp.einsum('cqhd,ckhd->chqk', queries, tile_keys, preferred_element_type=...  13.5 us
    reduce_sum x1, other arithmetic, per_device(): new_sum = start_sum * rescale + jnp.sum(expo, axis=-1)  11.1 us
    unnamed x22, local copies, waits for them, and re-layouts  8.88 us
  transfers between devices with their start and end apart: 2, of which 2 were waited for; matrix products, arithmetic and copies ran while one was open for 14% of the time, Pallas kernels for 0%

commit v1 on v0

v1 whole, which is shorter than its diff:
```python
import functools
import math

import jax
import jax.numpy as jnp
from jax import lax
from jax.experimental import pallas as pl
from jax.experimental.pallas import tpu as pltpu
from jax.sharding import PartitionSpec as P

HEAD = 128
EXTRA = 16
LOG2E = 1.4426950408889634
SCALE2 = HEAD ** (-0.5) * LOG2E
MIB = 1024 * 1024
BF = jnp.bfloat16
F32 = jnp.float32


def nt(a, b):
    return lax.dot_general(a, b, (((1,), (1,)), ((), ())), preferred_element_type=F32)


def nn(a, b):
    return lax.dot_general(a, b, (((1,), (0,)), ((), ())), preferred_element_type=F32)


def params(mib, **kw):
    return pltpu.CompilerParams(vmem_limit_bytes=mib * MIB, **kw)


def norm_heads(values, gain_row):
    parts = []
    for h in range(values.shape[1] // HEAD):
        v = values[:, h * HEAD : (h + 1) * HEAD]
        square_mean = jnp.mean(v * v, axis=-1, keepdims=True)
        parts.append((v * lax.rsqrt(square_mean + 1e-06) * gain_row).astype(BF))
    return jnp.concatenate(parts, axis=1)


def cut_kernel(groups, width, pos, stale, *rest):
    outs, sems = rest[:groups], rest[groups]
    copies = []
    for s in range(groups):
        first = pl.multiple_of(lax.rem(pos[0] + s, groups) * width, HEAD)
        copies.append(
            pltpu.make_async_copy(stale.at[:, :, :, pl.ds(first, width)], outs[s], sems.at[s])
        )
    for c in copies:
        c.start()
    for c in copies:
        c.wait()


def cut_stale(pos, stale, groups):
    kv, clips, rows, cols = stale.shape
    width = cols // groups
    shape = jax.ShapeDtypeStruct((kv, clips, rows, width), BF)
    return pl.pallas_call(
        functools.partial(cut_kernel, groups, width),
        out_shape=[shape] * groups,
        in_specs=[pl.BlockSpec(memory_space=pltpu.SMEM), pl.BlockSpec(memory_space=pl.ANY)],
        out_specs=[pl.BlockSpec(memory_space=pl.ANY)] * groups,
        scratch_shapes=[pltpu.SemaphoreType.DMA((groups,))],
        compiler_params=params(8),
        name="cut_stale",
    )(pos, stale)


def query_kernel(groups, per_step, pos, hidden, mod, gain, weight, normed, whole, *slots):
    clips, rows, width_all = hidden.shape
    step = pl.program_id(0)

    @pl.when(step == 0)
    def _():
        chunk = 32
        for c in range(clips):
            for r in range(0, rows, chunk):
                x = hidden[c, r : r + chunk, :].astype(F32)
                centered = x - jnp.mean(x, axis=-1, keepdims=True)
                var = jnp.mean(centered * centered, axis=-1, keepdims=True)
                y = centered * lax.rsqrt(var + 1e-06) * (1.0 + mod[1, c : c + 1, :])
                normed[c, r : r + chunk, :] = (y + mod[0, c : c + 1, :]).astype(BF)

    x = normed[...].reshape(clips * rows, width_all)
    q = norm_heads(nn(x, weight[0]), gain[0:1, :])
    whole[...] = q.reshape(clips, rows, -1)
    width = q.shape[1] // per_step
    for j in range(per_step):
        part = q[:, j * width : (j + 1) * width].reshape(clips, rows, width)
        slot = lax.rem(step * per_step + j - pos[0] + groups, groups)
        for s in range(groups):

            @pl.when(slot == s)
            def _(s=s, part=part):
                slots[s][...] = part


def make_queries(pos, hidden, mod, gain, weight, groups):
    clips, rows, width_all = hidden.shape
    cols = weight.shape[2]
    per_step = 2 if groups % 2 == 0 else 1
    steps = groups // per_step
    width = cols // groups
    full = lambda shape: pl.BlockSpec(shape, lambda i, pos: (0,) * len(shape))
    return pl.pallas_call(
        functools.partial(query_kernel, groups, per_step),
        grid_spec=pltpu.PrefetchScalarGridSpec(
            num_scalar_prefetch=1,
            grid=(steps,),
            in_specs=[
                full(hidden.shape),
                full(mod.shape),
                full(gain.shape),
                pl.BlockSpec((1, width_all, width * per_step), lambda i, pos: (0, 0, i)),
            ],
            out_specs=[
                full(hidden.shape),
                pl.BlockSpec((clips, rows, width * per_step), lambda i, pos: (0, 0, i)),
            ]
            + [full((clips, rows, width))] * groups,
        ),
        out_shape=[
            jax.ShapeDtypeStruct(hidden.shape, BF),
            jax.ShapeDtypeStruct((clips, rows, cols), BF),
        ]
        + [jax.ShapeDtypeStruct((clips, rows, width), BF)] * groups,
        compiler_params=params(32),
        cost_estimate=pl.CostEstimate(
            flops=2 * clips * rows * width_all * cols,
            bytes_accessed=2 * width_all * cols + 8 * clips * rows * width_all,
            transcendentals=0,
        ),
        name="norm_and_queries",
    )(pos, hidden, mod, gain, weight)


def fresh_kernel(normed, gain, weight, out):
    clips, rows, width_all = normed.shape
    x = normed[...].reshape(clips * rows, width_all)
    made = nn(x, weight[0])

    @pl.when(pl.program_id(0) == 0)
    def _():
        out[0] = norm_heads(made, gain[1:2, :]).reshape(clips, rows, -1)

    @pl.when(pl.program_id(0) == 1)
    def _():
        out[0] = made.astype(BF).reshape(clips, rows, -1)


def make_fresh(normed, gain, weight):
    clips, rows, width_all = normed.shape
    cols = weight.shape[2]
    block = math.gcd(cols, 768)
    return pl.pallas_call(
        fresh_kernel,
        grid=(2, cols // block),
        in_specs=[
            pl.BlockSpec(normed.shape, lambda j, i: (0, 0, 0)),
            pl.BlockSpec(gain.shape, lambda j, i: (0, 0)),
            pl.BlockSpec((1, width_all, block), lambda j, i: (j + 1, 0, i)),
        ],
        out_specs=pl.BlockSpec((1, clips, rows, block), lambda j, i: (j, 0, 0, i)),
        out_shape=jax.ShapeDtypeStruct((2, clips, rows, cols), BF),
        compiler_params=params(32),
        cost_estimate=pl.CostEstimate(
            flops=4 * clips * rows * width_all * cols,
            bytes_accessed=4 * width_all * cols,
            transcendentals=0,
        ),
        name="fresh_keys_and_values",
    )(normed, gain, weight)


def own_kernel(q, kv, acc, top, total):
    rows = q.shape[1]
    ones = jnp.ones((rows, HEAD), BF)
    for h in range(q.shape[2] // HEAD):
        at = slice(h * HEAD, (h + 1) * HEAD)
        scores = nt(q[0, :, at], kv[0, 0, :, at])
        peak = jnp.max(scores, axis=-1, keepdims=True)
        weights = jnp.exp2((scores - peak) * SCALE2).astype(BF)
        summed = nn(weights, jnp.concatenate([kv[1, 0, :, at], ones], axis=1))
        acc[0, :, at] = summed[:, :HEAD]
        total[0, :, at] = summed[:, HEAD:]
        top[0, :, at] = jnp.broadcast_to(peak * SCALE2, (rows, HEAD))


def attend_own(queries, fresh):
    clips, rows, cols = queries.shape
    wide = jax.ShapeDtypeStruct(queries.shape, F32)
    block = pl.BlockSpec((1, rows, cols), lambda c: (c, 0, 0))
    return pl.pallas_call(
        own_kernel,
        grid=(clips,),
        in_specs=[block, pl.BlockSpec((2, 1, rows, cols), lambda c: (0, c, 0, 0))],
        out_specs=[block] * 3,
        out_shape=[wide] * 3,
        compiler_params=params(24),
        cost_estimate=pl.CostEstimate(
            flops=4 * clips * rows * rows * cols,
            bytes_accessed=18 * clips * rows * cols,
            transcendentals=clips * rows * rows * cols // HEAD,
        ),
        name="attend_own",
    )(queries, fresh)


def group_kernel(shifts, inner, blocks, first, last, *refs):
    refs = list(refs)
    queries = [refs.pop(0) for _ in range(blocks)]
    cached = [[refs.pop(0) for _ in range(inner)] for _ in shifts]
    state = None if first else (refs.pop(0), refs.pop(0))
    outs = refs
    rows, width = queries[0].shape[1:]
    ones = jnp.ones((inner * rows, HEAD), BF)
    for h in range(width // HEAD):
        at = slice(h * HEAD, (h + 1) * HEAD)
        keys = [jnp.concatenate([r[0, 0, :, at] for r in g], axis=0) for g in cached]
        values = [
            jnp.concatenate([jnp.concatenate([r[1, 0, :, at] for r in g], axis=0), ones], axis=1)
            for g in cached
        ]
        for b in range(blocks):
            q = queries[b][0, :, at]
            scores = []
            for s, k in zip(shifts, keys):
                sc = nt(q, k)
                if s == b:
                    sc = jnp.concatenate(
                        [jnp.full((rows, rows), -1e30, F32), sc[:, rows:]], axis=1
                    )
                scores.append(sc)
            peak = functools.reduce(
                jnp.maximum, [jnp.max(sc, axis=-1, keepdims=True) for sc in scores]
            )
            if not first:
                before = state[0][0, h, b]
                peak = jnp.maximum(before, peak)
            peak = jnp.broadcast_to(peak, (rows, HEAD))
            wide = jnp.concatenate([peak] * inner, axis=1)
            summed = None
            for sc, v in zip(scores, values):
                part = nn(jnp.exp2((sc - wide) * SCALE2).astype(BF), v)
                summed = part if summed is None else summed + part
            if not first:
                keep = jnp.exp2((before - peak) * SCALE2)
                summed = summed + state[1][0, h, b] * jnp.concatenate([keep, keep], axis=1)
            if last:
                total = summed[:, HEAD:]
                outs[b][0, 0:rows, at] = (summed[:, :HEAD] / total).astype(BF)
                level = jnp.transpose(peak * SCALE2 + jnp.log2(total))[0:8, :]
                high = level.astype(BF)
                mid = (level - high.astype(F32)).astype(BF)
                low = (level - high.astype(F32) - mid.astype(F32)).astype(BF)
                row = lax.broadcasted_iota(jnp.int32, (8, HEAD), 0)
                three = jnp.where(
                    row == 0,
                    high.astype(F32),
                    jnp.where(row == 1, mid.astype(F32), low.astype(F32)),
                )
                outs[b][0, rows : rows + EXTRA, at] = jnp.concatenate([three, three], axis=0).astype(BF)
            else:
                outs[0][0, h, b] = peak
                outs[1][0, h, b] = summed


def attend_groups(queries, cached, shifts, state, last):
    blocks = len(queries)
    clips, rows, width = queries[0].shape
    heads = width // HEAD
    inner = len(cached[0])
    first = state is None
    q_spec = pl.BlockSpec((1, rows, width), lambda c: (c, 0, 0))
    kv_spec = pl.BlockSpec((2, 1, rows, width), lambda c: (0, c, 0, 0))
    top_spec = pl.BlockSpec((1, heads, blocks, rows, HEAD), lambda c: (c, 0, 0, 0, 0))
    sum_spec = pl.BlockSpec((1, heads, blocks, rows, 2 * HEAD), lambda c: (c, 0, 0, 0, 0))
    flat = [a for g in cached for a in g]
    args = list(queries) + flat + ([] if first else list(state))
    if last:
        out_specs = [pl.BlockSpec((1, rows + EXTRA, width), lambda c: (c, 0, 0))] * blocks
        out_shape = [jax.ShapeDtypeStruct((clips, rows + EXTRA, width), BF)] * blocks
    else:
        out_specs = [top_spec, sum_spec]
        out_shape = [
            jax.ShapeDtypeStruct((clips, heads, blocks, rows, HEAD), F32),
            jax.ShapeDtypeStruct((clips, heads, blocks, rows, 2 * HEAD), F32),
        ]
    pairs = clips * heads * blocks * rows * len(flat) * rows
    return pl.pallas_call(
        functools.partial(group_kernel, tuple(shifts), inner, blocks, first, last),
        grid=(clips,),
        in_specs=[q_spec] * blocks
        + [kv_spec] * len(flat)
        + ([] if first else [top_spec, sum_spec]),
        out_specs=out_specs,
        out_shape=out_shape,
        compiler_params=params(40),
        cost_estimate=pl.CostEstimate(
            flops=6 * pairs * HEAD,
            bytes_accessed=4 * clips * rows * width * len(flat),
            transcendentals=pairs,
        ),
        name="attend_groups",
    )(*args)


def out_kernel(groups, pos, *refs):
    back = refs[:groups]
    acc, top, total, weight, send, keep, product = refs[groups:]
    step = pl.program_id(0)
    clips, rows, width = acc.shape

    for s in range(groups):

        @pl.when(step == s)
        def _(s=s):
            parts = []
            for c in range(clips):
                cols = []
                for h in range(width // HEAD):
                    at = slice(h * HEAD, (h + 1) * HEAD)
                    three = back[s][c, rows : rows + 8, at].astype(F32)
                    level = three[0:1, :] + three[1:2, :] + three[2:3, :]
                    level = jnp.transpose(jnp.broadcast_to(level, (rows, HEAD)))
                    own = top[c, :, at]
                    peak = jnp.maximum(level, own)
                    w_own, w_back = jnp.exp2(own - peak), jnp.exp2(level - peak)
                    mixed = acc[c, :, at] * w_own + back[s][c, 0:rows, at].astype(F32) * w_back
                    cols.append((mixed / (total[c, :, at] * w_own + w_back)).astype(BF))
                parts.append(jnp.concatenate(cols, axis=1))
            part = nn(jnp.concatenate(parts, axis=0), weight[...])
            if s == 0:
                product[...] = part
            else:
                product[...] += part

    @pl.when(step == groups - 1)
    def _():
        half = product.shape[1] // 2
        mine = pl.multiple_of(pos[1] * half, HEAD)
        other = pl.multiple_of((1 - pos[1]) * half, HEAD)
        send[...] = product[:, pl.ds(other, half)].astype(BF).reshape(send.shape)
        keep[...] = product[:, pl.ds(mine, half)].reshape(keep.shape)


def project_out(pos, back, acc, top, total, weight):
    groups = len(back)
    clips, rows, width_all = acc.shape
    width = width_all // groups
    cols = weight.shape[1]
    full = lambda shape: pl.BlockSpec(shape, lambda i, pos: (0,) * len(shape))
    own = pl.BlockSpec((clips, rows, width), lambda i, pos: (0, 0, lax.rem(pos[0] + i, groups)))
    half = (clips, rows, cols // 2)
    return pl.pallas_call(
        functools.partial(out_kernel, groups),
        grid_spec=pltpu.PrefetchScalarGridSpec(
            num_scalar_prefetch=1,
            grid=(groups,),
            in_specs=[full(back[0].shape)] * groups
            + [own] * 3
            + [pl.BlockSpec((width, cols), lambda i, pos: (lax.rem(pos[0] + i, groups), 0))],
            out_specs=[full(half), full(half)],
            scratch_shapes=[pltpu.VMEM((clips * rows, cols), F32)],
        ),
        out_shape=[jax.ShapeDtypeStruct(half, BF), jax.ShapeDtypeStruct(half, F32)],
        compiler_params=params(32),
        cost_estimate=pl.CostEstimate(
            flops=2 * clips * rows * width_all * cols,
            bytes_accessed=2 * width_all * cols,
            transcendentals=2 * clips * rows * width_all,
        ),
        name="merge_and_project",
    )(pos, *back, acc, top, total, weight)


def final_kernel(pos, hidden, mod, keep, got, out):
    for c in range(hidden.shape[0]):
        total = keep[c] + got[c].astype(F32)
        out[c] = (hidden[c].astype(F32) + mod[2, c : c + 1, :] * total).astype(BF)


def finish(pos, hidden, mod, keep, got):
    full = lambda shape: pl.BlockSpec(shape, lambda i, pos: (0,) * len(shape))
    half = keep.shape
    return pl.pallas_call(
        final_kernel,
        grid_spec=pltpu.PrefetchScalarGridSpec(
            num_scalar_prefetch=1,
            grid=(1,),
            in_specs=[
                pl.BlockSpec(half, lambda i, pos: (0, 0, pos[1])),
                pl.BlockSpec(mod.shape[:2] + half[2:], lambda i, pos: (0, 0, pos[1])),
                full(half),
                full(half),
            ],
            out_specs=full(half),
        ),
        out_shape=jax.ShapeDtypeStruct(half, BF),
        compiler_params=params(24),
        name="gate_and_add",
    )(pos, hidden, mod, keep, got)


def spread_heads(groups, hidden_states, modulation, qkv_weight, out_weight, qk_gain, stale_kv):
    patches = lax.axis_size("patch")
    inner = patches // groups
    plane = lax.axis_index("patch") // inner
    pos = jnp.stack([plane, lax.axis_index("tp")]).astype(jnp.int32)

    def along(value, shift):
        pairs = [(i, (i + inner * shift) % patches) for i in range(patches)]
        return lax.ppermute(value, "patch", pairs)

    def across(value, bit):
        return lax.ppermute(value, "patch", [(i, i ^ bit) for i in range(patches)])

    weights = jnp.transpose(qkv_weight, (1, 0, 2))
    cut = cut_stale(pos, stale_kv, groups)
    order = [1, 3, 2] if groups == 4 else list(range(1, groups))
    held = {0: [cut[0]]}
    for s in order:
        held[s] = [along(cut[s], s)]
    bit = inner // 2
    while bit:
        for s in held:
            held[s] = held[s] + [across(v, bit) for v in held[s]]
        bit //= 2
    normed, queries, *slots = make_queries(pos, hidden_states, modulation, qk_gain, weights, groups)
    asked = [slots[0]] + [along(slots[s], s) for s in range(1, groups)]
    fresh_kv = make_fresh(normed, qk_gain, weights)
    acc, top, total = attend_own(queries, fresh_kv)

    calls = [[0, 1, 3], [2]] if groups == 4 else [[s] for s in range(groups)]
    state = None
    for at, shifts in enumerate(calls):
        state = attend_groups(asked, [held[s] for s in shifts], shifts, state, at == len(calls) - 1)
    back = [state[0]] + [along(state[s], -s) for s in range(1, groups)]
    send, keep = project_out(pos, back, acc, top, total, out_weight)
    got = lax.ppermute(send, "tp", [(0, 1), (1, 0)])
    mixed = finish(pos, hidden_states, modulation, keep, got)
    return mixed, fresh_kv


def head_norm(values_in, gain_row, heads_here):
    shaped = values_in.reshape(values_in.shape[0], values_in.shape[1], heads_here, HEAD)
    square_mean = jnp.mean(shaped * shaped, axis=-1, keepdims=True)
    return (shaped * lax.rsqrt(square_mean + 1e-06) * gain_row).astype(BF)


def gather_all(hidden_states, modulation, qkv_weight, out_weight, qk_gain, stale_kv):
    clip_count, row_count, width_all = hidden_states.shape
    heads_here = qkv_weight.shape[2] // HEAD
    inputs = hidden_states.astype(F32)
    feature_mean = jnp.mean(inputs, axis=-1, keepdims=True)
    centered = inputs - feature_mean
    feature_var = jnp.mean(centered * centered, axis=-1, keepdims=True)
    normed = (
        centered * lax.rsqrt(feature_var + 1e-06) * (1.0 + modulation[1][:, None, :])
        + modulation[0][:, None, :]
    ).astype(BF)
    projected = jnp.einsum("ctd,dkh->kcth", normed, qkv_weight, preferred_element_type=F32)
    queries = head_norm(projected[0], qk_gain[0], heads_here)
    keys_new = head_norm(projected[1], qk_gain[1], heads_here)
    values_new = projected[2].astype(BF).reshape(clip_count, row_count, heads_here, HEAD)
    fresh_kv = jnp.stack(
        [keys_new.reshape(clip_count, row_count, -1), values_new.reshape(clip_count, row_count, -1)]
    )
    own_first = lax.axis_index("patch") * row_count
    gathered = lax.all_gather(stale_kv, "patch", axis=2, tiled=True)
    gathered = lax.dynamic_update_slice_in_dim(gathered, fresh_kv, own_first, 2)
    count = gathered.shape[2]
    tile_keys = gathered[0].reshape(clip_count, count, heads_here, HEAD)
    tile_values = gathered[1].reshape(clip_count, count, heads_here, HEAD)
    scores = jnp.einsum("cqhd,ckhd->chqk", queries, tile_keys, preferred_element_type=F32)
    scores = scores * HEAD ** (-0.5)
    expo = jnp.exp(scores - jnp.max(scores, axis=-1, keepdims=True))
    summed = jnp.einsum(
        "chqk,ckhd->chqd", expo.astype(BF), tile_values, preferred_element_type=F32
    )
    attended = (summed / jnp.sum(expo, axis=-1)[..., None]).astype(BF)
    attended = jnp.transpose(attended, (0, 2, 1, 3)).reshape(clip_count, row_count, -1)
    product = jnp.einsum("cth,hd->ctd", attended, out_weight, preferred_element_type=F32)
    col_count = width_all // lax.axis_size("tp")
    col_first = lax.axis_index("tp") * col_count
    summed_part = lax.psum_scatter(
        product.astype(BF), "tp", scatter_dimension=2, tiled=True
    ).astype(F32)
    input_part = lax.dynamic_slice_in_dim(inputs, col_first, col_count, 2)
    gate_part = lax.dynamic_slice_in_dim(modulation[2], col_first, col_count, 1)
    mixed = (input_part + gate_part[:, None, :] * summed_part).astype(BF)
    return (mixed, fresh_kv)


def per_device(*arrays):
    heads_here = arrays[2].shape[2] // HEAD
    patches = lax.axis_size("patch")
    groups = math.gcd(heads_here, patches)
    inner = patches // groups
    if groups > 1 and inner & (inner - 1) == 0 and lax.axis_size("tp") == 2:
        return spread_heads(groups, *arrays)
    return gather_all(*arrays)


def solution(mesh):
    in_specs = (
        P(None, "patch", None),
        P(),
        P(None, None, "tp"),
        P("tp", None),
        P(),
        P(None, None, "patch", "tp"),
    )
    out_specs = (P(None, "patch", "tp"), P(None, None, "patch", "tp"))
    return jax.shard_map(
        per_device, mesh=mesh, in_specs=in_specs, out_specs=out_specs, check_vma=False
    )
```

time: 253 us -> 140 us (0.55)
  waiting for transfers between devices: 125 us -> 64.5 us
  matrix products: 53.6 us -> 0 us
  Pallas kernels: 0 us -> 43.4 us
  local copies, waits for them, and re-layouts: 38.4 us -> 4.41 us
  starting transfers between devices: 0.08 us -> 26.3 us
  other arithmetic: 21.1 us -> 0.08 us
  between operations: 14.2 us -> 0.8 us
    all_gather x1 -> x0, waiting for transfers between devices: 104 us -> none  [per_device(): gathered = lax.all_gather(stale_kv, 'patch', axis=2, tiled=True)]
    ppermute x0 -> x22, waiting for transfers between devices: none -> 64.5 us  [the longest x9 38.8 us: along(): return lax.ppermute(value, 'patch', pairs)]
    dot_general x6 -> x0, matrix products: 53.6 us -> none  [the longest x1 16.4 us: per_device(): jnp.einsum('chqk,ckhd->chqd', expo.astype(jnp.bfloat16), tile_values, pre...]
    pallas_call x0 -> x8, Pallas kernels: none -> 43.4 us  [the longest x1 11.6 us: make_fresh(): pl.pallas_call(fresh_kernel, grid=(2, cols // block), in_specs=[pl.BlockS...]
    ppermute x0 -> x22, starting transfers between devices: none -> 26.3 us  [the longest x9 18.1 us: along(): return lax.ppermute(value, 'patch', pairs)]
    slice x5 -> x0, local copies, waits for them, and re-layouts: 23.8 us -> none  [the longest x1 17.7 us: per_device(): tile_keys = gathered[0].reshape(clip_count, count, heads_here, HEAD)]
    reduce_scatter x1 -> x0, waiting for transfers between devices: 21.6 us -> none  [per_device(): lax.psum_scatter(product.astype(jnp.bfloat16), 'tp', scatter_dimension=2,...]
    reduce_sum x6 -> x0, other arithmetic: 12.5 us -> none  [the longest x1 11.1 us: per_device(): new_sum = start_sum * rescale + jnp.sum(expo, axis=-1)]
  transfers between devices with their start and end apart: 2 -> 22, of which waited for: 2 -> 6; matrix products, arithmetic and copies ran while one was open for 14% -> 0% of each run, Pallas kernels for 0% -> 18%
where the time goes in v1:
time: 140 us
  waiting for transfers between devices  64.5 us (46%)
  Pallas kernels  43.4 us (31%)
  starting transfers between devices  26.3 us (19%)
  local copies, waits for them, and re-layouts  4.41 us (3%)
    ppermute x9, waiting for transfers between devices, along(): return lax.ppermute(value, 'patch', pairs)  38.8 us
    ppermute x9, starting transfers between devices, along(): return lax.ppermute(value, 'patch', pairs)  18.1 us
    ppermute x1, waiting for transfers between devices, spread_heads(): got = lax.ppermute(send, 'tp', [(0, 1), (1, 0)])  17.7 us
    pallas_call x1, Pallas kernels, make_fresh(): pl.pallas_call(fresh_kernel, grid=(2, cols // block), in_specs=[pl.BlockS...  11.6 us
    pallas_call x2, Pallas kernels, attend_groups(): pl.pallas_call(functools.partial(group_kernel, tuple(shifts), inner, bloc...  9.83 us
    ppermute x12, waiting for transfers between devices, across(): return lax.ppermute(value, 'patch', [(i, i ^ bit) for i in range(patches)])  8.01 us
    pallas_call x1, Pallas kernels, make_queries(): pl.pallas_call(functools.partial(query_kernel, groups, per_step), grid_sp...  7.38 us
    ppermute x12, starting transfers between devices, across(): return lax.ppermute(value, 'patch', [(i, i ^ bit) for i in range(patches)])  6.54 us
  transfers between devices with their start and end apart: 22, of which 6 were waited for; matrix products, arithmetic and copies ran while one was open for 0% of the time, Pallas kernels for 18%

profile of v1, /device:TPU:0, one launch (start us, length us, event | category | flops | bytes accessed | tf_op | source)
XLA Modules:
  0.0 139.5 jit_solution(10927205610066633731)
XLA Ops:
  0.6 0.1 pad_add_fusion.pos
  0.7 1.4 %copy-done = bf16[2,128,3072]{2,1,0:T(8,128)(2,1)S(1)} copy-done((bf16[2,128,3072]{2,1,0:T(8,128)(2,1)S(1)}, bf16[2,128,3072]{2,1,0:T(8,128)(2,1)}, u32[]{:S(2)}) %copy-start) | copy-done | bytes 1572888
  2.1 0.9 copy-done.4
  3.0 0.7 copy-done.6
  3.7 7.4 %norm_and_queries.1 = (bf16[2,128,3072]{2,1,0:T(8,128)(2,1)S(1)}, bf16[2,128,1536]{2,1,0:T(8,128)(2,1)S(1)}, bf16[2,128,384]{2,1,0:T(8,128)(2,1)S(1)}, bf16[2,12...) custom-call(s32[2]{0:T(128)S(1)} %pad_add_fusion.pos, ...), custom_call_target="tpu_custom_call" | custom-call | flops 2415919104 | bytes 15728640 | tf_op jit(solution)/shard_map/norm_and_queries/pallas_call | solution.py:106
  11.1 3.1 %collective-permute-start = (bf16[2,128,384]{2,1,0:T(8,128)(2,1)S(1)}, bf16[2,128,384]{2,1,0:T(8,128)(2,1)S(1)}, u32[]{:S(2)}, u32[]{:S(2)}) collective-permute-start(bf16[2,128,384]{2,1,0:T(8,128)(2,1)S(1)} %get-tuple-element.24), channel_id=1, source_target_pairs={{0,8},{2,10},{4,12},{6,14},{8,16},{10,18},{12,20},{14,22},{16,24},... | collective-permute-start | bytes 589832 | tf_op jit(solution)/shard_map/ppermute | solution.py:414
  14.2 0.0 copy-done.3
  14.2 0.8 cut_stale.1
  14.9 1.6 %collective-permute-start.10 = (bf16[2,2,128,384]{3,2,1,0:T(8,128)(2,1)S(1)}, bf16[2,2,128,384]{3,2,1,0:T(8,128)(2,1)S(1)}, u32[]{:S(2)}, u32[]{:S(2)}) collective-permute-start(bf16[2,2,128,384]{3,2,1,0:T(8,128)(2,1)S(1)} %get-tuple-element.29), channel_id=1, source_target_pairs={{0,8},{2,10},{4,12},{6,14},{8,16},{10,18},{12,20},{14,22},{16,24},... | collective-permute-start | bytes 1179656 | tf_op jit(solution)/shard_map/ppermute | solution.py:414
  16.6 2.2 %collective-permute-start.14 = (bf16[2,2,128,384]{3,2,1,0:T(8,128)(2,1)S(1)}, bf16[2,2,128,384]{3,2,1,0:T(8,128)(2,1)S(1)}, u32[]{:S(2)}, u32[]{:S(2)}) collective-permute-start(bf16[2,2,128,384]{3,2,1,0:T(8,128)(2,1)S(1)} %get-tuple-element.30), channel_id=1, source_target_pairs={{0,24},{2,26},{4,28},{6,30},{8,0},{10,2},{12,4},{14,6},{16,8},{18,... | collective-permute-start | bytes 1179656 | tf_op jit(solution)/shard_map/ppermute | solution.py:414
  18.8 1.5 %collective-permute-start.7 = (bf16[2,2,128,384]{3,2,1,0:T(8,128)(2,1)S(1)}, bf16[2,2,128,384]{3,2,1,0:T(8,128)(2,1)S(1)}, u32[]{:S(2)}, u32[]{:S(2)}) collective-permute-start(bf16[2,2,128,384]{3,2,1,0:T(8,128)(2,1)S(1)} %get-tuple-element.28.refs_4_), channel_id=1, source_target_pairs={{0,4},{2,6},{4,0},{6,2},{8,12},{10,14},{12,8},{14,10},{16,20},{18,... | collective-permute-start | bytes 1179656 | tf_op jit(solution)/shard_map/ppermute | solution.py:417
  20.3 0.8 collective-permute-start.1
  21.1 1.0 collective-permute-done.refs_1_
  22.1 1.9 %collective-permute-start.2 = (bf16[2,128,384]{2,1,0:T(8,128)(2,1)S(1)}, bf16[2,128,384]{2,1,0:T(8,128)(2,1)S(1)}, u32[]{:S(2)}, u32[]{:S(2)}) collective-permute-start(bf16[2,128,384]{2,1,0:T(8,128)(2,1)S(1)} %get-tuple-element.26), channel_id=1, source_target_pairs={{0,24},{2,26},{4,28},{6,30},{8,0},{10,2},{12,4},{14,6},{16,8},{18,... | collective-permute-start | bytes 589832 | tf_op jit(solution)/shard_map/ppermute | solution.py:414
  24.0 22.5 %collective-permute-done.1.refs_2_ = bf16[2,128,384]{2,1,0:T(8,128)(2,1)S(1)} collective-permute-done((bf16[2,128,384]{2,1,0:T(8,128)(2,1)S(1)}, bf16[2,128,384]{2,1,0:T(8,128)(2,1)S(1)}, u32[]{:S(2)}, u32[]{:S(2)}) %collective-permute-start.1) | collective-permute-done | bytes 196640 | tf_op jit(solution)/shard_map/ppermute | solution.py:414
  46.5 0.0 collective-permute-start.8
  46.5 0.0 collective-permute-done.2.refs_3_
  46.5 3.7 %collective-permute-start.3 = (bf16[2,2,128,384]{3,2,1,0:T(8,128)(2,1)S(1)}, bf16[2,2,128,384]{3,2,1,0:T(8,128)(2,1)S(1)}, u32[]{:S(2)}, u32[]{:S(2)}) collective-permute-start(bf16[2,2,128,384]{3,2,1,0:T(8,128)(2,1)S(1)} %get-tuple-element.27), channel_id=1, source_target_pairs={{0,16},{2,18},{4,20},{6,22},{8,24},{10,26},{12,28},{14,30},{16,0},... | collective-permute-start | bytes 1179656 | tf_op jit(solution)/shard_map/ppermute | solution.py:414
  50.1 0.0 collective-permute-done.10.refs_8_
  50.1 1.5 %collective-permute-start.11 = (bf16[2,2,128,384]{3,2,1,0:T(8,128)(2,1)S(1)}, bf16[2,2,128,384]{3,2,1,0:T(8,128)(2,1)S(1)}, u32[]{:S(2)}, u32[]{:S(2)}) collective-permute-start(bf16[2,2,128,384]{3,2,1,0:T(8,128)(2,1)S(1)} %collective-permute-done.10.refs_8_), channel_id=1, source_target_pairs={{0,4},{2,6},{4,0},{6,2},{8,12},{10,14},{12,8},{14,10},{16,20},{18,... | collective-permute-start | bytes 1179656 | tf_op jit(solution)/shard_map/ppermute | solution.py:417
  51.6 0.0 collective-permute-done.14.refs_12_
  51.6 0.5 collective-permute-start.15
  52.2 0.0 collective-permute-done.7.refs_5_
  52.2 0.0 collective-permute-start.12
  52.2 0.0 collective-permute-done.8.refs_6_
  52.2 0.5 collective-permute-start.16
  52.7 15.2 %collective-permute-done.3.refs_4_ = bf16[2,2,128,384]{3,2,1,0:T(8,128)(2,1)S(1)} collective-permute-done((bf16[2,2,128,384]{3,2,1,0:T(8,128)(2,1)S(1)}, bf16[2,2,128,384]{3,2,1,0:T(8,128)(2,1)S(1)}, u32[]{:S(2)}, u32[]{:S(2)}) %collective-permute-start.3) | collective-permute-done | bytes 393248 | tf_op jit(solution)/shard_map/ppermute | solution.py:414
  67.8 1.5 %collective-permute-start.4 = (bf16[2,2,128,384]{3,2,1,0:T(8,128)(2,1)S(1)}, bf16[2,2,128,384]{3,2,1,0:T(8,128)(2,1)S(1)}, u32[]{:S(2)}, u32[]{:S(2)}) collective-permute-start(bf16[2,2,128,384]{3,2,1,0:T(8,128)(2,1)S(1)} %collective-permute-done.3.refs_4_), channel_id=1, source_target_pairs={{0,4},{2,6},{4,0},{6,2},{8,12},{10,14},{12,8},{14,10},{16,20},{18,... | collective-permute-start | bytes 1179656 | tf_op jit(solution)/shard_map/ppermute | solution.py:417
  69.3 0.0 collective-permute-done.11.refs_9_
  69.3 0.0 collective-permute-start.9
  69.3 0.0 collective-permute-done.15.refs_13_
  69.4 0.5 collective-permute-start.13
  69.9 0.0 collective-permute-done.12.refs_10_
  69.9 0.1 collective-permute-start.17
  69.9 0.0 collective-permute-done.16.refs_14_
  69.9 0.4 collective-permute-start.5
  70.4 8.0 %collective-permute-done.4.refs_5_ = bf16[2,2,128,384]{3,2,1,0:T(8,128)(2,1)S(1)} collective-permute-done((bf16[2,2,128,384]{3,2,1,0:T(8,128)(2,1)S(1)}, bf16[2,2,128,384]{3,2,1,0:T(8,128)(2,1)S(1)}, u32[]{:S(2)}, u32[]{:S(2)}) %collective-permute-start.4) | collective-permute-done | bytes 393248 | tf_op jit(solution)/shard_map/ppermute | solution.py:417
  78.4 0.0 collective-permute-start.6
  78.4 0.0 collective-permute-done.9.refs_7_
  78.4 0.0 collective-permute-done.13.refs_11_
  78.4 0.0 collective-permute-done.17.refs_15_
  78.4 7.0 %attend_groups.2 = (f32[2,3,4,128,128]{4,3,2,1,0:T(8,128)S(1)}, f32[2,3,4,128,256]{4,3,2,1,0:T(8,128)S(1)}) custom-call(bf16[2,128,384]{2,1,0:T(8,128)(2,1)S(1)} %get-tuple-element.23.refs_0_, bf16[2,128,384]{2,1,0:T(8,128)(2,1)S(1)} %collective-permute-done.refs_1_, bf16[2,128,384]{2,1,0:T(8,128)(2,1)S(1)} %collective-permute-done.1.refs_2_, ...), custom_call_target="tpu_custom_call" | custom-call | flops 3623878656 | bytes 4718592 | tf_op jit(solution)/shard_map/attend_groups/pallas_call | solution.py:291
  85.3 0.0 collective-permute-done.5.refs_6_
  85.4 0.0 collective-permute-done.6.refs_7_
  85.4 0.0 copy-start.7
  85.4 2.9 %attend_groups.3 = (bf16[2,144,384]{2,1,0:T(8,128)(2,1)S(1)}, bf16[2,144,384]{2,1,0:T(8,128)(2,1)S(1)}, bf16[2,144,384]{2,1,0:T(8,128)(2,1)S(1)}, bf16[2,144,384]{2,1,0:T(8,128)(2,1)S(1)}) custom-call(bf16[2,128,384]{2,1,0:T(8,128)(2,1)S(1)} %get-tuple-element.23.refs_0_, bf16[2,128,384]{2,1,0:T(8,128)(2,1)S(1)} %collective-permute-done.refs_1_, ...), custom_call_target="tpu_custom_call" | custom-call | flops 1207959552 | bytes 1572864 | tf_op jit(solution)/shard_map/attend_groups/pallas_call | solution.py:291
  88.3 4.2 %collective-permute-start.18 = (bf16[2,144,384]{2,1,0:T(8,128)(2,1)S(1)}, bf16[2,144,384]{2,1,0:T(8,128)(2,1)S(1)}, u32[]{:S(2)}, u32[]{:S(2)}) collective-permute-start(bf16[2,144,384]{2,1,0:T(8,128)(2,1)S(1)} %get-tuple-element.34), channel_id=1, source_target_pairs={{0,24},{2,26},{4,28},{6,30},{8,0},{10,2},{12,4},{14,6},{16,8},{18,... | collective-permute-start | bytes 663560 | tf_op jit(solution)/shard_map/ppermute | solution.py:414
  92.4 0.0 collective-permute-start.19
  92.4 0.6 collective-permute-start.20
  93.1 0.0 copy-done.7
  93.1 11.6 %fresh_keys_and_values.1.kv = bf16[2,2,128,1536]{3,2,1,0:T(8,128)(2,1)} custom-call(bf16[2,128,3072]{2,1,0:T(8,128)(2,1)S(1)} %get-tuple-element.38.normed, f32[2,128]{1,0:T(2,128)S(1)} %copy-done.7, bf16[3,3072,1536]{2,1,0:T(8,128)(2,1)} %bitcast.6), custom_call_target="tpu_custom_call" | custom-call | flops 4831838208 | bytes 18874368 | tf_op jit(solution)/shard_map/fresh_keys_and_values/pallas_call | solution.py:156
  104.7 1.4 %copy-done.2 = bf16[2,2,128,1536]{3,2,1,0:T(8,128)(2,1)S(1)} copy-done((bf16[2,2,128,1536]{3,2,1,0:T(8,128)(2,1)S(1)}, bf16[2,2,128,1536]{3,2,1,0:T(8,128)(2,1)}, u32[]{:S(2)}) %copy-start.2) | copy-done | bytes 1572888
  106.1 6.1 %attend_own.1 = (f32[2,128,1536]{2,1,0:T(8,128)S(1)}, f32[2,128,1536]{2,1,0:T(8,128)S(1)}, f32[2,128,1536]{2,1,0:T(8,128)S(1)}) custom-call(bf16[2,128,1536]{2,1,0:T(8,128)(2,1)S(1)} %get-tuple-element.37.q, bf16[2,2,128,1536]{3,2,1,0:T(8,128)(2,1)S(1)} %copy-done.2), custom_call_target="tpu_custom_call" | custom-call | flops 201326592 | bytes 7077888 | tf_op jit(solution)/shard_map/attend_own/pallas_call | solution.py:194
  112.1 0.0 collective-permute-done.18.refs_1_
  112.2 0.2 collective-permute-done.19.refs_2_
  112.3 0.0 collective-permute-done.20.refs_3_
  112.3 0.0 slice-done
  112.3 0.0 copy-start.1
  112.4 0.0 copy-start.5
  112.4 5.8 %merge_and_project.1 = (bf16[2,128,1536]{2,1,0:T(8,128)(2,1)S(1)}, f32[2,128,1536]{2,1,0:T(8,128)S(1)}) custom-call(s32[2]{0:T(128)S(1)} %pad_add_fusion.pos, bf16[2,144,384]{2,1,0:T(8,128)(2,1)S(1)} %get-tuple-element.33.refs_0_, bf16[2,144,384]{2,1,0:T(8,128)(2,1)S(1)} %collective-permute-done.18.refs_1_, ...), custom_call_target="tpu_custom_call" | custom-call | flops 2415919104 | bytes 9437184 | tf_op jit(solution)/shard_map/merge_and_project/pallas_call | solution.py:356
  118.2 1.6 %collective-permute-start.21 = (bf16[2,128,1536]{2,1,0:T(8,128)(2,1)S(1)}, bf16[2,128,1536]{2,1,0:T(8,128)(2,1)S(1)}, u32[]{:S(2)}, u32[]{:S(2)}) collective-permute-start(bf16[2,128,1536]{2,1,0:T(8,128)(2,1)S(1)} %get-tuple-element.43), channel_id=1, source_target_pairs={{0,1},{1,0},{2,3},{3,2},{4,5},{5,4},{6,7},{7,6},{8,9},{9,8},{10,11... | collective-permute-start | bytes 2359304 | tf_op jit(solution)/shard_map/ppermute | solution.py:441
  119.8 17.7 %collective-permute-done.21.got = bf16[2,128,1536]{2,1,0:T(8,128)(2,1)S(1)} collective-permute-done((bf16[2,128,1536]{2,1,0:T(8,128)(2,1)S(1)}, bf16[2,128,1536]{2,1,0:T(8,128)(2,1)S(1)}, u32[]{:S(2)}, u32[]{:S(2)}) %collective-permute-start.21) | collective-permute-done | bytes 786464 | tf_op jit(solution)/shard_map/ppermute | solution.py:441
  137.5 0.0 copy-done.5
  137.5 2.0 %gate_and_add.1 = bf16[2,128,1536]{2,1,0:T(8,128)(2,1)} custom-call(s32[2]{0:T(128)S(1)} %pad_add_fusion.pos, bf16[2,128,3072]{2,1,0:T(8,128)(2,1)S(1)} %copy-done.1, f32[3,2,3072]{2,1,0:T(2,128)S(1)} %copy-done.5, f32[2,128,1536]{2,1,0:T(8,128)S(1)} %get-tuple-element.42.keep, bf16[2,128,1536]{2,1,0:T(8,128)(2,1)S(1)} %collective-permute-done.21.got), custom_call_target="tpu_custom_call" | custom-call | tf_op jit(solution)/shard_map/gate_and_add/pallas_call | solution.py:387
  (12 shorter events, 0.0 us)
Async XLA Ops:
  0.7 1.4 %copy-start = (bf16[2,128,3072]{2,1,0:T(8,128)(2,1)S(1)}, bf16[2,128,3072]{2,1,0:T(8,128)(2,1)}, u32[]{:S(2)}) copy-start(bf16[2,128,3072]{2,1,0:T(8,128)(2,1)} %hidden.3) | copy-start | bytes 4718596
  2.1 0.9 copy-start.4
  3.0 0.7 copy-start.6
  3.7 10.5 %copy-start.3 = (bf16[2,2,128,1536]{3,2,1,0:T(8,128)(2,1)S(1)}, bf16[2,2,128,1536]{3,2,1,0:T(8,128)(2,1)}, u32[]{:S(2)}) copy-start(bf16[2,2,128,1536]{3,2,1,0:T(8,128)(2,1)} %stale.1) | copy-start | bytes 4718596
  11.1 11.0 %collective-permute-start = (bf16[2,128,384]{2,1,0:T(8,128)(2,1)S(1)}, bf16[2,128,384]{2,1,0:T(8,128)(2,1)S(1)}, u32[]{:S(2)}, u32[]{:S(2)}) collective-permute-start(bf16[2,128,384]{2,1,0:T(8,128)(2,1)S(1)} %get-tuple-element.24), channel_id=1, source_target_pairs={{0,8},{2,10},{4,12},{6,14},{8,16},{10,18},{12,20},{14,22},{16,24},... | collective-permute-start | bytes 589832 | tf_op jit(solution)/shard_map/ppermute | solution.py:414
  14.9 35.2 %collective-permute-start.10 = (bf16[2,2,128,384]{3,2,1,0:T(8,128)(2,1)S(1)}, bf16[2,2,128,384]{3,2,1,0:T(8,128)(2,1)S(1)}, u32[]{:S(2)}, u32[]{:S(2)}) collective-permute-start(bf16[2,2,128,384]{3,2,1,0:T(8,128)(2,1)S(1)} %get-tuple-element.29), channel_id=1, source_target_pairs={{0,8},{2,10},{4,12},{6,14},{8,16},{10,18},{12,20},{14,22},{16,24},... | collective-permute-start | bytes 1179656 | tf_op jit(solution)/shard_map/ppermute | solution.py:414
  16.6 35.1 %collective-permute-start.14 = (bf16[2,2,128,384]{3,2,1,0:T(8,128)(2,1)S(1)}, bf16[2,2,128,384]{3,2,1,0:T(8,128)(2,1)S(1)}, u32[]{:S(2)}, u32[]{:S(2)}) collective-permute-start(bf16[2,2,128,384]{3,2,1,0:T(8,128)(2,1)S(1)} %get-tuple-element.30), channel_id=1, source_target_pairs={{0,24},{2,26},{4,28},{6,30},{8,0},{10,2},{12,4},{14,6},{16,8},{18,... | collective-permute-start | bytes 1179656 | tf_op jit(solution)/shard_map/ppermute | solution.py:414
  18.8 33.4 %collective-permute-start.7 = (bf16[2,2,128,384]{3,2,1,0:T(8,128)(2,1)S(1)}, bf16[2,2,128,384]{3,2,1,0:T(8,128)(2,1)S(1)}, u32[]{:S(2)}, u32[]{:S(2)}) collective-permute-start(bf16[2,2,128,384]{3,2,1,0:T(8,128)(2,1)S(1)} %get-tuple-element.28.refs_4_), channel_id=1, source_target_pairs={{0,4},{2,6},{4,0},{6,2},{8,12},{10,14},{12,8},{14,10},{16,20},{18,... | collective-permute-start | bytes 1179656 | tf_op jit(solution)/shard_map/ppermute | solution.py:417
  20.3 26.2 %collective-permute-start.1 = (bf16[2,128,384]{2,1,0:T(8,128)(2,1)S(1)}, bf16[2,128,384]{2,1,0:T(8,128)(2,1)S(1)}, u32[]{:S(2)}, u32[]{:S(2)}) collective-permute-start(bf16[2,128,384]{2,1,0:T(8,128)(2,1)S(1)} %get-tuple-element.25), channel_id=1, source_target_pairs={{0,16},{2,18},{4,20},{6,22},{8,24},{10,26},{12,28},{14,30},{16,0},... | collective-permute-start | bytes 589832 | tf_op jit(solution)/shard_map/ppermute | solution.py:414
  22.1 24.4 %collective-permute-start.2 = (bf16[2,128,384]{2,1,0:T(8,128)(2,1)S(1)}, bf16[2,128,384]{2,1,0:T(8,128)(2,1)S(1)}, u32[]{:S(2)}, u32[]{:S(2)}) collective-permute-start(bf16[2,128,384]{2,1,0:T(8,128)(2,1)S(1)} %get-tuple-element.26), channel_id=1, source_target_pairs={{0,24},{2,26},{4,28},{6,30},{8,0},{10,2},{12,4},{14,6},{16,8},{18,... | collective-permute-start | bytes 589832 | tf_op jit(solution)/shard_map/ppermute | solution.py:414
  46.5 5.7 %collective-permute-start.8 = (bf16[2,2,128,384]{3,2,1,0:T(8,128)(2,1)S(1)}, bf16[2,2,128,384]{3,2,1,0:T(8,128)(2,1)S(1)}, u32[]{:S(2)}, u32[]{:S(2)}) collective-permute-start(bf16[2,2,128,384]{3,2,1,0:T(8,128)(2,1)S(1)} %get-tuple-element.28.refs_4_), channel_id=1, source_target_pairs={{0,2},{2,0},{4,6},{6,4},{8,10},{10,8},{12,14},{14,12},{16,18},{18,... | collective-permute-start | bytes 1179656 | tf_op jit(solution)/shard_map/ppermute | solution.py:417
  46.5 21.4 %collective-permute-start.3 = (bf16[2,2,128,384]{3,2,1,0:T(8,128)(2,1)S(1)}, bf16[2,2,128,384]{3,2,1,0:T(8,128)(2,1)S(1)}, u32[]{:S(2)}, u32[]{:S(2)}) collective-permute-start(bf16[2,2,128,384]{3,2,1,0:T(8,128)(2,1)S(1)} %get-tuple-element.27), channel_id=1, source_target_pairs={{0,16},{2,18},{4,20},{6,22},{8,24},{10,26},{12,28},{14,30},{16,0},... | collective-permute-start | bytes 1179656 | tf_op jit(solution)/shard_map/ppermute | solution.py:414
  50.1 19.2 %collective-permute-start.11 = (bf16[2,2,128,384]{3,2,1,0:T(8,128)(2,1)S(1)}, bf16[2,2,128,384]{3,2,1,0:T(8,128)(2,1)S(1)}, u32[]{:S(2)}, u32[]{:S(2)}) collective-permute-start(bf16[2,2,128,384]{3,2,1,0:T(8,128)(2,1)S(1)} %collective-permute-done.10.refs_8_), channel_id=1, source_target_pairs={{0,4},{2,6},{4,0},{6,2},{8,12},{10,14},{12,8},{14,10},{16,20},{18,... | collective-permute-start | bytes 1179656 | tf_op jit(solution)/shard_map/ppermute | solution.py:417
  51.6 17.7 %collective-permute-start.15 = (bf16[2,2,128,384]{3,2,1,0:T(8,128)(2,1)S(1)}, bf16[2,2,128,384]{3,2,1,0:T(8,128)(2,1)S(1)}, u32[]{:S(2)}, u32[]{:S(2)}) collective-permute-start(bf16[2,2,128,384]{3,2,1,0:T(8,128)(2,1)S(1)} %collective-permute-done.14.refs_12_), channel_id=1, source_target_pairs={{0,4},{2,6},{4,0},{6,2},{8,12},{10,14},{12,8},{14,10},{16,20},{18,... | collective-permute-start | bytes 1179656 | tf_op jit(solution)/shard_map/ppermute | solution.py:417
  52.2 17.7 %collective-permute-start.12 = (bf16[2,2,128,384]{3,2,1,0:T(8,128)(2,1)S(1)}, bf16[2,2,128,384]{3,2,1,0:T(8,128)(2,1)S(1)}, u32[]{:S(2)}, u32[]{:S(2)}) collective-permute-start(bf16[2,2,128,384]{3,2,1,0:T(8,128)(2,1)S(1)} %collective-permute-done.10.refs_8_), channel_id=1, source_target_pairs={{0,2},{2,0},{4,6},{6,4},{8,10},{10,8},{12,14},{14,12},{16,18},{18,... | collective-permute-start | bytes 1179656 | tf_op jit(solution)/shard_map/ppermute | solution.py:417
  52.2 17.8 %collective-permute-start.16 = (bf16[2,2,128,384]{3,2,1,0:T(8,128)(2,1)S(1)}, bf16[2,2,128,384]{3,2,1,0:T(8,128)(2,1)S(1)}, u32[]{:S(2)}, u32[]{:S(2)}) collective-permute-start(bf16[2,2,128,384]{3,2,1,0:T(8,128)(2,1)S(1)} %collective-permute-done.14.refs_12_), channel_id=1, source_target_pairs={{0,2},{2,0},{4,6},{6,4},{8,10},{10,8},{12,14},{14,12},{16,18},{18,... | collective-permute-start | bytes 1179656 | tf_op jit(solution)/shard_map/ppermute | solution.py:417
  67.8 10.5 %collective-permute-start.4 = (bf16[2,2,128,384]{3,2,1,0:T(8,128)(2,1)S(1)}, bf16[2,2,128,384]{3,2,1,0:T(8,128)(2,1)S(1)}, u32[]{:S(2)}, u32[]{:S(2)}) collective-permute-start(bf16[2,2,128,384]{3,2,1,0:T(8,128)(2,1)S(1)} %collective-permute-done.3.refs_4_), channel_id=1, source_target_pairs={{0,4},{2,6},{4,0},{6,2},{8,12},{10,14},{12,8},{14,10},{16,20},{18,... | collective-permute-start | bytes 1179656 | tf_op jit(solution)/shard_map/ppermute | solution.py:417
  69.3 9.0 %collective-permute-start.9 = (bf16[2,2,128,384]{3,2,1,0:T(8,128)(2,1)S(1)}, bf16[2,2,128,384]{3,2,1,0:T(8,128)(2,1)S(1)}, u32[]{:S(2)}, u32[]{:S(2)}) collective-permute-start(bf16[2,2,128,384]{3,2,1,0:T(8,128)(2,1)S(1)} %collective-permute-done.7.refs_5_), channel_id=1, source_target_pairs={{0,2},{2,0},{4,6},{6,4},{8,10},{10,8},{12,14},{14,12},{16,18},{18,... | collective-permute-start | bytes 1179656 | tf_op jit(solution)/shard_map/ppermute | solution.py:417
  69.4 9.0 %collective-permute-start.13 = (bf16[2,2,128,384]{3,2,1,0:T(8,128)(2,1)S(1)}, bf16[2,2,128,384]{3,2,1,0:T(8,128)(2,1)S(1)}, u32[]{:S(2)}, u32[]{:S(2)}) collective-permute-start(bf16[2,2,128,384]{3,2,1,0:T(8,128)(2,1)S(1)} %collective-permute-done.11.refs_9_), channel_id=1, source_target_pairs={{0,2},{2,0},{4,6},{6,4},{8,10},{10,8},{12,14},{14,12},{16,18},{18,... | collective-permute-start | bytes 1179656 | tf_op jit(solution)/shard_map/ppermute | solution.py:417
  69.9 8.5 %collective-permute-start.17 = (bf16[2,2,128,384]{3,2,1,0:T(8,128)(2,1)S(1)}, bf16[2,2,128,384]{3,2,1,0:T(8,128)(2,1)S(1)}, u32[]{:S(2)}, u32[]{:S(2)}) collective-permute-start(bf16[2,2,128,384]{3,2,1,0:T(8,128)(2,1)S(1)} %collective-permute-done.15.refs_13_), channel_id=1, source_target_pairs={{0,2},{2,0},{4,6},{6,4},{8,10},{10,8},{12,14},{14,12},{16,18},{18,... | collective-permute-start | bytes 1179656 | tf_op jit(solution)/shard_map/ppermute | solution.py:417
  69.9 15.4 %collective-permute-start.5 = (bf16[2,2,128,384]{3,2,1,0:T(8,128)(2,1)S(1)}, bf16[2,2,128,384]{3,2,1,0:T(8,128)(2,1)S(1)}, u32[]{:S(2)}, u32[]{:S(2)}) collective-permute-start(bf16[2,2,128,384]{3,2,1,0:T(8,128)(2,1)S(1)} %collective-permute-done.3.refs_4_), channel_id=1, source_target_pairs={{0,2},{2,0},{4,6},{6,4},{8,10},{10,8},{12,14},{14,12},{16,18},{18,... | collective-permute-start | bytes 1179656 | tf_op jit(solution)/shard_map/ppermute | solution.py:417
  78.4 7.0 %collective-permute-start.6 = (bf16[2,2,128,384]{3,2,1,0:T(8,128)(2,1)S(1)}, bf16[2,2,128,384]{3,2,1,0:T(8,128)(2,1)S(1)}, u32[]{:S(2)}, u32[]{:S(2)}) collective-permute-start(bf16[2,2,128,384]{3,2,1,0:T(8,128)(2,1)S(1)} %collective-permute-done.4.refs_5_), channel_id=1, source_target_pairs={{0,2},{2,0},{4,6},{6,4},{8,10},{10,8},{12,14},{14,12},{16,18},{18,... | collective-permute-start | bytes 1179656 | tf_op jit(solution)/shard_map/ppermute | solution.py:417
  85.4 7.7 %copy-start.7 = (f32[2,128]{1,0:T(2,128)S(1)}, f32[2,128]{1,0:T(2,128)}, u32[]{:S(2)}) copy-start(f32[2,128]{1,0:T(2,128)} %gain.3) | copy-start | bytes 3076
  88.3 23.9 %collective-permute-start.18 = (bf16[2,144,384]{2,1,0:T(8,128)(2,1)S(1)}, bf16[2,144,384]{2,1,0:T(8,128)(2,1)S(1)}, u32[]{:S(2)}, u32[]{:S(2)}) collective-permute-start(bf16[2,144,384]{2,1,0:T(8,128)(2,1)S(1)} %get-tuple-element.34), channel_id=1, source_target_pairs={{0,24},{2,26},{4,28},{6,30},{8,0},{10,2},{12,4},{14,6},{16,8},{18,... | collective-permute-start | bytes 663560 | tf_op jit(solution)/shard_map/ppermute | solution.py:414
  92.4 19.9 %collective-permute-start.19 = (bf16[2,144,384]{2,1,0:T(8,128)(2,1)S(1)}, bf16[2,144,384]{2,1,0:T(8,128)(2,1)S(1)}, u32[]{:S(2)}, u32[]{:S(2)}) collective-permute-start(bf16[2,144,384]{2,1,0:T(8,128)(2,1)S(1)} %get-tuple-element.35), channel_id=1, source_target_pairs={{0,16},{2,18},{4,20},{6,22},{8,24},{10,26},{12,28},{14,30},{16,0},... | collective-permute-start | bytes 663560 | tf_op jit(solution)/shard_map/ppermute | solution.py:414
  92.4 19.9 %collective-permute-start.20 = (bf16[2,144,384]{2,1,0:T(8,128)(2,1)S(1)}, bf16[2,144,384]{2,1,0:T(8,128)(2,1)S(1)}, u32[]{:S(2)}, u32[]{:S(2)}) collective-permute-start(bf16[2,144,384]{2,1,0:T(8,128)(2,1)S(1)} %get-tuple-element.36), channel_id=1, source_target_pairs={{0,8},{2,10},{4,12},{6,14},{8,16},{10,18},{12,20},{14,22},{16,24},... | collective-permute-start | bytes 663560 | tf_op jit(solution)/shard_map/ppermute | solution.py:414
  93.1 19.2 %slice-start = ((s8[9437184]{0:T(1024)(128)(4,1)}), s8[4194304]{0:T(1024)(128)(4,1)S(1)}, s32[]{:S(2)}) async-start(s8[9437184]{0:T(1024)(128)(4,1)} %bitcast.3), calls=%async_computation | async-start | bytes 8388608
  93.1 19.2 %slice-start.1 = ((s8[9437184]{0:T(1024)(128)(4,1)}), s8[4194304]{0:T(1024)(128)(4,1)S(1)}, s32[]{:S(2)}) async-start(s8[9437184]{0:T(1024)(128)(4,1)} %bitcast.3), calls=%async_computation.1 | async-start | bytes 8388608
  93.1 19.3 %slice-start.2 = ((s8[9437184]{0:T(1024)(128)(4,1)}), s8[1048576]{0:T(1024)(128)(4,1)S(1)}, s32[]{:S(2)}) async-start(s8[9437184]{0:T(1024)(128)(4,1)} %bitcast.3), calls=%async_computation.2 | async-start | bytes 2097152
  104.7 1.4 %copy-start.2 = (bf16[2,2,128,1536]{3,2,1,0:T(8,128)(2,1)S(1)}, bf16[2,2,128,1536]{3,2,1,0:T(8,128)(2,1)}, u32[]{:S(2)}) copy-start(bf16[2,2,128,1536]{3,2,1,0:T(8,128)(2,1)} %fresh_keys_and_values.1.kv) | copy-start | bytes 4718596
  112.3 25.2 %copy-start.1 = (bf16[2,128,3072]{2,1,0:T(8,128)(2,1)S(1)}, bf16[2,128,3072]{2,1,0:T(8,128)(2,1)}, u32[]{:S(2)}) copy-start(bf16[2,128,3072]{2,1,0:T(8,128)(2,1)} %hidden.3) | copy-start | bytes 4718596
  112.4 25.2 %copy-start.5 = (f32[3,2,3072]{2,1,0:T(2,128)S(1)}, f32[3,2,3072]{2,1,0:T(2,128)}, u32[]{:S(2)}) copy-start(f32[3,2,3072]{2,1,0:T(2,128)} %mod.3) | copy-start | bytes 221188
  118.2 19.3 %collective-permute-start.21 = (bf16[2,128,1536]{2,1,0:T(8,128)(2,1)S(1)}, bf16[2,128,1536]{2,1,0:T(8,128)(2,1)S(1)}, u32[]{:S(2)}, u32[]{:S(2)}) collective-permute-start(bf16[2,128,1536]{2,1,0:T(8,128)(2,1)S(1)} %get-tuple-element.43), channel_id=1, source_target_pairs={{0,1},{1,0},{2,3},{3,2},{4,5},{5,4},{6,7},{7,6},{8,9},{9,8},{10,11... | collective-permute-start | bytes 2359304 | tf_op jit(solution)/shard_map/ppermute | solution.py:441

commit v2 on v0

v2 whole, which is shorter than its diff:
```python
import functools
import math

import jax
import jax.numpy as jnp
from jax import lax
from jax.experimental import pallas as pl
from jax.experimental.pallas import tpu as pltpu
from jax.sharding import PartitionSpec as P

HEAD = 128
EXTRA = 16
LOG2E = 1.4426950408889634
SCALE2 = HEAD ** (-0.5) * LOG2E
MIB = 1024 * 1024
BF = jnp.bfloat16
F32 = jnp.float32


SMALL = pl.CostEstimate(flops=1000, bytes_accessed=1000, transcendentals=0)
LARGE = pl.CostEstimate(flops=10**10, bytes_accessed=10**8, transcendentals=0)


def nt(a, b):
    return lax.dot_general(a, b, (((1,), (1,)), ((), ())), preferred_element_type=F32)


def nn(a, b):
    return lax.dot_general(a, b, (((1,), (0,)), ((), ())), preferred_element_type=F32)


def params(mib, **kw):
    return pltpu.CompilerParams(vmem_limit_bytes=mib * MIB, **kw)


def norm_heads(values, gain_row):
    parts = []
    for h in range(values.shape[1] // HEAD):
        v = values[:, h * HEAD : (h + 1) * HEAD]
        square_mean = jnp.mean(v * v, axis=-1, keepdims=True)
        parts.append((v * lax.rsqrt(square_mean + 1e-06) * gain_row).astype(BF))
    return jnp.concatenate(parts, axis=1)


def full(shape):
    return pl.BlockSpec(shape, lambda *_: (0,) * len(shape))


def out_of(shape, dtype=BF):
    return jax.ShapeDtypeStruct(shape, dtype)


ANYWHERE = pl.BlockSpec(memory_space=pltpu.HBM)
SCALARS = pl.BlockSpec(memory_space=pltpu.SMEM)


def copy_all(sems, pairs):
    copies = [pltpu.make_async_copy(a, b, sems.at[i]) for i, (a, b) in enumerate(pairs)]
    for c in copies:
        c.start()
    for c in copies:
        c.wait()


def cut_kernel(width, pos, stale, *rest):
    outs, sems = rest[:-1], rest[-1]
    pairs = []
    for s, out in enumerate(outs):
        cols = pl.ds(pl.multiple_of((pos[0] ^ s) * width, HEAD), width)
        pairs.append((stale.at[:, :, :, cols], out))
    copy_all(sems, pairs)


def cut_stale(pos, stale, groups):
    kv, clips, rows, cols = stale.shape
    width = cols // groups
    return pl.pallas_call(
        functools.partial(cut_kernel, width),
        out_shape=[out_of((kv, clips, rows, width))] * groups,
        in_specs=[SCALARS, ANYWHERE],
        out_specs=[ANYWHERE] * groups,
        scratch_shapes=[pltpu.SemaphoreType.DMA((groups,))],
        compiler_params=params(8),
        name="cut_stale",
    )(pos, stale)


def pack_kernel(pos, *refs):
    blocks, out, sems = refs[:-2], refs[-2], refs[-1]
    copy_all(sems, [(r.at[:, 1 - pos[2]], out.at[i]) for i, r in enumerate(blocks)])


def pack(pos, *blocks):
    kv, clips, rows, width = blocks[0].shape
    return pl.pallas_call(
        pack_kernel,
        out_shape=out_of((len(blocks), kv, rows, width)),
        in_specs=[SCALARS] + [ANYWHERE] * len(blocks),
        out_specs=ANYWHERE,
        scratch_shapes=[pltpu.SemaphoreType.DMA((len(blocks),))],
        compiler_params=params(8),
        name="pack",
    )(pos, *blocks)


def query_kernel(groups, per_step, pos, hidden, got, mod, gain, weight, normed, whole, *slots):
    rows = got.shape[0]
    step = pl.program_id(0)

    @pl.when(step == 0)
    def _():
        chunk = 32
        shift, scale = mod[0, pl.ds(pos[2], 1), :], 1.0 + mod[1, pl.ds(pos[2], 1), :]
        for half in range(2):
            for r in range(0, rows, chunk):
                x = hidden[0, r : r + chunk, :] if half == 0 else got[r : r + chunk, :]
                x = x.astype(F32)
                centered = x - jnp.mean(x, axis=-1, keepdims=True)
                var = jnp.mean(centered * centered, axis=-1, keepdims=True)
                y = centered * lax.rsqrt(var + 1e-06) * scale + shift
                normed[half * rows + r : half * rows + r + chunk, :] = y.astype(BF)

    q = norm_heads(nn(normed[...], weight[0]), gain[0:1, :])
    whole[...] = q
    width = q.shape[1] // per_step
    for j in range(per_step):
        part = q[:, j * width : (j + 1) * width]
        slot = (step * per_step + j) ^ pos[0]
        for s in range(groups):

            @pl.when(slot == s)
            def _(s=s, part=part):
                if s < 2:
                    slots[s][...] = part
                else:
                    slots[2 * s - 2][...] = part[:rows]
                    slots[2 * s - 1][...] = part[rows:]


def make_queries(pos, hidden, got, mod, gain, weight, groups):
    rows, width_all = got.shape
    cols = weight.shape[2]
    per_step = 2 if groups % 2 == 0 else 1
    steps = groups // per_step
    width = cols // groups
    wide = width * per_step
    return pl.pallas_call(
        functools.partial(query_kernel, groups, per_step),
        grid_spec=pltpu.PrefetchScalarGridSpec(
            num_scalar_prefetch=1,
            grid=(steps,),
            in_specs=[
                pl.BlockSpec((1, rows, width_all), lambda i, pos: (pos[2], 0, 0)),
                full(got.shape),
                full(mod.shape),
                full(gain.shape),
                pl.BlockSpec((1, width_all, wide), lambda i, pos: (0, 0, i)),
            ],
            out_specs=[
                full((2 * rows, width_all)),
                pl.BlockSpec((2 * rows, wide), lambda i, pos: (0, i)),
            ]
            + [full((2 * rows, width))] * 2
            + [full((rows, width))] * (2 * groups - 4),
        ),
        out_shape=[out_of((2 * rows, width_all)), out_of((2 * rows, cols))]
        + [out_of((2 * rows, width))] * 2
        + [out_of((rows, width))] * (2 * groups - 4),
        compiler_params=params(32),
        cost_estimate=SMALL,
        name="norm_and_queries",
    )(pos, hidden, got, mod, gain, weight)


def fresh_kernel(slot, normed, gain, weight, *refs):
    mine, other = refs[-2:]
    rows = mine.shape[1]
    made = nn(normed[...], weight[0])
    made = norm_heads(made, gain[1:2, :]) if slot == 0 else made.astype(BF)
    mine[0] = made[:rows]
    other[0] = made[rows:]


def make_fresh(slot, normed, gain, weight, before=()):
    rows, width_all = normed.shape
    cols = weight.shape[2]
    block = math.gcd(cols, 768)
    out = pl.BlockSpec((1, rows // 2, block), lambda i: (slot, 0, i))
    return pl.pallas_call(
        functools.partial(fresh_kernel, slot),
        grid=(cols // block,),
        in_specs=[
            full(normed.shape),
            full(gain.shape),
            pl.BlockSpec((1, width_all, block), lambda i: (slot + 1, 0, i)),
        ]
        + [ANYWHERE] * len(before),
        out_specs=[out, out],
        out_shape=[out_of((2, rows // 2, cols))] * 2,
        input_output_aliases={3 + i: i for i in range(len(before))},
        compiler_params=params(32),
        cost_estimate=SMALL,
        name="fresh_keys" if slot == 0 else "fresh_values",
    )(normed, gain, weight, *before)


def place_kernel(pos, mine, got, out, sems):
    clip = pos[2]
    copy_all(sems, [(mine, out.at[:, clip]), (got, out.at[:, 1 - clip])])


def place_fresh(pos, mine, got):
    kv, rows, cols = mine.shape
    return pl.pallas_call(
        place_kernel,
        out_shape=out_of((kv, 2, rows, cols)),
        in_specs=[SCALARS, ANYWHERE, ANYWHERE],
        out_specs=ANYWHERE,
        scratch_shapes=[pltpu.SemaphoreType.DMA((2,))],
        compiler_params=params(8),
        name="place_fresh",
    )(pos, mine, got)


def own_kernel(q, mine, other, acc, top, total):
    rows = mine.shape[1]
    ones = jnp.ones((rows, HEAD), BF)
    for j, kv in enumerate((mine, other)):
        here = slice(j * rows, (j + 1) * rows)
        for h in range(q.shape[1] // HEAD):
            at = slice(h * HEAD, (h + 1) * HEAD)
            scores = nt(q[here, at], kv[0, :, at])
            peak = jnp.max(scores, axis=-1, keepdims=True)
            weights = jnp.exp2((scores - peak) * SCALE2).astype(BF)
            summed = nn(weights, jnp.concatenate([kv[1, :, at], ones], axis=1))
            acc[here, at] = summed[:, :HEAD]
            total[here, at] = summed[:, HEAD:]
            top[here, at] = jnp.broadcast_to(peak * SCALE2, (rows, HEAD))


def attend_own(queries, mine, other):
    block = math.gcd(queries.shape[1], 768)
    rows, cols = queries.shape
    wide = pl.BlockSpec((rows, block), lambda i: (0, i))
    kv = pl.BlockSpec((2, rows // 2, block), lambda i: (0, 0, i))
    return pl.pallas_call(
        own_kernel,
        grid=(cols // block,),
        in_specs=[wide, kv, kv],
        out_specs=[wide] * 3,
        out_shape=[out_of((rows, cols), F32)] * 3,
        compiler_params=params(24),
        cost_estimate=SMALL,
        name="attend_own",
    )(queries, mine, other)


def group_kernel(part, blocks, pos, *refs):
    queries = refs[:blocks]
    cached = [refs[blocks + 4 * g : blocks + 4 * g + 4] for g in range(blocks)]
    outs = refs[5 * blocks :]
    rows = queries[0].shape[0]
    ones = jnp.ones((4 * rows, HEAD), BF)
    keys = [jnp.concatenate([r[0] for r in g], axis=0) for g in cached]
    values = [jnp.concatenate([r[1] for r in g], axis=0) for g in cached]
    values = [jnp.concatenate([v, ones], axis=1) for v in values]
    for b in range(blocks):
        q = queries[b][...]
        scores = []
        for s in range(blocks):
            sc = nt(q, keys[s])
            if s == b:
                own = [sc[:, j * rows : (j + 1) * rows] for j in range(4)]
                own[part] = jnp.full((rows, rows), -1e30, F32)
                sc = jnp.concatenate(own, axis=1)
            scores.append(sc)
        peak = functools.reduce(
            jnp.maximum, [jnp.max(sc, axis=-1, keepdims=True) for sc in scores]
        )
        summed = None
        for sc, v in zip(scores, values):
            term = nn(jnp.exp2((sc - peak) * SCALE2).astype(BF), v)
            summed = term if summed is None else summed + term
        total = summed[:, HEAD:]
        outs[b][0:rows, :] = (summed[:, :HEAD] / total).astype(BF)
        level = jnp.transpose(peak * SCALE2 + jnp.log2(total))[0:8, :]
        high = level.astype(BF).astype(F32)
        mid = (level - high).astype(BF).astype(F32)
        low = level - high - mid
        row = lax.broadcasted_iota(jnp.int32, (8, HEAD), 0)
        three = jnp.where(row == 0, high, jnp.where(row == 1, mid, low))
        outs[b][rows : rows + EXTRA, :] = jnp.concatenate([three, three], axis=0).astype(BF)


def attend_groups(part, pos, queries, cached):
    blocks = len(queries)
    rows, width = queries[-1].shape
    flat = [a for g in cached for a in g]

    def spec(place):
        if place is None:
            return pl.BlockSpec((2, None, rows, HEAD), lambda h, pos: (0, pos[2], 0, h))
        return pl.BlockSpec((None, 2, rows, HEAD), lambda h, pos: (place, 0, 0, h))

    return pl.pallas_call(
        functools.partial(group_kernel, part, blocks),
        grid_spec=pltpu.PrefetchScalarGridSpec(
            num_scalar_prefetch=1,
            grid=(width // HEAD,),
            in_specs=[pl.BlockSpec((rows, HEAD), lambda h, pos: (part, h))] * 2
            + [pl.BlockSpec((rows, HEAD), lambda h, pos: (0, h))] * (blocks - 2)
            + [spec(place) for _, place in flat],
            out_specs=[pl.BlockSpec((rows + EXTRA, HEAD), lambda h, pos: (0, h))] * blocks,
        ),
        out_shape=[out_of((rows + EXTRA, width))] * blocks,
        compiler_params=params(32),
        cost_estimate=SMALL,
        name="attend_groups",
    )(pos, *queries, *[array for array, _ in flat])


def out_kernel(groups, pos, *refs):
    back = refs[:groups]
    acc, top, total, weight, send, keep, product = refs[groups:]
    step = pl.program_id(0)
    rows, width = acc.shape

    for s in range(groups):

        @pl.when(step == s)
        def _(s=s):
            cols = []
            for h in range(width // HEAD):
                at = slice(h * HEAD, (h + 1) * HEAD)
                three = back[s][rows : rows + 8, at].astype(F32)
                level = three[0:1, :] + three[1:2, :] + three[2:3, :]
                level = jnp.transpose(jnp.broadcast_to(level, (rows, HEAD)))
                own = top[:, at]
                peak = jnp.maximum(level, own)
                w_own, w_back = jnp.exp2(own - peak), jnp.exp2(level - peak)
                mixed = acc[:, at] * w_own + back[s][0:rows, at].astype(F32) * w_back
                cols.append((mixed / (total[:, at] * w_own + w_back)).astype(BF))
            part = nn(jnp.concatenate(cols, axis=1), weight[...])
            if s == 0:
                product[...] = part
            else:
                product[...] += part

    @pl.when(step == groups - 1)
    def _():
        half = product.shape[1] // 2
        mine = pl.multiple_of(pos[1] * half, HEAD)
        other = pl.multiple_of((1 - pos[1]) * half, HEAD)
        send[...] = product[:, pl.ds(other, half)].astype(BF)
        keep[...] = product[:, pl.ds(mine, half)]


def project_out(part, pos, back, acc, top, total, weight):
    groups = len(back)
    rows, width_all = acc.shape[0] // 2, acc.shape[1]
    width = width_all // groups
    cols = weight.shape[1]
    own = pl.BlockSpec((rows, width), lambda i, pos: (part, pos[0] ^ i))
    half = (rows, cols // 2)
    return pl.pallas_call(
        functools.partial(out_kernel, groups),
        grid_spec=pltpu.PrefetchScalarGridSpec(
            num_scalar_prefetch=1,
            grid=(groups,),
            in_specs=[full(back[0].shape)] * groups
            + [own] * 3
            + [pl.BlockSpec((width, cols), lambda i, pos: (pos[0] ^ i, 0))],
            out_specs=[full(half), full(half)],
            scratch_shapes=[pltpu.VMEM((rows, cols), F32)],
        ),
        out_shape=[out_of(half), out_of(half, F32)],
        compiler_params=params(24),
        cost_estimate=LARGE,
        name="merge_and_project",
    )(pos, *back, acc, top, total, weight)


def gated(pos, rows_in, mod, keep, got):
    gate = mod[2, pl.ds(pos[2], 1), :]
    return (rows_in.astype(F32) + gate * (keep[...] + got[...].astype(F32))).astype(BF)


def other_rows_kernel(pos, hidden, mod, keep, got, out):
    out[...] = gated(pos, hidden[...], mod, keep, got)


def my_rows_kernel(pos, hidden, mod, keep, got, theirs, out):
    out[pl.ds(pos[2], 1)] = gated(pos, hidden[0], mod, keep, got)[None]
    out[pl.ds(1 - pos[2], 1)] = theirs[...][None]


def finish(pos, hidden, mod, keep, got, theirs=None):
    half = keep.shape
    if theirs is None:
        hidden_spec = pl.BlockSpec(half, lambda i, pos: (0, pos[1]))
        extra, shape, body = [], half, other_rows_kernel
    else:
        hidden_spec = pl.BlockSpec((1,) + half, lambda i, pos: (pos[2], 0, pos[1]))
        extra, shape, body = [theirs], (2,) + half, my_rows_kernel
    return pl.pallas_call(
        body,
        grid_spec=pltpu.PrefetchScalarGridSpec(
            num_scalar_prefetch=1,
            grid=(1,),
            in_specs=[
                hidden_spec,
                pl.BlockSpec(mod.shape[:2] + half[1:], lambda i, pos: (0, 0, pos[1])),
            ]
            + [full(half)] * (2 + len(extra)),
            out_specs=full(shape),
        ),
        out_shape=out_of(shape),
        compiler_params=params(24),
        cost_estimate=SMALL,
        name="gate_and_add",
    )(pos, hidden, mod, keep, got, *extra)


def tie(value, *others):
    return lax.optimization_barrier((value, others))[0]


def spread_heads(groups, hidden_states, modulation, qkv_weight, out_weight, qk_gain, stale_kv):
    patches = lax.axis_size("patch")
    inner = patches // groups
    patch = lax.axis_index("patch")
    pos = jnp.stack([patch // inner, lax.axis_index("tp"), patch % 2]).astype(jnp.int32)

    def across(value, bit):
        return lax.ppermute(value, "patch", [(i, i ^ bit) for i in range(patches)])

    def along(value, step):
        return across(value, inner * step)

    weights = jnp.transpose(qkv_weight, (1, 0, 2))
    step = lax.optimization_barrier

    cut = cut_stale(pos, stale_kv, groups)
    near, one, two = cut[0], along(cut[1], 1), along(cut[2], 2)
    far_near = across(near, 2)
    hidden_now = tie(hidden_states, *cut)
    hidden_for = lax.dynamic_index_in_dim(hidden_now, 1 - pos[2], 0, keepdims=False)
    hidden_got = across(hidden_for, 1)
    normed, queries, *slots = make_queries(
        pos, hidden_states, hidden_got, modulation, qk_gain, weights, groups
    )
    fresh = make_fresh(0, normed, qk_gain, weights)
    normed, queries, slots, fresh, near, one, two, far_near, cut_three = step(
        (normed, queries, slots, fresh, near, one, two, far_near, cut[3])
    )

    three, asked_one = along(cut_three, 3), along(slots[1], 1)
    far_one, far_two = across(one, 2), across(two, 2)
    swap_a = across(pack(pos, near, far_near, one, two), 1)
    fresh = make_fresh(1, normed, qk_gain, weights, fresh)
    own = attend_own(queries, *fresh)
    three, asked_one, far_one, far_two, swap_a, own, slots = step(
        (three, asked_one, far_one, far_two, swap_a, own, slots)
    )

    far_three = across(three, 2)
    their_queries = [slots[0], asked_one] + [along(slots[2 * s - 1], s) for s in (2, 3)]
    swap_b = across(pack(pos, far_one, far_two, three), 1)
    far_three, their_queries, swap_b, slots, asked_one = step(
        (far_three, their_queries, swap_b, slots, asked_one)
    )

    my_queries = [slots[0], asked_one] + [along(slots[2 * s - 2], s) for s in (2, 3)]
    held = [
        [(near, None), (swap_a, 0), (far_near, None), (swap_a, 1)],
        [(one, None), (swap_a, 2), (far_one, None), (swap_b, 0)],
        [(two, None), (swap_a, 3), (far_two, None), (swap_b, 1)],
        [(three, None), (swap_b, 2), (far_three, None), (across(far_three, 1), None)],
    ]
    theirs = attend_groups(1, pos, their_queries, held)
    theirs, my_queries = step((theirs, my_queries))

    back = [theirs[0]] + [along(theirs[s], s) for s in range(1, groups)]
    mine = attend_groups(0, pos, my_queries, held)
    mine, back = step((mine, back))

    mine_back = [mine[0]] + [along(mine[s], s) for s in range(1, groups)]
    swap = [(0, 1), (1, 0)]
    send, keep = project_out(1, pos, back, *own, out_weight)
    got = lax.ppermute(send, "tp", swap)
    mine_back[0] = tie(mine_back[0], send)

    my_send, my_keep = project_out(0, pos, mine_back, *own, out_weight)
    my_got = lax.ppermute(my_send, "tp", swap)
    fresh_got = across(tie(fresh[1], send), 1)
    fresh_kv = place_fresh(pos, tie(fresh[0], my_send), fresh_got)
    theirs = finish(pos, hidden_got, modulation, tie(keep, my_send), got)
    mixed = finish(pos, hidden_states, modulation, my_keep, my_got, across(theirs, 1))
    return mixed, fresh_kv


def head_norm(values_in, gain_row, heads_here):
    shaped = values_in.reshape(values_in.shape[0], values_in.shape[1], heads_here, HEAD)
    square_mean = jnp.mean(shaped * shaped, axis=-1, keepdims=True)
    return (shaped * lax.rsqrt(square_mean + 1e-06) * gain_row).astype(BF)


def gather_all(hidden_states, modulation, qkv_weight, out_weight, qk_gain, stale_kv):
    clip_count, row_count, width_all = hidden_states.shape
    heads_here = qkv_weight.shape[2] // HEAD
    inputs = hidden_states.astype(F32)
    feature_mean = jnp.mean(inputs, axis=-1, keepdims=True)
    centered = inputs - feature_mean
    feature_var = jnp.mean(centered * centered, axis=-1, keepdims=True)
    normed = (
        centered * lax.rsqrt(feature_var + 1e-06) * (1.0 + modulation[1][:, None, :])
        + modulation[0][:, None, :]
    ).astype(BF)
    projected = jnp.einsum("ctd,dkh->kcth", normed, qkv_weight, preferred_element_type=F32)
    queries = head_norm(projected[0], qk_gain[0], heads_here)
    keys_new = head_norm(projected[1], qk_gain[1], heads_here)
    values_new = projected[2].astype(BF).reshape(clip_count, row_count, heads_here, HEAD)
    fresh_kv = jnp.stack(
        [keys_new.reshape(clip_count, row_count, -1), values_new.reshape(clip_count, row_count, -1)]
    )
    own_first = lax.axis_index("patch") * row_count
    gathered = lax.all_gather(stale_kv, "patch", axis=2, tiled=True)
    gathered = lax.dynamic_update_slice_in_dim(gathered, fresh_kv, own_first, 2)
    count = gathered.shape[2]
    tile_keys = gathered[0].reshape(clip_count, count, heads_here, HEAD)
    tile_values = gathered[1].reshape(clip_count, count, heads_here, HEAD)
    scores = jnp.einsum("cqhd,ckhd->chqk", queries, tile_keys, preferred_element_type=F32)
    scores = scores * HEAD ** (-0.5)
    expo = jnp.exp(scores - jnp.max(scores, axis=-1, keepdims=True))
    summed = jnp.einsum(
        "chqk,ckhd->chqd", expo.astype(BF), tile_values, preferred_element_type=F32
    )
    attended = (summed / jnp.sum(expo, axis=-1)[..., None]).astype(BF)
    attended = jnp.transpose(attended, (0, 2, 1, 3)).reshape(clip_count, row_count, -1)
    product = jnp.einsum("cth,hd->ctd", attended, out_weight, preferred_element_type=F32)
    col_count = width_all // lax.axis_size("tp")
    col_first = lax.axis_index("tp") * col_count
    summed_part = lax.psum_scatter(
        product.astype(BF), "tp", scatter_dimension=2, tiled=True
    ).astype(F32)
    input_part = lax.dynamic_slice_in_dim(inputs, col_first, col_count, 2)
    gate_part = lax.dynamic_slice_in_dim(modulation[2], col_first, col_count, 1)
    mixed = (input_part + gate_part[:, None, :] * summed_part).astype(BF)
    return (mixed, fresh_kv)


def per_device(*arrays):
    clips = arrays[0].shape[0]
    heads_here = arrays[2].shape[2] // HEAD
    patches = lax.axis_size("patch")
    groups = math.gcd(heads_here, patches)
    if clips == 2 and groups == 4 and patches == 4 * groups and lax.axis_size("tp") == 2:
        return spread_heads(groups, *arrays)
    return gather_all(*arrays)


def solution(mesh):
    in_specs = (
        P(None, "patch", None),
        P(),
        P(None, None, "tp"),
        P("tp", None),
        P(),
        P(None, None, "patch", "tp"),
    )
    out_specs = (P(None, "patch", "tp"), P(None, None, "patch", "tp"))
    return jax.shard_map(
        per_device, mesh=mesh, in_specs=in_specs, out_specs=out_specs, check_vma=False
    )
```

time: 253 us -> 115 us (0.45)
  waiting for transfers between devices: 125 us -> 27.9 us
  matrix products: 53.6 us -> 0 us
  Pallas kernels: 0 us -> 53.3 us
  local copies, waits for them, and re-layouts: 38.4 us -> 1.59 us
  starting transfers between devices: 0.08 us -> 30.9 us
  other arithmetic: 21.1 us -> 0.08 us
  between operations: 14.2 us -> 0.89 us
    all_gather x1 -> x0, waiting for transfers between devices: 104 us -> none  [per_device(): gathered = lax.all_gather(stale_kv, 'patch', axis=2, tiled=True)]
    dot_general x6 -> x0, matrix products: 53.6 us -> none  [the longest x1 16.4 us: per_device(): jnp.einsum('chqk,ckhd->chqd', expo.astype(jnp.bfloat16), tile_values, pre...]
    pallas_call x0 -> x14, Pallas kernels: none -> 53.3 us  [the longest x2 14.3 us: attend_groups(): pl.pallas_call(functools.partial(group_kernel, part, blocks), grid_spec=p...]
    ppermute x0 -> x26, starting transfers between devices: none -> 30.9 us  [the longest x24 27.7 us: across(): return lax.ppermute(value, 'patch', [(i, i ^ bit) for i in range(patches)])]
    ppermute x0 -> x26, waiting for transfers between devices: none -> 27.9 us  [the longest x24 21.6 us: across(): return lax.ppermute(value, 'patch', [(i, i ^ bit) for i in range(patches)])]
    slice x5 -> x0, local copies, waits for them, and re-layouts: 23.8 us -> none  [the longest x1 17.7 us: per_device(): tile_keys = gathered[0].reshape(clip_count, count, heads_here, HEAD)]
    reduce_scatter x1 -> x0, waiting for transfers between devices: 21.6 us -> none  [per_device(): lax.psum_scatter(product.astype(jnp.bfloat16), 'tp', scatter_dimension=2,...]
    reduce_sum x6 -> x0, other arithmetic: 12.5 us -> none  [the longest x1 11.1 us: per_device(): new_sum = start_sum * rescale + jnp.sum(expo, axis=-1)]
  transfers between devices with their start and end apart: 2 -> 26, of which waited for: 2 -> 10; matrix products, arithmetic and copies ran while one was open for 14% -> 0% of each run, Pallas kernels for 0% -> 43%
where the time goes in v2:
time: 115 us
  Pallas kernels  53.3 us (46%)
  starting transfers between devices  30.9 us (27%)
  waiting for transfers between devices  27.9 us (24%)
  local copies, waits for them, and re-layouts  1.59 us (1%)
    ppermute x24, starting transfers between devices, across(): return lax.ppermute(value, 'patch', [(i, i ^ bit) for i in range(patches)])  27.7 us
    ppermute x24, waiting for transfers between devices, across(): return lax.ppermute(value, 'patch', [(i, i ^ bit) for i in range(patches)])  21.6 us
    pallas_call x2, Pallas kernels, attend_groups(): pl.pallas_call(functools.partial(group_kernel, part, blocks), grid_spec=p...  14.3 us
    pallas_call x2, Pallas kernels, make_fresh(): pl.pallas_call(functools.partial(fresh_kernel, slot), grid=(cols // block...  10.7 us
    pallas_call x2, Pallas kernels, project_out(): pl.pallas_call(functools.partial(out_kernel, groups), grid_spec=pltpu.Pre...  7.44 us
    pallas_call x1, Pallas kernels, make_queries(): pl.pallas_call(functools.partial(query_kernel, groups, per_step), grid_sp...  7.39 us
    pallas_call x1, Pallas kernels, attend_own(): pl.pallas_call(own_kernel, grid=(cols // block,), in_specs=[wide, kv, kv]...  6.39 us
    ppermute x1, waiting for transfers between devices, spread_heads(): my_got = lax.ppermute(my_send, 'tp', swap)  5.01 us
  transfers between devices with their start and end apart: 26, of which 10 were waited for; matrix products, arithmetic and copies ran while one was open for 0% of the time, Pallas kernels for 43%

profile of v2, /device:TPU:0, one launch (start us, length us, event | category | flops | bytes accessed | tf_op | source)
XLA Modules:
  0.0 114.7 jit_solution(16276243507500255127)
XLA Ops:
  0.7 0.1 pad_add_fusion.pos
  0.7 1.5 %copy-done.1 = bf16[2,2,128,1536]{3,2,1,0:T(8,128)(2,1)S(1)} copy-done((bf16[2,2,128,1536]{3,2,1,0:T(8,128)(2,1)S(1)}, bf16[2,2,128,1536]{3,2,1,0:T(8,128)(2,1)}, u32[]{:S(2)}) %copy-start.1) | copy-done | bytes 1572888
  2.3 0.8 cut_stale.1
  3.0 0.1 dynamic-slice_bitcast_fusion
  3.1 0.5 collective-permute-start
  3.6 2.6 %collective-permute-start.1 = (bf16[2,2,128,384]{3,2,1,0:T(8,128)(2,1)S(1)}, bf16[2,2,128,384]{3,2,1,0:T(8,128)(2,1)S(1)}, u32[]{:S(2)}, u32[]{:S(2)}) collective-permute-start(bf16[2,2,128,384]{3,2,1,0:T(8,128)(2,1)S(1)} %get-tuple-element.93), channel_id=1, source_target_pairs={{0,8},{2,10},{4,12},{6,14},{8,0},{10,2},{12,4},{14,6},{16,24},{18,... | collective-permute-start | bytes 1179656 | tf_op jit(solution)/shard_map/ppermute | solution.py:435
  6.3 2.6 %collective-permute-start.2 = (bf16[2,2,128,384]{3,2,1,0:T(8,128)(2,1)S(1)}, bf16[2,2,128,384]{3,2,1,0:T(8,128)(2,1)S(1)}, u32[]{:S(2)}, u32[]{:S(2)}) collective-permute-start(bf16[2,2,128,384]{3,2,1,0:T(8,128)(2,1)S(1)} %get-tuple-element.94), channel_id=1, source_target_pairs={{0,16},{2,18},{4,20},{6,22},{8,24},{10,26},{12,28},{14,30},{16,0},... | collective-permute-start | bytes 1179656 | tf_op jit(solution)/shard_map/ppermute | solution.py:435
  8.9 1.5 %collective-permute-start.3 = (bf16[2,2,128,384]{3,2,1,0:T(8,128)(2,1)S(1)}, bf16[2,2,128,384]{3,2,1,0:T(8,128)(2,1)S(1)}, u32[]{:S(2)}, u32[]{:S(2)}) collective-permute-start(bf16[2,2,128,384]{3,2,1,0:T(8,128)(2,1)S(1)} %get-tuple-element.111.refs_0_.refs_4_), channel_id=1, source_target_pairs={{0,4},{2,6},{4,0},{6,2},{8,12},{10,14},{12,8},{14,10},{16,20},{18,... | collective-permute-start | bytes 1179656 | tf_op jit(solution)/shard_map/ppermute | solution.py:435
  10.3 0.0 collective-permute-done.got.hidden
  10.4 7.4 %norm_and_queries.1 = (bf16[256,3072]{1,0:T(8,128)(2,1)S(1)}, bf16[256,1536]{1,0:T(8,128)(2,1)S(1)}, bf16[256,384]{1,0:T(8,128)(2,1)S(1)}, bf16[256,384]{1,0:T(8...) custom-call(s32[3]{0:T(128)S(1)} %pad_add_fusion.pos, ...), custom_call_target="tpu_custom_call" | custom-call | flops 1000 | bytes 1000 | tf_op jit(solution)/shard_map/norm_and_queries/pallas_call | solution.py:147
  17.8 5.5 %fresh_keys.1 = (bf16[2,128,1536]{2,1,0:T(8,128)(2,1)S(1)}, bf16[2,128,1536]{2,1,0:T(8,128)(2,1)S(1)}) custom-call(bf16[256,3072]{1,0:T(8,128)(2,1)S(1)} %get-tuple-element.114.normed, f32[2,128]{1,0:T(2,128)S(1)} %copy-done.3, bf16[3,3072,1536]{2,1,0:T(8,128)(2,1)} %bitcast.9), custom_call_target="tpu_custom_call" | custom-call | flops 1000 | bytes 1000 | tf_op jit(solution)/shard_map/fresh_keys/pallas_call | solution.py:189
  23.3 1.0 collective-permute-done.1.refs_2_.refs_8_
  24.3 2.5 %collective-permute-done.2.refs_3_.refs_12_ = bf16[2,2,128,384]{3,2,1,0:T(8,128)(2,1)S(1)} collective-permute-done((bf16[2,2,128,384]{3,2,1,0:T(8,128)(2,1)S(1)}, bf16[2,2,128,384]{3,2,1,0:T(8,128)(2,1)S(1)}, u32[]{:S(2)}, u32[]{:S(2)}) %collective-permute-start.2) | collective-permute-done | bytes 393248 | tf_op jit(solution)/shard_map/ppermute | solution.py:435
  26.8 0.0 collective-permute-done.3.refs_1_.refs_6_
  26.8 1.1 pack.2
  27.9 0.1 collective-permute-start.8
  28.0 2.5 %collective-permute-start.4 = (bf16[2,2,128,384]{3,2,1,0:T(8,128)(2,1)S(1)}, bf16[2,2,128,384]{3,2,1,0:T(8,128)(2,1)S(1)}, u32[]{:S(2)}, u32[]{:S(2)}) collective-permute-start(bf16[2,2,128,384]{3,2,1,0:T(8,128)(2,1)S(1)} %get-tuple-element.107), channel_id=1, source_target_pairs={{0,24},{2,26},{4,28},{6,30},{8,16},{10,18},{12,20},{14,22},{16,8},... | collective-permute-start | bytes 1179656 | tf_op jit(solution)/shard_map/ppermute | solution.py:435
  30.5 1.5 %collective-permute-start.6 = (bf16[2,2,128,384]{3,2,1,0:T(8,128)(2,1)S(1)}, bf16[2,2,128,384]{3,2,1,0:T(8,128)(2,1)S(1)}, u32[]{:S(2)}, u32[]{:S(2)}) collective-permute-start(bf16[2,2,128,384]{3,2,1,0:T(8,128)(2,1)S(1)} %collective-permute-done.1.refs_2_.refs_8_), channel_id=1, source_target_pairs={{0,4},{2,6},{4,0},{6,2},{8,12},{10,14},{12,8},{14,10},{16,20},{18,... | collective-permute-start | bytes 1179656 | tf_op jit(solution)/shard_map/ppermute | solution.py:435
  32.0 0.5 collective-permute-start.7
  32.6 0.0 collective-permute-start.5
  32.6 5.2 %fresh_values.1 = (bf16[2,128,1536]{2,1,0:T(8,128)(2,1)S(1)}, bf16[2,128,1536]{2,1,0:T(8,128)(2,1)S(1)}) custom-call(bf16[256,3072]{1,0:T(8,128)(2,1)S(1)} %get-tuple-element.114.normed, f32[2,128]{1,0:T(2,128)S(1)} %copy-done.3, bf16[3,3072,1536]{2,1,0:T(8,128)(2,1)} %bitcast.10, ...), custom_call_target="tpu_custom_call", output_to_operand_aliasing={{0}: (3, {}), {1}: (4, {})} | custom-call | flops 1000 | bytes 1000 | tf_op jit(solution)/shard_map/fresh_values/pallas_call | solution.py:189
  37.8 6.4 %attend_own.1 = (f32[256,1536]{1,0:T(8,128)S(1)}, f32[256,1536]{1,0:T(8,128)S(1)}, f32[256,1536]{1,0:T(8,128)S(1)}) custom-call(bf16[256,1536]{1,0:T(8,128)(2,1)S(1)} %get-tuple-element.113.q, bf16[2,128,1536]{2,1,0:T(8,128)(2,1)S(1)} %get-tuple-element.180.mine, bf16[2,128,1536]{2,1,0:T(8,128)(2,1)S(1)} %get-tuple-element.181.other), custom_call_target="tpu_custom_call" | custom-call | flops 1000 | bytes 1000 | tf_op jit(solution)/shard_map/attend_own/pallas_call | solution.py:246
  44.2 1.5 %collective-permute-done.5.refs_1_ = bf16[256,384]{1,0:T(8,128)(2,1)S(1)} collective-permute-done((bf16[256,384]{1,0:T(8,128)(2,1)S(1)}, bf16[256,384]{1,0:T(8,128)(2,1)S(1)}, u32[]{:S(2)}, u32[]{:S(2)}) %collective-permute-start.5) | collective-permute-done | bytes 196640 | tf_op jit(solution)/shard_map/ppermute | solution.py:435
  45.7 0.0 collective-permute-done.4.refs_2_.refs_16_
  45.7 0.0 collective-permute-done.6.refs_0_.refs_10_
  45.7 4.5 %collective-permute-done.7.refs_1_.refs_14_ = bf16[2,2,128,384]{3,2,1,0:T(8,128)(2,1)S(1)} collective-permute-done((bf16[2,2,128,384]{3,2,1,0:T(8,128)(2,1)S(1)}, bf16[2,2,128,384]{3,2,1,0:T(8,128)(2,1)S(1)}, u32[]{:S(2)}, u32[]{:S(2)}) %collective-permute-start.7) | collective-permute-done | bytes 393248 | tf_op jit(solution)/shard_map/ppermute | solution.py:435
  50.2 0.0 collective-permute-done.8.refs_5_.refs_7_.refs_9_.refs_13_
  50.2 1.0 pack.3
  51.1 0.1 collective-permute-start.12
  51.2 1.6 %collective-permute-start.9 = (bf16[2,2,128,384]{3,2,1,0:T(8,128)(2,1)S(1)}, bf16[2,2,128,384]{3,2,1,0:T(8,128)(2,1)S(1)}, u32[]{:S(2)}, u32[]{:S(2)}) collective-permute-start(bf16[2,2,128,384]{3,2,1,0:T(8,128)(2,1)S(1)} %collective-permute-done.4.refs_2_.refs_16_), channel_id=1, source_target_pairs={{0,4},{2,6},{4,0},{6,2},{8,12},{10,14},{12,8},{14,10},{16,20},{18,... | collective-permute-start | bytes 1179656 | tf_op jit(solution)/shard_map/ppermute | solution.py:435
  52.8 0.0 collective-permute-start.10
  52.8 1.4 %collective-permute-start.11 = (bf16[128,384]{1,0:T(8,128)(2,1)S(1)}, bf16[128,384]{1,0:T(8,128)(2,1)S(1)}, u32[]{:S(2)}, u32[]{:S(2)}) collective-permute-start(bf16[128,384]{1,0:T(8,128)(2,1)S(1)} %get-tuple-element.131), channel_id=1, source_target_pairs={{0,24},{2,26},{4,28},{6,30},{8,16},{10,18},{12,20},{14,22},{16,8},... | collective-permute-start | bytes 294920 | tf_op jit(solution)/shard_map/ppermute | solution.py:435
  54.1 7.4 %collective-permute-done.10.refs_2_ = bf16[128,384]{1,0:T(8,128)(2,1)S(1)} collective-permute-done((bf16[128,384]{1,0:T(8,128)(2,1)S(1)}, bf16[128,384]{1,0:T(8,128)(2,1)S(1)}, u32[]{:S(2)}, u32[]{:S(2)}) %collective-permute-start.10) | collective-permute-done | bytes 98336 | tf_op jit(solution)/shard_map/ppermute | solution.py:435
  61.5 0.0 collective-permute-done.11.refs_3_
  61.5 1.2 %collective-permute-done.9.refs_18_ = bf16[2,2,128,384]{3,2,1,0:T(8,128)(2,1)S(1)} collective-permute-done((bf16[2,2,128,384]{3,2,1,0:T(8,128)(2,1)S(1)}, bf16[2,2,128,384]{3,2,1,0:T(8,128)(2,1)S(1)}, u32[]{:S(2)}, u32[]{:S(2)}) %collective-permute-start.9) | collective-permute-done | bytes 393248 | tf_op jit(solution)/shard_map/ppermute | solution.py:435
  62.7 0.0 collective-permute-done.12.refs_11_.refs_15_.refs_17_
  62.7 2.5 %collective-permute-start.14 = (bf16[128,384]{1,0:T(8,128)(2,1)S(1)}, bf16[128,384]{1,0:T(8,128)(2,1)S(1)}, u32[]{:S(2)}, u32[]{:S(2)}) collective-permute-start(bf16[128,384]{1,0:T(8,128)(2,1)S(1)} %get-tuple-element.149), channel_id=1, source_target_pairs={{0,16},{2,18},{4,20},{6,22},{8,24},{10,26},{12,28},{14,30},{16,0},... | collective-permute-start | bytes 294920 | tf_op jit(solution)/shard_map/ppermute | solution.py:435
  65.2 1.4 %collective-permute-start.15 = (bf16[128,384]{1,0:T(8,128)(2,1)S(1)}, bf16[128,384]{1,0:T(8,128)(2,1)S(1)}, u32[]{:S(2)}, u32[]{:S(2)}) collective-permute-start(bf16[128,384]{1,0:T(8,128)(2,1)S(1)} %get-tuple-element.150), channel_id=1, source_target_pairs={{0,24},{2,26},{4,28},{6,30},{8,16},{10,18},{12,20},{14,22},{16,8},... | collective-permute-start | bytes 294920 | tf_op jit(solution)/shard_map/ppermute | solution.py:435
  66.6 0.0 collective-permute-done.13.refs_19_
  66.6 7.1 %attend_groups.2 = (bf16[144,384]{1,0:T(8,128)(2,1)S(1)}, bf16[144,384]{1,0:T(8,128)(2,1)S(1)}, bf16[144,384]{1,0:T(8,128)(2,1)S(1)}, bf16[144,384]{1,0:T(8,128)(2,1)S(1)}) custom-call(s32[3]{0:T(128)S(1)} %pad_add_fusion.pos, bf16[256,384]{1,0:T(8,128)(2,1)S(1)} %get-tuple-element.151.refs_0_, bf16[256,384]{1,0:T(8,128)(2,1)S(1)} %collective-permute-done.5.refs_1_, ...), custom_call_target="tpu_custom_call" | custom-call | flops 1000 | bytes 1000 | tf_op jit(solution)/shard_map/attend_groups/pallas_call | solution.py:305
  73.7 0.0 collective-permute-done.14.refs_2_
  73.7 0.0 collective-permute-done.15.refs_3_
  73.7 0.0 slice-start.2
  73.7 2.0 %collective-permute-start.16 = (bf16[144,384]{1,0:T(8,128)(2,1)S(1)}, bf16[144,384]{1,0:T(8,128)(2,1)S(1)}, u32[]{:S(2)}, u32[]{:S(2)}) collective-permute-start(bf16[144,384]{1,0:T(8,128)(2,1)S(1)} %get-tuple-element.160), channel_id=1, source_target_pairs={{0,8},{2,10},{4,12},{6,14},{8,0},{10,2},{12,4},{14,6},{16,24},{18,... | collective-permute-start | bytes 331784 | tf_op jit(solution)/shard_map/ppermute | solution.py:435
  75.7 1.1 collective-permute-start.17
  76.8 1.4 %collective-permute-start.18 = (bf16[144,384]{1,0:T(8,128)(2,1)S(1)}, bf16[144,384]{1,0:T(8,128)(2,1)S(1)}, u32[]{:S(2)}, u32[]{:S(2)}) collective-permute-start(bf16[144,384]{1,0:T(8,128)(2,1)S(1)} %get-tuple-element.162), channel_id=1, source_target_pairs={{0,24},{2,26},{4,28},{6,30},{8,16},{10,18},{12,20},{14,22},{16,8},... | collective-permute-start | bytes 331784 | tf_op jit(solution)/shard_map/ppermute | solution.py:435
  78.2 7.2 %attend_groups.3 = (bf16[144,384]{1,0:T(8,128)(2,1)S(1)}, bf16[144,384]{1,0:T(8,128)(2,1)S(1)}, bf16[144,384]{1,0:T(8,128)(2,1)S(1)}, bf16[144,384]{1,0:T(8,128)(2,1)S(1)}) custom-call(s32[3]{0:T(128)S(1)} %pad_add_fusion.pos, bf16[256,384]{1,0:T(8,128)(2,1)S(1)} %get-tuple-element.151.refs_0_, bf16[256,384]{1,0:T(8,128)(2,1)S(1)} %collective-permute-done.5.refs_1_, ...), custom_call_target="tpu_custom_call" | custom-call | flops 1000 | bytes 1000 | tf_op jit(solution)/shard_map/attend_groups/pallas_call | solution.py:305
  85.4 1.0 collective-permute-done.17.refs_2_
  86.5 2.1 %collective-permute-start.19 = (bf16[144,384]{1,0:T(8,128)(2,1)S(1)}, bf16[144,384]{1,0:T(8,128)(2,1)S(1)}, u32[]{:S(2)}, u32[]{:S(2)}) collective-permute-start(bf16[144,384]{1,0:T(8,128)(2,1)S(1)} %get-tuple-element.173), channel_id=1, source_target_pairs={{0,8},{2,10},{4,12},{6,14},{8,0},{10,2},{12,4},{14,6},{16,24},{18,... | collective-permute-start | bytes 331784 | tf_op jit(solution)/shard_map/ppermute | solution.py:435
  88.6 0.3 collective-permute-start.20
  88.9 2.0 %collective-permute-start.21 = (bf16[144,384]{1,0:T(8,128)(2,1)S(1)}, bf16[144,384]{1,0:T(8,128)(2,1)S(1)}, u32[]{:S(2)}, u32[]{:S(2)}) collective-permute-start(bf16[144,384]{1,0:T(8,128)(2,1)S(1)} %get-tuple-element.175), channel_id=1, source_target_pairs={{0,24},{2,26},{4,28},{6,30},{8,16},{10,18},{12,20},{14,22},{16,8},... | collective-permute-start | bytes 331784 | tf_op jit(solution)/shard_map/ppermute | solution.py:435
  90.9 3.7 %merge_and_project.2 = (bf16[128,1536]{1,0:T(8,128)(2,1)S(1)}, f32[128,1536]{1,0:T(8,128)S(1)}) custom-call(s32[3]{0:T(128)S(1)} %pad_add_fusion.pos, bf16[144,384]{1,0:T(8,128)(2,1)S(1)} %get-tuple-element.164.refs_0_, bf16[144,384]{1,0:T(8,128)(2,1)S(1)} %collective-permute-done.16.refs_1_, bf16[144,384]{1,0:T(8,128)(2,1)S(1)} %collective-permute-done.17.refs_2_, ...), custom_call_target="tpu_custom_call" | custom-call | flops 10000000000 | bytes 100000000 | tf_op jit(solution)/shard_map/merge_and_project/pallas_call | solution.py:365
  94.7 1.6 %collective-permute-start.23 = (bf16[128,1536]{1,0:T(8,128)(2,1)S(1)}, bf16[128,1536]{1,0:T(8,128)(2,1)S(1)}, u32[]{:S(2)}, u32[]{:S(2)}) collective-permute-start(bf16[128,1536]{1,0:T(8,128)(2,1)S(1)} %get-tuple-element.171), channel_id=1, source_target_pairs={{0,1},{1,0},{2,3},{3,2},{4,5},{5,4},{6,7},{7,6},{8,9},{9,8},{10,11... | collective-permute-start | bytes 1179656 | tf_op jit(solution)/shard_map/ppermute | solution.py:490
  96.3 2.4 %collective-permute-done.20.refs_2_ = bf16[144,384]{1,0:T(8,128)(2,1)S(1)} collective-permute-done((bf16[144,384]{1,0:T(8,128)(2,1)S(1)}, bf16[144,384]{1,0:T(8,128)(2,1)S(1)}, u32[]{:S(2)}, u32[]{:S(2)}) %collective-permute-start.20) | collective-permute-done | bytes 110624 | tf_op jit(solution)/shard_map/ppermute | solution.py:435
  98.7 3.7 %merge_and_project.3 = (bf16[128,1536]{1,0:T(8,128)(2,1)S(1)}, f32[128,1536]{1,0:T(8,128)S(1)}) custom-call(s32[3]{0:T(128)S(1)} %pad_add_fusion.pos, bf16[144,384]{1,0:T(8,128)(2,1)S(1)} %get-tuple-element.172.refs_0_, bf16[144,384]{1,0:T(8,128)(2,1)S(1)} %collective-permute-done.19.refs_1_, bf16[144,384]{1,0:T(8,128)(2,1)S(1)} %collective-permute-done.20.refs_2_, ...), custom_call_target="tpu_custom_call" | custom-call | flops 10000000000 | bytes 100000000 | tf_op jit(solution)/shard_map/merge_and_project/pallas_call | solution.py:365
  102.4 1.6 %collective-permute-start.22 = (bf16[128,1536]{1,0:T(8,128)(2,1)S(1)}, bf16[128,1536]{1,0:T(8,128)(2,1)S(1)}, u32[]{:S(2)}, u32[]{:S(2)}) collective-permute-start(bf16[128,1536]{1,0:T(8,128)(2,1)S(1)} %get-tuple-element.177), channel_id=1, source_target_pairs={{0,1},{1,0},{2,3},{3,2},{4,5},{5,4},{6,7},{7,6},{8,9},{9,8},{10,11... | collective-permute-start | bytes 1179656 | tf_op jit(solution)/shard_map/ppermute | solution.py:494
  104.0 1.3 %collective-permute-done.23.got = bf16[128,1536]{1,0:T(8,128)(2,1)S(1)} collective-permute-done((bf16[128,1536]{1,0:T(8,128)(2,1)S(1)}, bf16[128,1536]{1,0:T(8,128)(2,1)S(1)}, u32[]{:S(2)}, u32[]{:S(2)}) %collective-permute-start.23) | collective-permute-done | bytes 393248 | tf_op jit(solution)/shard_map/ppermute | solution.py:490
  105.3 0.8 gate_and_add.2
  106.1 0.1 collective-permute-start.24
  106.2 0.0 collective-permute-done.25.got
  106.2 1.7 %place_fresh.1 = bf16[2,2,128,1536]{3,2,1,0:T(8,128)(2,1)} custom-call(s32[3]{0:T(128)S(1)} %pad_add_fusion.pos, bf16[2,128,1536]{2,1,0:T(8,128)(2,1)S(1)} %get-tuple-element.180.mine, bf16[2,128,1536]{2,1,0:T(8,128)(2,1)S(1)} %collective-permute-done.25.got), custom_call_target="tpu_custom_call" | custom-call | tf_op jit(solution)/shard_map/place_fresh/pallas_call | solution.py:214
  107.9 5.0 %collective-permute-done.22.got = bf16[128,1536]{1,0:T(8,128)(2,1)S(1)} collective-permute-done((bf16[128,1536]{1,0:T(8,128)(2,1)S(1)}, bf16[128,1536]{1,0:T(8,128)(2,1)S(1)}, u32[]{:S(2)}, u32[]{:S(2)}) %collective-permute-start.22) | collective-permute-done | bytes 393248 | tf_op jit(solution)/shard_map/ppermute | solution.py:494
  112.9 0.0 collective-permute-done.24.theirs
  112.9 1.7 %gate_and_add.3 = bf16[2,128,1536]{2,1,0:T(8,128)(2,1)} custom-call(s32[3]{0:T(128)S(1)} %pad_add_fusion.pos, bf16[2,128,3072]{2,1,0:T(8,128)(2,1)S(1)} %copy-done, f32[3,2,3072]{2,1,0:T(2,128)S(1)} %copy-done.2, f32[128,1536]{1,0:T(8,128)S(1)} %get-tuple-element.176.keep, bf16[128,1536]{1,0:T(8,128)(2,1)S(1)} %collective-permute-done.22.got, ...), custom_call_target="tpu_custom_call" | custom-call | flops 1000 | bytes 1000 | tf_op jit(solution)/shard_map/gate_and_add/pallas_call | solution.py:405
  (19 shorter events, 0.0 us)
Async XLA Ops:
  0.6 2.4 %copy-start = (bf16[2,128,3072]{2,1,0:T(8,128)(2,1)S(1)}, bf16[2,128,3072]{2,1,0:T(8,128)(2,1)}, u32[]{:S(2)}) copy-start(bf16[2,128,3072]{2,1,0:T(8,128)(2,1)} %hidden.3) | copy-start | bytes 4718596
  0.7 1.5 %copy-start.1 = (bf16[2,2,128,1536]{3,2,1,0:T(8,128)(2,1)S(1)}, bf16[2,2,128,1536]{3,2,1,0:T(8,128)(2,1)}, u32[]{:S(2)}) copy-start(bf16[2,2,128,1536]{3,2,1,0:T(8,128)(2,1)} %stale.1) | copy-start | bytes 4718596
  2.2 8.1 %copy-start.2 = (f32[3,2,3072]{2,1,0:T(2,128)S(1)}, f32[3,2,3072]{2,1,0:T(2,128)}, u32[]{:S(2)}) copy-start(f32[3,2,3072]{2,1,0:T(2,128)} %mod.5) | copy-start | bytes 221188
  2.2 8.1 %copy-start.3 = (f32[2,128]{1,0:T(2,128)S(1)}, f32[2,128]{1,0:T(2,128)}, u32[]{:S(2)}) copy-start(f32[2,128]{1,0:T(2,128)} %gain.5) | copy-start | bytes 3076
  3.1 7.3 %collective-permute-start = (bf16[128,3072]{1,0:T(8,128)(2,1)S(1)}, bf16[128,3072]{1,0:T(8,128)(2,1)S(1)}, u32[]{:S(2)}, u32[]{:S(2)}) collective-permute-start(bf16[128,3072]{1,0:T(8,128)(2,1)S(1)} %dynamic-slice_bitcast_fusion), channel_id=1, source_target_pairs={{0,2},{2,0},{4,6},{6,4},{8,10},{10,8},{12,14},{14,12},{16,18},{18,... | collective-permute-start | bytes 2359304 | tf_op jit(solution)/shard_map/ppermute | solution.py:435
  3.6 20.7 %collective-permute-start.1 = (bf16[2,2,128,384]{3,2,1,0:T(8,128)(2,1)S(1)}, bf16[2,2,128,384]{3,2,1,0:T(8,128)(2,1)S(1)}, u32[]{:S(2)}, u32[]{:S(2)}) collective-permute-start(bf16[2,2,128,384]{3,2,1,0:T(8,128)(2,1)S(1)} %get-tuple-element.93), channel_id=1, source_target_pairs={{0,8},{2,10},{4,12},{6,14},{8,0},{10,2},{12,4},{14,6},{16,24},{18,... | collective-permute-start | bytes 1179656 | tf_op jit(solution)/shard_map/ppermute | solution.py:435
  6.3 20.6 %collective-permute-start.2 = (bf16[2,2,128,384]{3,2,1,0:T(8,128)(2,1)S(1)}, bf16[2,2,128,384]{3,2,1,0:T(8,128)(2,1)S(1)}, u32[]{:S(2)}, u32[]{:S(2)}) collective-permute-start(bf16[2,2,128,384]{3,2,1,0:T(8,128)(2,1)S(1)} %get-tuple-element.94), channel_id=1, source_target_pairs={{0,16},{2,18},{4,20},{6,22},{8,24},{10,26},{12,28},{14,30},{16,0},... | collective-permute-start | bytes 1179656 | tf_op jit(solution)/shard_map/ppermute | solution.py:435
  8.9 18.0 %collective-permute-start.3 = (bf16[2,2,128,384]{3,2,1,0:T(8,128)(2,1)S(1)}, bf16[2,2,128,384]{3,2,1,0:T(8,128)(2,1)S(1)}, u32[]{:S(2)}, u32[]{:S(2)}) collective-permute-start(bf16[2,2,128,384]{3,2,1,0:T(8,128)(2,1)S(1)} %get-tuple-element.111.refs_0_.refs_4_), channel_id=1, source_target_pairs={{0,4},{2,6},{4,0},{6,2},{8,12},{10,14},{12,8},{14,10},{16,20},{18,... | collective-permute-start | bytes 1179656 | tf_op jit(solution)/shard_map/ppermute | solution.py:435
  27.9 22.2 %collective-permute-start.8 = (bf16[4,2,128,384]{3,2,1,0:T(8,128)(2,1)S(1)}, bf16[4,2,128,384]{3,2,1,0:T(8,128)(2,1)S(1)}, u32[]{:S(2)}, u32[]{:S(2)}) collective-permute-start(bf16[4,2,128,384]{3,2,1,0:T(8,128)(2,1)S(1)} %pack.2), channel_id=1, source_target_pairs={{0,2},{2,0},{4,6},{6,4},{8,10},{10,8},{12,14},{14,12},{16,18},{18,... | collective-permute-start | bytes 2359304 | tf_op jit(solution)/shard_map/ppermute | solution.py:435
  28.0 17.6 %collective-permute-start.4 = (bf16[2,2,128,384]{3,2,1,0:T(8,128)(2,1)S(1)}, bf16[2,2,128,384]{3,2,1,0:T(8,128)(2,1)S(1)}, u32[]{:S(2)}, u32[]{:S(2)}) collective-permute-start(bf16[2,2,128,384]{3,2,1,0:T(8,128)(2,1)S(1)} %get-tuple-element.107), channel_id=1, source_target_pairs={{0,24},{2,26},{4,28},{6,30},{8,16},{10,18},{12,20},{14,22},{16,8},... | collective-permute-start | bytes 1179656 | tf_op jit(solution)/shard_map/ppermute | solution.py:435
  30.5 15.1 %collective-permute-start.6 = (bf16[2,2,128,384]{3,2,1,0:T(8,128)(2,1)S(1)}, bf16[2,2,128,384]{3,2,1,0:T(8,128)(2,1)S(1)}, u32[]{:S(2)}, u32[]{:S(2)}) collective-permute-start(bf16[2,2,128,384]{3,2,1,0:T(8,128)(2,1)S(1)} %collective-permute-done.1.refs_2_.refs_8_), channel_id=1, source_target_pairs={{0,4},{2,6},{4,0},{6,2},{8,12},{10,14},{12,8},{14,10},{16,20},{18,... | collective-permute-start | bytes 1179656 | tf_op jit(solution)/shard_map/ppermute | solution.py:435
  32.0 18.1 %collective-permute-start.7 = (bf16[2,2,128,384]{3,2,1,0:T(8,128)(2,1)S(1)}, bf16[2,2,128,384]{3,2,1,0:T(8,128)(2,1)S(1)}, u32[]{:S(2)}, u32[]{:S(2)}) collective-permute-start(bf16[2,2,128,384]{3,2,1,0:T(8,128)(2,1)S(1)} %collective-permute-done.2.refs_3_.refs_12_), channel_id=1, source_target_pairs={{0,4},{2,6},{4,0},{6,2},{8,12},{10,14},{12,8},{14,10},{16,20},{18,... | collective-permute-start | bytes 1179656 | tf_op jit(solution)/shard_map/ppermute | solution.py:435
  32.6 13.1 %collective-permute-start.5 = (bf16[256,384]{1,0:T(8,128)(2,1)S(1)}, bf16[256,384]{1,0:T(8,128)(2,1)S(1)}, u32[]{:S(2)}, u32[]{:S(2)}) collective-permute-start(bf16[256,384]{1,0:T(8,128)(2,1)S(1)} %get-tuple-element.108), channel_id=1, source_target_pairs={{0,8},{2,10},{4,12},{6,14},{8,0},{10,2},{12,4},{14,6},{16,24},{18,... | collective-permute-start | bytes 589832 | tf_op jit(solution)/shard_map/ppermute | solution.py:435
  51.1 11.6 %collective-permute-start.12 = (bf16[3,2,128,384]{3,2,1,0:T(8,128)(2,1)S(1)}, bf16[3,2,128,384]{3,2,1,0:T(8,128)(2,1)S(1)}, u32[]{:S(2)}, u32[]{:S(2)}) collective-permute-start(bf16[3,2,128,384]{3,2,1,0:T(8,128)(2,1)S(1)} %pack.3), channel_id=1, source_target_pairs={{0,2},{2,0},{4,6},{6,4},{8,10},{10,8},{12,14},{14,12},{16,18},{18,... | collective-permute-start | bytes 1769480 | tf_op jit(solution)/shard_map/ppermute | solution.py:435
  51.2 11.5 %collective-permute-start.9 = (bf16[2,2,128,384]{3,2,1,0:T(8,128)(2,1)S(1)}, bf16[2,2,128,384]{3,2,1,0:T(8,128)(2,1)S(1)}, u32[]{:S(2)}, u32[]{:S(2)}) collective-permute-start(bf16[2,2,128,384]{3,2,1,0:T(8,128)(2,1)S(1)} %collective-permute-done.4.refs_2_.refs_16_), channel_id=1, source_target_pairs={{0,4},{2,6},{4,0},{6,2},{8,12},{10,14},{12,8},{14,10},{16,20},{18,... | collective-permute-start | bytes 1179656 | tf_op jit(solution)/shard_map/ppermute | solution.py:435
  52.8 8.8 %collective-permute-start.10 = (bf16[128,384]{1,0:T(8,128)(2,1)S(1)}, bf16[128,384]{1,0:T(8,128)(2,1)S(1)}, u32[]{:S(2)}, u32[]{:S(2)}) collective-permute-start(bf16[128,384]{1,0:T(8,128)(2,1)S(1)} %get-tuple-element.130), channel_id=1, source_target_pairs={{0,16},{2,18},{4,20},{6,22},{8,24},{10,26},{12,28},{14,30},{16,0},... | collective-permute-start | bytes 294920 | tf_op jit(solution)/shard_map/ppermute | solution.py:435
  52.8 8.8 %collective-permute-start.11 = (bf16[128,384]{1,0:T(8,128)(2,1)S(1)}, bf16[128,384]{1,0:T(8,128)(2,1)S(1)}, u32[]{:S(2)}, u32[]{:S(2)}) collective-permute-start(bf16[128,384]{1,0:T(8,128)(2,1)S(1)} %get-tuple-element.131), channel_id=1, source_target_pairs={{0,24},{2,26},{4,28},{6,30},{8,16},{10,18},{12,20},{14,22},{16,8},... | collective-permute-start | bytes 294920 | tf_op jit(solution)/shard_map/ppermute | solution.py:435
  62.7 3.8 %collective-permute-start.13 = (bf16[2,2,128,384]{3,2,1,0:T(8,128)(2,1)S(1)}, bf16[2,2,128,384]{3,2,1,0:T(8,128)(2,1)S(1)}, u32[]{:S(2)}, u32[]{:S(2)}) collective-permute-start(bf16[2,2,128,384]{3,2,1,0:T(8,128)(2,1)S(1)} %collective-permute-done.9.refs_18_), channel_id=1, source_target_pairs={{0,2},{2,0},{4,6},{6,4},{8,10},{10,8},{12,14},{14,12},{16,18},{18,... | collective-permute-start | bytes 1179656 | tf_op jit(solution)/shard_map/ppermute | solution.py:435
  62.7 10.9 %collective-permute-start.14 = (bf16[128,384]{1,0:T(8,128)(2,1)S(1)}, bf16[128,384]{1,0:T(8,128)(2,1)S(1)}, u32[]{:S(2)}, u32[]{:S(2)}) collective-permute-start(bf16[128,384]{1,0:T(8,128)(2,1)S(1)} %get-tuple-element.149), channel_id=1, source_target_pairs={{0,16},{2,18},{4,20},{6,22},{8,24},{10,26},{12,28},{14,30},{16,0},... | collective-permute-start | bytes 294920 | tf_op jit(solution)/shard_map/ppermute | solution.py:435
  65.2 8.5 %collective-permute-start.15 = (bf16[128,384]{1,0:T(8,128)(2,1)S(1)}, bf16[128,384]{1,0:T(8,128)(2,1)S(1)}, u32[]{:S(2)}, u32[]{:S(2)}) collective-permute-start(bf16[128,384]{1,0:T(8,128)(2,1)S(1)} %get-tuple-element.150), channel_id=1, source_target_pairs={{0,24},{2,26},{4,28},{6,30},{8,16},{10,18},{12,20},{14,22},{16,8},... | collective-permute-start | bytes 294920 | tf_op jit(solution)/shard_map/ppermute | solution.py:435
  66.6 24.4 %slice-start = ((s8[9437184]{0:T(1024)(128)(4,1)}), s8[4194304]{0:T(1024)(128)(4,1)S(1)}, s32[]{:S(2)}) async-start(s8[9437184]{0:T(1024)(128)(4,1)} %bitcast.6), calls=%async_computation | async-start | bytes 8388608
  66.6 24.4 %slice-start.1 = ((s8[9437184]{0:T(1024)(128)(4,1)}), s8[4194304]{0:T(1024)(128)(4,1)S(1)}, s32[]{:S(2)}) async-start(s8[9437184]{0:T(1024)(128)(4,1)} %bitcast.6), calls=%async_computation.1 | async-start | bytes 8388608
  73.7 17.2 %slice-start.2 = ((s8[9437184]{0:T(1024)(128)(4,1)}), s8[1048576]{0:T(1024)(128)(4,1)S(1)}, s32[]{:S(2)}) async-start(s8[9437184]{0:T(1024)(128)(4,1)} %bitcast.6), calls=%async_computation.2 | async-start | bytes 2097152
  73.7 11.7 %collective-permute-start.16 = (bf16[144,384]{1,0:T(8,128)(2,1)S(1)}, bf16[144,384]{1,0:T(8,128)(2,1)S(1)}, u32[]{:S(2)}, u32[]{:S(2)}) collective-permute-start(bf16[144,384]{1,0:T(8,128)(2,1)S(1)} %get-tuple-element.160), channel_id=1, source_target_pairs={{0,8},{2,10},{4,12},{6,14},{8,0},{10,2},{12,4},{14,6},{16,24},{18,... | collective-permute-start | bytes 331784 | tf_op jit(solution)/shard_map/ppermute | solution.py:435
  75.7 10.7 %collective-permute-start.17 = (bf16[144,384]{1,0:T(8,128)(2,1)S(1)}, bf16[144,384]{1,0:T(8,128)(2,1)S(1)}, u32[]{:S(2)}, u32[]{:S(2)}) collective-permute-start(bf16[144,384]{1,0:T(8,128)(2,1)S(1)} %get-tuple-element.161), channel_id=1, source_target_pairs={{0,16},{2,18},{4,20},{6,22},{8,24},{10,26},{12,28},{14,30},{16,0},... | collective-permute-start | bytes 331784 | tf_op jit(solution)/shard_map/ppermute | solution.py:435
  76.8 9.6 %collective-permute-start.18 = (bf16[144,384]{1,0:T(8,128)(2,1)S(1)}, bf16[144,384]{1,0:T(8,128)(2,1)S(1)}, u32[]{:S(2)}, u32[]{:S(2)}) collective-permute-start(bf16[144,384]{1,0:T(8,128)(2,1)S(1)} %get-tuple-element.162), channel_id=1, source_target_pairs={{0,24},{2,26},{4,28},{6,30},{8,16},{10,18},{12,20},{14,22},{16,8},... | collective-permute-start | bytes 331784 | tf_op jit(solution)/shard_map/ppermute | solution.py:435
  86.5 9.8 %collective-permute-start.19 = (bf16[144,384]{1,0:T(8,128)(2,1)S(1)}, bf16[144,384]{1,0:T(8,128)(2,1)S(1)}, u32[]{:S(2)}, u32[]{:S(2)}) collective-permute-start(bf16[144,384]{1,0:T(8,128)(2,1)S(1)} %get-tuple-element.173), channel_id=1, source_target_pairs={{0,8},{2,10},{4,12},{6,14},{8,0},{10,2},{12,4},{14,6},{16,24},{18,... | collective-permute-start | bytes 331784 | tf_op jit(solution)/shard_map/ppermute | solution.py:435
  88.6 10.1 %collective-permute-start.20 = (bf16[144,384]{1,0:T(8,128)(2,1)S(1)}, bf16[144,384]{1,0:T(8,128)(2,1)S(1)}, u32[]{:S(2)}, u32[]{:S(2)}) collective-permute-start(bf16[144,384]{1,0:T(8,128)(2,1)S(1)} %get-tuple-element.174), channel_id=1, source_target_pairs={{0,16},{2,18},{4,20},{6,22},{8,24},{10,26},{12,28},{14,30},{16,0},... | collective-permute-start | bytes 331784 | tf_op jit(solution)/shard_map/ppermute | solution.py:435
  88.9 9.8 %collective-permute-start.21 = (bf16[144,384]{1,0:T(8,128)(2,1)S(1)}, bf16[144,384]{1,0:T(8,128)(2,1)S(1)}, u32[]{:S(2)}, u32[]{:S(2)}) collective-permute-start(bf16[144,384]{1,0:T(8,128)(2,1)S(1)} %get-tuple-element.175), channel_id=1, source_target_pairs={{0,24},{2,26},{4,28},{6,30},{8,16},{10,18},{12,20},{14,22},{16,8},... | collective-permute-start | bytes 331784 | tf_op jit(solution)/shard_map/ppermute | solution.py:435
  94.7 10.6 %collective-permute-start.23 = (bf16[128,1536]{1,0:T(8,128)(2,1)S(1)}, bf16[128,1536]{1,0:T(8,128)(2,1)S(1)}, u32[]{:S(2)}, u32[]{:S(2)}) collective-permute-start(bf16[128,1536]{1,0:T(8,128)(2,1)S(1)} %get-tuple-element.171), channel_id=1, source_target_pairs={{0,1},{1,0},{2,3},{3,2},{4,5},{5,4},{6,7},{7,6},{8,9},{9,8},{10,11... | collective-permute-start | bytes 1179656 | tf_op jit(solution)/shard_map/ppermute | solution.py:490
  96.3 9.9 %collective-permute-start.25 = (bf16[2,128,1536]{2,1,0:T(8,128)(2,1)S(1)}, bf16[2,128,1536]{2,1,0:T(8,128)(2,1)S(1)}, u32[]{:S(2)}, u32[]{:S(2)}) collective-permute-start(bf16[2,128,1536]{2,1,0:T(8,128)(2,1)S(1)} %get-tuple-element.181.other), channel_id=1, source_target_pairs={{0,2},{2,0},{4,6},{6,4},{8,10},{10,8},{12,14},{14,12},{16,18},{18,... | collective-permute-start | bytes 2359304 | tf_op jit(solution)/shard_map/ppermute | solution.py:435
  102.4 10.5 %collective-permute-start.22 = (bf16[128,1536]{1,0:T(8,128)(2,1)S(1)}, bf16[128,1536]{1,0:T(8,128)(2,1)S(1)}, u32[]{:S(2)}, u32[]{:S(2)}) collective-permute-start(bf16[128,1536]{1,0:T(8,128)(2,1)S(1)} %get-tuple-element.177), channel_id=1, source_target_pairs={{0,1},{1,0},{2,3},{3,2},{4,5},{5,4},{6,7},{7,6},{8,9},{9,8},{10,11... | collective-permute-start | bytes 1179656 | tf_op jit(solution)/shard_map/ppermute | solution.py:494
  106.1 6.8 %collective-permute-start.24 = (bf16[128,1536]{1,0:T(8,128)(2,1)S(1)}, bf16[128,1536]{1,0:T(8,128)(2,1)S(1)}, u32[]{:S(2)}, u32[]{:S(2)}) collective-permute-start(bf16[128,1536]{1,0:T(8,128)(2,1)S(1)} %gate_and_add.2), channel_id=1, source_target_pairs={{0,2},{2,0},{4,6},{6,4},{8,10},{10,8},{12,14},{14,12},{16,18},{18,... | collective-permute-start | bytes 1179656 | tf_op jit(solution)/shard_map/ppermute | solution.py:435

commit v3 on v2

--- a/solution.py
+++ b/solution.py
@@ -52,6 +52,7 @@
 
 ANYWHERE = pl.BlockSpec(memory_space=pltpu.HBM)
 SCALARS = pl.BlockSpec(memory_space=pltpu.SMEM)
+RESIDENT = pl.BlockSpec(memory_space=pltpu.VMEM)
 
 
 def copy_all(sems, pairs):
@@ -85,22 +86,45 @@
     )(pos, stale)
 
 
-def pack_kernel(pos, *refs):
-    blocks, out, sems = refs[:-2], refs[-2], refs[-1]
-    copy_all(sems, [(r.at[:, 1 - pos[2]], out.at[i]) for i, r in enumerate(blocks)])
+def halves_kernel(block, keys, values, sems):
+    copy_all(sems, [(block.at[0], keys), (block.at[1], values)])
+
+
+def halves(block):
+    return pl.pallas_call(
+        halves_kernel,
+        out_shape=[out_of(block.shape[1:])] * 2,
+        in_specs=[ANYWHERE],
+        out_specs=[ANYWHERE] * 2,
+        scratch_shapes=[pltpu.SemaphoreType.DMA((2,))],
+        compiler_params=params(8),
+        name="halves",
+    )(block)
+
+
+def pack_kernel(counts, pos, *refs):
+    refs, out, sems = list(refs[:-2]), refs[-2], refs[-1]
+    pairs, other = [], 1 - pos[2]
+    for i, count in enumerate(counts):
+        if count == 1:
+            pairs.append((refs.pop(0).at[:, other], out.at[i]))
+        else:
+            pairs += [(refs.pop(0).at[other], out.at[i, kv]) for kv in range(2)]
+    copy_all(sems, pairs)
 
 
 def pack(pos, *blocks):
-    kv, clips, rows, width = blocks[0].shape
-    return pl.pallas_call(
-        pack_kernel,
-        out_shape=out_of((len(blocks), kv, rows, width)),
-        in_specs=[SCALARS] + [ANYWHERE] * len(blocks),
+    rows, width = blocks[0][0].shape[-2:]
+    flat = [a for block in blocks for a in block]
+    return pl.pallas_call(
+        functools.partial(pack_kernel, [len(block) for block in blocks]),
+        out_shape=out_of((len(blocks), 2, rows, width)),
+        in_specs=[SCALARS] + [ANYWHERE] * len(flat),
         out_specs=ANYWHERE,
-        scratch_shapes=[pltpu.SemaphoreType.DMA((len(blocks),))],
+        scratch_shapes=[pltpu.SemaphoreType.DMA((len(flat),))],
         compiler_params=params(8),
         name="pack",
-    )(pos, *blocks)
+    )(pos, *flat)
 
 
 def query_kernel(groups, per_step, pos, hidden, got, mod, gain, weight, normed, whole, *slots):
@@ -255,170 +279,148 @@
     )(queries, mine, other)
 
 
-def group_kernel(part, blocks, pos, *refs):
-    queries = refs[:blocks]
-    cached = [refs[blocks + 4 * g : blocks + 4 * g + 4] for g in range(blocks)]
-    outs = refs[5 * blocks :]
-    rows = queries[0].shape[0]
+def group_kernel(part, blocks, places, pos, *refs):
+    count = sum(n for n, _ in places)
+    queries, refs, outs = refs[:blocks], list(refs[blocks : blocks + count]), refs[blocks + count :]
+    cached = [[refs.pop(0) for _ in range(n)] for n, _ in places]
+    rows, width = queries[-1].shape
+    mine = slice(part * rows, (part + 1) * rows)
+    clip = pl.ds(pos[2], 1)
     ones = jnp.ones((4 * rows, HEAD), BF)
-    keys = [jnp.concatenate([r[0] for r in g], axis=0) for g in cached]
-    values = [jnp.concatenate([r[1] for r in g], axis=0) for g in cached]
-    values = [jnp.concatenate([v, ones], axis=1) for v in values]
-    for b in range(blocks):
-        q = queries[b][...]
-        scores = []
-        for s in range(blocks):
-            sc = nt(q, keys[s])
-            if s == b:
-                own = [sc[:, j * rows : (j + 1) * rows] for j in range(4)]
-                own[part] = jnp.full((rows, rows), -1e30, F32)
-                sc = jnp.concatenate(own, axis=1)
-            scores.append(sc)
-        peak = functools.reduce(
-            jnp.maximum, [jnp.max(sc, axis=-1, keepdims=True) for sc in scores]
-        )
-        summed = None
-        for sc, v in zip(scores, values):
-            term = nn(jnp.exp2((sc - peak) * SCALE2).astype(BF), v)
-            summed = term if summed is None else summed + term
-        total = summed[:, HEAD:]
-        outs[b][0:rows, :] = (summed[:, :HEAD] / total).astype(BF)
-        level = jnp.transpose(peak * SCALE2 + jnp.log2(total))[0:8, :]
-        high = level.astype(BF).astype(F32)
-        mid = (level - high).astype(BF).astype(F32)
-        low = level - high - mid
-        row = lax.broadcasted_iota(jnp.int32, (8, HEAD), 0)
-        three = jnp.where(row == 0, high, jnp.where(row == 1, mid, low))
-        outs[b][rows : rows + EXTRA, :] = jnp.concatenate([three, three], axis=0).astype(BF)
+
+    def load(kv, group, at):
+        parts = []
+        for block, (n, place) in list(zip(cached, places))[4 * group : 4 * group + 4]:
+            if place is not None:
+                parts.append(block[0][place, kv, :, at])
+            elif n == 2:
+                parts.append(block[kv][clip, :, at][0])
+            else:
+                parts.append(block[0][kv, clip, :, at][0])
+        return jnp.concatenate(parts, axis=0)
+
+    for h in range(width // HEAD):
+        at = slice(h * HEAD, (h + 1) * HEAD)
+        keys = [load(0, g, at) for g in range(blocks)]
+        values = [jnp.concatenate([load(1, g, at), ones], axis=1) for g in range(blocks)]
+        for b in range(blocks):
+            q = queries[b][mine if b < 2 else slice(None), at]
+            scores = []
+            for s in range(blocks):
+                sc = nt(q, keys[s])
+                if s == b:
+                    own = [sc[:, j * rows : (j + 1) * rows] for j in range(4)]
+                    own[part] = jnp.full((rows, rows), -1e30, F32)
+                    sc = jnp.concatenate(own, axis=1)
+                scores.append(sc)
+            peak = functools.reduce(
+                jnp.maximum, [jnp.max(sc, axis=-1, keepdims=True) for sc in scores]
+            )
+            summed = None
+            for sc, v in zip(scores, values):
+                term = nn(jnp.exp2((sc - peak) * SCALE2).astype(BF), v)
+                summed = term if summed is None else summed + term
+            total = summed[:, HEAD:]
+            outs[b][0:rows, at] = (summed[:, :HEAD] / total).astype(BF)
+            level = jnp.transpose(peak * SCALE2 + jnp.log2(total))[0:8, :]
+            high = level.astype(BF).astype(F32)
+            mid = (level - high).astype(BF).astype(F32)
+            low = level - high - mid
+            row = lax.broadcasted_iota(jnp.int32, (8, HEAD), 0)
+            three = jnp.where(row == 0, high, jnp.where(row == 1, mid, low))
+            outs[b][rows : rows + EXTRA, at] = jnp.concatenate([three, three], axis=0).astype(BF)
 
 
 def attend_groups(part, pos, queries, cached):
     blocks = len(queries)
     rows, width = queries[-1].shape
     flat = [a for g in cached for a in g]
-
-    def spec(place):
-        if place is None:
-            return pl.BlockSpec((2, None, rows, HEAD), lambda h, pos: (0, pos[2], 0, h))
-        return pl.BlockSpec((None, 2, rows, HEAD), lambda h, pos: (place, 0, 0, h))
-
-    return pl.pallas_call(
-        functools.partial(group_kernel, part, blocks),
-        grid_spec=pltpu.PrefetchScalarGridSpec(
-            num_scalar_prefetch=1,
-            grid=(width // HEAD,),
-            in_specs=[pl.BlockSpec((rows, HEAD), lambda h, pos: (part, h))] * 2
-            + [pl.BlockSpec((rows, HEAD), lambda h, pos: (0, h))] * (blocks - 2)
-            + [spec(place) for _, place in flat],
-            out_specs=[pl.BlockSpec((rows + EXTRA, HEAD), lambda h, pos: (0, h))] * blocks,
-        ),
+    arrays = [a for block, _ in flat for a in block]
+    places = [(len(block), place) for block, place in flat]
+    return pl.pallas_call(
+        functools.partial(group_kernel, part, blocks, places),
+        in_specs=[SCALARS] + [RESIDENT] * (blocks + len(arrays)),
+        out_specs=[RESIDENT] * blocks,
         out_shape=[out_of((rows + EXTRA, width))] * blocks,
         compiler_params=params(32),
         cost_estimate=SMALL,
         name="attend_groups",
-    )(pos, *queries, *[array for array, _ in flat])
-
-
-def out_kernel(groups, pos, *refs):
+    )(pos, *queries, *arrays)
+
+
+def out_kernel(part, groups, pos, *refs):
     back = refs[:groups]
-    acc, top, total, weight, send, keep, product = refs[groups:]
-    step = pl.program_id(0)
-    rows, width = acc.shape
-
+    acc, top, total, weight, send, keep, attended = refs[groups:]
+    rows = send.shape[0]
+    width = acc.shape[1] // groups
+    mine = slice(part * rows, (part + 1) * rows)
     for s in range(groups):
-
-        @pl.when(step == s)
-        def _(s=s):
-            cols = []
-            for h in range(width // HEAD):
-                at = slice(h * HEAD, (h + 1) * HEAD)
-                three = back[s][rows : rows + 8, at].astype(F32)
-                level = three[0:1, :] + three[1:2, :] + three[2:3, :]
-                level = jnp.transpose(jnp.broadcast_to(level, (rows, HEAD)))
-                own = top[:, at]
-                peak = jnp.maximum(level, own)
-                w_own, w_back = jnp.exp2(own - peak), jnp.exp2(level - peak)
-                mixed = acc[:, at] * w_own + back[s][0:rows, at].astype(F32) * w_back
-                cols.append((mixed / (total[:, at] * w_own + w_back)).astype(BF))
-            part = nn(jnp.concatenate(cols, axis=1), weight[...])
-            if s == 0:
-                product[...] = part
-            else:
-                product[...] += part
-
-    @pl.when(step == groups - 1)
-    def _():
-        half = product.shape[1] // 2
-        mine = pl.multiple_of(pos[1] * half, HEAD)
-        other = pl.multiple_of((1 - pos[1]) * half, HEAD)
-        send[...] = product[:, pl.ds(other, half)].astype(BF)
-        keep[...] = product[:, pl.ds(mine, half)]
+        for h in range(width // HEAD):
+            at = slice(h * HEAD, (h + 1) * HEAD)
+            cols = pl.ds(pl.multiple_of((pos[0] ^ s) * width + h * HEAD, HEAD), HEAD)
+            three = back[s][rows : rows + 8, at].astype(F32)
+            level = three[0:1, :] + three[1:2, :] + three[2:3, :]
+            level = jnp.transpose(jnp.broadcast_to(level, (rows, HEAD)))
+            own = top[mine, cols]
+            peak = jnp.maximum(level, own)
+            w_own, w_back = jnp.exp2(own - peak), jnp.exp2(level - peak)
+            mixed = acc[mine, cols] * w_own + back[s][0:rows, at].astype(F32) * w_back
+            attended[:, cols] = (mixed / (total[mine, cols] * w_own + w_back)).astype(BF)
+    half = weight.shape[1] // 2
+    block = math.gcd(half, 768)
+    for out, place in ((send, 1 - pos[1]), (keep, pos[1])):
+        for i in range(0, half, block):
+            cols = pl.ds(pl.multiple_of(place * half + i, HEAD), block)
+            out[:, i : i + block] = nn(attended[...], weight[:, cols]).astype(out.dtype)
 
 
 def project_out(part, pos, back, acc, top, total, weight):
     groups = len(back)
     rows, width_all = acc.shape[0] // 2, acc.shape[1]
-    width = width_all // groups
-    cols = weight.shape[1]
-    own = pl.BlockSpec((rows, width), lambda i, pos: (part, pos[0] ^ i))
-    half = (rows, cols // 2)
-    return pl.pallas_call(
-        functools.partial(out_kernel, groups),
-        grid_spec=pltpu.PrefetchScalarGridSpec(
-            num_scalar_prefetch=1,
-            grid=(groups,),
-            in_specs=[full(back[0].shape)] * groups
-            + [own] * 3
-            + [pl.BlockSpec((width, cols), lambda i, pos: (pos[0] ^ i, 0))],
-            out_specs=[full(half), full(half)],
-            scratch_shapes=[pltpu.VMEM((rows, cols), F32)],
-        ),
+    half = (rows, weight.shape[1] // 2)
+    return pl.pallas_call(
+        functools.partial(out_kernel, part, groups),
+        in_specs=[SCALARS] + [RESIDENT] * (groups + 4),
+        out_specs=[RESIDENT] * 2,
         out_shape=[out_of(half), out_of(half, F32)],
-        compiler_params=params(24),
+        scratch_shapes=[pltpu.VMEM((rows, width_all), BF)],
+        compiler_params=params(32),
         cost_estimate=LARGE,
         name="merge_and_project",
     )(pos, *back, acc, top, total, weight)
 
 
 def gated(pos, rows_in, mod, keep, got):
-    gate = mod[2, pl.ds(pos[2], 1), :]
+    half = keep.shape[1]
+    gate = mod[2, pl.ds(pos[2], 1), pl.ds(pl.multiple_of(pos[1] * half, HEAD), half)]
     return (rows_in.astype(F32) + gate * (keep[...] + got[...].astype(F32))).astype(BF)
 
 
 def other_rows_kernel(pos, hidden, mod, keep, got, out):
-    out[...] = gated(pos, hidden[...], mod, keep, got)
+    half = keep.shape[1]
+    cols = pl.ds(pl.multiple_of(pos[1] * half, HEAD), half)
+    out[...] = gated(pos, hidden[:, cols], mod, keep, got)
 
 
 def my_rows_kernel(pos, hidden, mod, keep, got, theirs, out):
-    out[pl.ds(pos[2], 1)] = gated(pos, hidden[0], mod, keep, got)[None]
-    out[pl.ds(1 - pos[2], 1)] = theirs[...][None]
-
-
-def finish(pos, hidden, mod, keep, got, theirs=None):
-    half = keep.shape
-    if theirs is None:
-        hidden_spec = pl.BlockSpec(half, lambda i, pos: (0, pos[1]))
-        extra, shape, body = [], half, other_rows_kernel
-    else:
-        hidden_spec = pl.BlockSpec((1,) + half, lambda i, pos: (pos[2], 0, pos[1]))
-        extra, shape, body = [theirs], (2,) + half, my_rows_kernel
-    return pl.pallas_call(
-        body,
-        grid_spec=pltpu.PrefetchScalarGridSpec(
-            num_scalar_prefetch=1,
-            grid=(1,),
-            in_specs=[
-                hidden_spec,
-                pl.BlockSpec(mod.shape[:2] + half[1:], lambda i, pos: (0, 0, pos[1])),
-            ]
-            + [full(half)] * (2 + len(extra)),
-            out_specs=full(shape),
-        ),
+    half = keep.shape[1]
+    cols = pl.ds(pl.multiple_of(pos[1] * half, HEAD), half)
+    mine, other = pl.ds(pos[2], 1), pl.ds(1 - pos[2], 1)
+    out[mine] = gated(pos, hidden[mine, :, cols][0], mod, keep, got)[None]
+    out[other] = theirs[...][None]
+
+
+def finish(pos, hidden, mod, keep, got, *theirs):
+    shape = (2,) * len(theirs) + keep.shape
+    return pl.pallas_call(
+        my_rows_kernel if theirs else other_rows_kernel,
+        in_specs=[SCALARS] + [RESIDENT] * (4 + len(theirs)),
+        out_specs=RESIDENT,
         out_shape=out_of(shape),
         compiler_params=params(24),
         cost_estimate=SMALL,
         name="gate_and_add",
-    )(pos, hidden, mod, keep, got, *extra)
+    )(pos, hidden, mod, keep, got, *theirs)
 
 
 def tie(value, *others):
@@ -441,50 +443,55 @@
     step = lax.optimization_barrier
 
     cut = cut_stale(pos, stale_kv, groups)
-    near, one, two = cut[0], along(cut[1], 1), along(cut[2], 2)
-    far_near = across(near, 2)
+    near, two, one = cut[:1], [along(cut[2], 2)], [along(cut[1], 1)]
+    far_near = [across(near[0], 2)]
     hidden_now = tie(hidden_states, *cut)
     hidden_for = lax.dynamic_index_in_dim(hidden_now, 1 - pos[2], 0, keepdims=False)
     hidden_got = across(hidden_for, 1)
     normed, queries, *slots = make_queries(
         pos, hidden_states, hidden_got, modulation, qk_gain, weights, groups
     )
+    normed, queries, slots, near, one, far_near, cut_three = step(
+        (normed, queries, slots, near, one, far_near, cut[3])
+    )
+
+    three = [along(cut_three, 3)]
+    far_one = [across(a, 2) for a in halves(one[0])]
     fresh = make_fresh(0, normed, qk_gain, weights)
-    normed, queries, slots, fresh, near, one, two, far_near, cut_three = step(
-        (normed, queries, slots, fresh, near, one, two, far_near, cut[3])
-    )
-
-    three, asked_one = along(cut_three, 3), along(slots[1], 1)
-    far_one, far_two = across(one, 2), across(two, 2)
-    swap_a = across(pack(pos, near, far_near, one, two), 1)
+    two, far_one, fresh, slots, queries, normed = step(
+        (two, far_one, fresh, slots, queries, normed)
+    )
+
+    far_two = [across(a, 2) for a in halves(two[0])]
+    asked = [slots[0], along(slots[1], 1)]
     fresh = make_fresh(1, normed, qk_gain, weights, fresh)
+    three, far_two, asked, fresh, slots, queries = step(
+        (three, far_two, asked, fresh, slots, queries)
+    )
+
+    far_three = [across(three[0], 2)]
+    their_far = [along(slots[2 * s - 1], s) for s in (2, 3)]
+    swapped = [across(pack(pos, near, far_near, one, far_one, two, far_two, three), 1)]
     own = attend_own(queries, *fresh)
-    three, asked_one, far_one, far_two, swap_a, own, slots = step(
-        (three, asked_one, far_one, far_two, swap_a, own, slots)
-    )
-
-    far_three = across(three, 2)
-    their_queries = [slots[0], asked_one] + [along(slots[2 * s - 1], s) for s in (2, 3)]
-    swap_b = across(pack(pos, far_one, far_two, three), 1)
-    far_three, their_queries, swap_b, slots, asked_one = step(
-        (far_three, their_queries, swap_b, slots, asked_one)
-    )
-
-    my_queries = [slots[0], asked_one] + [along(slots[2 * s - 2], s) for s in (2, 3)]
+    far_three, their_far, asked, swapped, own, slots = step(
+        (far_three, their_far, asked, swapped, own, slots)
+    )
+
+    my_far = [along(slots[2 * s - 2], s) for s in (2, 3)]
+    their_queries, my_queries = asked + their_far, asked + my_far
     held = [
-        [(near, None), (swap_a, 0), (far_near, None), (swap_a, 1)],
-        [(one, None), (swap_a, 2), (far_one, None), (swap_b, 0)],
-        [(two, None), (swap_a, 3), (far_two, None), (swap_b, 1)],
-        [(three, None), (swap_b, 2), (far_three, None), (across(far_three, 1), None)],
+        [(near, None), (swapped, 0), (far_near, None), (swapped, 1)],
+        [(one, None), (swapped, 2), (far_one, None), (swapped, 3)],
+        [(two, None), (swapped, 4), (far_two, None), (swapped, 5)],
+        [(three, None), (swapped, 6), (far_three, None), ([across(far_three[0], 1)], None)],
     ]
     theirs = attend_groups(1, pos, their_queries, held)
     theirs, my_queries = step((theirs, my_queries))
-
     back = [theirs[0]] + [along(theirs[s], s) for s in range(1, groups)]
+    my_queries[0] = tie(my_queries[0], theirs)
     mine = attend_groups(0, pos, my_queries, held)
-    mine, back = step((mine, back))
-
     mine_back = [mine[0]] + [along(mine[s], s) for s in range(1, groups)]
+    back[0] = tie(back[0], mine)
     swap = [(0, 1), (1, 0)]
     send, keep = project_out(1, pos, back, *own, out_weight)
     got = lax.ppermute(send, "tp", swap)

time: 115 us -> 110 us (0.957)
  the two profiles are of different devices: /device:TPU:0 before, /device:TPU:12 now
where the time goes in v3:
time: 110 us; the launch traced here: 109 us
  Pallas kernels  47.3 us (43%)
  waiting for transfers between devices  32.6 us (30%)
  starting transfers between devices  27 us (25%)
  local copies, waits for them, and re-layouts  1.59 us (1%)
    ppermute x25, starting transfers between devices, across(): return lax.ppermute(value, 'patch', [(i, i ^ bit) for i in range(patches)])  25.5 us
    ppermute x25, waiting for transfers between devices, across(): return lax.ppermute(value, 'patch', [(i, i ^ bit) for i in range(patches)])  23.5 us
    pallas_call x2, Pallas kernels, make_fresh(): pl.pallas_call(functools.partial(fresh_kernel, slot), grid=(cols // block...  10.7 us
    pallas_call x2, Pallas kernels, attend_groups(): pl.pallas_call(functools.partial(group_kernel, part, blocks, places), in_...  10.3 us
    pallas_call x1, Pallas kernels, make_queries(): pl.pallas_call(functools.partial(query_kernel, groups, per_step), grid_sp...  7.36 us
    pallas_call x1, Pallas kernels, attend_own(): pl.pallas_call(own_kernel, grid=(cols // block,), in_specs=[wide, kv, kv]...  6.55 us
    pallas_call x2, Pallas kernels, project_out(): pl.pallas_call(functools.partial(out_kernel, part, groups), in_specs=[SCA...  4.88 us
    ppermute x1, waiting for transfers between devices, spread_heads(): got = lax.ppermute(send, 'tp', swap)  4.78 us
  transfers between devices with their start and end apart: 27, of which 14 were waited for; matrix products, arithmetic and copies ran while one was open for 0% of the time, Pallas kernels for 39%

profile of v3, /device:TPU:12, one launch (start us, length us, event | category | flops | bytes accessed | tf_op | source)
XLA Modules:
  0.0 109.5 jit_solution(6351400131616305939)
XLA Ops:
  0.7 0.1 pad_add_fusion.pos
  0.7 1.5 %copy-done.1 = bf16[2,2,128,1536]{3,2,1,0:T(8,128)(2,1)S(1)} copy-done((bf16[2,2,128,1536]{3,2,1,0:T(8,128)(2,1)S(1)}, bf16[2,2,128,1536]{3,2,1,0:T(8,128)(2,1)}, u32[]{:S(2)}) %copy-start.1) | copy-done | bytes 1572888
  2.3 0.8 cut_stale.1
  3.0 0.1 dynamic-slice_bitcast_fusion
  3.1 0.1 collective-permute-start
  3.2 0.5 collective-permute-start.1
  3.7 1.5 %collective-permute-start.2 = (bf16[2,2,128,384]{3,2,1,0:T(8,128)(2,1)S(1)}, bf16[2,2,128,384]{3,2,1,0:T(8,128)(2,1)S(1)}, u32[]{:S(2)}, u32[]{:S(2)}) collective-permute-start(bf16[2,2,128,384]{3,2,1,0:T(8,128)(2,1)S(1)} %get-tuple-element.147.refs_0_.refs_4_), channel_id=1, source_target_pairs={{0,4},{2,6},{4,0},{6,2},{8,12},{10,14},{12,8},{14,10},{16,20},{18,... | collective-permute-start | bytes 1179656 | tf_op jit(solution)/shard_map/ppermute | solution.py:437
  5.2 2.6 %collective-permute-start.4 = (bf16[2,2,128,384]{3,2,1,0:T(8,128)(2,1)S(1)}, bf16[2,2,128,384]{3,2,1,0:T(8,128)(2,1)S(1)}, u32[]{:S(2)}, u32[]{:S(2)}) collective-permute-start(bf16[2,2,128,384]{3,2,1,0:T(8,128)(2,1)S(1)} %get-tuple-element.102), channel_id=1, source_target_pairs={{0,16},{2,18},{4,20},{6,22},{8,24},{10,26},{12,28},{14,30},{16,0},... | collective-permute-start | bytes 1179656 | tf_op jit(solution)/shard_map/ppermute | solution.py:437
  7.8 0.0 collective-permute-done.got.hidden
  7.8 7.4 %norm_and_queries.1 = (bf16[256,3072]{1,0:T(8,128)(2,1)S(1)}, bf16[256,1536]{1,0:T(8,128)(2,1)S(1)}, bf16[256,384]{1,0:T(8,128)(2,1)S(1)}, bf16[256,384]{1,0:T(8...) custom-call(s32[3]{0:T(128)S(1)} %pad_add_fusion.pos, ...), custom_call_target="tpu_custom_call" | custom-call | flops 1000 | bytes 1000 | tf_op jit(solution)/shard_map/norm_and_queries/pallas_call | solution.py:171
  15.2 4.6 %collective-permute-done.1.block.refs_2_.refs_8_ = bf16[2,2,128,384]{3,2,1,0:T(8,128)(2,1)S(1)} collective-permute-done((bf16[2,2,128,384]{3,2,1,0:T(8,128)(2,1)S(1)}, bf16[2,2,128,384]{3,2,1,0:T(8,128)(2,1)S(1)}, u32[]{:S(2)}, u32[]{:S(2)}) %collective-permute-start.1) | collective-permute-done | bytes 393248 | tf_op jit(solution)/shard_map/ppermute | solution.py:437
  19.8 0.5 halves.2
  20.3 2.5 %collective-permute-start.5 = (bf16[2,128,384]{2,1,0:T(8,128)(2,1)S(1)}, bf16[2,128,384]{2,1,0:T(8,128)(2,1)S(1)}, u32[]{:S(2)}, u32[]{:S(2)}) collective-permute-start(bf16[2,128,384]{2,1,0:T(8,128)(2,1)S(1)} %get-tuple-element.115), channel_id=1, source_target_pairs={{0,4},{2,6},{4,0},{6,2},{8,12},{10,14},{12,8},{14,10},{16,20},{18,... | collective-permute-start | bytes 589832 | tf_op jit(solution)/shard_map/ppermute | solution.py:437
  22.8 0.1 collective-permute-start.6
  22.9 1.6 %collective-permute-start.3 = (bf16[2,2,128,384]{3,2,1,0:T(8,128)(2,1)S(1)}, bf16[2,2,128,384]{3,2,1,0:T(8,128)(2,1)S(1)}, u32[]{:S(2)}, u32[]{:S(2)}) collective-permute-start(bf16[2,2,128,384]{3,2,1,0:T(8,128)(2,1)S(1)} %get-tuple-element.113), channel_id=1, source_target_pairs={{0,24},{2,26},{4,28},{6,30},{8,16},{10,18},{12,20},{14,22},{16,8},... | collective-permute-start | bytes 1179656 | tf_op jit(solution)/shard_map/ppermute | solution.py:437
  24.5 5.5 %fresh_keys.1 = (bf16[2,128,1536]{2,1,0:T(8,128)(2,1)S(1)}, bf16[2,128,1536]{2,1,0:T(8,128)(2,1)S(1)}) custom-call(bf16[256,3072]{1,0:T(8,128)(2,1)S(1)} %get-tuple-element.132.normed, f32[2,128]{1,0:T(2,128)S(1)} %copy-done.3, bf16[3,3072,1536]{2,1,0:T(8,128)(2,1)} %bitcast.9), custom_call_target="tpu_custom_call" | custom-call | flops 1000 | bytes 1000 | tf_op jit(solution)/shard_map/fresh_keys/pallas_call | solution.py:213
  30.0 0.0 collective-permute-done.5.refs_3_.refs_10_
  30.0 1.8 %collective-permute-done.6.refs_4_.refs_11_ = bf16[2,128,384]{2,1,0:T(8,128)(2,1)S(1)} collective-permute-done((bf16[2,128,384]{2,1,0:T(8,128)(2,1)S(1)}, bf16[2,128,384]{2,1,0:T(8,128)(2,1)S(1)}, u32[]{:S(2)}, u32[]{:S(2)}) %collective-permute-start.6) | collective-permute-done | bytes 196640 | tf_op jit(solution)/shard_map/ppermute | solution.py:437
  31.8 2.5 %collective-permute-start.9 = (bf16[256,384]{1,0:T(8,128)(2,1)S(1)}, bf16[256,384]{1,0:T(8,128)(2,1)S(1)}, u32[]{:S(2)}, u32[]{:S(2)}) collective-permute-start(bf16[256,384]{1,0:T(8,128)(2,1)S(1)} %get-tuple-element.131), channel_id=1, source_target_pairs={{0,8},{2,10},{4,12},{6,14},{8,0},{10,2},{12,4},{14,6},{16,24},{18,... | collective-permute-start | bytes 589832 | tf_op jit(solution)/shard_map/ppermute | solution.py:437
  34.2 0.5 halves.3
  34.7 1.8 %collective-permute-start.7 = (bf16[2,128,384]{2,1,0:T(8,128)(2,1)S(1)}, bf16[2,128,384]{2,1,0:T(8,128)(2,1)S(1)}, u32[]{:S(2)}, u32[]{:S(2)}) collective-permute-start(bf16[2,128,384]{2,1,0:T(8,128)(2,1)S(1)} %get-tuple-element.128), channel_id=1, source_target_pairs={{0,4},{2,6},{4,0},{6,2},{8,12},{10,14},{12,8},{14,10},{16,20},{18,... | collective-permute-start | bytes 589832 | tf_op jit(solution)/shard_map/ppermute | solution.py:437
  36.5 0.3 collective-permute-start.8
  36.8 5.2 %fresh_values.1 = (bf16[2,128,1536]{2,1,0:T(8,128)(2,1)S(1)}, bf16[2,128,1536]{2,1,0:T(8,128)(2,1)S(1)}) custom-call(bf16[256,3072]{1,0:T(8,128)(2,1)S(1)} %get-tuple-element.132.normed, f32[2,128]{1,0:T(2,128)S(1)} %copy-done.3, bf16[3,3072,1536]{2,1,0:T(8,128)(2,1)} %bitcast.10, ...), custom_call_target="tpu_custom_call", output_to_operand_aliasing={{0}: (3, {}), {1}: (4, {})} | custom-call | flops 1000 | bytes 1000 | tf_op jit(solution)/shard_map/fresh_values/pallas_call | solution.py:213
  42.0 0.4 collective-permute-done.3.refs_8_.refs_18_
  42.4 0.1 collective-permute-done.7.refs_6_.refs_15_
  42.5 2.1 %collective-permute-done.8.refs_7_.refs_16_ = bf16[2,128,384]{2,1,0:T(8,128)(2,1)S(1)} collective-permute-done((bf16[2,128,384]{2,1,0:T(8,128)(2,1)S(1)}, bf16[2,128,384]{2,1,0:T(8,128)(2,1)S(1)}, u32[]{:S(2)}, u32[]{:S(2)}) %collective-permute-start.8) | collective-permute-done | bytes 196640 | tf_op jit(solution)/shard_map/ppermute | solution.py:437
  44.6 1.8 %pack.1 = bf16[7,2,128,384]{3,2,1,0:T(8,128)(2,1)S(1)} custom-call(s32[3]{0:T(128)S(1)} %pad_add_fusion.pos, bf16[2,2,128,384]{3,2,1,0:T(8,128)(2,1)S(1)} %get-tuple-element.147.refs_0_.refs_4_, bf16[2,2,128,384]{3,2,1,0:T(8,128)(2,1)S(1)} %collective-permute-done.2.refs_1_.refs_6_, ...), custom_call_target="tpu_custom_call" | custom-call | tf_op jit(solution)/shard_map/pack/pallas_call | solution.py:119
  46.4 0.1 collective-permute-start.13
  46.5 1.5 %collective-permute-start.10 = (bf16[2,2,128,384]{3,2,1,0:T(8,128)(2,1)S(1)}, bf16[2,2,128,384]{3,2,1,0:T(8,128)(2,1)S(1)}, u32[]{:S(2)}, u32[]{:S(2)}) collective-permute-start(bf16[2,2,128,384]{3,2,1,0:T(8,128)(2,1)S(1)} %collective-permute-done.3.refs_8_.refs_18_), channel_id=1, source_target_pairs={{0,4},{2,6},{4,0},{6,2},{8,12},{10,14},{12,8},{14,10},{16,20},{18,... | collective-permute-start | bytes 1179656 | tf_op jit(solution)/shard_map/ppermute | solution.py:437
  48.0 1.3 %collective-permute-start.11 = (bf16[128,384]{1,0:T(8,128)(2,1)S(1)}, bf16[128,384]{1,0:T(8,128)(2,1)S(1)}, u32[]{:S(2)}, u32[]{:S(2)}) collective-permute-start(bf16[128,384]{1,0:T(8,128)(2,1)S(1)} %get-tuple-element.143), channel_id=1, source_target_pairs={{0,16},{2,18},{4,20},{6,22},{8,24},{10,26},{12,28},{14,30},{16,0},... | collective-permute-start | bytes 294920 | tf_op jit(solution)/shard_map/ppermute | solution.py:437
  49.3 0.5 collective-permute-start.12
  49.7 6.6 %attend_own.1 = (f32[256,1536]{1,0:T(8,128)S(1)}, f32[256,1536]{1,0:T(8,128)S(1)}, f32[256,1536]{1,0:T(8,128)S(1)}) custom-call(bf16[256,1536]{1,0:T(8,128)(2,1)S(1)} %get-tuple-element.153.q, bf16[2,128,1536]{2,1,0:T(8,128)(2,1)S(1)} %get-tuple-element.196.mine, bf16[2,128,1536]{2,1,0:T(8,128)(2,1)S(1)} %get-tuple-element.197.other), custom_call_target="tpu_custom_call" | custom-call | flops 1000 | bytes 1000 | tf_op jit(solution)/shard_map/attend_own/pallas_call | solution.py:270
  56.3 0.4 collective-permute-done.11.refs_2_
  56.7 2.3 %collective-permute-done.12.refs_3_ = bf16[128,384]{1,0:T(8,128)(2,1)S(1)} collective-permute-done((bf16[128,384]{1,0:T(8,128)(2,1)S(1)}, bf16[128,384]{1,0:T(8,128)(2,1)S(1)}, u32[]{:S(2)}, u32[]{:S(2)}) %collective-permute-start.12) | collective-permute-done | bytes 98336 | tf_op jit(solution)/shard_map/ppermute | solution.py:437
  59.0 0.0 collective-permute-done.10.refs_20_
  59.0 0.0 collective-permute-done.13.refs_5_.refs_7_.refs_9_.refs_12_.refs_14_.refs_17_.refs_19_
  59.0 0.0 collective-permute-start.14
  59.0 1.2 %collective-permute-start.15 = (bf16[128,384]{1,0:T(8,128)(2,1)S(1)}, bf16[128,384]{1,0:T(8,128)(2,1)S(1)}, u32[]{:S(2)}, u32[]{:S(2)}) collective-permute-start(bf16[128,384]{1,0:T(8,128)(2,1)S(1)} %get-tuple-element.171), channel_id=1, source_target_pairs={{0,16},{2,18},{4,20},{6,22},{8,24},{10,26},{12,28},{14,30},{16,0},... | collective-permute-start | bytes 294920 | tf_op jit(solution)/shard_map/ppermute | solution.py:437
  60.2 0.5 collective-permute-start.16
  60.6 0.1 collective-permute-done.14.refs_21_
  60.7 5.1 %attend_groups.2 = (bf16[144,384]{1,0:T(8,128)(2,1)S(1)}, bf16[144,384]{1,0:T(8,128)(2,1)S(1)}, bf16[144,384]{1,0:T(8,128)(2,1)S(1)}, bf16[144,384]{1,0:T(8,128)(2,1)S(1)}) custom-call(s32[3]{0:T(128)S(1)} %pad_add_fusion.pos, bf16[256,384]{1,0:T(8,128)(2,1)S(1)} %get-tuple-element.178.refs_0_, bf16[256,384]{1,0:T(8,128)(2,1)S(1)} %collective-permute-done.9.refs_1_, ...), custom_call_target="tpu_custom_call" | custom-call | flops 1000 | bytes 1000 | tf_op jit(solution)/shard_map/attend_groups/pallas_call | solution.py:340
  65.9 1.7 %collective-permute-done.15.refs_2_ = bf16[128,384]{1,0:T(8,128)(2,1)S(1)} collective-permute-done((bf16[128,384]{1,0:T(8,128)(2,1)S(1)}, bf16[128,384]{1,0:T(8,128)(2,1)S(1)}, u32[]{:S(2)}, u32[]{:S(2)}) %collective-permute-start.15) | collective-permute-done | bytes 98336 | tf_op jit(solution)/shard_map/ppermute | solution.py:437
  67.5 2.7 %collective-permute-done.16.refs_3_ = bf16[128,384]{1,0:T(8,128)(2,1)S(1)} collective-permute-done((bf16[128,384]{1,0:T(8,128)(2,1)S(1)}, bf16[128,384]{1,0:T(8,128)(2,1)S(1)}, u32[]{:S(2)}, u32[]{:S(2)}) %collective-permute-start.16) | collective-permute-done | bytes 98336 | tf_op jit(solution)/shard_map/ppermute | solution.py:437
  70.3 2.9 %collective-permute-start.18 = (bf16[144,384]{1,0:T(8,128)(2,1)S(1)}, bf16[144,384]{1,0:T(8,128)(2,1)S(1)}, u32[]{:S(2)}, u32[]{:S(2)}) collective-permute-start(bf16[144,384]{1,0:T(8,128)(2,1)S(1)} %get-tuple-element.176), channel_id=1, source_target_pairs={{0,16},{2,18},{4,20},{6,22},{8,24},{10,26},{12,28},{14,30},{16,0},... | collective-permute-start | bytes 331784 | tf_op jit(solution)/shard_map/ppermute | solution.py:437
  73.1 0.6 collective-permute-start.19
  73.8 5.1 %attend_groups.3 = (bf16[144,384]{1,0:T(8,128)(2,1)S(1)}, bf16[144,384]{1,0:T(8,128)(2,1)S(1)}, bf16[144,384]{1,0:T(8,128)(2,1)S(1)}, bf16[144,384]{1,0:T(8,128)(2,1)S(1)}) custom-call(s32[3]{0:T(128)S(1)} %pad_add_fusion.pos, bf16[256,384]{1,0:T(8,128)(2,1)S(1)} %get-tuple-element.178.refs_0_, bf16[256,384]{1,0:T(8,128)(2,1)S(1)} %collective-permute-done.9.refs_1_, ...), custom_call_target="tpu_custom_call" | custom-call | flops 1000 | bytes 1000 | tf_op jit(solution)/shard_map/attend_groups/pallas_call | solution.py:340
  78.9 0.9 collective-permute-start.20
  79.8 2.0 %collective-permute-start.21 = (bf16[144,384]{1,0:T(8,128)(2,1)S(1)}, bf16[144,384]{1,0:T(8,128)(2,1)S(1)}, u32[]{:S(2)}, u32[]{:S(2)}) collective-permute-start(bf16[144,384]{1,0:T(8,128)(2,1)S(1)} %get-tuple-element.184), channel_id=1, source_target_pairs={{0,16},{2,18},{4,20},{6,22},{8,24},{10,26},{12,28},{14,30},{16,0},... | collective-permute-start | bytes 331784 | tf_op jit(solution)/shard_map/ppermute | solution.py:437
  81.8 0.6 collective-permute-start.22
  82.4 6.7 %collective-permute-done.19.refs_3_ = bf16[144,384]{1,0:T(8,128)(2,1)S(1)} collective-permute-done((bf16[144,384]{1,0:T(8,128)(2,1)S(1)}, bf16[144,384]{1,0:T(8,128)(2,1)S(1)}, u32[]{:S(2)}, u32[]{:S(2)}) %collective-permute-start.19) | collective-permute-done | bytes 110624 | tf_op jit(solution)/shard_map/ppermute | solution.py:437
  89.1 2.4 %merge_and_project.2 = (bf16[128,1536]{1,0:T(8,128)(2,1)S(1)}, f32[128,1536]{1,0:T(8,128)S(1)}) custom-call(s32[3]{0:T(128)S(1)} %pad_add_fusion.pos, bf16[144,384]{1,0:T(8,128)(2,1)S(1)} %get-tuple-element.186.refs_0_, bf16[144,384]{1,0:T(8,128)(2,1)S(1)} %collective-permute-done.17.refs_1_, bf16[144,384]{1,0:T(8,128)(2,1)S(1)} %collective-permute-done.18.refs_2_, ...), custom_call_target="tpu_custom_call" | custom-call | flops 10000000000 | bytes 100000000 | tf_op jit(solution)/shard_map/merge_and_project/pallas_call | solution.py:381
  91.6 0.6 collective-permute-start.24
  92.2 0.0 collective-permute-start.26
  92.2 0.0 collective-permute-done.20.refs_1_
  92.2 0.0 collective-permute-done.21.refs_2_
  92.2 0.6 collective-permute-done.22.refs_3_
  92.8 2.4 %merge_and_project.3 = (bf16[128,1536]{1,0:T(8,128)(2,1)S(1)}, f32[128,1536]{1,0:T(8,128)S(1)}) custom-call(s32[3]{0:T(128)S(1)} %pad_add_fusion.pos, bf16[144,384]{1,0:T(8,128)(2,1)S(1)} %get-tuple-element.191.refs_0_, bf16[144,384]{1,0:T(8,128)(2,1)S(1)} %collective-permute-done.20.refs_1_, bf16[144,384]{1,0:T(8,128)(2,1)S(1)} %collective-permute-done.21.refs_2_, ...), custom_call_target="tpu_custom_call" | custom-call | flops 10000000000 | bytes 100000000 | tf_op jit(solution)/shard_map/merge_and_project/pallas_call | solution.py:381
  95.2 1.0 collective-permute-start.23
  96.2 4.8 %collective-permute-done.24.got = bf16[128,1536]{1,0:T(8,128)(2,1)S(1)} collective-permute-done((bf16[128,1536]{1,0:T(8,128)(2,1)S(1)}, bf16[128,1536]{1,0:T(8,128)(2,1)S(1)}, u32[]{:S(2)}, u32[]{:S(2)}) %collective-permute-start.24) | collective-permute-done | bytes 393248 | tf_op jit(solution)/shard_map/ppermute | solution.py:497
  101.0 0.7 gate_and_add.2
  101.7 0.1 collective-permute-start.25
  101.8 1.7 %place_fresh.1 = bf16[2,2,128,1536]{3,2,1,0:T(8,128)(2,1)} custom-call(s32[3]{0:T(128)S(1)} %pad_add_fusion.pos, bf16[2,128,1536]{2,1,0:T(8,128)(2,1)S(1)} %get-tuple-element.196.mine, bf16[2,128,1536]{2,1,0:T(8,128)(2,1)S(1)} %collective-permute-done.26.got), custom_call_target="tpu_custom_call" | custom-call | tf_op jit(solution)/shard_map/place_fresh/pallas_call | solution.py:238
  103.5 4.4 %collective-permute-done.23.got = bf16[128,1536]{1,0:T(8,128)(2,1)S(1)} collective-permute-done((bf16[128,1536]{1,0:T(8,128)(2,1)S(1)}, bf16[128,1536]{1,0:T(8,128)(2,1)S(1)}, u32[]{:S(2)}, u32[]{:S(2)}) %collective-permute-start.23) | collective-permute-done | bytes 393248 | tf_op jit(solution)/shard_map/ppermute | solution.py:501
  107.9 1.6 %gate_and_add.3 = bf16[2,128,1536]{2,1,0:T(8,128)(2,1)} custom-call(s32[3]{0:T(128)S(1)} %pad_add_fusion.pos, bf16[2,128,3072]{2,1,0:T(8,128)(2,1)S(1)} %copy-done, f32[3,2,3072]{2,1,0:T(2,128)S(1)} %copy-done.2, f32[128,1536]{1,0:T(8,128)S(1)} %get-tuple-element.192.keep, bf16[128,1536]{1,0:T(8,128)(2,1)S(1)} %collective-permute-done.23.got, ...), custom_call_target="tpu_custom_call" | custom-call | flops 1000 | bytes 1000 | tf_op jit(solution)/shard_map/gate_and_add/pallas_call | solution.py:415
  (22 shorter events, 0.0 us)
Async XLA Ops:
  0.6 2.4 %copy-start = (bf16[2,128,3072]{2,1,0:T(8,128)(2,1)S(1)}, bf16[2,128,3072]{2,1,0:T(8,128)(2,1)}, u32[]{:S(2)}) copy-start(bf16[2,128,3072]{2,1,0:T(8,128)(2,1)} %hidden.3) | copy-start | bytes 4718596
  0.7 1.5 %copy-start.1 = (bf16[2,2,128,1536]{3,2,1,0:T(8,128)(2,1)S(1)}, bf16[2,2,128,1536]{3,2,1,0:T(8,128)(2,1)}, u32[]{:S(2)}) copy-start(bf16[2,2,128,1536]{3,2,1,0:T(8,128)(2,1)} %stale.1) | copy-start | bytes 4718596
  2.2 5.5 %copy-start.2 = (f32[3,2,3072]{2,1,0:T(2,128)S(1)}, f32[3,2,3072]{2,1,0:T(2,128)}, u32[]{:S(2)}) copy-start(f32[3,2,3072]{2,1,0:T(2,128)} %mod.5) | copy-start | bytes 221188
  2.2 5.5 %copy-start.3 = (f32[2,128]{1,0:T(2,128)S(1)}, f32[2,128]{1,0:T(2,128)}, u32[]{:S(2)}) copy-start(f32[2,128]{1,0:T(2,128)} %gain.5) | copy-start | bytes 3076
  3.1 4.7 %collective-permute-start = (bf16[128,3072]{1,0:T(8,128)(2,1)S(1)}, bf16[128,3072]{1,0:T(8,128)(2,1)S(1)}, u32[]{:S(2)}, u32[]{:S(2)}) collective-permute-start(bf16[128,3072]{1,0:T(8,128)(2,1)S(1)} %dynamic-slice_bitcast_fusion), channel_id=1, source_target_pairs={{0,2},{2,0},{4,6},{6,4},{8,10},{10,8},{12,14},{14,12},{16,18},{18,... | collective-permute-start | bytes 2359304 | tf_op jit(solution)/shard_map/ppermute | solution.py:437
  3.2 16.6 %collective-permute-start.1 = (bf16[2,2,128,384]{3,2,1,0:T(8,128)(2,1)S(1)}, bf16[2,2,128,384]{3,2,1,0:T(8,128)(2,1)S(1)}, u32[]{:S(2)}, u32[]{:S(2)}) collective-permute-start(bf16[2,2,128,384]{3,2,1,0:T(8,128)(2,1)S(1)} %get-tuple-element.101), channel_id=1, source_target_pairs={{0,8},{2,10},{4,12},{6,14},{8,0},{10,2},{12,4},{14,6},{16,24},{18,... | collective-permute-start | bytes 1179656 | tf_op jit(solution)/shard_map/ppermute | solution.py:437
  3.7 16.1 %collective-permute-start.2 = (bf16[2,2,128,384]{3,2,1,0:T(8,128)(2,1)S(1)}, bf16[2,2,128,384]{3,2,1,0:T(8,128)(2,1)S(1)}, u32[]{:S(2)}, u32[]{:S(2)}) collective-permute-start(bf16[2,2,128,384]{3,2,1,0:T(8,128)(2,1)S(1)} %get-tuple-element.147.refs_0_.refs_4_), channel_id=1, source_target_pairs={{0,4},{2,6},{4,0},{6,2},{8,12},{10,14},{12,8},{14,10},{16,20},{18,... | collective-permute-start | bytes 1179656 | tf_op jit(solution)/shard_map/ppermute | solution.py:437
  5.2 24.8 %collective-permute-start.4 = (bf16[2,2,128,384]{3,2,1,0:T(8,128)(2,1)S(1)}, bf16[2,2,128,384]{3,2,1,0:T(8,128)(2,1)S(1)}, u32[]{:S(2)}, u32[]{:S(2)}) collective-permute-start(bf16[2,2,128,384]{3,2,1,0:T(8,128)(2,1)S(1)} %get-tuple-element.102), channel_id=1, source_target_pairs={{0,16},{2,18},{4,20},{6,22},{8,24},{10,26},{12,28},{14,30},{16,0},... | collective-permute-start | bytes 1179656 | tf_op jit(solution)/shard_map/ppermute | solution.py:437
  20.3 9.7 %collective-permute-start.5 = (bf16[2,128,384]{2,1,0:T(8,128)(2,1)S(1)}, bf16[2,128,384]{2,1,0:T(8,128)(2,1)S(1)}, u32[]{:S(2)}, u32[]{:S(2)}) collective-permute-start(bf16[2,128,384]{2,1,0:T(8,128)(2,1)S(1)} %get-tuple-element.115), channel_id=1, source_target_pairs={{0,4},{2,6},{4,0},{6,2},{8,12},{10,14},{12,8},{14,10},{16,20},{18,... | collective-permute-start | bytes 589832 | tf_op jit(solution)/shard_map/ppermute | solution.py:437
  22.8 8.9 %collective-permute-start.6 = (bf16[2,128,384]{2,1,0:T(8,128)(2,1)S(1)}, bf16[2,128,384]{2,1,0:T(8,128)(2,1)S(1)}, u32[]{:S(2)}, u32[]{:S(2)}) collective-permute-start(bf16[2,128,384]{2,1,0:T(8,128)(2,1)S(1)} %get-tuple-element.116), channel_id=1, source_target_pairs={{0,4},{2,6},{4,0},{6,2},{8,12},{10,14},{12,8},{14,10},{16,20},{18,... | collective-permute-start | bytes 589832 | tf_op jit(solution)/shard_map/ppermute | solution.py:437
  22.9 19.5 %collective-permute-start.3 = (bf16[2,2,128,384]{3,2,1,0:T(8,128)(2,1)S(1)}, bf16[2,2,128,384]{3,2,1,0:T(8,128)(2,1)S(1)}, u32[]{:S(2)}, u32[]{:S(2)}) collective-permute-start(bf16[2,2,128,384]{3,2,1,0:T(8,128)(2,1)S(1)} %get-tuple-element.113), channel_id=1, source_target_pairs={{0,24},{2,26},{4,28},{6,30},{8,16},{10,18},{12,20},{14,22},{16,8},... | collective-permute-start | bytes 1179656 | tf_op jit(solution)/shard_map/ppermute | solution.py:437
  31.8 10.7 %collective-permute-start.9 = (bf16[256,384]{1,0:T(8,128)(2,1)S(1)}, bf16[256,384]{1,0:T(8,128)(2,1)S(1)}, u32[]{:S(2)}, u32[]{:S(2)}) collective-permute-start(bf16[256,384]{1,0:T(8,128)(2,1)S(1)} %get-tuple-element.131), channel_id=1, source_target_pairs={{0,8},{2,10},{4,12},{6,14},{8,0},{10,2},{12,4},{14,6},{16,24},{18,... | collective-permute-start | bytes 589832 | tf_op jit(solution)/shard_map/ppermute | solution.py:437
  34.7 7.8 %collective-permute-start.7 = (bf16[2,128,384]{2,1,0:T(8,128)(2,1)S(1)}, bf16[2,128,384]{2,1,0:T(8,128)(2,1)S(1)}, u32[]{:S(2)}, u32[]{:S(2)}) collective-permute-start(bf16[2,128,384]{2,1,0:T(8,128)(2,1)S(1)} %get-tuple-element.128), channel_id=1, source_target_pairs={{0,4},{2,6},{4,0},{6,2},{8,12},{10,14},{12,8},{14,10},{16,20},{18,... | collective-permute-start | bytes 589832 | tf_op jit(solution)/shard_map/ppermute | solution.py:437
  36.5 8.1 %collective-permute-start.8 = (bf16[2,128,384]{2,1,0:T(8,128)(2,1)S(1)}, bf16[2,128,384]{2,1,0:T(8,128)(2,1)S(1)}, u32[]{:S(2)}, u32[]{:S(2)}) collective-permute-start(bf16[2,128,384]{2,1,0:T(8,128)(2,1)S(1)} %get-tuple-element.129), channel_id=1, source_target_pairs={{0,4},{2,6},{4,0},{6,2},{8,12},{10,14},{12,8},{14,10},{16,20},{18,... | collective-permute-start | bytes 589832 | tf_op jit(solution)/shard_map/ppermute | solution.py:437
  46.4 12.6 %collective-permute-start.13 = (bf16[7,2,128,384]{3,2,1,0:T(8,128)(2,1)S(1)}, bf16[7,2,128,384]{3,2,1,0:T(8,128)(2,1)S(1)}, u32[]{:S(2)}, u32[]{:S(2)}) collective-permute-start(bf16[7,2,128,384]{3,2,1,0:T(8,128)(2,1)S(1)} %pack.1), channel_id=1, source_target_pairs={{0,2},{2,0},{4,6},{6,4},{8,10},{10,8},{12,14},{14,12},{16,18},{18,... | collective-permute-start | bytes 4128776 | tf_op jit(solution)/shard_map/ppermute | solution.py:437
  46.5 12.5 %collective-permute-start.10 = (bf16[2,2,128,384]{3,2,1,0:T(8,128)(2,1)S(1)}, bf16[2,2,128,384]{3,2,1,0:T(8,128)(2,1)S(1)}, u32[]{:S(2)}, u32[]{:S(2)}) collective-permute-start(bf16[2,2,128,384]{3,2,1,0:T(8,128)(2,1)S(1)} %collective-permute-done.3.refs_8_.refs_18_), channel_id=1, source_target_pairs={{0,4},{2,6},{4,0},{6,2},{8,12},{10,14},{12,8},{14,10},{16,20},{18,... | collective-permute-start | bytes 1179656 | tf_op jit(solution)/shard_map/ppermute | solution.py:437
  48.0 8.7 %collective-permute-start.11 = (bf16[128,384]{1,0:T(8,128)(2,1)S(1)}, bf16[128,384]{1,0:T(8,128)(2,1)S(1)}, u32[]{:S(2)}, u32[]{:S(2)}) collective-permute-start(bf16[128,384]{1,0:T(8,128)(2,1)S(1)} %get-tuple-element.143), channel_id=1, source_target_pairs={{0,16},{2,18},{4,20},{6,22},{8,24},{10,26},{12,28},{14,30},{16,0},... | collective-permute-start | bytes 294920 | tf_op jit(solution)/shard_map/ppermute | solution.py:437
  49.3 9.7 %collective-permute-start.12 = (bf16[128,384]{1,0:T(8,128)(2,1)S(1)}, bf16[128,384]{1,0:T(8,128)(2,1)S(1)}, u32[]{:S(2)}, u32[]{:S(2)}) collective-permute-start(bf16[128,384]{1,0:T(8,128)(2,1)S(1)} %get-tuple-element.144), channel_id=1, source_target_pairs={{0,24},{2,26},{4,28},{6,30},{8,16},{10,18},{12,20},{14,22},{16,8},... | collective-permute-start | bytes 294920 | tf_op jit(solution)/shard_map/ppermute | solution.py:437
  59.0 1.7 %collective-permute-start.14 = (bf16[2,2,128,384]{3,2,1,0:T(8,128)(2,1)S(1)}, bf16[2,2,128,384]{3,2,1,0:T(8,128)(2,1)S(1)}, u32[]{:S(2)}, u32[]{:S(2)}) collective-permute-start(bf16[2,2,128,384]{3,2,1,0:T(8,128)(2,1)S(1)} %collective-permute-done.10.refs_20_), channel_id=1, source_target_pairs={{0,2},{2,0},{4,6},{6,4},{8,10},{10,8},{12,14},{14,12},{16,18},{18,... | collective-permute-start | bytes 1179656 | tf_op jit(solution)/shard_map/ppermute | solution.py:437
  59.0 8.5 %collective-permute-start.15 = (bf16[128,384]{1,0:T(8,128)(2,1)S(1)}, bf16[128,384]{1,0:T(8,128)(2,1)S(1)}, u32[]{:S(2)}, u32[]{:S(2)}) collective-permute-start(bf16[128,384]{1,0:T(8,128)(2,1)S(1)} %get-tuple-element.171), channel_id=1, source_target_pairs={{0,16},{2,18},{4,20},{6,22},{8,24},{10,26},{12,28},{14,30},{16,0},... | collective-permute-start | bytes 294920 | tf_op jit(solution)/shard_map/ppermute | solution.py:437
  60.2 10.1 %collective-permute-start.16 = (bf16[128,384]{1,0:T(8,128)(2,1)S(1)}, bf16[128,384]{1,0:T(8,128)(2,1)S(1)}, u32[]{:S(2)}, u32[]{:S(2)}) collective-permute-start(bf16[128,384]{1,0:T(8,128)(2,1)S(1)} %get-tuple-element.172), channel_id=1, source_target_pairs={{0,24},{2,26},{4,28},{6,30},{8,16},{10,18},{12,20},{14,22},{16,8},... | collective-permute-start | bytes 294920 | tf_op jit(solution)/shard_map/ppermute | solution.py:437
  60.7 28.4 %slice-start = ((s8[9437184]{0:T(1024)(128)(4,1)}), s8[4194304]{0:T(1024)(128)(4,1)S(1)}, s32[]{:S(2)}) async-start(s8[9437184]{0:T(1024)(128)(4,1)} %bitcast.6), calls=%async_computation | async-start | bytes 8388608
  60.7 28.4 %slice-start.1 = ((s8[9437184]{0:T(1024)(128)(4,1)}), s8[4194304]{0:T(1024)(128)(4,1)S(1)}, s32[]{:S(2)}) async-start(s8[9437184]{0:T(1024)(128)(4,1)} %bitcast.6), calls=%async_computation.1 | async-start | bytes 8388608
  70.3 18.9 %slice-start.2 = ((s8[9437184]{0:T(1024)(128)(4,1)}), s8[1048576]{0:T(1024)(128)(4,1)S(1)}, s32[]{:S(2)}) async-start(s8[9437184]{0:T(1024)(128)(4,1)} %bitcast.6), calls=%async_computation.2 | async-start | bytes 2097152
  70.3 11.5 %collective-permute-start.17 = (bf16[144,384]{1,0:T(8,128)(2,1)S(1)}, bf16[144,384]{1,0:T(8,128)(2,1)S(1)}, u32[]{:S(2)}, u32[]{:S(2)}) collective-permute-start(bf16[144,384]{1,0:T(8,128)(2,1)S(1)} %get-tuple-element.175), channel_id=1, source_target_pairs={{0,8},{2,10},{4,12},{6,14},{8,0},{10,2},{12,4},{14,6},{16,24},{18,... | collective-permute-start | bytes 331784 | tf_op jit(solution)/shard_map/ppermute | solution.py:437
  70.3 12.2 %collective-permute-start.18 = (bf16[144,384]{1,0:T(8,128)(2,1)S(1)}, bf16[144,384]{1,0:T(8,128)(2,1)S(1)}, u32[]{:S(2)}, u32[]{:S(2)}) collective-permute-start(bf16[144,384]{1,0:T(8,128)(2,1)S(1)} %get-tuple-element.176), channel_id=1, source_target_pairs={{0,16},{2,18},{4,20},{6,22},{8,24},{10,26},{12,28},{14,30},{16,0},... | collective-permute-start | bytes 331784 | tf_op jit(solution)/shard_map/ppermute | solution.py:437
  73.1 16.0 %collective-permute-start.19 = (bf16[144,384]{1,0:T(8,128)(2,1)S(1)}, bf16[144,384]{1,0:T(8,128)(2,1)S(1)}, u32[]{:S(2)}, u32[]{:S(2)}) collective-permute-start(bf16[144,384]{1,0:T(8,128)(2,1)S(1)} %get-tuple-element.177), channel_id=1, source_target_pairs={{0,24},{2,26},{4,28},{6,30},{8,16},{10,18},{12,20},{14,22},{16,8},... | collective-permute-start | bytes 331784 | tf_op jit(solution)/shard_map/ppermute | solution.py:437
  78.9 13.3 %collective-permute-start.20 = (bf16[144,384]{1,0:T(8,128)(2,1)S(1)}, bf16[144,384]{1,0:T(8,128)(2,1)S(1)}, u32[]{:S(2)}, u32[]{:S(2)}) collective-permute-start(bf16[144,384]{1,0:T(8,128)(2,1)S(1)} %get-tuple-element.183), channel_id=1, source_target_pairs={{0,8},{2,10},{4,12},{6,14},{8,0},{10,2},{12,4},{14,6},{16,24},{18,... | collective-permute-start | bytes 331784 | tf_op jit(solution)/shard_map/ppermute | solution.py:437
  79.8 12.3 %collective-permute-start.21 = (bf16[144,384]{1,0:T(8,128)(2,1)S(1)}, bf16[144,384]{1,0:T(8,128)(2,1)S(1)}, u32[]{:S(2)}, u32[]{:S(2)}) collective-permute-start(bf16[144,384]{1,0:T(8,128)(2,1)S(1)} %get-tuple-element.184), channel_id=1, source_target_pairs={{0,16},{2,18},{4,20},{6,22},{8,24},{10,26},{12,28},{14,30},{16,0},... | collective-permute-start | bytes 331784 | tf_op jit(solution)/shard_map/ppermute | solution.py:437
  81.8 11.0 %collective-permute-start.22 = (bf16[144,384]{1,0:T(8,128)(2,1)S(1)}, bf16[144,384]{1,0:T(8,128)(2,1)S(1)}, u32[]{:S(2)}, u32[]{:S(2)}) collective-permute-start(bf16[144,384]{1,0:T(8,128)(2,1)S(1)} %get-tuple-element.185), channel_id=1, source_target_pairs={{0,24},{2,26},{4,28},{6,30},{8,16},{10,18},{12,20},{14,22},{16,8},... | collective-permute-start | bytes 331784 | tf_op jit(solution)/shard_map/ppermute | solution.py:437
  91.6 9.4 %collective-permute-start.24 = (bf16[128,1536]{1,0:T(8,128)(2,1)S(1)}, bf16[128,1536]{1,0:T(8,128)(2,1)S(1)}, u32[]{:S(2)}, u32[]{:S(2)}) collective-permute-start(bf16[128,1536]{1,0:T(8,128)(2,1)S(1)} %get-tuple-element.190), channel_id=1, source_target_pairs={{0,1},{1,0},{2,3},{3,2},{4,5},{5,4},{6,7},{7,6},{8,9},{9,8},{10,11... | collective-permute-start | bytes 1179656 | tf_op jit(solution)/shard_map/ppermute | solution.py:497
  92.2 9.6 %collective-permute-start.26 = (bf16[2,128,1536]{2,1,0:T(8,128)(2,1)S(1)}, bf16[2,128,1536]{2,1,0:T(8,128)(2,1)S(1)}, u32[]{:S(2)}, u32[]{:S(2)}) collective-permute-start(bf16[2,128,1536]{2,1,0:T(8,128)(2,1)S(1)} %get-tuple-element.197.other), channel_id=1, source_target_pairs={{0,2},{2,0},{4,6},{6,4},{8,10},{10,8},{12,14},{14,12},{16,18},{18,... | collective-permute-start | bytes 2359304 | tf_op jit(solution)/shard_map/ppermute | solution.py:437
  95.2 12.6 %collective-permute-start.23 = (bf16[128,1536]{1,0:T(8,128)(2,1)S(1)}, bf16[128,1536]{1,0:T(8,128)(2,1)S(1)}, u32[]{:S(2)}, u32[]{:S(2)}) collective-permute-start(bf16[128,1536]{1,0:T(8,128)(2,1)S(1)} %get-tuple-element.193), channel_id=1, source_target_pairs={{0,1},{1,0},{2,3},{3,2},{4,5},{5,4},{6,7},{7,6},{8,9},{9,8},{10,11... | collective-permute-start | bytes 1179656 | tf_op jit(solution)/shard_map/ppermute | solution.py:501
  101.7 6.2 %collective-permute-start.25 = (bf16[128,1536]{1,0:T(8,128)(2,1)S(1)}, bf16[128,1536]{1,0:T(8,128)(2,1)S(1)}, u32[]{:S(2)}, u32[]{:S(2)}) collective-permute-start(bf16[128,1536]{1,0:T(8,128)(2,1)S(1)} %gate_and_add.2), channel_id=1, source_target_pairs={{0,2},{2,0},{4,6},{6,4},{8,10},{10,8},{12,14},{14,12},{16,18},{18,... | collective-permute-start | bytes 1179656 | tf_op jit(solution)/shard_map/ppermute | solution.py:437

commit v4 on v3

--- a/solution.py
+++ b/solution.py
@@ -12,6 +12,7 @@
 EXTRA = 16
 LOG2E = 1.4426950408889634
 SCALE2 = HEAD ** (-0.5) * LOG2E
+ORDER = (0, 3, 2, 1)
 MIB = 1024 * 1024
 BF = jnp.bfloat16
 F32 = jnp.float32
@@ -249,17 +250,20 @@
 def own_kernel(q, mine, other, acc, top, total):
     rows = mine.shape[1]
     ones = jnp.ones((rows, HEAD), BF)
+    heads = q.shape[1] // HEAD
     for j, kv in enumerate((mine, other)):
         here = slice(j * rows, (j + 1) * rows)
-        for h in range(q.shape[1] // HEAD):
-            at = slice(h * HEAD, (h + 1) * HEAD)
-            scores = nt(q[here, at], kv[0, :, at])
-            peak = jnp.max(scores, axis=-1, keepdims=True)
-            weights = jnp.exp2((scores - peak) * SCALE2).astype(BF)
-            summed = nn(weights, jnp.concatenate([kv[1, :, at], ones], axis=1))
-            acc[here, at] = summed[:, :HEAD]
-            total[here, at] = summed[:, HEAD:]
-            top[here, at] = jnp.broadcast_to(peak * SCALE2, (rows, HEAD))
+        for first in range(0, heads, 3):
+            ats = [slice(h * HEAD, (h + 1) * HEAD) for h in range(first, min(first + 3, heads))]
+            scores = [nt(q[here, at], kv[0, :, at]) for at in ats]
+            values = [jnp.concatenate([kv[1, :, at], ones], axis=1) for at in ats]
+            peaks = [jnp.max(sc, axis=-1, keepdims=True) for sc in scores]
+            weights = [jnp.exp2((sc - p) * SCALE2).astype(BF) for sc, p in zip(scores, peaks)]
+            summed = [nn(w, v) for w, v in zip(weights, values)]
+            for at, p, s in zip(ats, peaks, summed):
+                acc[here, at] = s[:, :HEAD]
+                total[here, at] = s[:, HEAD:]
+                top[here, at] = jnp.broadcast_to(p * SCALE2, (rows, HEAD))
 
 
 def attend_own(queries, mine, other):
@@ -282,11 +286,13 @@
 def group_kernel(part, blocks, places, pos, *refs):
     count = sum(n for n, _ in places)
     queries, refs, outs = refs[:blocks], list(refs[blocks : blocks + count]), refs[blocks + count :]
+    outs = [outs[ORDER.index(b)] for b in range(blocks)]
     cached = [[refs.pop(0) for _ in range(n)] for n, _ in places]
     rows, width = queries[-1].shape
     mine = slice(part * rows, (part + 1) * rows)
     clip = pl.ds(pos[2], 1)
     ones = jnp.ones((4 * rows, HEAD), BF)
+    heads, levels = width // HEAD, [None] * blocks
 
     def load(kv, group, at):
         parts = []
@@ -299,36 +305,41 @@
                 parts.append(block[0][kv, clip, :, at][0])
         return jnp.concatenate(parts, axis=0)
 
-    for h in range(width // HEAD):
+    for h in range(heads):
         at = slice(h * HEAD, (h + 1) * HEAD)
         keys = [load(0, g, at) for g in range(blocks)]
         values = [jnp.concatenate([load(1, g, at), ones], axis=1) for g in range(blocks)]
-        for b in range(blocks):
-            q = queries[b][mine if b < 2 else slice(None), at]
-            scores = []
+        for first in range(0, blocks, 2):
+            pair = [queries[b][mine if b < 2 else slice(None), at] for b in (first, first + 1)]
+            q = jnp.concatenate(pair, axis=0)
+            peak = summed = None
             for s in range(blocks):
                 sc = nt(q, keys[s])
-                if s == b:
-                    own = [sc[:, j * rows : (j + 1) * rows] for j in range(4)]
+                if s // 2 == first // 2:
+                    halves = [sc[:rows], sc[rows:]]
+                    own = [halves[s % 2][:, j * rows : (j + 1) * rows] for j in range(4)]
                     own[part] = jnp.full((rows, rows), -1e30, F32)
-                    sc = jnp.concatenate(own, axis=1)
-                scores.append(sc)
-            peak = functools.reduce(
-                jnp.maximum, [jnp.max(sc, axis=-1, keepdims=True) for sc in scores]
-            )
-            summed = None
-            for sc, v in zip(scores, values):
-                term = nn(jnp.exp2((sc - peak) * SCALE2).astype(BF), v)
-                summed = term if summed is None else summed + term
+                    halves[s % 2] = jnp.concatenate(own, axis=1)
+                    sc = jnp.concatenate(halves, axis=0)
+                top = jnp.max(sc, axis=-1, keepdims=True)
+                top = top if s == 0 else jnp.maximum(peak, top)
+                term = nn(jnp.exp2((sc - top) * SCALE2).astype(BF), values[s])
+                summed = term if s == 0 else summed * jnp.exp2((peak - top) * SCALE2) + term
+                peak = top
             total = summed[:, HEAD:]
-            outs[b][0:rows, at] = (summed[:, :HEAD] / total).astype(BF)
-            level = jnp.transpose(peak * SCALE2 + jnp.log2(total))[0:8, :]
-            high = level.astype(BF).astype(F32)
-            mid = (level - high).astype(BF).astype(F32)
-            low = level - high - mid
-            row = lax.broadcasted_iota(jnp.int32, (8, HEAD), 0)
-            three = jnp.where(row == 0, high, jnp.where(row == 1, mid, low))
-            outs[b][rows : rows + EXTRA, at] = jnp.concatenate([three, three], axis=0).astype(BF)
+            result = (summed[:, :HEAD] / total).astype(BF)
+            level_all = peak * SCALE2 + jnp.log2(total)
+            for i, b in enumerate((first, first + 1)):
+                here = slice(i * rows, (i + 1) * rows)
+                outs[b][h * rows : (h + 1) * rows, :] = result[here]
+                level = jnp.transpose(level_all[here])[0:EXTRA, :]
+                high = level.astype(BF).astype(F32)
+                mid = (level - high).astype(BF).astype(F32)
+                row = lax.broadcasted_iota(jnp.int32, (EXTRA, HEAD), 0) - 3 * h
+                three = jnp.where(row == 0, high, jnp.where(row == 1, mid, level - high - mid))
+                levels[b] = three if h == 0 else jnp.where(row < 0, levels[b], three)
+    for b in range(blocks):
+        outs[b][heads * rows :, :] = levels[b].astype(BF)
 
 
 def attend_groups(part, pos, queries, cached):
@@ -341,7 +352,7 @@
         functools.partial(group_kernel, part, blocks, places),
         in_specs=[SCALARS] + [RESIDENT] * (blocks + len(arrays)),
         out_specs=[RESIDENT] * blocks,
-        out_shape=[out_of((rows + EXTRA, width))] * blocks,
+        out_shape=[out_of((rows * width // HEAD + EXTRA, HEAD))] * blocks,
         compiler_params=params(32),
         cost_estimate=SMALL,
         name="attend_groups",
@@ -354,17 +365,16 @@
     rows = send.shape[0]
     width = acc.shape[1] // groups
     mine = slice(part * rows, (part + 1) * rows)
-    for s in range(groups):
+    for s, block in zip(ORDER, back):
         for h in range(width // HEAD):
-            at = slice(h * HEAD, (h + 1) * HEAD)
             cols = pl.ds(pl.multiple_of((pos[0] ^ s) * width + h * HEAD, HEAD), HEAD)
-            three = back[s][rows : rows + 8, at].astype(F32)
+            three = block[rows * width // HEAD :, :].astype(F32)[3 * h : 3 * h + 3, :]
             level = three[0:1, :] + three[1:2, :] + three[2:3, :]
             level = jnp.transpose(jnp.broadcast_to(level, (rows, HEAD)))
             own = top[mine, cols]
             peak = jnp.maximum(level, own)
             w_own, w_back = jnp.exp2(own - peak), jnp.exp2(level - peak)
-            mixed = acc[mine, cols] * w_own + back[s][0:rows, at].astype(F32) * w_back
+            mixed = acc[mine, cols] * w_own + block[h * rows : (h + 1) * rows, :].astype(F32) * w_back
             attended[:, cols] = (mixed / (total[mine, cols] * w_own + w_back)).astype(BF)
     half = weight.shape[1] // 2
     block = math.gcd(half, 768)
@@ -462,8 +472,10 @@
         (two, far_one, fresh, slots, queries, normed)
     )
 
-    far_two = [across(a, 2) for a in halves(two[0])]
-    asked = [slots[0], along(slots[1], 1)]
+    parts = halves(two[0])
+    far_two = [across(a, 2) for a in parts]
+    asked = [slots[0], along(tie(slots[1], *parts), 1)]
+    swap_a = [across(pack(pos, near, far_near, one, far_one), 1)]
     fresh = make_fresh(1, normed, qk_gain, weights, fresh)
     three, far_two, asked, fresh, slots, queries = step(
         (three, far_two, asked, fresh, slots, queries)
@@ -471,26 +483,26 @@
 
     far_three = [across(three[0], 2)]
     their_far = [along(slots[2 * s - 1], s) for s in (2, 3)]
-    swapped = [across(pack(pos, near, far_near, one, far_one, two, far_two, three), 1)]
+    swap_b = [across(pack(pos, two, far_two, three), 1)]
     own = attend_own(queries, *fresh)
-    far_three, their_far, asked, swapped, own, slots = step(
-        (far_three, their_far, asked, swapped, own, slots)
+    far_three, their_far, asked, swap_a, swap_b, own, slots = step(
+        (far_three, their_far, asked, swap_a, swap_b, own, slots)
     )
 
     my_far = [along(slots[2 * s - 2], s) for s in (2, 3)]
     their_queries, my_queries = asked + their_far, asked + my_far
     held = [
-        [(near, None), (swapped, 0), (far_near, None), (swapped, 1)],
-        [(one, None), (swapped, 2), (far_one, None), (swapped, 3)],
-        [(two, None), (swapped, 4), (far_two, None), (swapped, 5)],
-        [(three, None), (swapped, 6), (far_three, None), ([across(far_three[0], 1)], None)],
+        [(near, None), (swap_a, 0), (far_near, None), (swap_a, 1)],
+        [(one, None), (swap_a, 2), (far_one, None), (swap_a, 3)],
+        [(two, None), (swap_b, 0), (far_two, None), (swap_b, 1)],
+        [(three, None), (swap_b, 2), (far_three, None), ([across(far_three[0], 1)], None)],
     ]
     theirs = attend_groups(1, pos, their_queries, held)
     theirs, my_queries = step((theirs, my_queries))
-    back = [theirs[0]] + [along(theirs[s], s) for s in range(1, groups)]
+    back = [theirs[0]] + [along(a, s) for a, s in zip(theirs[1:], ORDER[1:])]
     my_queries[0] = tie(my_queries[0], theirs)
     mine = attend_groups(0, pos, my_queries, held)
-    mine_back = [mine[0]] + [along(mine[s], s) for s in range(1, groups)]
+    mine_back = [mine[0]] + [along(a, s) for a, s in zip(mine[1:], ORDER[1:])]
     back[0] = tie(back[0], mine)
     swap = [(0, 1), (1, 0)]
     send, keep = project_out(1, pos, back, *own, out_weight)

time: 110 us -> 107 us (0.973)
  the two profiles are of different devices: /device:TPU:12 before, /device:TPU:0 now
where the time goes in v4:
time: 107 us
  Pallas kernels  43.8 us (41%)
  starting transfers between devices  36.8 us (34%)
  waiting for transfers between devices  23.5 us (22%)
  local copies, waits for them, and re-layouts  1.59 us (1%)
    ppermute x26, starting transfers between devices, across(): return lax.ppermute(value, 'patch', [(i, i ^ bit) for i in range(patches)])  33.6 us
    ppermute x26, waiting for transfers between devices, across(): return lax.ppermute(value, 'patch', [(i, i ^ bit) for i in range(patches)])  16.7 us
    pallas_call x2, Pallas kernels, make_fresh(): pl.pallas_call(functools.partial(fresh_kernel, slot), grid=(cols // block...  10.7 us
    pallas_call x2, Pallas kernels, attend_groups(): pl.pallas_call(functools.partial(group_kernel, part, blocks, places), in_...  9.71 us
    pallas_call x1, Pallas kernels, make_queries(): pl.pallas_call(functools.partial(query_kernel, groups, per_step), grid_sp...  7.39 us
    ppermute x1, waiting for transfers between devices, spread_heads(): my_got = lax.ppermute(my_send, 'tp', swap)  6.23 us
    pallas_call x2, Pallas kernels, project_out(): pl.pallas_call(functools.partial(out_kernel, part, groups), in_specs=[SCA...  4.82 us
    pallas_call x1, Pallas kernels, attend_own(): pl.pallas_call(own_kernel, grid=(cols // block,), in_specs=[wide, kv, kv]...  3.1 us
  transfers between devices with their start and end apart: 28, of which 9 were waited for; matrix products, arithmetic and copies ran while one was open for 0% of the time, Pallas kernels for 39%

profile of v4, /device:TPU:0, one launch (start us, length us, event | category | flops | bytes accessed | tf_op | source)
XLA Modules:
  0.0 106.8 jit_solution(2315798367607163430)
XLA Ops:
  0.7 0.1 pad_add_fusion.pos
  0.7 1.5 %copy-done.1 = bf16[2,2,128,1536]{3,2,1,0:T(8,128)(2,1)S(1)} copy-done((bf16[2,2,128,1536]{3,2,1,0:T(8,128)(2,1)S(1)}, bf16[2,2,128,1536]{3,2,1,0:T(8,128)(2,1)}, u32[]{:S(2)}) %copy-start.1) | copy-done | bytes 1572888
  2.3 0.8 cut_stale.1
  3.0 0.1 dynamic-slice_bitcast_fusion
  3.1 0.5 collective-permute-start
  3.6 2.6 %collective-permute-start.1 = (bf16[2,2,128,384]{3,2,1,0:T(8,128)(2,1)S(1)}, bf16[2,2,128,384]{3,2,1,0:T(8,128)(2,1)S(1)}, u32[]{:S(2)}, u32[]{:S(2)}) collective-permute-start(bf16[2,2,128,384]{3,2,1,0:T(8,128)(2,1)S(1)} %get-tuple-element.103), channel_id=1, source_target_pairs={{0,8},{2,10},{4,12},{6,14},{8,0},{10,2},{12,4},{14,6},{16,24},{18,... | collective-permute-start | bytes 1179656 | tf_op jit(solution)/shard_map/ppermute | solution.py:447
  6.3 1.5 %collective-permute-start.2 = (bf16[2,2,128,384]{3,2,1,0:T(8,128)(2,1)S(1)}, bf16[2,2,128,384]{3,2,1,0:T(8,128)(2,1)S(1)}, u32[]{:S(2)}, u32[]{:S(2)}) collective-permute-start(bf16[2,2,128,384]{3,2,1,0:T(8,128)(2,1)S(1)} %get-tuple-element.150.refs_0_.refs_4_), channel_id=1, source_target_pairs={{0,4},{2,6},{4,0},{6,2},{8,12},{10,14},{12,8},{14,10},{16,20},{18,... | collective-permute-start | bytes 1179656 | tf_op jit(solution)/shard_map/ppermute | solution.py:447
  7.8 2.6 %collective-permute-start.4 = (bf16[2,2,128,384]{3,2,1,0:T(8,128)(2,1)S(1)}, bf16[2,2,128,384]{3,2,1,0:T(8,128)(2,1)S(1)}, u32[]{:S(2)}, u32[]{:S(2)}) collective-permute-start(bf16[2,2,128,384]{3,2,1,0:T(8,128)(2,1)S(1)} %get-tuple-element.104), channel_id=1, source_target_pairs={{0,16},{2,18},{4,20},{6,22},{8,24},{10,26},{12,28},{14,30},{16,0},... | collective-permute-start | bytes 1179656 | tf_op jit(solution)/shard_map/ppermute | solution.py:447
  10.3 0.0 collective-permute-done.got.hidden
  10.4 7.4 %norm_and_queries.1 = (bf16[256,3072]{1,0:T(8,128)(2,1)S(1)}, bf16[256,1536]{1,0:T(8,128)(2,1)S(1)}, bf16[256,384]{1,0:T(8,128)(2,1)S(1)}, bf16[256,384]{1,0:T(8...) custom-call(s32[3]{0:T(128)S(1)} %pad_add_fusion.pos, ...), custom_call_target="tpu_custom_call" | custom-call | flops 1000 | bytes 1000 | tf_op jit(solution)/shard_map/norm_and_queries/pallas_call | solution.py:172
  17.8 5.3 %collective-permute-done.1.block.refs_2_.refs_8_ = bf16[2,2,128,384]{3,2,1,0:T(8,128)(2,1)S(1)} collective-permute-done((bf16[2,2,128,384]{3,2,1,0:T(8,128)(2,1)S(1)}, bf16[2,2,128,384]{3,2,1,0:T(8,128)(2,1)S(1)}, u32[]{:S(2)}, u32[]{:S(2)}) %collective-permute-start.1) | collective-permute-done | bytes 393248 | tf_op jit(solution)/shard_map/ppermute | solution.py:447
  23.1 0.5 halves.2
  23.6 2.7 %collective-permute-start.5 = (bf16[2,128,384]{2,1,0:T(8,128)(2,1)S(1)}, bf16[2,128,384]{2,1,0:T(8,128)(2,1)S(1)}, u32[]{:S(2)}, u32[]{:S(2)}) collective-permute-start(bf16[2,128,384]{2,1,0:T(8,128)(2,1)S(1)} %get-tuple-element.117), channel_id=1, source_target_pairs={{0,4},{2,6},{4,0},{6,2},{8,12},{10,14},{12,8},{14,10},{16,20},{18,... | collective-permute-start | bytes 589832 | tf_op jit(solution)/shard_map/ppermute | solution.py:447
  26.3 0.1 collective-permute-start.6
  26.4 2.5 %collective-permute-start.3 = (bf16[2,2,128,384]{3,2,1,0:T(8,128)(2,1)S(1)}, bf16[2,2,128,384]{3,2,1,0:T(8,128)(2,1)S(1)}, u32[]{:S(2)}, u32[]{:S(2)}) collective-permute-start(bf16[2,2,128,384]{3,2,1,0:T(8,128)(2,1)S(1)} %get-tuple-element.115), channel_id=1, source_target_pairs={{0,24},{2,26},{4,28},{6,30},{8,16},{10,18},{12,20},{14,22},{16,8},... | collective-permute-start | bytes 1179656 | tf_op jit(solution)/shard_map/ppermute | solution.py:447
  28.8 5.5 %fresh_keys.1 = (bf16[2,128,1536]{2,1,0:T(8,128)(2,1)S(1)}, bf16[2,128,1536]{2,1,0:T(8,128)(2,1)S(1)}) custom-call(bf16[256,3072]{1,0:T(8,128)(2,1)S(1)} %get-tuple-element.135.normed, f32[2,128]{1,0:T(2,128)S(1)} %copy-done.3, bf16[3,3072,1536]{2,1,0:T(8,128)(2,1)} %bitcast.9), custom_call_target="tpu_custom_call" | custom-call | flops 1000 | bytes 1000 | tf_op jit(solution)/shard_map/fresh_keys/pallas_call | solution.py:214
  34.4 0.0 collective-permute-done.5.refs_3_.refs_10_
  34.4 0.9 collective-permute-done.6.refs_4_.refs_11_
  35.2 0.5 halves.3
  35.7 0.1 collective-permute-start.9
  35.8 1.8 %collective-permute-start.7 = (bf16[2,128,384]{2,1,0:T(8,128)(2,1)S(1)}, bf16[2,128,384]{2,1,0:T(8,128)(2,1)S(1)}, u32[]{:S(2)}, u32[]{:S(2)}) collective-permute-start(bf16[2,128,384]{2,1,0:T(8,128)(2,1)S(1)} %get-tuple-element.130), channel_id=1, source_target_pairs={{0,4},{2,6},{4,0},{6,2},{8,12},{10,14},{12,8},{14,10},{16,20},{18,... | collective-permute-start | bytes 589832 | tf_op jit(solution)/shard_map/ppermute | solution.py:447
  37.6 0.3 collective-permute-start.8
  37.9 1.2 %pack.2 = bf16[4,2,128,384]{3,2,1,0:T(8,128)(2,1)S(1)} custom-call(s32[3]{0:T(128)S(1)} %pad_add_fusion.pos, bf16[2,2,128,384]{3,2,1,0:T(8,128)(2,1)S(1)} %get-tuple-element.150.refs_0_.refs_4_, bf16[2,2,128,384]{3,2,1,0:T(8,128)(2,1)S(1)} %collective-permute-done.2.refs_1_.refs_6_, ...), custom_call_target="tpu_custom_call" | custom-call | tf_op jit(solution)/shard_map/pack/pallas_call | solution.py:120
  39.1 0.1 collective-permute-start.13
  39.2 5.2 %fresh_values.1 = (bf16[2,128,1536]{2,1,0:T(8,128)(2,1)S(1)}, bf16[2,128,1536]{2,1,0:T(8,128)(2,1)S(1)}) custom-call(bf16[256,3072]{1,0:T(8,128)(2,1)S(1)} %get-tuple-element.135.normed, f32[2,128]{1,0:T(2,128)S(1)} %copy-done.3, bf16[3,3072,1536]{2,1,0:T(8,128)(2,1)} %bitcast.10, ...), custom_call_target="tpu_custom_call", output_to_operand_aliasing={{0}: (3, {}), {1}: (4, {})} | custom-call | flops 1000 | bytes 1000 | tf_op jit(solution)/shard_map/fresh_values/pallas_call | solution.py:214
  44.5 0.0 collective-permute-done.3.refs_3_.refs_18_
  44.5 0.0 collective-permute-done.7.refs_1_.refs_15_
  44.5 1.5 %collective-permute-done.8.refs_2_.refs_16_ = bf16[2,128,384]{2,1,0:T(8,128)(2,1)S(1)} collective-permute-done((bf16[2,128,384]{2,1,0:T(8,128)(2,1)S(1)}, bf16[2,128,384]{2,1,0:T(8,128)(2,1)S(1)}, u32[]{:S(2)}, u32[]{:S(2)}) %collective-permute-start.8) | collective-permute-done | bytes 196640 | tf_op jit(solution)/shard_map/ppermute | solution.py:447
  46.0 1.1 %pack.3 = bf16[3,2,128,384]{3,2,1,0:T(8,128)(2,1)S(1)} custom-call(s32[3]{0:T(128)S(1)} %pad_add_fusion.pos, bf16[2,2,128,384]{3,2,1,0:T(8,128)(2,1)S(1)} %collective-permute-done.4.block.refs_0_.refs_13_, bf16[2,128,384]{2,1,0:T(8,128)(2,1)S(1)} %collective-permute-done.7.refs_1_.refs_15_, bf16[2,128,384]{2,1,0:T(8,128)(2,1)S(1)} %collective-permute-done.8.refs_2_.refs_16_, ...), custom_call_target="tpu_custom_call" | custom-call | tf_op jit(solution)/shard_map/pack/pallas_call | solution.py:120
  47.1 0.1 collective-permute-start.14
  47.2 1.5 %collective-permute-start.10 = (bf16[2,2,128,384]{3,2,1,0:T(8,128)(2,1)S(1)}, bf16[2,2,128,384]{3,2,1,0:T(8,128)(2,1)S(1)}, u32[]{:S(2)}, u32[]{:S(2)}) collective-permute-start(bf16[2,2,128,384]{3,2,1,0:T(8,128)(2,1)S(1)} %collective-permute-done.3.refs_3_.refs_18_), channel_id=1, source_target_pairs={{0,4},{2,6},{4,0},{6,2},{8,12},{10,14},{12,8},{14,10},{16,20},{18,... | collective-permute-start | bytes 1179656 | tf_op jit(solution)/shard_map/ppermute | solution.py:447
  48.7 2.7 %collective-permute-start.11 = (bf16[128,384]{1,0:T(8,128)(2,1)S(1)}, bf16[128,384]{1,0:T(8,128)(2,1)S(1)}, u32[]{:S(2)}, u32[]{:S(2)}) collective-permute-start(bf16[128,384]{1,0:T(8,128)(2,1)S(1)} %get-tuple-element.146), channel_id=1, source_target_pairs={{0,16},{2,18},{4,20},{6,22},{8,24},{10,26},{12,28},{14,30},{16,0},... | collective-permute-start | bytes 294920 | tf_op jit(solution)/shard_map/ppermute | solution.py:447
  51.3 1.4 %collective-permute-start.12 = (bf16[128,384]{1,0:T(8,128)(2,1)S(1)}, bf16[128,384]{1,0:T(8,128)(2,1)S(1)}, u32[]{:S(2)}, u32[]{:S(2)}) collective-permute-start(bf16[128,384]{1,0:T(8,128)(2,1)S(1)} %get-tuple-element.147), channel_id=1, source_target_pairs={{0,24},{2,26},{4,28},{6,30},{8,16},{10,18},{12,20},{14,22},{16,8},... | collective-permute-start | bytes 294920 | tf_op jit(solution)/shard_map/ppermute | solution.py:447
  52.7 3.1 %attend_own.1 = (f32[256,1536]{1,0:T(8,128)S(1)}, f32[256,1536]{1,0:T(8,128)S(1)}, f32[256,1536]{1,0:T(8,128)S(1)}) custom-call(bf16[256,1536]{1,0:T(8,128)(2,1)S(1)} %get-tuple-element.156.q, bf16[2,128,1536]{2,1,0:T(8,128)(2,1)S(1)} %get-tuple-element.200.mine, bf16[2,128,1536]{2,1,0:T(8,128)(2,1)S(1)} %get-tuple-element.201.other), custom_call_target="tpu_custom_call" | custom-call | flops 1000 | bytes 1000 | tf_op jit(solution)/shard_map/attend_own/pallas_call | solution.py:274
  55.8 3.6 %collective-permute-done.11.refs_2_ = bf16[128,384]{1,0:T(8,128)(2,1)S(1)} collective-permute-done((bf16[128,384]{1,0:T(8,128)(2,1)S(1)}, bf16[128,384]{1,0:T(8,128)(2,1)S(1)}, u32[]{:S(2)}, u32[]{:S(2)}) %collective-permute-start.11) | collective-permute-done | bytes 98336 | tf_op jit(solution)/shard_map/ppermute | solution.py:447
  59.4 0.0 collective-permute-done.12.refs_3_
  59.4 0.0 collective-permute-done.10.refs_20_
  59.4 0.0 collective-permute-done.13.refs_5_.refs_7_.refs_9_.refs_12_
  59.4 0.1 collective-permute-start.15
  59.5 3.0 %collective-permute-start.16 = (bf16[128,384]{1,0:T(8,128)(2,1)S(1)}, bf16[128,384]{1,0:T(8,128)(2,1)S(1)}, u32[]{:S(2)}, u32[]{:S(2)}) collective-permute-start(bf16[128,384]{1,0:T(8,128)(2,1)S(1)} %get-tuple-element.175), channel_id=1, source_target_pairs={{0,16},{2,18},{4,20},{6,22},{8,24},{10,26},{12,28},{14,30},{16,0},... | collective-permute-start | bytes 294920 | tf_op jit(solution)/shard_map/ppermute | solution.py:447
  62.5 1.4 %collective-permute-start.17 = (bf16[128,384]{1,0:T(8,128)(2,1)S(1)}, bf16[128,384]{1,0:T(8,128)(2,1)S(1)}, u32[]{:S(2)}, u32[]{:S(2)}) collective-permute-start(bf16[128,384]{1,0:T(8,128)(2,1)S(1)} %get-tuple-element.176), channel_id=1, source_target_pairs={{0,24},{2,26},{4,28},{6,30},{8,16},{10,18},{12,20},{14,22},{16,8},... | collective-permute-start | bytes 294920 | tf_op jit(solution)/shard_map/ppermute | solution.py:447
  63.9 4.8 %attend_groups.2 = (bf16[400,128]{1,0:T(8,128)(2,1)S(1)}, bf16[400,128]{1,0:T(8,128)(2,1)S(1)}, bf16[400,128]{1,0:T(8,128)(2,1)S(1)}, bf16[400,128]{1,0:T(8,128)(2,1)S(1)}) custom-call(s32[3]{0:T(128)S(1)} %pad_add_fusion.pos, bf16[256,384]{1,0:T(8,128)(2,1)S(1)} %get-tuple-element.182.refs_0_, bf16[256,384]{1,0:T(8,128)(2,1)S(1)} %collective-permute-done.9.refs_1_, ...), custom_call_target="tpu_custom_call" | custom-call | flops 1000 | bytes 1000 | tf_op jit(solution)/shard_map/attend_groups/pallas_call | solution.py:351
  68.7 1.6 %collective-permute-done.16.refs_2_ = bf16[128,384]{1,0:T(8,128)(2,1)S(1)} collective-permute-done((bf16[128,384]{1,0:T(8,128)(2,1)S(1)}, bf16[128,384]{1,0:T(8,128)(2,1)S(1)}, u32[]{:S(2)}, u32[]{:S(2)}) %collective-permute-start.16) | collective-permute-done | bytes 98336 | tf_op jit(solution)/shard_map/ppermute | solution.py:447
  70.3 0.0 collective-permute-done.17.refs_3_
  70.4 2.4 %collective-permute-start.18 = (bf16[400,128]{1,0:T(8,128)(2,1)S(1)}, bf16[400,128]{1,0:T(8,128)(2,1)S(1)}, u32[]{:S(2)}, u32[]{:S(2)}) collective-permute-start(bf16[400,128]{1,0:T(8,128)(2,1)S(1)} %get-tuple-element.179), channel_id=1, source_target_pairs={{0,24},{2,26},{4,28},{6,30},{8,16},{10,18},{12,20},{14,22},{16,8},... | collective-permute-start | bytes 307208 | tf_op jit(solution)/shard_map/ppermute | solution.py:447
  72.8 1.4 %collective-permute-start.19 = (bf16[400,128]{1,0:T(8,128)(2,1)S(1)}, bf16[400,128]{1,0:T(8,128)(2,1)S(1)}, u32[]{:S(2)}, u32[]{:S(2)}) collective-permute-start(bf16[400,128]{1,0:T(8,128)(2,1)S(1)} %get-tuple-element.180), channel_id=1, source_target_pairs={{0,16},{2,18},{4,20},{6,22},{8,24},{10,26},{12,28},{14,30},{16,0},... | collective-permute-start | bytes 307208 | tf_op jit(solution)/shard_map/ppermute | solution.py:447
  74.2 0.5 collective-permute-start.20
  74.7 4.9 %attend_groups.3 = (bf16[400,128]{1,0:T(8,128)(2,1)S(1)}, bf16[400,128]{1,0:T(8,128)(2,1)S(1)}, bf16[400,128]{1,0:T(8,128)(2,1)S(1)}, bf16[400,128]{1,0:T(8,128)(2,1)S(1)}) custom-call(s32[3]{0:T(128)S(1)} %pad_add_fusion.pos, bf16[256,384]{1,0:T(8,128)(2,1)S(1)} %get-tuple-element.182.refs_0_, bf16[256,384]{1,0:T(8,128)(2,1)S(1)} %collective-permute-done.9.refs_1_, ...), custom_call_target="tpu_custom_call" | custom-call | flops 1000 | bytes 1000 | tf_op jit(solution)/shard_map/attend_groups/pallas_call | solution.py:351
  79.6 2.5 %collective-permute-start.21 = (bf16[400,128]{1,0:T(8,128)(2,1)S(1)}, bf16[400,128]{1,0:T(8,128)(2,1)S(1)}, u32[]{:S(2)}, u32[]{:S(2)}) collective-permute-start(bf16[400,128]{1,0:T(8,128)(2,1)S(1)} %get-tuple-element.187), channel_id=1, source_target_pairs={{0,24},{2,26},{4,28},{6,30},{8,16},{10,18},{12,20},{14,22},{16,8},... | collective-permute-start | bytes 307208 | tf_op jit(solution)/shard_map/ppermute | solution.py:447
  82.1 0.5 collective-permute-start.22
  82.6 0.0 collective-permute-done.18.refs_1_
  82.6 1.4 %collective-permute-start.23 = (bf16[400,128]{1,0:T(8,128)(2,1)S(1)}, bf16[400,128]{1,0:T(8,128)(2,1)S(1)}, u32[]{:S(2)}, u32[]{:S(2)}) collective-permute-start(bf16[400,128]{1,0:T(8,128)(2,1)S(1)} %get-tuple-element.189), channel_id=1, source_target_pairs={{0,8},{2,10},{4,12},{6,14},{8,0},{10,2},{12,4},{14,6},{16,24},{18,... | collective-permute-start | bytes 307208 | tf_op jit(solution)/shard_map/ppermute | solution.py:447
  84.1 2.1 %collective-permute-done.19.refs_2_ = bf16[400,128]{1,0:T(8,128)(2,1)S(1)} collective-permute-done((bf16[400,128]{1,0:T(8,128)(2,1)S(1)}, bf16[400,128]{1,0:T(8,128)(2,1)S(1)}, u32[]{:S(2)}, u32[]{:S(2)}) %collective-permute-start.19) | collective-permute-done | bytes 102432 | tf_op jit(solution)/shard_map/ppermute | solution.py:447
  86.2 2.4 %merge_and_project.2 = (bf16[128,1536]{1,0:T(8,128)(2,1)S(1)}, f32[128,1536]{1,0:T(8,128)S(1)}) custom-call(s32[3]{0:T(128)S(1)} %pad_add_fusion.pos, bf16[400,128]{1,0:T(8,128)(2,1)S(1)} %get-tuple-element.190.refs_0_, bf16[400,128]{1,0:T(8,128)(2,1)S(1)} %collective-permute-done.18.refs_1_, bf16[400,128]{1,0:T(8,128)(2,1)S(1)} %collective-permute-done.19.refs_2_, ...), custom_call_target="tpu_custom_call" | custom-call | flops 10000000000 | bytes 100000000 | tf_op jit(solution)/shard_map/merge_and_project/pallas_call | solution.py:391
  88.6 1.6 %collective-permute-start.25 = (bf16[128,1536]{1,0:T(8,128)(2,1)S(1)}, bf16[128,1536]{1,0:T(8,128)(2,1)S(1)}, u32[]{:S(2)}, u32[]{:S(2)}) collective-permute-start(bf16[128,1536]{1,0:T(8,128)(2,1)S(1)} %get-tuple-element.194), channel_id=1, source_target_pairs={{0,1},{1,0},{2,3},{3,2},{4,5},{5,4},{6,7},{7,6},{8,9},{9,8},{10,11... | collective-permute-start | bytes 1179656 | tf_op jit(solution)/shard_map/ppermute | solution.py:509
  90.2 1.7 %collective-permute-done.22.refs_2_ = bf16[400,128]{1,0:T(8,128)(2,1)S(1)} collective-permute-done((bf16[400,128]{1,0:T(8,128)(2,1)S(1)}, bf16[400,128]{1,0:T(8,128)(2,1)S(1)}, u32[]{:S(2)}, u32[]{:S(2)}) %collective-permute-start.22) | collective-permute-done | bytes 102432 | tf_op jit(solution)/shard_map/ppermute | solution.py:447
  91.9 2.4 %merge_and_project.3 = (bf16[128,1536]{1,0:T(8,128)(2,1)S(1)}, f32[128,1536]{1,0:T(8,128)S(1)}) custom-call(s32[3]{0:T(128)S(1)} %pad_add_fusion.pos, bf16[400,128]{1,0:T(8,128)(2,1)S(1)} %get-tuple-element.195.refs_0_, bf16[400,128]{1,0:T(8,128)(2,1)S(1)} %collective-permute-done.21.refs_1_, bf16[400,128]{1,0:T(8,128)(2,1)S(1)} %collective-permute-done.22.refs_2_, ...), custom_call_target="tpu_custom_call" | custom-call | flops 10000000000 | bytes 100000000 | tf_op jit(solution)/shard_map/merge_and_project/pallas_call | solution.py:391
  94.3 1.6 %collective-permute-start.24 = (bf16[128,1536]{1,0:T(8,128)(2,1)S(1)}, bf16[128,1536]{1,0:T(8,128)(2,1)S(1)}, u32[]{:S(2)}, u32[]{:S(2)}) collective-permute-start(bf16[128,1536]{1,0:T(8,128)(2,1)S(1)} %get-tuple-element.197), channel_id=1, source_target_pairs={{0,1},{1,0},{2,3},{3,2},{4,5},{5,4},{6,7},{7,6},{8,9},{9,8},{10,11... | collective-permute-start | bytes 1179656 | tf_op jit(solution)/shard_map/ppermute | solution.py:513
  95.9 0.6 collective-permute-done.25.got
  96.4 0.7 gate_and_add.2
  97.1 0.1 collective-permute-start.26
  97.2 1.7 %place_fresh.1 = bf16[2,2,128,1536]{3,2,1,0:T(8,128)(2,1)} custom-call(s32[3]{0:T(128)S(1)} %pad_add_fusion.pos, bf16[2,128,1536]{2,1,0:T(8,128)(2,1)S(1)} %get-tuple-element.200.mine, bf16[2,128,1536]{2,1,0:T(8,128)(2,1)S(1)} %collective-permute-done.27.got), custom_call_target="tpu_custom_call" | custom-call | tf_op jit(solution)/shard_map/place_fresh/pallas_call | solution.py:239
  98.9 6.2 %collective-permute-done.24.got = bf16[128,1536]{1,0:T(8,128)(2,1)S(1)} collective-permute-done((bf16[128,1536]{1,0:T(8,128)(2,1)S(1)}, bf16[128,1536]{1,0:T(8,128)(2,1)S(1)}, u32[]{:S(2)}, u32[]{:S(2)}) %collective-permute-start.24) | collective-permute-done | bytes 393248 | tf_op jit(solution)/shard_map/ppermute | solution.py:513
  105.2 1.6 %gate_and_add.3 = bf16[2,128,1536]{2,1,0:T(8,128)(2,1)} custom-call(s32[3]{0:T(128)S(1)} %pad_add_fusion.pos, bf16[2,128,3072]{2,1,0:T(8,128)(2,1)S(1)} %copy-done, f32[3,2,3072]{2,1,0:T(2,128)S(1)} %copy-done.2, f32[128,1536]{1,0:T(8,128)S(1)} %get-tuple-element.196.keep, bf16[128,1536]{1,0:T(8,128)(2,1)S(1)} %collective-permute-done.24.got, ...), custom_call_target="tpu_custom_call" | custom-call | flops 1000 | bytes 1000 | tf_op jit(solution)/shard_map/gate_and_add/pallas_call | solution.py:425
  (25 shorter events, 0.1 us)
Async XLA Ops:
  0.6 2.4 %copy-start = (bf16[2,128,3072]{2,1,0:T(8,128)(2,1)S(1)}, bf16[2,128,3072]{2,1,0:T(8,128)(2,1)}, u32[]{:S(2)}) copy-start(bf16[2,128,3072]{2,1,0:T(8,128)(2,1)} %hidden.3) | copy-start | bytes 4718596
  0.7 1.5 %copy-start.1 = (bf16[2,2,128,1536]{3,2,1,0:T(8,128)(2,1)S(1)}, bf16[2,2,128,1536]{3,2,1,0:T(8,128)(2,1)}, u32[]{:S(2)}) copy-start(bf16[2,2,128,1536]{3,2,1,0:T(8,128)(2,1)} %stale.1) | copy-start | bytes 4718596
  2.2 8.1 %copy-start.2 = (f32[3,2,3072]{2,1,0:T(2,128)S(1)}, f32[3,2,3072]{2,1,0:T(2,128)}, u32[]{:S(2)}) copy-start(f32[3,2,3072]{2,1,0:T(2,128)} %mod.5) | copy-start | bytes 221188
  2.2 8.1 %copy-start.3 = (f32[2,128]{1,0:T(2,128)S(1)}, f32[2,128]{1,0:T(2,128)}, u32[]{:S(2)}) copy-start(f32[2,128]{1,0:T(2,128)} %gain.5) | copy-start | bytes 3076
  3.1 7.3 %collective-permute-start = (bf16[128,3072]{1,0:T(8,128)(2,1)S(1)}, bf16[128,3072]{1,0:T(8,128)(2,1)S(1)}, u32[]{:S(2)}, u32[]{:S(2)}) collective-permute-start(bf16[128,3072]{1,0:T(8,128)(2,1)S(1)} %dynamic-slice_bitcast_fusion), channel_id=1, source_target_pairs={{0,2},{2,0},{4,6},{6,4},{8,10},{10,8},{12,14},{14,12},{16,18},{18,... | collective-permute-start | bytes 2359304 | tf_op jit(solution)/shard_map/ppermute | solution.py:447
  3.6 19.5 %collective-permute-start.1 = (bf16[2,2,128,384]{3,2,1,0:T(8,128)(2,1)S(1)}, bf16[2,2,128,384]{3,2,1,0:T(8,128)(2,1)S(1)}, u32[]{:S(2)}, u32[]{:S(2)}) collective-permute-start(bf16[2,2,128,384]{3,2,1,0:T(8,128)(2,1)S(1)} %get-tuple-element.103), channel_id=1, source_target_pairs={{0,8},{2,10},{4,12},{6,14},{8,0},{10,2},{12,4},{14,6},{16,24},{18,... | collective-permute-start | bytes 1179656 | tf_op jit(solution)/shard_map/ppermute | solution.py:447
  6.3 16.8 %collective-permute-start.2 = (bf16[2,2,128,384]{3,2,1,0:T(8,128)(2,1)S(1)}, bf16[2,2,128,384]{3,2,1,0:T(8,128)(2,1)S(1)}, u32[]{:S(2)}, u32[]{:S(2)}) collective-permute-start(bf16[2,2,128,384]{3,2,1,0:T(8,128)(2,1)S(1)} %get-tuple-element.150.refs_0_.refs_4_), channel_id=1, source_target_pairs={{0,4},{2,6},{4,0},{6,2},{8,12},{10,14},{12,8},{14,10},{16,20},{18,... | collective-permute-start | bytes 1179656 | tf_op jit(solution)/shard_map/ppermute | solution.py:447
  7.8 26.6 %collective-permute-start.4 = (bf16[2,2,128,384]{3,2,1,0:T(8,128)(2,1)S(1)}, bf16[2,2,128,384]{3,2,1,0:T(8,128)(2,1)S(1)}, u32[]{:S(2)}, u32[]{:S(2)}) collective-permute-start(bf16[2,2,128,384]{3,2,1,0:T(8,128)(2,1)S(1)} %get-tuple-element.104), channel_id=1, source_target_pairs={{0,16},{2,18},{4,20},{6,22},{8,24},{10,26},{12,28},{14,30},{16,0},... | collective-permute-start | bytes 1179656 | tf_op jit(solution)/shard_map/ppermute | solution.py:447
  23.6 10.8 %collective-permute-start.5 = (bf16[2,128,384]{2,1,0:T(8,128)(2,1)S(1)}, bf16[2,128,384]{2,1,0:T(8,128)(2,1)S(1)}, u32[]{:S(2)}, u32[]{:S(2)}) collective-permute-start(bf16[2,128,384]{2,1,0:T(8,128)(2,1)S(1)} %get-tuple-element.117), channel_id=1, source_target_pairs={{0,4},{2,6},{4,0},{6,2},{8,12},{10,14},{12,8},{14,10},{16,20},{18,... | collective-permute-start | bytes 589832 | tf_op jit(solution)/shard_map/ppermute | solution.py:447
  26.3 8.9 %collective-permute-start.6 = (bf16[2,128,384]{2,1,0:T(8,128)(2,1)S(1)}, bf16[2,128,384]{2,1,0:T(8,128)(2,1)S(1)}, u32[]{:S(2)}, u32[]{:S(2)}) collective-permute-start(bf16[2,128,384]{2,1,0:T(8,128)(2,1)S(1)} %get-tuple-element.118), channel_id=1, source_target_pairs={{0,4},{2,6},{4,0},{6,2},{8,12},{10,14},{12,8},{14,10},{16,20},{18,... | collective-permute-start | bytes 589832 | tf_op jit(solution)/shard_map/ppermute | solution.py:447
  26.4 18.1 %collective-permute-start.3 = (bf16[2,2,128,384]{3,2,1,0:T(8,128)(2,1)S(1)}, bf16[2,2,128,384]{3,2,1,0:T(8,128)(2,1)S(1)}, u32[]{:S(2)}, u32[]{:S(2)}) collective-permute-start(bf16[2,2,128,384]{3,2,1,0:T(8,128)(2,1)S(1)} %get-tuple-element.115), channel_id=1, source_target_pairs={{0,24},{2,26},{4,28},{6,30},{8,16},{10,18},{12,20},{14,22},{16,8},... | collective-permute-start | bytes 1179656 | tf_op jit(solution)/shard_map/ppermute | solution.py:447
  35.7 8.7 %collective-permute-start.9 = (bf16[256,384]{1,0:T(8,128)(2,1)S(1)}, bf16[256,384]{1,0:T(8,128)(2,1)S(1)}, u32[]{:S(2)}, u32[]{:S(2)}) collective-permute-start(bf16[256,384]{1,0:T(8,128)(2,1)S(1)} %get-tuple-element.134), channel_id=1, source_target_pairs={{0,8},{2,10},{4,12},{6,14},{8,0},{10,2},{12,4},{14,6},{16,24},{18,... | collective-permute-start | bytes 589832 | tf_op jit(solution)/shard_map/ppermute | solution.py:447
  35.8 8.7 %collective-permute-start.7 = (bf16[2,128,384]{2,1,0:T(8,128)(2,1)S(1)}, bf16[2,128,384]{2,1,0:T(8,128)(2,1)S(1)}, u32[]{:S(2)}, u32[]{:S(2)}) collective-permute-start(bf16[2,128,384]{2,1,0:T(8,128)(2,1)S(1)} %get-tuple-element.130), channel_id=1, source_target_pairs={{0,4},{2,6},{4,0},{6,2},{8,12},{10,14},{12,8},{14,10},{16,20},{18,... | collective-permute-start | bytes 589832 | tf_op jit(solution)/shard_map/ppermute | solution.py:447
  37.6 8.4 %collective-permute-start.8 = (bf16[2,128,384]{2,1,0:T(8,128)(2,1)S(1)}, bf16[2,128,384]{2,1,0:T(8,128)(2,1)S(1)}, u32[]{:S(2)}, u32[]{:S(2)}) collective-permute-start(bf16[2,128,384]{2,1,0:T(8,128)(2,1)S(1)} %get-tuple-element.131), channel_id=1, source_target_pairs={{0,4},{2,6},{4,0},{6,2},{8,12},{10,14},{12,8},{14,10},{16,20},{18,... | collective-permute-start | bytes 589832 | tf_op jit(solution)/shard_map/ppermute | solution.py:447
  39.1 20.3 %collective-permute-start.13 = (bf16[4,2,128,384]{3,2,1,0:T(8,128)(2,1)S(1)}, bf16[4,2,128,384]{3,2,1,0:T(8,128)(2,1)S(1)}, u32[]{:S(2)}, u32[]{:S(2)}) collective-permute-start(bf16[4,2,128,384]{3,2,1,0:T(8,128)(2,1)S(1)} %pack.2), channel_id=1, source_target_pairs={{0,2},{2,0},{4,6},{6,4},{8,10},{10,8},{12,14},{14,12},{16,18},{18,... | collective-permute-start | bytes 2359304 | tf_op jit(solution)/shard_map/ppermute | solution.py:447
  47.1 12.3 %collective-permute-start.14 = (bf16[3,2,128,384]{3,2,1,0:T(8,128)(2,1)S(1)}, bf16[3,2,128,384]{3,2,1,0:T(8,128)(2,1)S(1)}, u32[]{:S(2)}, u32[]{:S(2)}) collective-permute-start(bf16[3,2,128,384]{3,2,1,0:T(8,128)(2,1)S(1)} %pack.3), channel_id=1, source_target_pairs={{0,2},{2,0},{4,6},{6,4},{8,10},{10,8},{12,14},{14,12},{16,18},{18,... | collective-permute-start | bytes 1769480 | tf_op jit(solution)/shard_map/ppermute | solution.py:447
  47.2 12.2 %collective-permute-start.10 = (bf16[2,2,128,384]{3,2,1,0:T(8,128)(2,1)S(1)}, bf16[2,2,128,384]{3,2,1,0:T(8,128)(2,1)S(1)}, u32[]{:S(2)}, u32[]{:S(2)}) collective-permute-start(bf16[2,2,128,384]{3,2,1,0:T(8,128)(2,1)S(1)} %collective-permute-done.3.refs_3_.refs_18_), channel_id=1, source_target_pairs={{0,4},{2,6},{4,0},{6,2},{8,12},{10,14},{12,8},{14,10},{16,20},{18,... | collective-permute-start | bytes 1179656 | tf_op jit(solution)/shard_map/ppermute | solution.py:447
  48.7 10.7 %collective-permute-start.11 = (bf16[128,384]{1,0:T(8,128)(2,1)S(1)}, bf16[128,384]{1,0:T(8,128)(2,1)S(1)}, u32[]{:S(2)}, u32[]{:S(2)}) collective-permute-start(bf16[128,384]{1,0:T(8,128)(2,1)S(1)} %get-tuple-element.146), channel_id=1, source_target_pairs={{0,16},{2,18},{4,20},{6,22},{8,24},{10,26},{12,28},{14,30},{16,0},... | collective-permute-start | bytes 294920 | tf_op jit(solution)/shard_map/ppermute | solution.py:447
  51.3 8.1 %collective-permute-start.12 = (bf16[128,384]{1,0:T(8,128)(2,1)S(1)}, bf16[128,384]{1,0:T(8,128)(2,1)S(1)}, u32[]{:S(2)}, u32[]{:S(2)}) collective-permute-start(bf16[128,384]{1,0:T(8,128)(2,1)S(1)} %get-tuple-element.147), channel_id=1, source_target_pairs={{0,24},{2,26},{4,28},{6,30},{8,16},{10,18},{12,20},{14,22},{16,8},... | collective-permute-start | bytes 294920 | tf_op jit(solution)/shard_map/ppermute | solution.py:447
  59.4 4.4 %collective-permute-start.15 = (bf16[2,2,128,384]{3,2,1,0:T(8,128)(2,1)S(1)}, bf16[2,2,128,384]{3,2,1,0:T(8,128)(2,1)S(1)}, u32[]{:S(2)}, u32[]{:S(2)}) collective-permute-start(bf16[2,2,128,384]{3,2,1,0:T(8,128)(2,1)S(1)} %collective-permute-done.10.refs_20_), channel_id=1, source_target_pairs={{0,2},{2,0},{4,6},{6,4},{8,10},{10,8},{12,14},{14,12},{16,18},{18,... | collective-permute-start | bytes 1179656 | tf_op jit(solution)/shard_map/ppermute | solution.py:447
  59.5 10.8 %collective-permute-start.16 = (bf16[128,384]{1,0:T(8,128)(2,1)S(1)}, bf16[128,384]{1,0:T(8,128)(2,1)S(1)}, u32[]{:S(2)}, u32[]{:S(2)}) collective-permute-start(bf16[128,384]{1,0:T(8,128)(2,1)S(1)} %get-tuple-element.175), channel_id=1, source_target_pairs={{0,16},{2,18},{4,20},{6,22},{8,24},{10,26},{12,28},{14,30},{16,0},... | collective-permute-start | bytes 294920 | tf_op jit(solution)/shard_map/ppermute | solution.py:447
  62.5 7.9 %collective-permute-start.17 = (bf16[128,384]{1,0:T(8,128)(2,1)S(1)}, bf16[128,384]{1,0:T(8,128)(2,1)S(1)}, u32[]{:S(2)}, u32[]{:S(2)}) collective-permute-start(bf16[128,384]{1,0:T(8,128)(2,1)S(1)} %get-tuple-element.176), channel_id=1, source_target_pairs={{0,24},{2,26},{4,28},{6,30},{8,16},{10,18},{12,20},{14,22},{16,8},... | collective-permute-start | bytes 294920 | tf_op jit(solution)/shard_map/ppermute | solution.py:447
  63.9 22.3 %slice-start = ((s8[9437184]{0:T(1024)(128)(4,1)}), s8[4194304]{0:T(1024)(128)(4,1)S(1)}, s32[]{:S(2)}) async-start(s8[9437184]{0:T(1024)(128)(4,1)} %bitcast.6), calls=%async_computation | async-start | bytes 8388608
  63.9 22.3 %slice-start.1 = ((s8[9437184]{0:T(1024)(128)(4,1)}), s8[4194304]{0:T(1024)(128)(4,1)S(1)}, s32[]{:S(2)}) async-start(s8[9437184]{0:T(1024)(128)(4,1)} %bitcast.6), calls=%async_computation.1 | async-start | bytes 8388608
  70.4 15.8 %slice-start.2 = ((s8[9437184]{0:T(1024)(128)(4,1)}), s8[1048576]{0:T(1024)(128)(4,1)S(1)}, s32[]{:S(2)}) async-start(s8[9437184]{0:T(1024)(128)(4,1)} %bitcast.6), calls=%async_computation.2 | async-start | bytes 2097152
  70.4 12.3 %collective-permute-start.18 = (bf16[400,128]{1,0:T(8,128)(2,1)S(1)}, bf16[400,128]{1,0:T(8,128)(2,1)S(1)}, u32[]{:S(2)}, u32[]{:S(2)}) collective-permute-start(bf16[400,128]{1,0:T(8,128)(2,1)S(1)} %get-tuple-element.179), channel_id=1, source_target_pairs={{0,24},{2,26},{4,28},{6,30},{8,16},{10,18},{12,20},{14,22},{16,8},... | collective-permute-start | bytes 307208 | tf_op jit(solution)/shard_map/ppermute | solution.py:447
  72.8 13.4 %collective-permute-start.19 = (bf16[400,128]{1,0:T(8,128)(2,1)S(1)}, bf16[400,128]{1,0:T(8,128)(2,1)S(1)}, u32[]{:S(2)}, u32[]{:S(2)}) collective-permute-start(bf16[400,128]{1,0:T(8,128)(2,1)S(1)} %get-tuple-element.180), channel_id=1, source_target_pairs={{0,16},{2,18},{4,20},{6,22},{8,24},{10,26},{12,28},{14,30},{16,0},... | collective-permute-start | bytes 307208 | tf_op jit(solution)/shard_map/ppermute | solution.py:447
  74.2 11.9 %collective-permute-start.20 = (bf16[400,128]{1,0:T(8,128)(2,1)S(1)}, bf16[400,128]{1,0:T(8,128)(2,1)S(1)}, u32[]{:S(2)}, u32[]{:S(2)}) collective-permute-start(bf16[400,128]{1,0:T(8,128)(2,1)S(1)} %get-tuple-element.181), channel_id=1, source_target_pairs={{0,8},{2,10},{4,12},{6,14},{8,0},{10,2},{12,4},{14,6},{16,24},{18,... | collective-permute-start | bytes 307208 | tf_op jit(solution)/shard_map/ppermute | solution.py:447
  79.6 10.6 %collective-permute-start.21 = (bf16[400,128]{1,0:T(8,128)(2,1)S(1)}, bf16[400,128]{1,0:T(8,128)(2,1)S(1)}, u32[]{:S(2)}, u32[]{:S(2)}) collective-permute-start(bf16[400,128]{1,0:T(8,128)(2,1)S(1)} %get-tuple-element.187), channel_id=1, source_target_pairs={{0,24},{2,26},{4,28},{6,30},{8,16},{10,18},{12,20},{14,22},{16,8},... | collective-permute-start | bytes 307208 | tf_op jit(solution)/shard_map/ppermute | solution.py:447
  82.1 9.8 %collective-permute-start.22 = (bf16[400,128]{1,0:T(8,128)(2,1)S(1)}, bf16[400,128]{1,0:T(8,128)(2,1)S(1)}, u32[]{:S(2)}, u32[]{:S(2)}) collective-permute-start(bf16[400,128]{1,0:T(8,128)(2,1)S(1)} %get-tuple-element.188), channel_id=1, source_target_pairs={{0,16},{2,18},{4,20},{6,22},{8,24},{10,26},{12,28},{14,30},{16,0},... | collective-permute-start | bytes 307208 | tf_op jit(solution)/shard_map/ppermute | solution.py:447
  82.6 9.2 %collective-permute-start.23 = (bf16[400,128]{1,0:T(8,128)(2,1)S(1)}, bf16[400,128]{1,0:T(8,128)(2,1)S(1)}, u32[]{:S(2)}, u32[]{:S(2)}) collective-permute-start(bf16[400,128]{1,0:T(8,128)(2,1)S(1)} %get-tuple-element.189), channel_id=1, source_target_pairs={{0,8},{2,10},{4,12},{6,14},{8,0},{10,2},{12,4},{14,6},{16,24},{18,... | collective-permute-start | bytes 307208 | tf_op jit(solution)/shard_map/ppermute | solution.py:447
  88.6 7.8 %collective-permute-start.25 = (bf16[128,1536]{1,0:T(8,128)(2,1)S(1)}, bf16[128,1536]{1,0:T(8,128)(2,1)S(1)}, u32[]{:S(2)}, u32[]{:S(2)}) collective-permute-start(bf16[128,1536]{1,0:T(8,128)(2,1)S(1)} %get-tuple-element.194), channel_id=1, source_target_pairs={{0,1},{1,0},{2,3},{3,2},{4,5},{5,4},{6,7},{7,6},{8,9},{9,8},{10,11... | collective-permute-start | bytes 1179656 | tf_op jit(solution)/shard_map/ppermute | solution.py:509
  90.2 7.0 %collective-permute-start.27 = (bf16[2,128,1536]{2,1,0:T(8,128)(2,1)S(1)}, bf16[2,128,1536]{2,1,0:T(8,128)(2,1)S(1)}, u32[]{:S(2)}, u32[]{:S(2)}) collective-permute-start(bf16[2,128,1536]{2,1,0:T(8,128)(2,1)S(1)} %get-tuple-element.201.other), channel_id=1, source_target_pairs={{0,2},{2,0},{4,6},{6,4},{8,10},{10,8},{12,14},{14,12},{16,18},{18,... | collective-permute-start | bytes 2359304 | tf_op jit(solution)/shard_map/ppermute | solution.py:447
  94.3 10.9 %collective-permute-start.24 = (bf16[128,1536]{1,0:T(8,128)(2,1)S(1)}, bf16[128,1536]{1,0:T(8,128)(2,1)S(1)}, u32[]{:S(2)}, u32[]{:S(2)}) collective-permute-start(bf16[128,1536]{1,0:T(8,128)(2,1)S(1)} %get-tuple-element.197), channel_id=1, source_target_pairs={{0,1},{1,0},{2,3},{3,2},{4,5},{5,4},{6,7},{7,6},{8,9},{9,8},{10,11... | collective-permute-start | bytes 1179656 | tf_op jit(solution)/shard_map/ppermute | solution.py:513
  97.1 8.0 %collective-permute-start.26 = (bf16[128,1536]{1,0:T(8,128)(2,1)S(1)}, bf16[128,1536]{1,0:T(8,128)(2,1)S(1)}, u32[]{:S(2)}, u32[]{:S(2)}) collective-permute-start(bf16[128,1536]{1,0:T(8,128)(2,1)S(1)} %gate_and_add.2), channel_id=1, source_target_pairs={{0,2},{2,0},{4,6},{6,4},{8,10},{10,8},{12,14},{14,12},{16,18},{18,... | collective-permute-start | bytes 1179656 | tf_op jit(solution)/shard_map/ppermute | solution.py:447

commit v5 on v4

--- a/solution.py
+++ b/solution.py
@@ -64,13 +64,9 @@
         c.wait()
 
 
-def cut_kernel(width, pos, stale, *rest):
-    outs, sems = rest[:-1], rest[-1]
-    pairs = []
+def cut_kernel(width, pos, stale, *outs):
     for s, out in enumerate(outs):
-        cols = pl.ds(pl.multiple_of((pos[0] ^ s) * width, HEAD), width)
-        pairs.append((stale.at[:, :, :, cols], out))
-    copy_all(sems, pairs)
+        out[...] = stale[:, :, :, pl.ds(pl.multiple_of((pos[0] ^ s) * width, HEAD), width)]
 
 
 def cut_stale(pos, stale, groups):
@@ -79,39 +75,38 @@
     return pl.pallas_call(
         functools.partial(cut_kernel, width),
         out_shape=[out_of((kv, clips, rows, width))] * groups,
-        in_specs=[SCALARS, ANYWHERE],
-        out_specs=[ANYWHERE] * groups,
-        scratch_shapes=[pltpu.SemaphoreType.DMA((groups,))],
+        in_specs=[SCALARS, RESIDENT],
+        out_specs=[RESIDENT] * groups,
         compiler_params=params(8),
         name="cut_stale",
     )(pos, stale)
 
 
-def halves_kernel(block, keys, values, sems):
-    copy_all(sems, [(block.at[0], keys), (block.at[1], values)])
+def halves_kernel(block, keys, values):
+    keys[...] = block[0]
+    values[...] = block[1]
 
 
 def halves(block):
     return pl.pallas_call(
         halves_kernel,
         out_shape=[out_of(block.shape[1:])] * 2,
-        in_specs=[ANYWHERE],
-        out_specs=[ANYWHERE] * 2,
-        scratch_shapes=[pltpu.SemaphoreType.DMA((2,))],
+        in_specs=[RESIDENT],
+        out_specs=[RESIDENT] * 2,
         compiler_params=params(8),
         name="halves",
     )(block)
 
 
 def pack_kernel(counts, pos, *refs):
-    refs, out, sems = list(refs[:-2]), refs[-2], refs[-1]
-    pairs, other = [], 1 - pos[2]
+    refs, out = list(refs[:-1]), refs[-1]
+    other = pl.ds(1 - pos[2], 1)
     for i, count in enumerate(counts):
         if count == 1:
-            pairs.append((refs.pop(0).at[:, other], out.at[i]))
+            out[i] = refs.pop(0)[:, other][:, 0]
         else:
-            pairs += [(refs.pop(0).at[other], out.at[i, kv]) for kv in range(2)]
-    copy_all(sems, pairs)
+            for kv in range(2):
+                out[i, kv] = refs.pop(0)[other][0]
 
 
 def pack(pos, *blocks):
@@ -120,9 +115,8 @@
     return pl.pallas_call(
         functools.partial(pack_kernel, [len(block) for block in blocks]),
         out_shape=out_of((len(blocks), 2, rows, width)),
-        in_specs=[SCALARS] + [ANYWHERE] * len(flat),
-        out_specs=ANYWHERE,
-        scratch_shapes=[pltpu.SemaphoreType.DMA((len(flat),))],
+        in_specs=[SCALARS] + [RESIDENT] * len(flat),
+        out_specs=RESIDENT,
         compiler_params=params(8),
         name="pack",
     )(pos, *flat)
@@ -361,7 +355,7 @@
 
 def out_kernel(part, groups, pos, *refs):
     back = refs[:groups]
-    acc, top, total, weight, send, keep, attended = refs[groups:]
+    acc, top, total, weight, send, attended = refs[groups:]
     rows = send.shape[0]
     width = acc.shape[1] // groups
     mine = slice(part * rows, (part + 1) * rows)
@@ -376,30 +370,47 @@
             w_own, w_back = jnp.exp2(own - peak), jnp.exp2(level - peak)
             mixed = acc[mine, cols] * w_own + block[h * rows : (h + 1) * rows, :].astype(F32) * w_back
             attended[:, cols] = (mixed / (total[mine, cols] * w_own + w_back)).astype(BF)
-    half = weight.shape[1] // 2
+    project(attended, weight, 1 - pos[1], send)
+
+
+def project(attended, weight, place, out):
+    half = out.shape[1]
     block = math.gcd(half, 768)
-    for out, place in ((send, 1 - pos[1]), (keep, pos[1])):
-        for i in range(0, half, block):
-            cols = pl.ds(pl.multiple_of(place * half + i, HEAD), block)
-            out[:, i : i + block] = nn(attended[...], weight[:, cols]).astype(out.dtype)
+    for i in range(0, half, block):
+        cols = pl.ds(pl.multiple_of(place * half + i, HEAD), block)
+        out[:, i : i + block] = nn(attended[...], weight[:, cols]).astype(out.dtype)
 
 
 def project_out(part, pos, back, acc, top, total, weight):
     groups = len(back)
     rows, width_all = acc.shape[0] // 2, acc.shape[1]
-    half = (rows, weight.shape[1] // 2)
     return pl.pallas_call(
         functools.partial(out_kernel, part, groups),
         in_specs=[SCALARS] + [RESIDENT] * (groups + 4),
         out_specs=[RESIDENT] * 2,
-        out_shape=[out_of(half), out_of(half, F32)],
-        scratch_shapes=[pltpu.VMEM((rows, width_all), BF)],
+        out_shape=[out_of((rows, weight.shape[1] // 2)), out_of((rows, width_all))],
         compiler_params=params(32),
         cost_estimate=LARGE,
         name="merge_and_project",
     )(pos, *back, acc, top, total, weight)
 
 
+def keep_kernel(pos, attended, weight, keep):
+    project(attended, weight, pos[1], keep)
+
+
+def project_kept(pos, attended, weight):
+    return pl.pallas_call(
+        keep_kernel,
+        in_specs=[SCALARS] + [RESIDENT] * 2,
+        out_specs=RESIDENT,
+        out_shape=out_of((attended.shape[0], weight.shape[1] // 2), F32),
+        compiler_params=params(32),
+        cost_estimate=SMALL,
+        name="project_kept",
+    )(pos, attended, weight)
+
+
 def gated(pos, rows_in, mod, keep, got):
     half = keep.shape[1]
     gate = mod[2, pl.ds(pos[2], 1), pl.ds(pl.multiple_of(pos[1] * half, HEAD), half)]
@@ -412,21 +423,34 @@
     out[...] = gated(pos, hidden[:, cols], mod, keep, got)
 
 
-def my_rows_kernel(pos, hidden, mod, keep, got, theirs, out):
+def my_rows_kernel(pos, hidden, mod, keep, got, theirs, out, rows, sems):
     half = keep.shape[1]
-    cols = pl.ds(pl.multiple_of(pos[1] * half, HEAD), half)
-    mine, other = pl.ds(pos[2], 1), pl.ds(1 - pos[2], 1)
-    out[mine] = gated(pos, hidden[mine, :, cols][0], mod, keep, got)[None]
-    out[other] = theirs[...][None]
+    mine, other = pos[2], 1 - pos[2]
+    copies = [pltpu.make_async_copy(theirs, out.at[other], sems.at[0])]
+    copies[0].start()
+    block = half // 2
+    for i in range(2):
+        here = slice(i * block, (i + 1) * block)
+        cols = pl.ds(pl.multiple_of(pos[1] * half + i * block, HEAD), block)
+        gate = mod[2, pl.ds(mine, 1), cols]
+        total = keep[:, here] + got[:, here].astype(F32)
+        before = hidden[pl.ds(mine, 1), :, cols][0].astype(F32)
+        rows[:, here] = (before + gate * total).astype(BF)
+        copy = pltpu.make_async_copy(rows.at[:, here], out.at[mine, :, here], sems.at[i + 1])
+        copy.start()
+        copies.append(copy)
+    for copy in copies:
+        copy.wait()
 
 
 def finish(pos, hidden, mod, keep, got, *theirs):
-    shape = (2,) * len(theirs) + keep.shape
+    scratch = [pltpu.VMEM(keep.shape, BF), pltpu.SemaphoreType.DMA((3,))]
     return pl.pallas_call(
         my_rows_kernel if theirs else other_rows_kernel,
         in_specs=[SCALARS] + [RESIDENT] * (4 + len(theirs)),
-        out_specs=RESIDENT,
-        out_shape=out_of(shape),
+        out_specs=ANYWHERE if theirs else RESIDENT,
+        out_shape=out_of((2,) * len(theirs) + keep.shape),
+        scratch_shapes=scratch if theirs else [],
         compiler_params=params(24),
         cost_estimate=SMALL,
         name="gate_and_add",
@@ -505,15 +529,17 @@
     mine_back = [mine[0]] + [along(a, s) for a, s in zip(mine[1:], ORDER[1:])]
     back[0] = tie(back[0], mine)
     swap = [(0, 1), (1, 0)]
-    send, keep = project_out(1, pos, back, *own, out_weight)
+    send, attended = project_out(1, pos, back, *own, out_weight)
     got = lax.ppermute(send, "tp", swap)
     mine_back[0] = tie(mine_back[0], send)
 
-    my_send, my_keep = project_out(0, pos, mine_back, *own, out_weight)
+    my_send, my_attended = project_out(0, pos, mine_back, *own, out_weight)
     my_got = lax.ppermute(my_send, "tp", swap)
     fresh_got = across(tie(fresh[1], send), 1)
     fresh_kv = place_fresh(pos, tie(fresh[0], my_send), fresh_got)
-    theirs = finish(pos, hidden_got, modulation, tie(keep, my_send), got)
+    keep = project_kept(pos, tie(attended, my_send), out_weight)
+    my_keep = project_kept(pos, my_attended, out_weight)
+    theirs = finish(pos, hidden_got, modulation, keep, got)
     mixed = finish(pos, hidden_states, modulation, my_keep, my_got, across(theirs, 1))
     return mixed, fresh_kv
 
@@ -573,7 +599,7 @@
     heads_here = arrays[2].shape[2] // HEAD
     patches = lax.axis_size("patch")
     groups = math.gcd(heads_here, patches)
-    if clips == 2 and groups == 4 and patches == 4 * groups and lax.axis_size("tp") == 2:
+    if clips == 2 and groups == 4 and heads_here <= 5 * groups and patches == 4 * groups and lax.axis_size("tp") == 2:
         return spread_heads(groups, *arrays)
     return gather_all(*arrays)
 

time: 107 us -> 105 us (0.981)
  waiting for transfers between devices: 23.5 us -> 22 us
    pallas_call x0 -> x2, Pallas kernels: none -> 2.76 us  [project_kept(): pl.pallas_call(keep_kernel, in_specs=[SCALARS] + [RESIDENT] * 2, out_spec...]
    ppermute x1, waiting for transfers between devices: 6.23 us -> 4.01 us  [spread_heads(): my_got = lax.ppermute(my_send, 'tp', swap)]
    pallas_call x2, Pallas kernels: 4.82 us -> 3.57 us  [project_out(): pl.pallas_call(functools.partial(out_kernel, part, groups), in_specs=[SCA...]
    ppermute x26, waiting for transfers between devices: 16.7 us -> 18 us  [across(): return lax.ppermute(value, 'patch', [(i, i ^ bit) for i in range(patches)])]
    pallas_call x2, Pallas kernels: 2.32 us -> 1.21 us  [pack(): pl.pallas_call(functools.partial(pack_kernel, [len(block) for block in bl...]
  transfers between devices with their start and end apart: 28 -> 28, of which waited for: 9 -> 8; matrix products, arithmetic and copies ran while one was open for 0% -> 0% of each run, Pallas kernels for 39% -> 39%
where the time goes in v5:
time: 105 us
  Pallas kernels  43 us (41%)
  starting transfers between devices  36.8 us (35%)
  waiting for transfers between devices  22 us (21%)
  local copies, waits for them, and re-layouts  1.59 us (2%)
  between operations  1.11 us (1%)
    ppermute x26, starting transfers between devices, across(): return lax.ppermute(value, 'patch', [(i, i ^ bit) for i in range(patches)])  33.6 us
    ppermute x26, waiting for transfers between devices, across(): return lax.ppermute(value, 'patch', [(i, i ^ bit) for i in range(patches)])  18 us
    pallas_call x2, Pallas kernels, make_fresh(): pl.pallas_call(functools.partial(fresh_kernel, slot), grid=(cols // block...  10.7 us
    pallas_call x2, Pallas kernels, attend_groups(): pl.pallas_call(functools.partial(group_kernel, part, blocks, places), in_...  9.71 us
    pallas_call x1, Pallas kernels, make_queries(): pl.pallas_call(functools.partial(query_kernel, groups, per_step), grid_sp...  7.39 us
    ppermute x1, waiting for transfers between devices, spread_heads(): my_got = lax.ppermute(my_send, 'tp', swap)  4.01 us
    pallas_call x2, Pallas kernels, project_out(): pl.pallas_call(functools.partial(out_kernel, part, groups), in_specs=[SCA...  3.57 us
    pallas_call x1, Pallas kernels, attend_own(): pl.pallas_call(own_kernel, grid=(cols // block,), in_specs=[wide, kv, kv]...  3.09 us
  transfers between devices with their start and end apart: 28, of which 8 were waited for; matrix products, arithmetic and copies ran while one was open for 0% of the time, Pallas kernels for 39%

profile of v5, /device:TPU:0, one launch (start us, length us, event | category | flops | bytes accessed | tf_op | source)
XLA Modules:
  0.0 104.6 jit_solution(13251695362879504501)
XLA Ops:
  0.7 0.1 pad_add_fusion.pos
  0.7 1.5 %copy-done.1 = bf16[2,2,128,1536]{3,2,1,0:T(8,128)(2,1)S(1)} copy-done((bf16[2,2,128,1536]{3,2,1,0:T(8,128)(2,1)S(1)}, bf16[2,2,128,1536]{3,2,1,0:T(8,128)(2,1)}, u32[]{:S(2)}) %copy-start.1) | copy-done | bytes 1572888
  2.3 0.7 cut_stale.1
  3.0 0.1 dynamic-slice_bitcast_fusion
  3.0 0.5 collective-permute-start
  3.5 2.6 %collective-permute-start.1 = (bf16[2,2,128,384]{3,2,1,0:T(8,128)(2,1)S(1)}, bf16[2,2,128,384]{3,2,1,0:T(8,128)(2,1)S(1)}, u32[]{:S(2)}, u32[]{:S(2)}) collective-permute-start(bf16[2,2,128,384]{3,2,1,0:T(8,128)(2,1)S(1)} %get-tuple-element.103), channel_id=1, source_target_pairs={{0,8},{2,10},{4,12},{6,14},{8,0},{10,2},{12,4},{14,6},{16,24},{18,... | collective-permute-start | bytes 1179656 | tf_op jit(solution)/shard_map/ppermute | solution.py:471
  6.2 1.5 %collective-permute-start.2 = (bf16[2,2,128,384]{3,2,1,0:T(8,128)(2,1)S(1)}, bf16[2,2,128,384]{3,2,1,0:T(8,128)(2,1)S(1)}, u32[]{:S(2)}, u32[]{:S(2)}) collective-permute-start(bf16[2,2,128,384]{3,2,1,0:T(8,128)(2,1)S(1)} %get-tuple-element.150.refs_0_.refs_4_), channel_id=1, source_target_pairs={{0,4},{2,6},{4,0},{6,2},{8,12},{10,14},{12,8},{14,10},{16,20},{18,... | collective-permute-start | bytes 1179656 | tf_op jit(solution)/shard_map/ppermute | solution.py:471
  7.7 2.6 %collective-permute-start.4 = (bf16[2,2,128,384]{3,2,1,0:T(8,128)(2,1)S(1)}, bf16[2,2,128,384]{3,2,1,0:T(8,128)(2,1)S(1)}, u32[]{:S(2)}, u32[]{:S(2)}) collective-permute-start(bf16[2,2,128,384]{3,2,1,0:T(8,128)(2,1)S(1)} %get-tuple-element.104), channel_id=1, source_target_pairs={{0,16},{2,18},{4,20},{6,22},{8,24},{10,26},{12,28},{14,30},{16,0},... | collective-permute-start | bytes 1179656 | tf_op jit(solution)/shard_map/ppermute | solution.py:471
  10.3 0.0 collective-permute-done.got.hidden
  10.3 7.4 %norm_and_queries.1 = (bf16[256,3072]{1,0:T(8,128)(2,1)S(1)}, bf16[256,1536]{1,0:T(8,128)(2,1)S(1)}, bf16[256,384]{1,0:T(8,128)(2,1)S(1)}, bf16[256,384]{1,0:T(8...) custom-call(s32[3]{0:T(128)S(1)} %pad_add_fusion.pos, ...), custom_call_target="tpu_custom_call" | custom-call | flops 1000 | bytes 1000 | tf_op jit(solution)/shard_map/norm_and_queries/pallas_call | solution.py:166
  17.7 5.3 %collective-permute-done.1.block.refs_2_.refs_8_ = bf16[2,2,128,384]{3,2,1,0:T(8,128)(2,1)S(1)} collective-permute-done((bf16[2,2,128,384]{3,2,1,0:T(8,128)(2,1)S(1)}, bf16[2,2,128,384]{3,2,1,0:T(8,128)(2,1)S(1)}, u32[]{:S(2)}, u32[]{:S(2)}) %collective-permute-start.1) | collective-permute-done | bytes 393248 | tf_op jit(solution)/shard_map/ppermute | solution.py:471
  23.0 0.0 collective-permute-done.2.refs_1_.refs_6_
  23.0 2.7 %collective-permute-start.5 = (bf16[2,128,384]{2,1,0:T(8,128)(2,1)S(1)}, bf16[2,128,384]{2,1,0:T(8,128)(2,1)S(1)}, u32[]{:S(2)}, u32[]{:S(2)}) collective-permute-start(bf16[2,128,384]{2,1,0:T(8,128)(2,1)S(1)} %get-tuple-element.117), channel_id=1, source_target_pairs={{0,4},{2,6},{4,0},{6,2},{8,12},{10,14},{12,8},{14,10},{16,20},{18,... | collective-permute-start | bytes 589832 | tf_op jit(solution)/shard_map/ppermute | solution.py:471
  25.7 0.1 collective-permute-start.6
  25.8 2.5 %collective-permute-start.3 = (bf16[2,2,128,384]{3,2,1,0:T(8,128)(2,1)S(1)}, bf16[2,2,128,384]{3,2,1,0:T(8,128)(2,1)S(1)}, u32[]{:S(2)}, u32[]{:S(2)}) collective-permute-start(bf16[2,2,128,384]{3,2,1,0:T(8,128)(2,1)S(1)} %get-tuple-element.115), channel_id=1, source_target_pairs={{0,24},{2,26},{4,28},{6,30},{8,16},{10,18},{12,20},{14,22},{16,8},... | collective-permute-start | bytes 1179656 | tf_op jit(solution)/shard_map/ppermute | solution.py:471
  28.3 5.5 %fresh_keys.1 = (bf16[2,128,1536]{2,1,0:T(8,128)(2,1)S(1)}, bf16[2,128,1536]{2,1,0:T(8,128)(2,1)S(1)}) custom-call(bf16[256,3072]{1,0:T(8,128)(2,1)S(1)} %get-tuple-element.135.normed, f32[2,128]{1,0:T(2,128)S(1)} %copy-done.3, bf16[3,3072,1536]{2,1,0:T(8,128)(2,1)} %bitcast.9), custom_call_target="tpu_custom_call" | custom-call | flops 1000 | bytes 1000 | tf_op jit(solution)/shard_map/fresh_keys/pallas_call | solution.py:208
  33.8 0.0 collective-permute-done.5.refs_3_.refs_10_
  33.8 0.9 collective-permute-done.6.refs_4_.refs_11_
  34.7 0.1 collective-permute-start.9
  34.8 1.8 %collective-permute-start.7 = (bf16[2,128,384]{2,1,0:T(8,128)(2,1)S(1)}, bf16[2,128,384]{2,1,0:T(8,128)(2,1)S(1)}, u32[]{:S(2)}, u32[]{:S(2)}) collective-permute-start(bf16[2,128,384]{2,1,0:T(8,128)(2,1)S(1)} %get-tuple-element.130), channel_id=1, source_target_pairs={{0,4},{2,6},{4,0},{6,2},{8,12},{10,14},{12,8},{14,10},{16,20},{18,... | collective-permute-start | bytes 589832 | tf_op jit(solution)/shard_map/ppermute | solution.py:471
  36.6 0.3 collective-permute-start.8
  36.9 0.6 pack.2
  37.5 0.1 collective-permute-start.13
  37.6 5.2 %fresh_values.1 = (bf16[2,128,1536]{2,1,0:T(8,128)(2,1)S(1)}, bf16[2,128,1536]{2,1,0:T(8,128)(2,1)S(1)}) custom-call(bf16[256,3072]{1,0:T(8,128)(2,1)S(1)} %get-tuple-element.135.normed, f32[2,128]{1,0:T(2,128)S(1)} %copy-done.3, bf16[3,3072,1536]{2,1,0:T(8,128)(2,1)} %bitcast.10, ...), custom_call_target="tpu_custom_call", output_to_operand_aliasing={{0}: (3, {}), {1}: (4, {})} | custom-call | flops 1000 | bytes 1000 | tf_op jit(solution)/shard_map/fresh_values/pallas_call | solution.py:208
  42.8 0.0 collective-permute-done.3.refs_3_.refs_18_
  42.8 0.0 collective-permute-done.7.refs_1_.refs_15_
  42.8 2.1 %collective-permute-done.8.refs_2_.refs_16_ = bf16[2,128,384]{2,1,0:T(8,128)(2,1)S(1)} collective-permute-done((bf16[2,128,384]{2,1,0:T(8,128)(2,1)S(1)}, bf16[2,128,384]{2,1,0:T(8,128)(2,1)S(1)}, u32[]{:S(2)}, u32[]{:S(2)}) %collective-permute-start.8) | collective-permute-done | bytes 196640 | tf_op jit(solution)/shard_map/ppermute | solution.py:471
  45.0 0.6 pack.3
  45.6 0.1 collective-permute-start.14
  45.7 1.5 %collective-permute-start.10 = (bf16[2,2,128,384]{3,2,1,0:T(8,128)(2,1)S(1)}, bf16[2,2,128,384]{3,2,1,0:T(8,128)(2,1)S(1)}, u32[]{:S(2)}, u32[]{:S(2)}) collective-permute-start(bf16[2,2,128,384]{3,2,1,0:T(8,128)(2,1)S(1)} %collective-permute-done.3.refs_3_.refs_18_), channel_id=1, source_target_pairs={{0,4},{2,6},{4,0},{6,2},{8,12},{10,14},{12,8},{14,10},{16,20},{18,... | collective-permute-start | bytes 1179656 | tf_op jit(solution)/shard_map/ppermute | solution.py:471
  47.1 2.7 %collective-permute-start.11 = (bf16[128,384]{1,0:T(8,128)(2,1)S(1)}, bf16[128,384]{1,0:T(8,128)(2,1)S(1)}, u32[]{:S(2)}, u32[]{:S(2)}) collective-permute-start(bf16[128,384]{1,0:T(8,128)(2,1)S(1)} %get-tuple-element.146), channel_id=1, source_target_pairs={{0,16},{2,18},{4,20},{6,22},{8,24},{10,26},{12,28},{14,30},{16,0},... | collective-permute-start | bytes 294920 | tf_op jit(solution)/shard_map/ppermute | solution.py:471
  49.8 1.4 %collective-permute-start.12 = (bf16[128,384]{1,0:T(8,128)(2,1)S(1)}, bf16[128,384]{1,0:T(8,128)(2,1)S(1)}, u32[]{:S(2)}, u32[]{:S(2)}) collective-permute-start(bf16[128,384]{1,0:T(8,128)(2,1)S(1)} %get-tuple-element.147), channel_id=1, source_target_pairs={{0,24},{2,26},{4,28},{6,30},{8,16},{10,18},{12,20},{14,22},{16,8},... | collective-permute-start | bytes 294920 | tf_op jit(solution)/shard_map/ppermute | solution.py:471
  51.2 3.1 %attend_own.1 = (f32[256,1536]{1,0:T(8,128)S(1)}, f32[256,1536]{1,0:T(8,128)S(1)}, f32[256,1536]{1,0:T(8,128)S(1)}) custom-call(bf16[256,1536]{1,0:T(8,128)(2,1)S(1)} %get-tuple-element.156.q, bf16[2,128,1536]{2,1,0:T(8,128)(2,1)S(1)} %get-tuple-element.200.mine, bf16[2,128,1536]{2,1,0:T(8,128)(2,1)S(1)} %get-tuple-element.201.other), custom_call_target="tpu_custom_call" | custom-call | flops 1000 | bytes 1000 | tf_op jit(solution)/shard_map/attend_own/pallas_call | solution.py:268
  54.3 3.6 %collective-permute-done.11.refs_2_ = bf16[128,384]{1,0:T(8,128)(2,1)S(1)} collective-permute-done((bf16[128,384]{1,0:T(8,128)(2,1)S(1)}, bf16[128,384]{1,0:T(8,128)(2,1)S(1)}, u32[]{:S(2)}, u32[]{:S(2)}) %collective-permute-start.11) | collective-permute-done | bytes 98336 | tf_op jit(solution)/shard_map/ppermute | solution.py:471
  57.9 0.0 collective-permute-done.12.refs_3_
  57.9 0.0 collective-permute-done.10.refs_20_
  57.9 0.0 collective-permute-done.13.refs_5_.refs_7_.refs_9_.refs_12_
  57.9 0.0 collective-permute-done.14.refs_14_.refs_17_.refs_19_
  57.9 0.1 collective-permute-start.15
  58.0 3.0 %collective-permute-start.16 = (bf16[128,384]{1,0:T(8,128)(2,1)S(1)}, bf16[128,384]{1,0:T(8,128)(2,1)S(1)}, u32[]{:S(2)}, u32[]{:S(2)}) collective-permute-start(bf16[128,384]{1,0:T(8,128)(2,1)S(1)} %get-tuple-element.175), channel_id=1, source_target_pairs={{0,16},{2,18},{4,20},{6,22},{8,24},{10,26},{12,28},{14,30},{16,0},... | collective-permute-start | bytes 294920 | tf_op jit(solution)/shard_map/ppermute | solution.py:471
  61.0 1.4 %collective-permute-start.17 = (bf16[128,384]{1,0:T(8,128)(2,1)S(1)}, bf16[128,384]{1,0:T(8,128)(2,1)S(1)}, u32[]{:S(2)}, u32[]{:S(2)}) collective-permute-start(bf16[128,384]{1,0:T(8,128)(2,1)S(1)} %get-tuple-element.176), channel_id=1, source_target_pairs={{0,24},{2,26},{4,28},{6,30},{8,16},{10,18},{12,20},{14,22},{16,8},... | collective-permute-start | bytes 294920 | tf_op jit(solution)/shard_map/ppermute | solution.py:471
  62.3 4.8 %attend_groups.2 = (bf16[400,128]{1,0:T(8,128)(2,1)S(1)}, bf16[400,128]{1,0:T(8,128)(2,1)S(1)}, bf16[400,128]{1,0:T(8,128)(2,1)S(1)}, bf16[400,128]{1,0:T(8,128)(2,1)S(1)}) custom-call(s32[3]{0:T(128)S(1)} %pad_add_fusion.pos, bf16[256,384]{1,0:T(8,128)(2,1)S(1)} %get-tuple-element.182.refs_0_, bf16[256,384]{1,0:T(8,128)(2,1)S(1)} %collective-permute-done.9.refs_1_, ...), custom_call_target="tpu_custom_call" | custom-call | flops 1000 | bytes 1000 | tf_op jit(solution)/shard_map/attend_groups/pallas_call | solution.py:345
  67.2 1.6 %collective-permute-done.16.refs_2_ = bf16[128,384]{1,0:T(8,128)(2,1)S(1)} collective-permute-done((bf16[128,384]{1,0:T(8,128)(2,1)S(1)}, bf16[128,384]{1,0:T(8,128)(2,1)S(1)}, u32[]{:S(2)}, u32[]{:S(2)}) %collective-permute-start.16) | collective-permute-done | bytes 98336 | tf_op jit(solution)/shard_map/ppermute | solution.py:471
  68.8 0.0 collective-permute-done.17.refs_3_
  68.8 2.4 %collective-permute-start.18 = (bf16[400,128]{1,0:T(8,128)(2,1)S(1)}, bf16[400,128]{1,0:T(8,128)(2,1)S(1)}, u32[]{:S(2)}, u32[]{:S(2)}) collective-permute-start(bf16[400,128]{1,0:T(8,128)(2,1)S(1)} %get-tuple-element.179), channel_id=1, source_target_pairs={{0,24},{2,26},{4,28},{6,30},{8,16},{10,18},{12,20},{14,22},{16,8},... | collective-permute-start | bytes 307208 | tf_op jit(solution)/shard_map/ppermute | solution.py:471
  71.2 1.4 %collective-permute-start.19 = (bf16[400,128]{1,0:T(8,128)(2,1)S(1)}, bf16[400,128]{1,0:T(8,128)(2,1)S(1)}, u32[]{:S(2)}, u32[]{:S(2)}) collective-permute-start(bf16[400,128]{1,0:T(8,128)(2,1)S(1)} %get-tuple-element.180), channel_id=1, source_target_pairs={{0,16},{2,18},{4,20},{6,22},{8,24},{10,26},{12,28},{14,30},{16,0},... | collective-permute-start | bytes 307208 | tf_op jit(solution)/shard_map/ppermute | solution.py:471
  72.7 0.5 collective-permute-start.20
  73.2 4.9 %attend_groups.3 = (bf16[400,128]{1,0:T(8,128)(2,1)S(1)}, bf16[400,128]{1,0:T(8,128)(2,1)S(1)}, bf16[400,128]{1,0:T(8,128)(2,1)S(1)}, bf16[400,128]{1,0:T(8,128)(2,1)S(1)}) custom-call(s32[3]{0:T(128)S(1)} %pad_add_fusion.pos, bf16[256,384]{1,0:T(8,128)(2,1)S(1)} %get-tuple-element.182.refs_0_, bf16[256,384]{1,0:T(8,128)(2,1)S(1)} %collective-permute-done.9.refs_1_, ...), custom_call_target="tpu_custom_call" | custom-call | flops 1000 | bytes 1000 | tf_op jit(solution)/shard_map/attend_groups/pallas_call | solution.py:345
  78.1 2.5 %collective-permute-start.21 = (bf16[400,128]{1,0:T(8,128)(2,1)S(1)}, bf16[400,128]{1,0:T(8,128)(2,1)S(1)}, u32[]{:S(2)}, u32[]{:S(2)}) collective-permute-start(bf16[400,128]{1,0:T(8,128)(2,1)S(1)} %get-tuple-element.187), channel_id=1, source_target_pairs={{0,24},{2,26},{4,28},{6,30},{8,16},{10,18},{12,20},{14,22},{16,8},... | collective-permute-start | bytes 307208 | tf_op jit(solution)/shard_map/ppermute | solution.py:471
  80.6 0.5 collective-permute-start.22
  81.1 1.4 %collective-permute-start.23 = (bf16[400,128]{1,0:T(8,128)(2,1)S(1)}, bf16[400,128]{1,0:T(8,128)(2,1)S(1)}, u32[]{:S(2)}, u32[]{:S(2)}) collective-permute-start(bf16[400,128]{1,0:T(8,128)(2,1)S(1)} %get-tuple-element.189), channel_id=1, source_target_pairs={{0,8},{2,10},{4,12},{6,14},{8,0},{10,2},{12,4},{14,6},{16,24},{18,... | collective-permute-start | bytes 307208 | tf_op jit(solution)/shard_map/ppermute | solution.py:471
  82.5 2.1 %collective-permute-done.19.refs_2_ = bf16[400,128]{1,0:T(8,128)(2,1)S(1)} collective-permute-done((bf16[400,128]{1,0:T(8,128)(2,1)S(1)}, bf16[400,128]{1,0:T(8,128)(2,1)S(1)}, u32[]{:S(2)}, u32[]{:S(2)}) %collective-permute-start.19) | collective-permute-done | bytes 102432 | tf_op jit(solution)/shard_map/ppermute | solution.py:471
  84.7 1.8 %merge_and_project.2 = (bf16[128,1536]{1,0:T(8,128)(2,1)S(1)}, bf16[128,1536]{1,0:T(8,128)(2,1)S(1)}) custom-call(s32[3]{0:T(128)S(1)} %pad_add_fusion.pos, bf16[400,128]{1,0:T(8,128)(2,1)S(1)} %get-tuple-element.190.refs_0_, bf16[400,128]{1,0:T(8,128)(2,1)S(1)} %collective-permute-done.18.refs_1_, bf16[400,128]{1,0:T(8,128)(2,1)S(1)} %collective-permute-done.19.refs_2_, ...), custom_call_target="tpu_custom_call" | custom-call | flops 10000000000 | bytes 100000000 | tf_op jit(solution)/shard_map/merge_and_project/pallas_call | solution.py:387
  86.4 1.6 %collective-permute-start.25 = (bf16[128,1536]{1,0:T(8,128)(2,1)S(1)}, bf16[128,1536]{1,0:T(8,128)(2,1)S(1)}, u32[]{:S(2)}, u32[]{:S(2)}) collective-permute-start(bf16[128,1536]{1,0:T(8,128)(2,1)S(1)} %get-tuple-element.194), channel_id=1, source_target_pairs={{0,1},{1,0},{2,3},{3,2},{4,5},{5,4},{6,7},{7,6},{8,9},{9,8},{10,11... | collective-permute-start | bytes 1179656 | tf_op jit(solution)/shard_map/ppermute | solution.py:533
  88.0 2.3 %collective-permute-done.22.refs_2_ = bf16[400,128]{1,0:T(8,128)(2,1)S(1)} collective-permute-done((bf16[400,128]{1,0:T(8,128)(2,1)S(1)}, bf16[400,128]{1,0:T(8,128)(2,1)S(1)}, u32[]{:S(2)}, u32[]{:S(2)}) %collective-permute-start.22) | collective-permute-done | bytes 102432 | tf_op jit(solution)/shard_map/ppermute | solution.py:471
  90.3 1.8 %merge_and_project.3 = (bf16[128,1536]{1,0:T(8,128)(2,1)S(1)}, bf16[128,1536]{1,0:T(8,128)(2,1)S(1)}) custom-call(s32[3]{0:T(128)S(1)} %pad_add_fusion.pos, bf16[400,128]{1,0:T(8,128)(2,1)S(1)} %get-tuple-element.195.refs_0_, bf16[400,128]{1,0:T(8,128)(2,1)S(1)} %collective-permute-done.21.refs_1_, bf16[400,128]{1,0:T(8,128)(2,1)S(1)} %collective-permute-done.22.refs_2_, ...), custom_call_target="tpu_custom_call" | custom-call | flops 10000000000 | bytes 100000000 | tf_op jit(solution)/shard_map/merge_and_project/pallas_call | solution.py:387
  92.1 1.6 %collective-permute-start.24 = (bf16[128,1536]{1,0:T(8,128)(2,1)S(1)}, bf16[128,1536]{1,0:T(8,128)(2,1)S(1)}, u32[]{:S(2)}, u32[]{:S(2)}) collective-permute-start(bf16[128,1536]{1,0:T(8,128)(2,1)S(1)} %get-tuple-element.197), channel_id=1, source_target_pairs={{0,1},{1,0},{2,3},{3,2},{4,5},{5,4},{6,7},{7,6},{8,9},{9,8},{10,11... | collective-permute-start | bytes 1179656 | tf_op jit(solution)/shard_map/ppermute | solution.py:537
  93.7 1.4 %project_kept.3.keep = f32[128,1536]{1,0:T(8,128)S(1)} custom-call(s32[3]{0:T(128)S(1)} %pad_add_fusion.pos, bf16[128,1536]{1,0:T(8,128)(2,1)S(1)} %get-tuple-element.199.attended, bf16[1536,3072]{1,0:T(8,128)(2,1)S(1)} %bitcast.7), custom_call_target="tpu_custom_call" | custom-call | flops 1000 | bytes 1000 | tf_op jit(solution)/shard_map/project_kept/pallas_call | solution.py:403
  95.1 0.7 gate_and_add.2
  95.8 0.1 collective-permute-start.26
  95.9 1.4 %project_kept.2.keep = f32[128,1536]{1,0:T(8,128)S(1)} custom-call(s32[3]{0:T(128)S(1)} %pad_add_fusion.pos, bf16[128,1536]{1,0:T(8,128)(2,1)S(1)} %get-tuple-element.196.attended, bf16[1536,3072]{1,0:T(8,128)(2,1)S(1)} %bitcast.7), custom_call_target="tpu_custom_call" | custom-call | flops 1000 | bytes 1000 | tf_op jit(solution)/shard_map/project_kept/pallas_call | solution.py:403
  97.3 1.7 %place_fresh.1 = bf16[2,2,128,1536]{3,2,1,0:T(8,128)(2,1)} custom-call(s32[3]{0:T(128)S(1)} %pad_add_fusion.pos, bf16[2,128,1536]{2,1,0:T(8,128)(2,1)S(1)} %get-tuple-element.200.mine, bf16[2,128,1536]{2,1,0:T(8,128)(2,1)S(1)} %collective-permute-done.27.got), custom_call_target="tpu_custom_call" | custom-call | tf_op jit(solution)/shard_map/place_fresh/pallas_call | solution.py:233
  99.0 4.0 %collective-permute-done.24.got = bf16[128,1536]{1,0:T(8,128)(2,1)S(1)} collective-permute-done((bf16[128,1536]{1,0:T(8,128)(2,1)S(1)}, bf16[128,1536]{1,0:T(8,128)(2,1)S(1)}, u32[]{:S(2)}, u32[]{:S(2)}) %collective-permute-start.24) | collective-permute-done | bytes 393248 | tf_op jit(solution)/shard_map/ppermute | solution.py:537
  103.0 1.4 %gate_and_add.3 = bf16[2,128,1536]{2,1,0:T(8,128)(2,1)} custom-call(s32[3]{0:T(128)S(1)} %pad_add_fusion.pos, bf16[2,128,3072]{2,1,0:T(8,128)(2,1)S(1)} %copy-done, f32[3,2,3072]{2,1,0:T(2,128)S(1)} %copy-done.2, f32[128,1536]{1,0:T(8,128)S(1)} %project_kept.2.keep, bf16[128,1536]{1,0:T(8,128)(2,1)S(1)} %collective-permute-done.24.got, ...), custom_call_target="tpu_custom_call" | custom-call | flops 1000 | bytes 1000 | tf_op jit(solution)/shard_map/gate_and_add/pallas_call | solution.py:448
  (27 shorter events, 0.1 us)
Async XLA Ops:
  0.6 2.3 %copy-start = (bf16[2,128,3072]{2,1,0:T(8,128)(2,1)S(1)}, bf16[2,128,3072]{2,1,0:T(8,128)(2,1)}, u32[]{:S(2)}) copy-start(bf16[2,128,3072]{2,1,0:T(8,128)(2,1)} %hidden.3) | copy-start | bytes 4718596
  0.7 1.5 %copy-start.1 = (bf16[2,2,128,1536]{3,2,1,0:T(8,128)(2,1)S(1)}, bf16[2,2,128,1536]{3,2,1,0:T(8,128)(2,1)}, u32[]{:S(2)}) copy-start(bf16[2,2,128,1536]{3,2,1,0:T(8,128)(2,1)} %stale.1) | copy-start | bytes 4718596
  2.2 8.0 %copy-start.2 = (f32[3,2,3072]{2,1,0:T(2,128)S(1)}, f32[3,2,3072]{2,1,0:T(2,128)}, u32[]{:S(2)}) copy-start(f32[3,2,3072]{2,1,0:T(2,128)} %mod.5) | copy-start | bytes 221188
  2.2 8.0 %copy-start.3 = (f32[2,128]{1,0:T(2,128)S(1)}, f32[2,128]{1,0:T(2,128)}, u32[]{:S(2)}) copy-start(f32[2,128]{1,0:T(2,128)} %gain.5) | copy-start | bytes 3076
  3.0 7.3 %collective-permute-start = (bf16[128,3072]{1,0:T(8,128)(2,1)S(1)}, bf16[128,3072]{1,0:T(8,128)(2,1)S(1)}, u32[]{:S(2)}, u32[]{:S(2)}) collective-permute-start(bf16[128,3072]{1,0:T(8,128)(2,1)S(1)} %dynamic-slice_bitcast_fusion), channel_id=1, source_target_pairs={{0,2},{2,0},{4,6},{6,4},{8,10},{10,8},{12,14},{14,12},{16,18},{18,... | collective-permute-start | bytes 2359304 | tf_op jit(solution)/shard_map/ppermute | solution.py:471
  3.5 19.5 %collective-permute-start.1 = (bf16[2,2,128,384]{3,2,1,0:T(8,128)(2,1)S(1)}, bf16[2,2,128,384]{3,2,1,0:T(8,128)(2,1)S(1)}, u32[]{:S(2)}, u32[]{:S(2)}) collective-permute-start(bf16[2,2,128,384]{3,2,1,0:T(8,128)(2,1)S(1)} %get-tuple-element.103), channel_id=1, source_target_pairs={{0,8},{2,10},{4,12},{6,14},{8,0},{10,2},{12,4},{14,6},{16,24},{18,... | collective-permute-start | bytes 1179656 | tf_op jit(solution)/shard_map/ppermute | solution.py:471
  6.2 16.8 %collective-permute-start.2 = (bf16[2,2,128,384]{3,2,1,0:T(8,128)(2,1)S(1)}, bf16[2,2,128,384]{3,2,1,0:T(8,128)(2,1)S(1)}, u32[]{:S(2)}, u32[]{:S(2)}) collective-permute-start(bf16[2,2,128,384]{3,2,1,0:T(8,128)(2,1)S(1)} %get-tuple-element.150.refs_0_.refs_4_), channel_id=1, source_target_pairs={{0,4},{2,6},{4,0},{6,2},{8,12},{10,14},{12,8},{14,10},{16,20},{18,... | collective-permute-start | bytes 1179656 | tf_op jit(solution)/shard_map/ppermute | solution.py:471
  7.7 26.1 %collective-permute-start.4 = (bf16[2,2,128,384]{3,2,1,0:T(8,128)(2,1)S(1)}, bf16[2,2,128,384]{3,2,1,0:T(8,128)(2,1)S(1)}, u32[]{:S(2)}, u32[]{:S(2)}) collective-permute-start(bf16[2,2,128,384]{3,2,1,0:T(8,128)(2,1)S(1)} %get-tuple-element.104), channel_id=1, source_target_pairs={{0,16},{2,18},{4,20},{6,22},{8,24},{10,26},{12,28},{14,30},{16,0},... | collective-permute-start | bytes 1179656 | tf_op jit(solution)/shard_map/ppermute | solution.py:471
  23.0 10.8 %collective-permute-start.5 = (bf16[2,128,384]{2,1,0:T(8,128)(2,1)S(1)}, bf16[2,128,384]{2,1,0:T(8,128)(2,1)S(1)}, u32[]{:S(2)}, u32[]{:S(2)}) collective-permute-start(bf16[2,128,384]{2,1,0:T(8,128)(2,1)S(1)} %get-tuple-element.117), channel_id=1, source_target_pairs={{0,4},{2,6},{4,0},{6,2},{8,12},{10,14},{12,8},{14,10},{16,20},{18,... | collective-permute-start | bytes 589832 | tf_op jit(solution)/shard_map/ppermute | solution.py:471
  25.7 8.9 %collective-permute-start.6 = (bf16[2,128,384]{2,1,0:T(8,128)(2,1)S(1)}, bf16[2,128,384]{2,1,0:T(8,128)(2,1)S(1)}, u32[]{:S(2)}, u32[]{:S(2)}) collective-permute-start(bf16[2,128,384]{2,1,0:T(8,128)(2,1)S(1)} %get-tuple-element.118), channel_id=1, source_target_pairs={{0,4},{2,6},{4,0},{6,2},{8,12},{10,14},{12,8},{14,10},{16,20},{18,... | collective-permute-start | bytes 589832 | tf_op jit(solution)/shard_map/ppermute | solution.py:471
  25.8 17.0 %collective-permute-start.3 = (bf16[2,2,128,384]{3,2,1,0:T(8,128)(2,1)S(1)}, bf16[2,2,128,384]{3,2,1,0:T(8,128)(2,1)S(1)}, u32[]{:S(2)}, u32[]{:S(2)}) collective-permute-start(bf16[2,2,128,384]{3,2,1,0:T(8,128)(2,1)S(1)} %get-tuple-element.115), channel_id=1, source_target_pairs={{0,24},{2,26},{4,28},{6,30},{8,16},{10,18},{12,20},{14,22},{16,8},... | collective-permute-start | bytes 1179656 | tf_op jit(solution)/shard_map/ppermute | solution.py:471
  34.7 8.1 %collective-permute-start.9 = (bf16[256,384]{1,0:T(8,128)(2,1)S(1)}, bf16[256,384]{1,0:T(8,128)(2,1)S(1)}, u32[]{:S(2)}, u32[]{:S(2)}) collective-permute-start(bf16[256,384]{1,0:T(8,128)(2,1)S(1)} %get-tuple-element.134), channel_id=1, source_target_pairs={{0,8},{2,10},{4,12},{6,14},{8,0},{10,2},{12,4},{14,6},{16,24},{18,... | collective-permute-start | bytes 589832 | tf_op jit(solution)/shard_map/ppermute | solution.py:471
  34.8 8.0 %collective-permute-start.7 = (bf16[2,128,384]{2,1,0:T(8,128)(2,1)S(1)}, bf16[2,128,384]{2,1,0:T(8,128)(2,1)S(1)}, u32[]{:S(2)}, u32[]{:S(2)}) collective-permute-start(bf16[2,128,384]{2,1,0:T(8,128)(2,1)S(1)} %get-tuple-element.130), channel_id=1, source_target_pairs={{0,4},{2,6},{4,0},{6,2},{8,12},{10,14},{12,8},{14,10},{16,20},{18,... | collective-permute-start | bytes 589832 | tf_op jit(solution)/shard_map/ppermute | solution.py:471
  36.6 8.4 %collective-permute-start.8 = (bf16[2,128,384]{2,1,0:T(8,128)(2,1)S(1)}, bf16[2,128,384]{2,1,0:T(8,128)(2,1)S(1)}, u32[]{:S(2)}, u32[]{:S(2)}) collective-permute-start(bf16[2,128,384]{2,1,0:T(8,128)(2,1)S(1)} %get-tuple-element.131), channel_id=1, source_target_pairs={{0,4},{2,6},{4,0},{6,2},{8,12},{10,14},{12,8},{14,10},{16,20},{18,... | collective-permute-start | bytes 589832 | tf_op jit(solution)/shard_map/ppermute | solution.py:471
  37.5 20.4 %collective-permute-start.13 = (bf16[4,2,128,384]{3,2,1,0:T(8,128)(2,1)S(1)}, bf16[4,2,128,384]{3,2,1,0:T(8,128)(2,1)S(1)}, u32[]{:S(2)}, u32[]{:S(2)}) collective-permute-start(bf16[4,2,128,384]{3,2,1,0:T(8,128)(2,1)S(1)} %pack.2), channel_id=1, source_target_pairs={{0,2},{2,0},{4,6},{6,4},{8,10},{10,8},{12,14},{14,12},{16,18},{18,... | collective-permute-start | bytes 2359304 | tf_op jit(solution)/shard_map/ppermute | solution.py:471
  45.6 12.3 %collective-permute-start.14 = (bf16[3,2,128,384]{3,2,1,0:T(8,128)(2,1)S(1)}, bf16[3,2,128,384]{3,2,1,0:T(8,128)(2,1)S(1)}, u32[]{:S(2)}, u32[]{:S(2)}) collective-permute-start(bf16[3,2,128,384]{3,2,1,0:T(8,128)(2,1)S(1)} %pack.3), channel_id=1, source_target_pairs={{0,2},{2,0},{4,6},{6,4},{8,10},{10,8},{12,14},{14,12},{16,18},{18,... | collective-permute-start | bytes 1769480 | tf_op jit(solution)/shard_map/ppermute | solution.py:471
  45.7 12.2 %collective-permute-start.10 = (bf16[2,2,128,384]{3,2,1,0:T(8,128)(2,1)S(1)}, bf16[2,2,128,384]{3,2,1,0:T(8,128)(2,1)S(1)}, u32[]{:S(2)}, u32[]{:S(2)}) collective-permute-start(bf16[2,2,128,384]{3,2,1,0:T(8,128)(2,1)S(1)} %collective-permute-done.3.refs_3_.refs_18_), channel_id=1, source_target_pairs={{0,4},{2,6},{4,0},{6,2},{8,12},{10,14},{12,8},{14,10},{16,20},{18,... | collective-permute-start | bytes 1179656 | tf_op jit(solution)/shard_map/ppermute | solution.py:471
  47.1 10.7 %collective-permute-start.11 = (bf16[128,384]{1,0:T(8,128)(2,1)S(1)}, bf16[128,384]{1,0:T(8,128)(2,1)S(1)}, u32[]{:S(2)}, u32[]{:S(2)}) collective-permute-start(bf16[128,384]{1,0:T(8,128)(2,1)S(1)} %get-tuple-element.146), channel_id=1, source_target_pairs={{0,16},{2,18},{4,20},{6,22},{8,24},{10,26},{12,28},{14,30},{16,0},... | collective-permute-start | bytes 294920 | tf_op jit(solution)/shard_map/ppermute | solution.py:471
  49.8 8.1 %collective-permute-start.12 = (bf16[128,384]{1,0:T(8,128)(2,1)S(1)}, bf16[128,384]{1,0:T(8,128)(2,1)S(1)}, u32[]{:S(2)}, u32[]{:S(2)}) collective-permute-start(bf16[128,384]{1,0:T(8,128)(2,1)S(1)} %get-tuple-element.147), channel_id=1, source_target_pairs={{0,24},{2,26},{4,28},{6,30},{8,16},{10,18},{12,20},{14,22},{16,8},... | collective-permute-start | bytes 294920 | tf_op jit(solution)/shard_map/ppermute | solution.py:471
  57.9 4.4 %collective-permute-start.15 = (bf16[2,2,128,384]{3,2,1,0:T(8,128)(2,1)S(1)}, bf16[2,2,128,384]{3,2,1,0:T(8,128)(2,1)S(1)}, u32[]{:S(2)}, u32[]{:S(2)}) collective-permute-start(bf16[2,2,128,384]{3,2,1,0:T(8,128)(2,1)S(1)} %collective-permute-done.10.refs_20_), channel_id=1, source_target_pairs={{0,2},{2,0},{4,6},{6,4},{8,10},{10,8},{12,14},{14,12},{16,18},{18,... | collective-permute-start | bytes 1179656 | tf_op jit(solution)/shard_map/ppermute | solution.py:471
  58.0 10.8 %collective-permute-start.16 = (bf16[128,384]{1,0:T(8,128)(2,1)S(1)}, bf16[128,384]{1,0:T(8,128)(2,1)S(1)}, u32[]{:S(2)}, u32[]{:S(2)}) collective-permute-start(bf16[128,384]{1,0:T(8,128)(2,1)S(1)} %get-tuple-element.175), channel_id=1, source_target_pairs={{0,16},{2,18},{4,20},{6,22},{8,24},{10,26},{12,28},{14,30},{16,0},... | collective-permute-start | bytes 294920 | tf_op jit(solution)/shard_map/ppermute | solution.py:471
  61.0 7.9 %collective-permute-start.17 = (bf16[128,384]{1,0:T(8,128)(2,1)S(1)}, bf16[128,384]{1,0:T(8,128)(2,1)S(1)}, u32[]{:S(2)}, u32[]{:S(2)}) collective-permute-start(bf16[128,384]{1,0:T(8,128)(2,1)S(1)} %get-tuple-element.176), channel_id=1, source_target_pairs={{0,24},{2,26},{4,28},{6,30},{8,16},{10,18},{12,20},{14,22},{16,8},... | collective-permute-start | bytes 294920 | tf_op jit(solution)/shard_map/ppermute | solution.py:471
  62.3 22.3 %slice-start = ((s8[9437184]{0:T(1024)(128)(4,1)}), s8[4194304]{0:T(1024)(128)(4,1)S(1)}, s32[]{:S(2)}) async-start(s8[9437184]{0:T(1024)(128)(4,1)} %bitcast.6), calls=%async_computation | async-start | bytes 8388608
  62.3 22.3 %slice-start.1 = ((s8[9437184]{0:T(1024)(128)(4,1)}), s8[4194304]{0:T(1024)(128)(4,1)S(1)}, s32[]{:S(2)}) async-start(s8[9437184]{0:T(1024)(128)(4,1)} %bitcast.6), calls=%async_computation.1 | async-start | bytes 8388608
  68.8 15.8 %slice-start.2 = ((s8[9437184]{0:T(1024)(128)(4,1)}), s8[1048576]{0:T(1024)(128)(4,1)S(1)}, s32[]{:S(2)}) async-start(s8[9437184]{0:T(1024)(128)(4,1)} %bitcast.6), calls=%async_computation.2 | async-start | bytes 2097152
  68.8 12.3 %collective-permute-start.18 = (bf16[400,128]{1,0:T(8,128)(2,1)S(1)}, bf16[400,128]{1,0:T(8,128)(2,1)S(1)}, u32[]{:S(2)}, u32[]{:S(2)}) collective-permute-start(bf16[400,128]{1,0:T(8,128)(2,1)S(1)} %get-tuple-element.179), channel_id=1, source_target_pairs={{0,24},{2,26},{4,28},{6,30},{8,16},{10,18},{12,20},{14,22},{16,8},... | collective-permute-start | bytes 307208 | tf_op jit(solution)/shard_map/ppermute | solution.py:471
  71.2 13.4 %collective-permute-start.19 = (bf16[400,128]{1,0:T(8,128)(2,1)S(1)}, bf16[400,128]{1,0:T(8,128)(2,1)S(1)}, u32[]{:S(2)}, u32[]{:S(2)}) collective-permute-start(bf16[400,128]{1,0:T(8,128)(2,1)S(1)} %get-tuple-element.180), channel_id=1, source_target_pairs={{0,16},{2,18},{4,20},{6,22},{8,24},{10,26},{12,28},{14,30},{16,0},... | collective-permute-start | bytes 307208 | tf_op jit(solution)/shard_map/ppermute | solution.py:471
  72.7 11.9 %collective-permute-start.20 = (bf16[400,128]{1,0:T(8,128)(2,1)S(1)}, bf16[400,128]{1,0:T(8,128)(2,1)S(1)}, u32[]{:S(2)}, u32[]{:S(2)}) collective-permute-start(bf16[400,128]{1,0:T(8,128)(2,1)S(1)} %get-tuple-element.181), channel_id=1, source_target_pairs={{0,8},{2,10},{4,12},{6,14},{8,0},{10,2},{12,4},{14,6},{16,24},{18,... | collective-permute-start | bytes 307208 | tf_op jit(solution)/shard_map/ppermute | solution.py:471
  78.1 9.9 %collective-permute-start.21 = (bf16[400,128]{1,0:T(8,128)(2,1)S(1)}, bf16[400,128]{1,0:T(8,128)(2,1)S(1)}, u32[]{:S(2)}, u32[]{:S(2)}) collective-permute-start(bf16[400,128]{1,0:T(8,128)(2,1)S(1)} %get-tuple-element.187), channel_id=1, source_target_pairs={{0,24},{2,26},{4,28},{6,30},{8,16},{10,18},{12,20},{14,22},{16,8},... | collective-permute-start | bytes 307208 | tf_op jit(solution)/shard_map/ppermute | solution.py:471
  80.6 9.8 %collective-permute-start.22 = (bf16[400,128]{1,0:T(8,128)(2,1)S(1)}, bf16[400,128]{1,0:T(8,128)(2,1)S(1)}, u32[]{:S(2)}, u32[]{:S(2)}) collective-permute-start(bf16[400,128]{1,0:T(8,128)(2,1)S(1)} %get-tuple-element.188), channel_id=1, source_target_pairs={{0,16},{2,18},{4,20},{6,22},{8,24},{10,26},{12,28},{14,30},{16,0},... | collective-permute-start | bytes 307208 | tf_op jit(solution)/shard_map/ppermute | solution.py:471
  81.1 9.2 %collective-permute-start.23 = (bf16[400,128]{1,0:T(8,128)(2,1)S(1)}, bf16[400,128]{1,0:T(8,128)(2,1)S(1)}, u32[]{:S(2)}, u32[]{:S(2)}) collective-permute-start(bf16[400,128]{1,0:T(8,128)(2,1)S(1)} %get-tuple-element.189), channel_id=1, source_target_pairs={{0,8},{2,10},{4,12},{6,14},{8,0},{10,2},{12,4},{14,6},{16,24},{18,... | collective-permute-start | bytes 307208 | tf_op jit(solution)/shard_map/ppermute | solution.py:471
  86.4 8.7 %collective-permute-start.25 = (bf16[128,1536]{1,0:T(8,128)(2,1)S(1)}, bf16[128,1536]{1,0:T(8,128)(2,1)S(1)}, u32[]{:S(2)}, u32[]{:S(2)}) collective-permute-start(bf16[128,1536]{1,0:T(8,128)(2,1)S(1)} %get-tuple-element.194), channel_id=1, source_target_pairs={{0,1},{1,0},{2,3},{3,2},{4,5},{5,4},{6,7},{7,6},{8,9},{9,8},{10,11... | collective-permute-start | bytes 1179656 | tf_op jit(solution)/shard_map/ppermute | solution.py:533
  88.0 9.2 %collective-permute-start.27 = (bf16[2,128,1536]{2,1,0:T(8,128)(2,1)S(1)}, bf16[2,128,1536]{2,1,0:T(8,128)(2,1)S(1)}, u32[]{:S(2)}, u32[]{:S(2)}) collective-permute-start(bf16[2,128,1536]{2,1,0:T(8,128)(2,1)S(1)} %get-tuple-element.201.other), channel_id=1, source_target_pairs={{0,2},{2,0},{4,6},{6,4},{8,10},{10,8},{12,14},{14,12},{16,18},{18,... | collective-permute-start | bytes 2359304 | tf_op jit(solution)/shard_map/ppermute | solution.py:471
  92.1 10.9 %collective-permute-start.24 = (bf16[128,1536]{1,0:T(8,128)(2,1)S(1)}, bf16[128,1536]{1,0:T(8,128)(2,1)S(1)}, u32[]{:S(2)}, u32[]{:S(2)}) collective-permute-start(bf16[128,1536]{1,0:T(8,128)(2,1)S(1)} %get-tuple-element.197), channel_id=1, source_target_pairs={{0,1},{1,0},{2,3},{3,2},{4,5},{5,4},{6,7},{7,6},{8,9},{9,8},{10,11... | collective-permute-start | bytes 1179656 | tf_op jit(solution)/shard_map/ppermute | solution.py:537
  95.8 7.2 %collective-permute-start.26 = (bf16[128,1536]{1,0:T(8,128)(2,1)S(1)}, bf16[128,1536]{1,0:T(8,128)(2,1)S(1)}, u32[]{:S(2)}, u32[]{:S(2)}) collective-permute-start(bf16[128,1536]{1,0:T(8,128)(2,1)S(1)} %gate_and_add.2), channel_id=1, source_target_pairs={{0,2},{2,0},{4,6},{6,4},{8,10},{10,8},{12,14},{14,12},{16,18},{18,... | collective-permute-start | bytes 1179656 | tf_op jit(solution)/shard_map/ppermute | solution.py:471

commit v6 on v5

--- a/solution.py
+++ b/solution.py
@@ -12,7 +12,7 @@
 EXTRA = 16
 LOG2E = 1.4426950408889634
 SCALE2 = HEAD ** (-0.5) * LOG2E
-ORDER = (0, 3, 2, 1)
+ORDER = ((0, 1, 3, 2), (0, 3, 2, 1))
 MIB = 1024 * 1024
 BF = jnp.bfloat16
 F32 = jnp.float32
@@ -280,7 +280,7 @@
 def group_kernel(part, blocks, places, pos, *refs):
     count = sum(n for n, _ in places)
     queries, refs, outs = refs[:blocks], list(refs[blocks : blocks + count]), refs[blocks + count :]
-    outs = [outs[ORDER.index(b)] for b in range(blocks)]
+    outs = [outs[ORDER[part].index(b)] for b in range(blocks)]
     cached = [[refs.pop(0) for _ in range(n)] for n, _ in places]
     rows, width = queries[-1].shape
     mine = slice(part * rows, (part + 1) * rows)
@@ -359,7 +359,7 @@
     rows = send.shape[0]
     width = acc.shape[1] // groups
     mine = slice(part * rows, (part + 1) * rows)
-    for s, block in zip(ORDER, back):
+    for s, block in zip(ORDER[part], back):
         for h in range(width // HEAD):
             cols = pl.ds(pl.multiple_of((pos[0] ^ s) * width + h * HEAD, HEAD), HEAD)
             three = block[rows * width // HEAD :, :].astype(F32)[3 * h : 3 * h + 3, :]
@@ -523,10 +523,10 @@
     ]
     theirs = attend_groups(1, pos, their_queries, held)
     theirs, my_queries = step((theirs, my_queries))
-    back = [theirs[0]] + [along(a, s) for a, s in zip(theirs[1:], ORDER[1:])]
+    back = [theirs[0]] + [along(a, s) for a, s in zip(theirs[1:], ORDER[1][1:])]
     my_queries[0] = tie(my_queries[0], theirs)
     mine = attend_groups(0, pos, my_queries, held)
-    mine_back = [mine[0]] + [along(a, s) for a, s in zip(mine[1:], ORDER[1:])]
+    mine_back = [mine[0]] + [along(a, s) for a, s in zip(mine[1:], ORDER[0][1:])]
     back[0] = tie(back[0], mine)
     swap = [(0, 1), (1, 0)]
     send, attended = project_out(1, pos, back, *own, out_weight)

time: 105 us -> 104 us (level)
  no operation moved by 1% of the time
where the time goes in v6:
time: 104 us
  Pallas kernels  43 us (41%)
  starting transfers between devices  36.1 us (35%)
  waiting for transfers between devices  22.4 us (22%)
  local copies, waits for them, and re-layouts  1.59 us (2%)
  between operations  1.11 us (1%)
    ppermute x26, starting transfers between devices, across(): return lax.ppermute(value, 'patch', [(i, i ^ bit) for i in range(patches)])  33 us
    ppermute x26, waiting for transfers between devices, across(): return lax.ppermute(value, 'patch', [(i, i ^ bit) for i in range(patches)])  18.7 us
    pallas_call x2, Pallas kernels, make_fresh(): pl.pallas_call(functools.partial(fresh_kernel, slot), grid=(cols // block...  10.7 us
    pallas_call x2, Pallas kernels, attend_groups(): pl.pallas_call(functools.partial(group_kernel, part, blocks, places), in_...  9.71 us
    pallas_call x1, Pallas kernels, make_queries(): pl.pallas_call(functools.partial(query_kernel, groups, per_step), grid_sp...  7.39 us
    ppermute x1, waiting for transfers between devices, spread_heads(): my_got = lax.ppermute(my_send, 'tp', swap)  3.67 us
    pallas_call x2, Pallas kernels, project_out(): pl.pallas_call(functools.partial(out_kernel, part, groups), in_specs=[SCA...  3.58 us
    pallas_call x1, Pallas kernels, attend_own(): pl.pallas_call(own_kernel, grid=(cols // block,), in_specs=[wide, kv, kv]...  3.09 us
  transfers between devices with their start and end apart: 28, of which 8 were waited for; matrix products, arithmetic and copies ran while one was open for 0% of the time, Pallas kernels for 39%

profile of v6, /device:TPU:0, one launch (start us, length us, event | category | flops | bytes accessed | tf_op | source)
XLA Modules:
  0.0 104.3 jit_solution(17391736150259953746)
XLA Ops:
  0.7 0.1 pad_add_fusion.pos
  0.7 1.5 %copy-done.1 = bf16[2,2,128,1536]{3,2,1,0:T(8,128)(2,1)S(1)} copy-done((bf16[2,2,128,1536]{3,2,1,0:T(8,128)(2,1)S(1)}, bf16[2,2,128,1536]{3,2,1,0:T(8,128)(2,1)}, u32[]{:S(2)}) %copy-start.1) | copy-done | bytes 1572888
  2.3 0.7 cut_stale.1
  3.0 0.1 dynamic-slice_bitcast_fusion
  3.0 0.5 collective-permute-start
  3.5 2.6 %collective-permute-start.1 = (bf16[2,2,128,384]{3,2,1,0:T(8,128)(2,1)S(1)}, bf16[2,2,128,384]{3,2,1,0:T(8,128)(2,1)S(1)}, u32[]{:S(2)}, u32[]{:S(2)}) collective-permute-start(bf16[2,2,128,384]{3,2,1,0:T(8,128)(2,1)S(1)} %get-tuple-element.103), channel_id=1, source_target_pairs={{0,8},{2,10},{4,12},{6,14},{8,0},{10,2},{12,4},{14,6},{16,24},{18,... | collective-permute-start | bytes 1179656 | tf_op jit(solution)/shard_map/ppermute | solution.py:471
  6.2 1.5 %collective-permute-start.2 = (bf16[2,2,128,384]{3,2,1,0:T(8,128)(2,1)S(1)}, bf16[2,2,128,384]{3,2,1,0:T(8,128)(2,1)S(1)}, u32[]{:S(2)}, u32[]{:S(2)}) collective-permute-start(bf16[2,2,128,384]{3,2,1,0:T(8,128)(2,1)S(1)} %get-tuple-element.150.refs_0_.refs_4_), channel_id=1, source_target_pairs={{0,4},{2,6},{4,0},{6,2},{8,12},{10,14},{12,8},{14,10},{16,20},{18,... | collective-permute-start | bytes 1179656 | tf_op jit(solution)/shard_map/ppermute | solution.py:471
  7.7 2.6 %collective-permute-start.4 = (bf16[2,2,128,384]{3,2,1,0:T(8,128)(2,1)S(1)}, bf16[2,2,128,384]{3,2,1,0:T(8,128)(2,1)S(1)}, u32[]{:S(2)}, u32[]{:S(2)}) collective-permute-start(bf16[2,2,128,384]{3,2,1,0:T(8,128)(2,1)S(1)} %get-tuple-element.104), channel_id=1, source_target_pairs={{0,16},{2,18},{4,20},{6,22},{8,24},{10,26},{12,28},{14,30},{16,0},... | collective-permute-start | bytes 1179656 | tf_op jit(solution)/shard_map/ppermute | solution.py:471
  10.3 7.4 %norm_and_queries.1 = (bf16[256,3072]{1,0:T(8,128)(2,1)S(1)}, bf16[256,1536]{1,0:T(8,128)(2,1)S(1)}, bf16[256,384]{1,0:T(8,128)(2,1)S(1)}, bf16[256,384]{1,0:T(8...) custom-call(s32[3]{0:T(128)S(1)} %pad_add_fusion.pos, ...), custom_call_target="tpu_custom_call" | custom-call | flops 1000 | bytes 1000 | tf_op jit(solution)/shard_map/norm_and_queries/pallas_call | solution.py:166
  17.7 5.3 %collective-permute-done.1.block.refs_2_.refs_8_ = bf16[2,2,128,384]{3,2,1,0:T(8,128)(2,1)S(1)} collective-permute-done((bf16[2,2,128,384]{3,2,1,0:T(8,128)(2,1)S(1)}, bf16[2,2,128,384]{3,2,1,0:T(8,128)(2,1)S(1)}, u32[]{:S(2)}, u32[]{:S(2)}) %collective-permute-start.1) | collective-permute-done | bytes 393248 | tf_op jit(solution)/shard_map/ppermute | solution.py:471
  23.0 0.0 collective-permute-done.2.refs_1_.refs_6_
  23.0 2.7 %collective-permute-start.5 = (bf16[2,128,384]{2,1,0:T(8,128)(2,1)S(1)}, bf16[2,128,384]{2,1,0:T(8,128)(2,1)S(1)}, u32[]{:S(2)}, u32[]{:S(2)}) collective-permute-start(bf16[2,128,384]{2,1,0:T(8,128)(2,1)S(1)} %get-tuple-element.117), channel_id=1, source_target_pairs={{0,4},{2,6},{4,0},{6,2},{8,12},{10,14},{12,8},{14,10},{16,20},{18,... | collective-permute-start | bytes 589832 | tf_op jit(solution)/shard_map/ppermute | solution.py:471
  25.7 0.1 collective-permute-start.6
  25.8 2.5 %collective-permute-start.3 = (bf16[2,2,128,384]{3,2,1,0:T(8,128)(2,1)S(1)}, bf16[2,2,128,384]{3,2,1,0:T(8,128)(2,1)S(1)}, u32[]{:S(2)}, u32[]{:S(2)}) collective-permute-start(bf16[2,2,128,384]{3,2,1,0:T(8,128)(2,1)S(1)} %get-tuple-element.115), channel_id=1, source_target_pairs={{0,24},{2,26},{4,28},{6,30},{8,16},{10,18},{12,20},{14,22},{16,8},... | collective-permute-start | bytes 1179656 | tf_op jit(solution)/shard_map/ppermute | solution.py:471
  28.3 5.5 %fresh_keys.1 = (bf16[2,128,1536]{2,1,0:T(8,128)(2,1)S(1)}, bf16[2,128,1536]{2,1,0:T(8,128)(2,1)S(1)}) custom-call(bf16[256,3072]{1,0:T(8,128)(2,1)S(1)} %get-tuple-element.135.normed, f32[2,128]{1,0:T(2,128)S(1)} %copy-done.3, bf16[3,3072,1536]{2,1,0:T(8,128)(2,1)} %bitcast.9), custom_call_target="tpu_custom_call" | custom-call | flops 1000 | bytes 1000 | tf_op jit(solution)/shard_map/fresh_keys/pallas_call | solution.py:208
  33.8 0.0 collective-permute-done.5.refs_3_.refs_10_
  33.8 0.9 collective-permute-done.6.refs_4_.refs_11_
  34.7 0.1 collective-permute-start.9
  34.8 1.8 %collective-permute-start.7 = (bf16[2,128,384]{2,1,0:T(8,128)(2,1)S(1)}, bf16[2,128,384]{2,1,0:T(8,128)(2,1)S(1)}, u32[]{:S(2)}, u32[]{:S(2)}) collective-permute-start(bf16[2,128,384]{2,1,0:T(8,128)(2,1)S(1)} %get-tuple-element.130), channel_id=1, source_target_pairs={{0,4},{2,6},{4,0},{6,2},{8,12},{10,14},{12,8},{14,10},{16,20},{18,... | collective-permute-start | bytes 589832 | tf_op jit(solution)/shard_map/ppermute | solution.py:471
  36.6 0.3 collective-permute-start.8
  36.9 0.6 pack.2
  37.5 0.1 collective-permute-start.13
  37.6 5.2 %fresh_values.1 = (bf16[2,128,1536]{2,1,0:T(8,128)(2,1)S(1)}, bf16[2,128,1536]{2,1,0:T(8,128)(2,1)S(1)}) custom-call(bf16[256,3072]{1,0:T(8,128)(2,1)S(1)} %get-tuple-element.135.normed, f32[2,128]{1,0:T(2,128)S(1)} %copy-done.3, bf16[3,3072,1536]{2,1,0:T(8,128)(2,1)} %bitcast.10, ...), custom_call_target="tpu_custom_call", output_to_operand_aliasing={{0}: (3, {}), {1}: (4, {})} | custom-call | flops 1000 | bytes 1000 | tf_op jit(solution)/shard_map/fresh_values/pallas_call | solution.py:208
  42.8 0.0 collective-permute-done.3.refs_3_.refs_18_
  42.8 0.0 collective-permute-done.7.refs_1_.refs_15_
  42.8 2.1 %collective-permute-done.8.refs_2_.refs_16_ = bf16[2,128,384]{2,1,0:T(8,128)(2,1)S(1)} collective-permute-done((bf16[2,128,384]{2,1,0:T(8,128)(2,1)S(1)}, bf16[2,128,384]{2,1,0:T(8,128)(2,1)S(1)}, u32[]{:S(2)}, u32[]{:S(2)}) %collective-permute-start.8) | collective-permute-done | bytes 196640 | tf_op jit(solution)/shard_map/ppermute | solution.py:471
  45.0 0.6 pack.3
  45.6 0.1 collective-permute-start.14
  45.7 1.5 %collective-permute-start.10 = (bf16[2,2,128,384]{3,2,1,0:T(8,128)(2,1)S(1)}, bf16[2,2,128,384]{3,2,1,0:T(8,128)(2,1)S(1)}, u32[]{:S(2)}, u32[]{:S(2)}) collective-permute-start(bf16[2,2,128,384]{3,2,1,0:T(8,128)(2,1)S(1)} %collective-permute-done.3.refs_3_.refs_18_), channel_id=1, source_target_pairs={{0,4},{2,6},{4,0},{6,2},{8,12},{10,14},{12,8},{14,10},{16,20},{18,... | collective-permute-start | bytes 1179656 | tf_op jit(solution)/shard_map/ppermute | solution.py:471
  47.1 2.7 %collective-permute-start.11 = (bf16[128,384]{1,0:T(8,128)(2,1)S(1)}, bf16[128,384]{1,0:T(8,128)(2,1)S(1)}, u32[]{:S(2)}, u32[]{:S(2)}) collective-permute-start(bf16[128,384]{1,0:T(8,128)(2,1)S(1)} %get-tuple-element.146), channel_id=1, source_target_pairs={{0,16},{2,18},{4,20},{6,22},{8,24},{10,26},{12,28},{14,30},{16,0},... | collective-permute-start | bytes 294920 | tf_op jit(solution)/shard_map/ppermute | solution.py:471
  49.8 1.4 %collective-permute-start.12 = (bf16[128,384]{1,0:T(8,128)(2,1)S(1)}, bf16[128,384]{1,0:T(8,128)(2,1)S(1)}, u32[]{:S(2)}, u32[]{:S(2)}) collective-permute-start(bf16[128,384]{1,0:T(8,128)(2,1)S(1)} %get-tuple-element.147), channel_id=1, source_target_pairs={{0,24},{2,26},{4,28},{6,30},{8,16},{10,18},{12,20},{14,22},{16,8},... | collective-permute-start | bytes 294920 | tf_op jit(solution)/shard_map/ppermute | solution.py:471
  51.2 3.1 %attend_own.1 = (f32[256,1536]{1,0:T(8,128)S(1)}, f32[256,1536]{1,0:T(8,128)S(1)}, f32[256,1536]{1,0:T(8,128)S(1)}) custom-call(bf16[256,1536]{1,0:T(8,128)(2,1)S(1)} %get-tuple-element.156.q, bf16[2,128,1536]{2,1,0:T(8,128)(2,1)S(1)} %get-tuple-element.200.mine, bf16[2,128,1536]{2,1,0:T(8,128)(2,1)S(1)} %get-tuple-element.201.other), custom_call_target="tpu_custom_call" | custom-call | flops 1000 | bytes 1000 | tf_op jit(solution)/shard_map/attend_own/pallas_call | solution.py:268
  54.3 3.6 %collective-permute-done.11.refs_2_ = bf16[128,384]{1,0:T(8,128)(2,1)S(1)} collective-permute-done((bf16[128,384]{1,0:T(8,128)(2,1)S(1)}, bf16[128,384]{1,0:T(8,128)(2,1)S(1)}, u32[]{:S(2)}, u32[]{:S(2)}) %collective-permute-start.11) | collective-permute-done | bytes 98336 | tf_op jit(solution)/shard_map/ppermute | solution.py:471
  57.9 0.0 collective-permute-done.12.refs_3_
  57.9 0.0 collective-permute-done.10.refs_20_
  57.9 0.0 collective-permute-done.13.refs_5_.refs_7_.refs_9_.refs_12_
  57.9 0.0 collective-permute-done.14.refs_14_.refs_17_.refs_19_
  57.9 0.1 collective-permute-start.15
  58.0 3.0 %collective-permute-start.16 = (bf16[128,384]{1,0:T(8,128)(2,1)S(1)}, bf16[128,384]{1,0:T(8,128)(2,1)S(1)}, u32[]{:S(2)}, u32[]{:S(2)}) collective-permute-start(bf16[128,384]{1,0:T(8,128)(2,1)S(1)} %get-tuple-element.175), channel_id=1, source_target_pairs={{0,16},{2,18},{4,20},{6,22},{8,24},{10,26},{12,28},{14,30},{16,0},... | collective-permute-start | bytes 294920 | tf_op jit(solution)/shard_map/ppermute | solution.py:471
  61.0 1.4 %collective-permute-start.17 = (bf16[128,384]{1,0:T(8,128)(2,1)S(1)}, bf16[128,384]{1,0:T(8,128)(2,1)S(1)}, u32[]{:S(2)}, u32[]{:S(2)}) collective-permute-start(bf16[128,384]{1,0:T(8,128)(2,1)S(1)} %get-tuple-element.176), channel_id=1, source_target_pairs={{0,24},{2,26},{4,28},{6,30},{8,16},{10,18},{12,20},{14,22},{16,8},... | collective-permute-start | bytes 294920 | tf_op jit(solution)/shard_map/ppermute | solution.py:471
  62.3 0.0 collective-permute-done.15.refs_21_
  62.3 4.8 %attend_groups.2 = (bf16[400,128]{1,0:T(8,128)(2,1)S(1)}, bf16[400,128]{1,0:T(8,128)(2,1)S(1)}, bf16[400,128]{1,0:T(8,128)(2,1)S(1)}, bf16[400,128]{1,0:T(8,128)(2,1)S(1)}) custom-call(s32[3]{0:T(128)S(1)} %pad_add_fusion.pos, bf16[256,384]{1,0:T(8,128)(2,1)S(1)} %get-tuple-element.182.refs_0_, bf16[256,384]{1,0:T(8,128)(2,1)S(1)} %collective-permute-done.9.refs_1_, ...), custom_call_target="tpu_custom_call" | custom-call | flops 1000 | bytes 1000 | tf_op jit(solution)/shard_map/attend_groups/pallas_call | solution.py:345
  67.2 1.6 %collective-permute-done.16.refs_2_ = bf16[128,384]{1,0:T(8,128)(2,1)S(1)} collective-permute-done((bf16[128,384]{1,0:T(8,128)(2,1)S(1)}, bf16[128,384]{1,0:T(8,128)(2,1)S(1)}, u32[]{:S(2)}, u32[]{:S(2)}) %collective-permute-start.16) | collective-permute-done | bytes 98336 | tf_op jit(solution)/shard_map/ppermute | solution.py:471
  68.8 0.0 collective-permute-done.17.refs_3_
  68.8 2.4 %collective-permute-start.18 = (bf16[400,128]{1,0:T(8,128)(2,1)S(1)}, bf16[400,128]{1,0:T(8,128)(2,1)S(1)}, u32[]{:S(2)}, u32[]{:S(2)}) collective-permute-start(bf16[400,128]{1,0:T(8,128)(2,1)S(1)} %get-tuple-element.179), channel_id=1, source_target_pairs={{0,24},{2,26},{4,28},{6,30},{8,16},{10,18},{12,20},{14,22},{16,8},... | collective-permute-start | bytes 307208 | tf_op jit(solution)/shard_map/ppermute | solution.py:471
  71.2 1.4 %collective-permute-start.19 = (bf16[400,128]{1,0:T(8,128)(2,1)S(1)}, bf16[400,128]{1,0:T(8,128)(2,1)S(1)}, u32[]{:S(2)}, u32[]{:S(2)}) collective-permute-start(bf16[400,128]{1,0:T(8,128)(2,1)S(1)} %get-tuple-element.180), channel_id=1, source_target_pairs={{0,16},{2,18},{4,20},{6,22},{8,24},{10,26},{12,28},{14,30},{16,0},... | collective-permute-start | bytes 307208 | tf_op jit(solution)/shard_map/ppermute | solution.py:471
  72.7 0.5 collective-permute-start.20
  73.2 4.9 %attend_groups.3 = (bf16[400,128]{1,0:T(8,128)(2,1)S(1)}, bf16[400,128]{1,0:T(8,128)(2,1)S(1)}, bf16[400,128]{1,0:T(8,128)(2,1)S(1)}, bf16[400,128]{1,0:T(8,128)(2,1)S(1)}) custom-call(s32[3]{0:T(128)S(1)} %pad_add_fusion.pos, bf16[256,384]{1,0:T(8,128)(2,1)S(1)} %get-tuple-element.182.refs_0_, bf16[256,384]{1,0:T(8,128)(2,1)S(1)} %collective-permute-done.9.refs_1_, ...), custom_call_target="tpu_custom_call" | custom-call | flops 1000 | bytes 1000 | tf_op jit(solution)/shard_map/attend_groups/pallas_call | solution.py:345
  78.1 1.5 %collective-permute-start.21 = (bf16[400,128]{1,0:T(8,128)(2,1)S(1)}, bf16[400,128]{1,0:T(8,128)(2,1)S(1)}, u32[]{:S(2)}, u32[]{:S(2)}) collective-permute-start(bf16[400,128]{1,0:T(8,128)(2,1)S(1)} %get-tuple-element.187), channel_id=1, source_target_pairs={{0,8},{2,10},{4,12},{6,14},{8,0},{10,2},{12,4},{14,6},{16,24},{18,... | collective-permute-start | bytes 307208 | tf_op jit(solution)/shard_map/ppermute | solution.py:471
  79.6 2.2 %collective-permute-start.22 = (bf16[400,128]{1,0:T(8,128)(2,1)S(1)}, bf16[400,128]{1,0:T(8,128)(2,1)S(1)}, u32[]{:S(2)}, u32[]{:S(2)}) collective-permute-start(bf16[400,128]{1,0:T(8,128)(2,1)S(1)} %get-tuple-element.188), channel_id=1, source_target_pairs={{0,24},{2,26},{4,28},{6,30},{8,16},{10,18},{12,20},{14,22},{16,8},... | collective-permute-start | bytes 307208 | tf_op jit(solution)/shard_map/ppermute | solution.py:471
  81.9 0.0 collective-permute-done.19.refs_2_
  82.0 1.8 %merge_and_project.2 = (bf16[128,1536]{1,0:T(8,128)(2,1)S(1)}, bf16[128,1536]{1,0:T(8,128)(2,1)S(1)}) custom-call(s32[3]{0:T(128)S(1)} %pad_add_fusion.pos, bf16[400,128]{1,0:T(8,128)(2,1)S(1)} %get-tuple-element.190.refs_0_, bf16[400,128]{1,0:T(8,128)(2,1)S(1)} %collective-permute-done.18.refs_1_, bf16[400,128]{1,0:T(8,128)(2,1)S(1)} %collective-permute-done.19.refs_2_, ...), custom_call_target="tpu_custom_call" | custom-call | flops 10000000000 | bytes 100000000 | tf_op jit(solution)/shard_map/merge_and_project/pallas_call | solution.py:387
  83.8 1.6 %collective-permute-start.25 = (bf16[128,1536]{1,0:T(8,128)(2,1)S(1)}, bf16[128,1536]{1,0:T(8,128)(2,1)S(1)}, u32[]{:S(2)}, u32[]{:S(2)}) collective-permute-start(bf16[128,1536]{1,0:T(8,128)(2,1)S(1)} %get-tuple-element.194), channel_id=1, source_target_pairs={{0,1},{1,0},{2,3},{3,2},{4,5},{5,4},{6,7},{7,6},{8,9},{9,8},{10,11... | collective-permute-start | bytes 1179656 | tf_op jit(solution)/shard_map/ppermute | solution.py:533
  85.3 1.8 %collective-permute-done.22.refs_2_ = bf16[400,128]{1,0:T(8,128)(2,1)S(1)} collective-permute-done((bf16[400,128]{1,0:T(8,128)(2,1)S(1)}, bf16[400,128]{1,0:T(8,128)(2,1)S(1)}, u32[]{:S(2)}, u32[]{:S(2)}) %collective-permute-start.22) | collective-permute-done | bytes 102432 | tf_op jit(solution)/shard_map/ppermute | solution.py:471
  87.1 3.3 %collective-permute-done.23.refs_3_ = bf16[400,128]{1,0:T(8,128)(2,1)S(1)} collective-permute-done((bf16[400,128]{1,0:T(8,128)(2,1)S(1)}, bf16[400,128]{1,0:T(8,128)(2,1)S(1)}, u32[]{:S(2)}, u32[]{:S(2)}) %collective-permute-start.23) | collective-permute-done | bytes 102432 | tf_op jit(solution)/shard_map/ppermute | solution.py:471
  90.4 1.8 %merge_and_project.3 = (bf16[128,1536]{1,0:T(8,128)(2,1)S(1)}, bf16[128,1536]{1,0:T(8,128)(2,1)S(1)}) custom-call(s32[3]{0:T(128)S(1)} %pad_add_fusion.pos, bf16[400,128]{1,0:T(8,128)(2,1)S(1)} %get-tuple-element.195.refs_0_, bf16[400,128]{1,0:T(8,128)(2,1)S(1)} %collective-permute-done.21.refs_1_, bf16[400,128]{1,0:T(8,128)(2,1)S(1)} %collective-permute-done.22.refs_2_, ...), custom_call_target="tpu_custom_call" | custom-call | flops 10000000000 | bytes 100000000 | tf_op jit(solution)/shard_map/merge_and_project/pallas_call | solution.py:387
  92.2 1.6 %collective-permute-start.24 = (bf16[128,1536]{1,0:T(8,128)(2,1)S(1)}, bf16[128,1536]{1,0:T(8,128)(2,1)S(1)}, u32[]{:S(2)}, u32[]{:S(2)}) collective-permute-start(bf16[128,1536]{1,0:T(8,128)(2,1)S(1)} %get-tuple-element.197), channel_id=1, source_target_pairs={{0,1},{1,0},{2,3},{3,2},{4,5},{5,4},{6,7},{7,6},{8,9},{9,8},{10,11... | collective-permute-start | bytes 1179656 | tf_op jit(solution)/shard_map/ppermute | solution.py:537
  93.8 1.4 %project_kept.3.keep = f32[128,1536]{1,0:T(8,128)S(1)} custom-call(s32[3]{0:T(128)S(1)} %pad_add_fusion.pos, bf16[128,1536]{1,0:T(8,128)(2,1)S(1)} %get-tuple-element.199.attended, bf16[1536,3072]{1,0:T(8,128)(2,1)S(1)} %bitcast.7), custom_call_target="tpu_custom_call" | custom-call | flops 1000 | bytes 1000 | tf_op jit(solution)/shard_map/project_kept/pallas_call | solution.py:403
  95.2 0.7 gate_and_add.2
  95.9 0.1 collective-permute-start.26
  96.0 1.4 %project_kept.2.keep = f32[128,1536]{1,0:T(8,128)S(1)} custom-call(s32[3]{0:T(128)S(1)} %pad_add_fusion.pos, bf16[128,1536]{1,0:T(8,128)(2,1)S(1)} %get-tuple-element.196.attended, bf16[1536,3072]{1,0:T(8,128)(2,1)S(1)} %bitcast.7), custom_call_target="tpu_custom_call" | custom-call | flops 1000 | bytes 1000 | tf_op jit(solution)/shard_map/project_kept/pallas_call | solution.py:403
  97.4 1.7 %place_fresh.1 = bf16[2,2,128,1536]{3,2,1,0:T(8,128)(2,1)} custom-call(s32[3]{0:T(128)S(1)} %pad_add_fusion.pos, bf16[2,128,1536]{2,1,0:T(8,128)(2,1)S(1)} %get-tuple-element.200.mine, bf16[2,128,1536]{2,1,0:T(8,128)(2,1)S(1)} %collective-permute-done.27.got), custom_call_target="tpu_custom_call" | custom-call | tf_op jit(solution)/shard_map/place_fresh/pallas_call | solution.py:233
  99.1 3.7 %collective-permute-done.24.got = bf16[128,1536]{1,0:T(8,128)(2,1)S(1)} collective-permute-done((bf16[128,1536]{1,0:T(8,128)(2,1)S(1)}, bf16[128,1536]{1,0:T(8,128)(2,1)S(1)}, u32[]{:S(2)}, u32[]{:S(2)}) %collective-permute-start.24) | collective-permute-done | bytes 393248 | tf_op jit(solution)/shard_map/ppermute | solution.py:537
  102.7 1.4 %gate_and_add.3 = bf16[2,128,1536]{2,1,0:T(8,128)(2,1)} custom-call(s32[3]{0:T(128)S(1)} %pad_add_fusion.pos, bf16[2,128,3072]{2,1,0:T(8,128)(2,1)S(1)} %copy-done, f32[3,2,3072]{2,1,0:T(2,128)S(1)} %copy-done.2, f32[128,1536]{1,0:T(8,128)S(1)} %project_kept.2.keep, bf16[128,1536]{1,0:T(8,128)(2,1)S(1)} %collective-permute-done.24.got, ...), custom_call_target="tpu_custom_call" | custom-call | flops 1000 | bytes 1000 | tf_op jit(solution)/shard_map/gate_and_add/pallas_call | solution.py:448
  (27 shorter events, 0.1 us)
Async XLA Ops:
  0.6 2.3 %copy-start = (bf16[2,128,3072]{2,1,0:T(8,128)(2,1)S(1)}, bf16[2,128,3072]{2,1,0:T(8,128)(2,1)}, u32[]{:S(2)}) copy-start(bf16[2,128,3072]{2,1,0:T(8,128)(2,1)} %hidden.3) | copy-start | bytes 4718596
  0.7 1.5 %copy-start.1 = (bf16[2,2,128,1536]{3,2,1,0:T(8,128)(2,1)S(1)}, bf16[2,2,128,1536]{3,2,1,0:T(8,128)(2,1)}, u32[]{:S(2)}) copy-start(bf16[2,2,128,1536]{3,2,1,0:T(8,128)(2,1)} %stale.1) | copy-start | bytes 4718596
  2.2 8.0 %copy-start.2 = (f32[3,2,3072]{2,1,0:T(2,128)S(1)}, f32[3,2,3072]{2,1,0:T(2,128)}, u32[]{:S(2)}) copy-start(f32[3,2,3072]{2,1,0:T(2,128)} %mod.5) | copy-start | bytes 221188
  2.2 8.0 %copy-start.3 = (f32[2,128]{1,0:T(2,128)S(1)}, f32[2,128]{1,0:T(2,128)}, u32[]{:S(2)}) copy-start(f32[2,128]{1,0:T(2,128)} %gain.5) | copy-start | bytes 3076
  3.0 7.3 %collective-permute-start = (bf16[128,3072]{1,0:T(8,128)(2,1)S(1)}, bf16[128,3072]{1,0:T(8,128)(2,1)S(1)}, u32[]{:S(2)}, u32[]{:S(2)}) collective-permute-start(bf16[128,3072]{1,0:T(8,128)(2,1)S(1)} %dynamic-slice_bitcast_fusion), channel_id=1, source_target_pairs={{0,2},{2,0},{4,6},{6,4},{8,10},{10,8},{12,14},{14,12},{16,18},{18,... | collective-permute-start | bytes 2359304 | tf_op jit(solution)/shard_map/ppermute | solution.py:471
  3.5 19.5 %collective-permute-start.1 = (bf16[2,2,128,384]{3,2,1,0:T(8,128)(2,1)S(1)}, bf16[2,2,128,384]{3,2,1,0:T(8,128)(2,1)S(1)}, u32[]{:S(2)}, u32[]{:S(2)}) collective-permute-start(bf16[2,2,128,384]{3,2,1,0:T(8,128)(2,1)S(1)} %get-tuple-element.103), channel_id=1, source_target_pairs={{0,8},{2,10},{4,12},{6,14},{8,0},{10,2},{12,4},{14,6},{16,24},{18,... | collective-permute-start | bytes 1179656 | tf_op jit(solution)/shard_map/ppermute | solution.py:471
  6.2 16.8 %collective-permute-start.2 = (bf16[2,2,128,384]{3,2,1,0:T(8,128)(2,1)S(1)}, bf16[2,2,128,384]{3,2,1,0:T(8,128)(2,1)S(1)}, u32[]{:S(2)}, u32[]{:S(2)}) collective-permute-start(bf16[2,2,128,384]{3,2,1,0:T(8,128)(2,1)S(1)} %get-tuple-element.150.refs_0_.refs_4_), channel_id=1, source_target_pairs={{0,4},{2,6},{4,0},{6,2},{8,12},{10,14},{12,8},{14,10},{16,20},{18,... | collective-permute-start | bytes 1179656 | tf_op jit(solution)/shard_map/ppermute | solution.py:471
  7.7 26.1 %collective-permute-start.4 = (bf16[2,2,128,384]{3,2,1,0:T(8,128)(2,1)S(1)}, bf16[2,2,128,384]{3,2,1,0:T(8,128)(2,1)S(1)}, u32[]{:S(2)}, u32[]{:S(2)}) collective-permute-start(bf16[2,2,128,384]{3,2,1,0:T(8,128)(2,1)S(1)} %get-tuple-element.104), channel_id=1, source_target_pairs={{0,16},{2,18},{4,20},{6,22},{8,24},{10,26},{12,28},{14,30},{16,0},... | collective-permute-start | bytes 1179656 | tf_op jit(solution)/shard_map/ppermute | solution.py:471
  23.0 10.8 %collective-permute-start.5 = (bf16[2,128,384]{2,1,0:T(8,128)(2,1)S(1)}, bf16[2,128,384]{2,1,0:T(8,128)(2,1)S(1)}, u32[]{:S(2)}, u32[]{:S(2)}) collective-permute-start(bf16[2,128,384]{2,1,0:T(8,128)(2,1)S(1)} %get-tuple-element.117), channel_id=1, source_target_pairs={{0,4},{2,6},{4,0},{6,2},{8,12},{10,14},{12,8},{14,10},{16,20},{18,... | collective-permute-start | bytes 589832 | tf_op jit(solution)/shard_map/ppermute | solution.py:471
  25.7 8.9 %collective-permute-start.6 = (bf16[2,128,384]{2,1,0:T(8,128)(2,1)S(1)}, bf16[2,128,384]{2,1,0:T(8,128)(2,1)S(1)}, u32[]{:S(2)}, u32[]{:S(2)}) collective-permute-start(bf16[2,128,384]{2,1,0:T(8,128)(2,1)S(1)} %get-tuple-element.118), channel_id=1, source_target_pairs={{0,4},{2,6},{4,0},{6,2},{8,12},{10,14},{12,8},{14,10},{16,20},{18,... | collective-permute-start | bytes 589832 | tf_op jit(solution)/shard_map/ppermute | solution.py:471
  25.8 17.0 %collective-permute-start.3 = (bf16[2,2,128,384]{3,2,1,0:T(8,128)(2,1)S(1)}, bf16[2,2,128,384]{3,2,1,0:T(8,128)(2,1)S(1)}, u32[]{:S(2)}, u32[]{:S(2)}) collective-permute-start(bf16[2,2,128,384]{3,2,1,0:T(8,128)(2,1)S(1)} %get-tuple-element.115), channel_id=1, source_target_pairs={{0,24},{2,26},{4,28},{6,30},{8,16},{10,18},{12,20},{14,22},{16,8},... | collective-permute-start | bytes 1179656 | tf_op jit(solution)/shard_map/ppermute | solution.py:471
  34.7 8.1 %collective-permute-start.9 = (bf16[256,384]{1,0:T(8,128)(2,1)S(1)}, bf16[256,384]{1,0:T(8,128)(2,1)S(1)}, u32[]{:S(2)}, u32[]{:S(2)}) collective-permute-start(bf16[256,384]{1,0:T(8,128)(2,1)S(1)} %get-tuple-element.134), channel_id=1, source_target_pairs={{0,8},{2,10},{4,12},{6,14},{8,0},{10,2},{12,4},{14,6},{16,24},{18,... | collective-permute-start | bytes 589832 | tf_op jit(solution)/shard_map/ppermute | solution.py:471
  34.8 8.0 %collective-permute-start.7 = (bf16[2,128,384]{2,1,0:T(8,128)(2,1)S(1)}, bf16[2,128,384]{2,1,0:T(8,128)(2,1)S(1)}, u32[]{:S(2)}, u32[]{:S(2)}) collective-permute-start(bf16[2,128,384]{2,1,0:T(8,128)(2,1)S(1)} %get-tuple-element.130), channel_id=1, source_target_pairs={{0,4},{2,6},{4,0},{6,2},{8,12},{10,14},{12,8},{14,10},{16,20},{18,... | collective-permute-start | bytes 589832 | tf_op jit(solution)/shard_map/ppermute | solution.py:471
  36.6 8.4 %collective-permute-start.8 = (bf16[2,128,384]{2,1,0:T(8,128)(2,1)S(1)}, bf16[2,128,384]{2,1,0:T(8,128)(2,1)S(1)}, u32[]{:S(2)}, u32[]{:S(2)}) collective-permute-start(bf16[2,128,384]{2,1,0:T(8,128)(2,1)S(1)} %get-tuple-element.131), channel_id=1, source_target_pairs={{0,4},{2,6},{4,0},{6,2},{8,12},{10,14},{12,8},{14,10},{16,20},{18,... | collective-permute-start | bytes 589832 | tf_op jit(solution)/shard_map/ppermute | solution.py:471
  37.5 20.4 %collective-permute-start.13 = (bf16[4,2,128,384]{3,2,1,0:T(8,128)(2,1)S(1)}, bf16[4,2,128,384]{3,2,1,0:T(8,128)(2,1)S(1)}, u32[]{:S(2)}, u32[]{:S(2)}) collective-permute-start(bf16[4,2,128,384]{3,2,1,0:T(8,128)(2,1)S(1)} %pack.2), channel_id=1, source_target_pairs={{0,2},{2,0},{4,6},{6,4},{8,10},{10,8},{12,14},{14,12},{16,18},{18,... | collective-permute-start | bytes 2359304 | tf_op jit(solution)/shard_map/ppermute | solution.py:471
  45.6 12.3 %collective-permute-start.14 = (bf16[3,2,128,384]{3,2,1,0:T(8,128)(2,1)S(1)}, bf16[3,2,128,384]{3,2,1,0:T(8,128)(2,1)S(1)}, u32[]{:S(2)}, u32[]{:S(2)}) collective-permute-start(bf16[3,2,128,384]{3,2,1,0:T(8,128)(2,1)S(1)} %pack.3), channel_id=1, source_target_pairs={{0,2},{2,0},{4,6},{6,4},{8,10},{10,8},{12,14},{14,12},{16,18},{18,... | collective-permute-start | bytes 1769480 | tf_op jit(solution)/shard_map/ppermute | solution.py:471
  45.7 12.2 %collective-permute-start.10 = (bf16[2,2,128,384]{3,2,1,0:T(8,128)(2,1)S(1)}, bf16[2,2,128,384]{3,2,1,0:T(8,128)(2,1)S(1)}, u32[]{:S(2)}, u32[]{:S(2)}) collective-permute-start(bf16[2,2,128,384]{3,2,1,0:T(8,128)(2,1)S(1)} %collective-permute-done.3.refs_3_.refs_18_), channel_id=1, source_target_pairs={{0,4},{2,6},{4,0},{6,2},{8,12},{10,14},{12,8},{14,10},{16,20},{18,... | collective-permute-start | bytes 1179656 | tf_op jit(solution)/shard_map/ppermute | solution.py:471
  47.1 10.7 %collective-permute-start.11 = (bf16[128,384]{1,0:T(8,128)(2,1)S(1)}, bf16[128,384]{1,0:T(8,128)(2,1)S(1)}, u32[]{:S(2)}, u32[]{:S(2)}) collective-permute-start(bf16[128,384]{1,0:T(8,128)(2,1)S(1)} %get-tuple-element.146), channel_id=1, source_target_pairs={{0,16},{2,18},{4,20},{6,22},{8,24},{10,26},{12,28},{14,30},{16,0},... | collective-permute-start | bytes 294920 | tf_op jit(solution)/shard_map/ppermute | solution.py:471
  49.8 8.1 %collective-permute-start.12 = (bf16[128,384]{1,0:T(8,128)(2,1)S(1)}, bf16[128,384]{1,0:T(8,128)(2,1)S(1)}, u32[]{:S(2)}, u32[]{:S(2)}) collective-permute-start(bf16[128,384]{1,0:T(8,128)(2,1)S(1)} %get-tuple-element.147), channel_id=1, source_target_pairs={{0,24},{2,26},{4,28},{6,30},{8,16},{10,18},{12,20},{14,22},{16,8},... | collective-permute-start | bytes 294920 | tf_op jit(solution)/shard_map/ppermute | solution.py:471
  57.9 4.4 %collective-permute-start.15 = (bf16[2,2,128,384]{3,2,1,0:T(8,128)(2,1)S(1)}, bf16[2,2,128,384]{3,2,1,0:T(8,128)(2,1)S(1)}, u32[]{:S(2)}, u32[]{:S(2)}) collective-permute-start(bf16[2,2,128,384]{3,2,1,0:T(8,128)(2,1)S(1)} %collective-permute-done.10.refs_20_), channel_id=1, source_target_pairs={{0,2},{2,0},{4,6},{6,4},{8,10},{10,8},{12,14},{14,12},{16,18},{18,... | collective-permute-start | bytes 1179656 | tf_op jit(solution)/shard_map/ppermute | solution.py:471
  58.0 10.8 %collective-permute-start.16 = (bf16[128,384]{1,0:T(8,128)(2,1)S(1)}, bf16[128,384]{1,0:T(8,128)(2,1)S(1)}, u32[]{:S(2)}, u32[]{:S(2)}) collective-permute-start(bf16[128,384]{1,0:T(8,128)(2,1)S(1)} %get-tuple-element.175), channel_id=1, source_target_pairs={{0,16},{2,18},{4,20},{6,22},{8,24},{10,26},{12,28},{14,30},{16,0},... | collective-permute-start | bytes 294920 | tf_op jit(solution)/shard_map/ppermute | solution.py:471
  61.0 7.9 %collective-permute-start.17 = (bf16[128,384]{1,0:T(8,128)(2,1)S(1)}, bf16[128,384]{1,0:T(8,128)(2,1)S(1)}, u32[]{:S(2)}, u32[]{:S(2)}) collective-permute-start(bf16[128,384]{1,0:T(8,128)(2,1)S(1)} %get-tuple-element.176), channel_id=1, source_target_pairs={{0,24},{2,26},{4,28},{6,30},{8,16},{10,18},{12,20},{14,22},{16,8},... | collective-permute-start | bytes 294920 | tf_op jit(solution)/shard_map/ppermute | solution.py:471
  62.3 19.6 %slice-start = ((s8[9437184]{0:T(1024)(128)(4,1)}), s8[4194304]{0:T(1024)(128)(4,1)S(1)}, s32[]{:S(2)}) async-start(s8[9437184]{0:T(1024)(128)(4,1)} %bitcast.6), calls=%async_computation | async-start | bytes 8388608
  62.3 19.6 %slice-start.1 = ((s8[9437184]{0:T(1024)(128)(4,1)}), s8[4194304]{0:T(1024)(128)(4,1)S(1)}, s32[]{:S(2)}) async-start(s8[9437184]{0:T(1024)(128)(4,1)} %bitcast.6), calls=%async_computation.1 | async-start | bytes 8388608
  68.8 13.1 %slice-start.2 = ((s8[9437184]{0:T(1024)(128)(4,1)}), s8[1048576]{0:T(1024)(128)(4,1)S(1)}, s32[]{:S(2)}) async-start(s8[9437184]{0:T(1024)(128)(4,1)} %bitcast.6), calls=%async_computation.2 | async-start | bytes 2097152
  68.8 13.0 %collective-permute-start.18 = (bf16[400,128]{1,0:T(8,128)(2,1)S(1)}, bf16[400,128]{1,0:T(8,128)(2,1)S(1)}, u32[]{:S(2)}, u32[]{:S(2)}) collective-permute-start(bf16[400,128]{1,0:T(8,128)(2,1)S(1)} %get-tuple-element.179), channel_id=1, source_target_pairs={{0,24},{2,26},{4,28},{6,30},{8,16},{10,18},{12,20},{14,22},{16,8},... | collective-permute-start | bytes 307208 | tf_op jit(solution)/shard_map/ppermute | solution.py:471
  71.2 10.7 %collective-permute-start.19 = (bf16[400,128]{1,0:T(8,128)(2,1)S(1)}, bf16[400,128]{1,0:T(8,128)(2,1)S(1)}, u32[]{:S(2)}, u32[]{:S(2)}) collective-permute-start(bf16[400,128]{1,0:T(8,128)(2,1)S(1)} %get-tuple-element.180), channel_id=1, source_target_pairs={{0,16},{2,18},{4,20},{6,22},{8,24},{10,26},{12,28},{14,30},{16,0},... | collective-permute-start | bytes 307208 | tf_op jit(solution)/shard_map/ppermute | solution.py:471
  72.7 9.2 %collective-permute-start.20 = (bf16[400,128]{1,0:T(8,128)(2,1)S(1)}, bf16[400,128]{1,0:T(8,128)(2,1)S(1)}, u32[]{:S(2)}, u32[]{:S(2)}) collective-permute-start(bf16[400,128]{1,0:T(8,128)(2,1)S(1)} %get-tuple-element.181), channel_id=1, source_target_pairs={{0,8},{2,10},{4,12},{6,14},{8,0},{10,2},{12,4},{14,6},{16,24},{18,... | collective-permute-start | bytes 307208 | tf_op jit(solution)/shard_map/ppermute | solution.py:471
  78.1 7.3 %collective-permute-start.21 = (bf16[400,128]{1,0:T(8,128)(2,1)S(1)}, bf16[400,128]{1,0:T(8,128)(2,1)S(1)}, u32[]{:S(2)}, u32[]{:S(2)}) collective-permute-start(bf16[400,128]{1,0:T(8,128)(2,1)S(1)} %get-tuple-element.187), channel_id=1, source_target_pairs={{0,8},{2,10},{4,12},{6,14},{8,0},{10,2},{12,4},{14,6},{16,24},{18,... | collective-permute-start | bytes 307208 | tf_op jit(solution)/shard_map/ppermute | solution.py:471
  79.6 7.5 %collective-permute-start.22 = (bf16[400,128]{1,0:T(8,128)(2,1)S(1)}, bf16[400,128]{1,0:T(8,128)(2,1)S(1)}, u32[]{:S(2)}, u32[]{:S(2)}) collective-permute-start(bf16[400,128]{1,0:T(8,128)(2,1)S(1)} %get-tuple-element.188), channel_id=1, source_target_pairs={{0,24},{2,26},{4,28},{6,30},{8,16},{10,18},{12,20},{14,22},{16,8},... | collective-permute-start | bytes 307208 | tf_op jit(solution)/shard_map/ppermute | solution.py:471
  81.9 8.5 %collective-permute-start.23 = (bf16[400,128]{1,0:T(8,128)(2,1)S(1)}, bf16[400,128]{1,0:T(8,128)(2,1)S(1)}, u32[]{:S(2)}, u32[]{:S(2)}) collective-permute-start(bf16[400,128]{1,0:T(8,128)(2,1)S(1)} %get-tuple-element.189), channel_id=1, source_target_pairs={{0,16},{2,18},{4,20},{6,22},{8,24},{10,26},{12,28},{14,30},{16,0},... | collective-permute-start | bytes 307208 | tf_op jit(solution)/shard_map/ppermute | solution.py:471
  83.8 11.4 %collective-permute-start.25 = (bf16[128,1536]{1,0:T(8,128)(2,1)S(1)}, bf16[128,1536]{1,0:T(8,128)(2,1)S(1)}, u32[]{:S(2)}, u32[]{:S(2)}) collective-permute-start(bf16[128,1536]{1,0:T(8,128)(2,1)S(1)} %get-tuple-element.194), channel_id=1, source_target_pairs={{0,1},{1,0},{2,3},{3,2},{4,5},{5,4},{6,7},{7,6},{8,9},{9,8},{10,11... | collective-permute-start | bytes 1179656 | tf_op jit(solution)/shard_map/ppermute | solution.py:533
  85.3 12.0 %collective-permute-start.27 = (bf16[2,128,1536]{2,1,0:T(8,128)(2,1)S(1)}, bf16[2,128,1536]{2,1,0:T(8,128)(2,1)S(1)}, u32[]{:S(2)}, u32[]{:S(2)}) collective-permute-start(bf16[2,128,1536]{2,1,0:T(8,128)(2,1)S(1)} %get-tuple-element.201.other), channel_id=1, source_target_pairs={{0,2},{2,0},{4,6},{6,4},{8,10},{10,8},{12,14},{14,12},{16,18},{18,... | collective-permute-start | bytes 2359304 | tf_op jit(solution)/shard_map/ppermute | solution.py:471
  92.2 10.5 %collective-permute-start.24 = (bf16[128,1536]{1,0:T(8,128)(2,1)S(1)}, bf16[128,1536]{1,0:T(8,128)(2,1)S(1)}, u32[]{:S(2)}, u32[]{:S(2)}) collective-permute-start(bf16[128,1536]{1,0:T(8,128)(2,1)S(1)} %get-tuple-element.197), channel_id=1, source_target_pairs={{0,1},{1,0},{2,3},{3,2},{4,5},{5,4},{6,7},{7,6},{8,9},{9,8},{10,11... | collective-permute-start | bytes 1179656 | tf_op jit(solution)/shard_map/ppermute | solution.py:537
  95.9 6.9 %collective-permute-start.26 = (bf16[128,1536]{1,0:T(8,128)(2,1)S(1)}, bf16[128,1536]{1,0:T(8,128)(2,1)S(1)}, u32[]{:S(2)}, u32[]{:S(2)}) collective-permute-start(bf16[128,1536]{1,0:T(8,128)(2,1)S(1)} %gate_and_add.2), channel_id=1, source_target_pairs={{0,2},{2,0},{4,6},{6,4},{8,10},{10,8},{12,14},{14,12},{16,18},{18,... | collective-permute-start | bytes 1179656 | tf_op jit(solution)/shard_map/ppermute | solution.py:471

commit v7 on v6

--- a/solution.py
+++ b/solution.py
@@ -64,9 +64,19 @@
         c.wait()
 
 
-def cut_kernel(width, pos, stale, *outs):
-    for s, out in enumerate(outs):
-        out[...] = stale[:, :, :, pl.ds(pl.multiple_of((pos[0] ^ s) * width, HEAD), width)]
+def cut_kernel(width, pos, stale, *refs):
+    outs, held, sems = refs[:-2], refs[-2], refs[-1]
+    slabs = [(kv, c) for kv in range(held.shape[0]) for c in range(held.shape[1])]
+    copies = [
+        pltpu.make_async_copy(stale.at[kv, c], held.at[kv, c], sems.at[i])
+        for i, (kv, c) in enumerate(slabs)
+    ]
+    for copy in copies:
+        copy.start()
+    for (kv, c), copy in zip(slabs, copies):
+        copy.wait()
+        for s, out in enumerate(outs):
+            out[kv, c] = held[kv, c, :, pl.ds(pl.multiple_of((pos[0] ^ s) * width, HEAD), width)]
 
 
 def cut_stale(pos, stale, groups):
@@ -75,11 +85,12 @@
     return pl.pallas_call(
         functools.partial(cut_kernel, width),
         out_shape=[out_of((kv, clips, rows, width))] * groups,
-        in_specs=[SCALARS, RESIDENT],
+        in_specs=[SCALARS, ANYWHERE],
         out_specs=[RESIDENT] * groups,
+        scratch_shapes=[pltpu.VMEM(stale.shape, BF), pltpu.SemaphoreType.DMA((kv * clips,))],
         compiler_params=params(8),
         name="cut_stale",
-    )(pos, stale)
+    )(pos, pltpu.with_memory_space_constraint(stale, pltpu.HBM))
 
 
 def halves_kernel(block, keys, values):
@@ -482,8 +493,9 @@
     hidden_now = tie(hidden_states, *cut)
     hidden_for = lax.dynamic_index_in_dim(hidden_now, 1 - pos[2], 0, keepdims=False)
     hidden_got = across(hidden_for, 1)
+    in_place = pltpu.with_memory_space_constraint(hidden_states, pltpu.HBM)
     normed, queries, *slots = make_queries(
-        pos, hidden_states, hidden_got, modulation, qk_gain, weights, groups
+        pos, in_place, hidden_got, modulation, qk_gain, weights, groups
     )
     normed, queries, slots, near, one, far_near, cut_three = step(
         (normed, queries, slots, near, one, far_near, cut[3])

time: 104 us -> 104 us (level)
  Pallas kernels: 43 us -> 44.5 us
  local copies, waits for them, and re-layouts: 1.59 us -> 0.09 us
    unnamed x14, local copies, waits for them, and re-layouts: 1.53 us -> 0.03 us
    pallas_call x1, Pallas kernels: 0.68 us -> 1.96 us  [cut_stale(): pl.pallas_call(functools.partial(cut_kernel, width), out_shape=[out_of((k...]
where the time goes in v7:
time: 104 us
  Pallas kernels  44.5 us (43%)
  starting transfers between devices  36.1 us (35%)
  waiting for transfers between devices  22.2 us (21%)
  between operations  1.12 us (1%)
    ppermute x26, starting transfers between devices, across(): return lax.ppermute(value, 'patch', [(i, i ^ bit) for i in range(patches)])  33 us
    ppermute x26, waiting for transfers between devices, across(): return lax.ppermute(value, 'patch', [(i, i ^ bit) for i in range(patches)])  18.6 us
    pallas_call x2, Pallas kernels, make_fresh(): pl.pallas_call(functools.partial(fresh_kernel, slot), grid=(cols // block...  10.7 us
    pallas_call x2, Pallas kernels, attend_groups(): pl.pallas_call(functools.partial(group_kernel, part, blocks, places), in_...  9.71 us
    pallas_call x1, Pallas kernels, make_queries(): pl.pallas_call(functools.partial(query_kernel, groups, per_step), grid_sp...  7.59 us
    ppermute x1, waiting for transfers between devices, spread_heads(): my_got = lax.ppermute(my_send, 'tp', swap)  3.66 us
    pallas_call x2, Pallas kernels, project_out(): pl.pallas_call(functools.partial(out_kernel, part, groups), in_specs=[SCA...  3.58 us
    pallas_call x1, Pallas kernels, attend_own(): pl.pallas_call(own_kernel, grid=(cols // block,), in_specs=[wide, kv, kv]...  3.09 us
  transfers between devices with their start and end apart: 28, of which 8 were waited for; matrix products, arithmetic and copies ran while one was open for 0% of the time, Pallas kernels for 39%

profile of v7, /device:TPU:0, one launch (start us, length us, event | category | flops | bytes accessed | tf_op | source)
XLA Modules:
  0.0 104.1 jit_solution(9842691441305208136)
XLA Ops:
  0.6 0.0 copy-start
  0.7 0.1 pad_add_fusion.pos
  0.7 2.0 %cut_stale.1 = (bf16[2,2,128,384]{3,2,1,0:T(8,128)(2,1)S(1)}, bf16[2,2,128,384]{3,2,1,0:T(8,128)(2,1)S(1)}, bf16[2,2,128,384]{3,2,1,0:T(8,128)(2,1)S(1)}, bf16[2,2,128,384]{3,2,1,0:T(8,128)(2,1)S(1)}) custom-call(s32[3]{0:T(128)S(1)} %pad_add_fusion.pos, bf16[2,2,128,1536]{3,2,1,0:T(8,128)(2,1)} %stale.1), custom_call_target="tpu_custom_call" | custom-call | tf_op jit(solution)/shard_map/cut_stale/pallas_call | solution.py:85
  2.7 0.1 dynamic-slice_bitcast_fusion
  2.8 0.5 collective-permute-start
  3.3 2.6 %collective-permute-start.1 = (bf16[2,2,128,384]{3,2,1,0:T(8,128)(2,1)S(1)}, bf16[2,2,128,384]{3,2,1,0:T(8,128)(2,1)S(1)}, u32[]{:S(2)}, u32[]{:S(2)}) collective-permute-start(bf16[2,2,128,384]{3,2,1,0:T(8,128)(2,1)S(1)} %get-tuple-element.103), channel_id=1, source_target_pairs={{0,8},{2,10},{4,12},{6,14},{8,0},{10,2},{12,4},{14,6},{16,24},{18,... | collective-permute-start | bytes 1179656 | tf_op jit(solution)/shard_map/ppermute | solution.py:482
  6.0 1.5 %collective-permute-start.2 = (bf16[2,2,128,384]{3,2,1,0:T(8,128)(2,1)S(1)}, bf16[2,2,128,384]{3,2,1,0:T(8,128)(2,1)S(1)}, u32[]{:S(2)}, u32[]{:S(2)}) collective-permute-start(bf16[2,2,128,384]{3,2,1,0:T(8,128)(2,1)S(1)} %get-tuple-element.150.refs_0_.refs_4_), channel_id=1, source_target_pairs={{0,4},{2,6},{4,0},{6,2},{8,12},{10,14},{12,8},{14,10},{16,20},{18,... | collective-permute-start | bytes 1179656 | tf_op jit(solution)/shard_map/ppermute | solution.py:482
  7.5 2.6 %collective-permute-start.4 = (bf16[2,2,128,384]{3,2,1,0:T(8,128)(2,1)S(1)}, bf16[2,2,128,384]{3,2,1,0:T(8,128)(2,1)S(1)}, u32[]{:S(2)}, u32[]{:S(2)}) collective-permute-start(bf16[2,2,128,384]{3,2,1,0:T(8,128)(2,1)S(1)} %get-tuple-element.104), channel_id=1, source_target_pairs={{0,16},{2,18},{4,20},{6,22},{8,24},{10,26},{12,28},{14,30},{16,0},... | collective-permute-start | bytes 1179656 | tf_op jit(solution)/shard_map/ppermute | solution.py:482
  10.0 0.0 collective-permute-done.got.hidden
  10.1 7.6 %norm_and_queries.1 = (bf16[256,3072]{1,0:T(8,128)(2,1)S(1)}, bf16[256,1536]{1,0:T(8,128)(2,1)S(1)}, bf16[256,384]{1,0:T(8,128)(2,1)S(1)}, bf16[256,384]{1,0:T(8...) custom-call(s32[3]{0:T(128)S(1)} %pad_add_fusion.pos, ...), custom_call_target="tpu_custom_call" | custom-call | flops 1000 | bytes 1000 | tf_op jit(solution)/shard_map/norm_and_queries/pallas_call | solution.py:177
  17.7 5.1 %collective-permute-done.1.block.refs_2_.refs_8_ = bf16[2,2,128,384]{3,2,1,0:T(8,128)(2,1)S(1)} collective-permute-done((bf16[2,2,128,384]{3,2,1,0:T(8,128)(2,1)S(1)}, bf16[2,2,128,384]{3,2,1,0:T(8,128)(2,1)S(1)}, u32[]{:S(2)}, u32[]{:S(2)}) %collective-permute-start.1) | collective-permute-done | bytes 393248 | tf_op jit(solution)/shard_map/ppermute | solution.py:482
  22.8 0.0 collective-permute-done.2.refs_1_.refs_6_
  22.8 2.7 %collective-permute-start.5 = (bf16[2,128,384]{2,1,0:T(8,128)(2,1)S(1)}, bf16[2,128,384]{2,1,0:T(8,128)(2,1)S(1)}, u32[]{:S(2)}, u32[]{:S(2)}) collective-permute-start(bf16[2,128,384]{2,1,0:T(8,128)(2,1)S(1)} %get-tuple-element.117), channel_id=1, source_target_pairs={{0,4},{2,6},{4,0},{6,2},{8,12},{10,14},{12,8},{14,10},{16,20},{18,... | collective-permute-start | bytes 589832 | tf_op jit(solution)/shard_map/ppermute | solution.py:482
  25.5 0.1 collective-permute-start.6
  25.6 2.5 %collective-permute-start.3 = (bf16[2,2,128,384]{3,2,1,0:T(8,128)(2,1)S(1)}, bf16[2,2,128,384]{3,2,1,0:T(8,128)(2,1)S(1)}, u32[]{:S(2)}, u32[]{:S(2)}) collective-permute-start(bf16[2,2,128,384]{3,2,1,0:T(8,128)(2,1)S(1)} %get-tuple-element.115), channel_id=1, source_target_pairs={{0,24},{2,26},{4,28},{6,30},{8,16},{10,18},{12,20},{14,22},{16,8},... | collective-permute-start | bytes 1179656 | tf_op jit(solution)/shard_map/ppermute | solution.py:482
  28.1 5.5 %fresh_keys.1 = (bf16[2,128,1536]{2,1,0:T(8,128)(2,1)S(1)}, bf16[2,128,1536]{2,1,0:T(8,128)(2,1)S(1)}) custom-call(bf16[256,3072]{1,0:T(8,128)(2,1)S(1)} %get-tuple-element.135.normed, f32[2,128]{1,0:T(2,128)S(1)} %copy-done.3, bf16[3,3072,1536]{2,1,0:T(8,128)(2,1)} %bitcast.9), custom_call_target="tpu_custom_call" | custom-call | flops 1000 | bytes 1000 | tf_op jit(solution)/shard_map/fresh_keys/pallas_call | solution.py:219
  33.6 0.0 collective-permute-done.4.block.refs_0_.refs_13_
  33.6 0.9 collective-permute-done.6.refs_4_.refs_11_
  34.5 0.1 collective-permute-start.9
  34.6 1.8 %collective-permute-start.7 = (bf16[2,128,384]{2,1,0:T(8,128)(2,1)S(1)}, bf16[2,128,384]{2,1,0:T(8,128)(2,1)S(1)}, u32[]{:S(2)}, u32[]{:S(2)}) collective-permute-start(bf16[2,128,384]{2,1,0:T(8,128)(2,1)S(1)} %get-tuple-element.130), channel_id=1, source_target_pairs={{0,4},{2,6},{4,0},{6,2},{8,12},{10,14},{12,8},{14,10},{16,20},{18,... | collective-permute-start | bytes 589832 | tf_op jit(solution)/shard_map/ppermute | solution.py:482
  36.4 0.3 collective-permute-start.8
  36.7 0.6 pack.2
  37.3 0.1 collective-permute-start.13
  37.4 5.2 %fresh_values.1 = (bf16[2,128,1536]{2,1,0:T(8,128)(2,1)S(1)}, bf16[2,128,1536]{2,1,0:T(8,128)(2,1)S(1)}) custom-call(bf16[256,3072]{1,0:T(8,128)(2,1)S(1)} %get-tuple-element.135.normed, f32[2,128]{1,0:T(2,128)S(1)} %copy-done.3, bf16[3,3072,1536]{2,1,0:T(8,128)(2,1)} %bitcast.10, ...), custom_call_target="tpu_custom_call", output_to_operand_aliasing={{0}: (3, {}), {1}: (4, {})} | custom-call | flops 1000 | bytes 1000 | tf_op jit(solution)/shard_map/fresh_values/pallas_call | solution.py:219
  42.6 0.0 collective-permute-done.9.refs_1_
  42.6 0.0 collective-permute-done.7.refs_1_.refs_15_
  42.6 2.1 %collective-permute-done.8.refs_2_.refs_16_ = bf16[2,128,384]{2,1,0:T(8,128)(2,1)S(1)} collective-permute-done((bf16[2,128,384]{2,1,0:T(8,128)(2,1)S(1)}, bf16[2,128,384]{2,1,0:T(8,128)(2,1)S(1)}, u32[]{:S(2)}, u32[]{:S(2)}) %collective-permute-start.8) | collective-permute-done | bytes 196640 | tf_op jit(solution)/shard_map/ppermute | solution.py:482
  44.7 0.6 pack.3
  45.3 0.1 collective-permute-start.14
  45.4 1.5 %collective-permute-start.10 = (bf16[2,2,128,384]{3,2,1,0:T(8,128)(2,1)S(1)}, bf16[2,2,128,384]{3,2,1,0:T(8,128)(2,1)S(1)}, u32[]{:S(2)}, u32[]{:S(2)}) collective-permute-start(bf16[2,2,128,384]{3,2,1,0:T(8,128)(2,1)S(1)} %collective-permute-done.3.refs_3_.refs_18_), channel_id=1, source_target_pairs={{0,4},{2,6},{4,0},{6,2},{8,12},{10,14},{12,8},{14,10},{16,20},{18,... | collective-permute-start | bytes 1179656 | tf_op jit(solution)/shard_map/ppermute | solution.py:482
  46.9 2.7 %collective-permute-start.11 = (bf16[128,384]{1,0:T(8,128)(2,1)S(1)}, bf16[128,384]{1,0:T(8,128)(2,1)S(1)}, u32[]{:S(2)}, u32[]{:S(2)}) collective-permute-start(bf16[128,384]{1,0:T(8,128)(2,1)S(1)} %get-tuple-element.146), channel_id=1, source_target_pairs={{0,16},{2,18},{4,20},{6,22},{8,24},{10,26},{12,28},{14,30},{16,0},... | collective-permute-start | bytes 294920 | tf_op jit(solution)/shard_map/ppermute | solution.py:482
  49.6 1.4 %collective-permute-start.12 = (bf16[128,384]{1,0:T(8,128)(2,1)S(1)}, bf16[128,384]{1,0:T(8,128)(2,1)S(1)}, u32[]{:S(2)}, u32[]{:S(2)}) collective-permute-start(bf16[128,384]{1,0:T(8,128)(2,1)S(1)} %get-tuple-element.147), channel_id=1, source_target_pairs={{0,24},{2,26},{4,28},{6,30},{8,16},{10,18},{12,20},{14,22},{16,8},... | collective-permute-start | bytes 294920 | tf_op jit(solution)/shard_map/ppermute | solution.py:482
  50.9 3.1 %attend_own.1 = (f32[256,1536]{1,0:T(8,128)S(1)}, f32[256,1536]{1,0:T(8,128)S(1)}, f32[256,1536]{1,0:T(8,128)S(1)}) custom-call(bf16[256,1536]{1,0:T(8,128)(2,1)S(1)} %get-tuple-element.156.q, bf16[2,128,1536]{2,1,0:T(8,128)(2,1)S(1)} %get-tuple-element.200.mine, bf16[2,128,1536]{2,1,0:T(8,128)(2,1)S(1)} %get-tuple-element.201.other), custom_call_target="tpu_custom_call" | custom-call | flops 1000 | bytes 1000 | tf_op jit(solution)/shard_map/attend_own/pallas_call | solution.py:279
  54.0 3.6 %collective-permute-done.11.refs_2_ = bf16[128,384]{1,0:T(8,128)(2,1)S(1)} collective-permute-done((bf16[128,384]{1,0:T(8,128)(2,1)S(1)}, bf16[128,384]{1,0:T(8,128)(2,1)S(1)}, u32[]{:S(2)}, u32[]{:S(2)}) %collective-permute-start.11) | collective-permute-done | bytes 98336 | tf_op jit(solution)/shard_map/ppermute | solution.py:482
  57.7 0.0 collective-permute-done.12.refs_3_
  57.7 0.0 collective-permute-done.10.refs_20_
  57.7 0.0 collective-permute-done.13.refs_5_.refs_7_.refs_9_.refs_12_
  57.7 0.1 collective-permute-start.15
  57.8 3.0 %collective-permute-start.16 = (bf16[128,384]{1,0:T(8,128)(2,1)S(1)}, bf16[128,384]{1,0:T(8,128)(2,1)S(1)}, u32[]{:S(2)}, u32[]{:S(2)}) collective-permute-start(bf16[128,384]{1,0:T(8,128)(2,1)S(1)} %get-tuple-element.175), channel_id=1, source_target_pairs={{0,16},{2,18},{4,20},{6,22},{8,24},{10,26},{12,28},{14,30},{16,0},... | collective-permute-start | bytes 294920 | tf_op jit(solution)/shard_map/ppermute | solution.py:482
  60.7 1.4 %collective-permute-start.17 = (bf16[128,384]{1,0:T(8,128)(2,1)S(1)}, bf16[128,384]{1,0:T(8,128)(2,1)S(1)}, u32[]{:S(2)}, u32[]{:S(2)}) collective-permute-start(bf16[128,384]{1,0:T(8,128)(2,1)S(1)} %get-tuple-element.176), channel_id=1, source_target_pairs={{0,24},{2,26},{4,28},{6,30},{8,16},{10,18},{12,20},{14,22},{16,8},... | collective-permute-start | bytes 294920 | tf_op jit(solution)/shard_map/ppermute | solution.py:482
  62.1 4.8 %attend_groups.2 = (bf16[400,128]{1,0:T(8,128)(2,1)S(1)}, bf16[400,128]{1,0:T(8,128)(2,1)S(1)}, bf16[400,128]{1,0:T(8,128)(2,1)S(1)}, bf16[400,128]{1,0:T(8,128)(2,1)S(1)}) custom-call(s32[3]{0:T(128)S(1)} %pad_add_fusion.pos, bf16[256,384]{1,0:T(8,128)(2,1)S(1)} %get-tuple-element.182.refs_0_, bf16[256,384]{1,0:T(8,128)(2,1)S(1)} %collective-permute-done.9.refs_1_, ...), custom_call_target="tpu_custom_call" | custom-call | flops 1000 | bytes 1000 | tf_op jit(solution)/shard_map/attend_groups/pallas_call | solution.py:356
  67.0 1.6 %collective-permute-done.16.refs_2_ = bf16[128,384]{1,0:T(8,128)(2,1)S(1)} collective-permute-done((bf16[128,384]{1,0:T(8,128)(2,1)S(1)}, bf16[128,384]{1,0:T(8,128)(2,1)S(1)}, u32[]{:S(2)}, u32[]{:S(2)}) %collective-permute-start.16) | collective-permute-done | bytes 98336 | tf_op jit(solution)/shard_map/ppermute | solution.py:482
  68.6 0.0 collective-permute-done.17.refs_3_
  68.6 2.4 %collective-permute-start.18 = (bf16[400,128]{1,0:T(8,128)(2,1)S(1)}, bf16[400,128]{1,0:T(8,128)(2,1)S(1)}, u32[]{:S(2)}, u32[]{:S(2)}) collective-permute-start(bf16[400,128]{1,0:T(8,128)(2,1)S(1)} %get-tuple-element.179), channel_id=1, source_target_pairs={{0,24},{2,26},{4,28},{6,30},{8,16},{10,18},{12,20},{14,22},{16,8},... | collective-permute-start | bytes 307208 | tf_op jit(solution)/shard_map/ppermute | solution.py:482
  71.0 1.4 %collective-permute-start.19 = (bf16[400,128]{1,0:T(8,128)(2,1)S(1)}, bf16[400,128]{1,0:T(8,128)(2,1)S(1)}, u32[]{:S(2)}, u32[]{:S(2)}) collective-permute-start(bf16[400,128]{1,0:T(8,128)(2,1)S(1)} %get-tuple-element.180), channel_id=1, source_target_pairs={{0,16},{2,18},{4,20},{6,22},{8,24},{10,26},{12,28},{14,30},{16,0},... | collective-permute-start | bytes 307208 | tf_op jit(solution)/shard_map/ppermute | solution.py:482
  72.5 0.5 collective-permute-start.20
  73.0 4.9 %attend_groups.3 = (bf16[400,128]{1,0:T(8,128)(2,1)S(1)}, bf16[400,128]{1,0:T(8,128)(2,1)S(1)}, bf16[400,128]{1,0:T(8,128)(2,1)S(1)}, bf16[400,128]{1,0:T(8,128)(2,1)S(1)}) custom-call(s32[3]{0:T(128)S(1)} %pad_add_fusion.pos, bf16[256,384]{1,0:T(8,128)(2,1)S(1)} %get-tuple-element.182.refs_0_, bf16[256,384]{1,0:T(8,128)(2,1)S(1)} %collective-permute-done.9.refs_1_, ...), custom_call_target="tpu_custom_call" | custom-call | flops 1000 | bytes 1000 | tf_op jit(solution)/shard_map/attend_groups/pallas_call | solution.py:356
  77.9 1.5 %collective-permute-start.21 = (bf16[400,128]{1,0:T(8,128)(2,1)S(1)}, bf16[400,128]{1,0:T(8,128)(2,1)S(1)}, u32[]{:S(2)}, u32[]{:S(2)}) collective-permute-start(bf16[400,128]{1,0:T(8,128)(2,1)S(1)} %get-tuple-element.187), channel_id=1, source_target_pairs={{0,8},{2,10},{4,12},{6,14},{8,0},{10,2},{12,4},{14,6},{16,24},{18,... | collective-permute-start | bytes 307208 | tf_op jit(solution)/shard_map/ppermute | solution.py:482
  79.4 2.2 %collective-permute-start.22 = (bf16[400,128]{1,0:T(8,128)(2,1)S(1)}, bf16[400,128]{1,0:T(8,128)(2,1)S(1)}, u32[]{:S(2)}, u32[]{:S(2)}) collective-permute-start(bf16[400,128]{1,0:T(8,128)(2,1)S(1)} %get-tuple-element.188), channel_id=1, source_target_pairs={{0,24},{2,26},{4,28},{6,30},{8,16},{10,18},{12,20},{14,22},{16,8},... | collective-permute-start | bytes 307208 | tf_op jit(solution)/shard_map/ppermute | solution.py:482
  81.7 0.0 collective-permute-done.19.refs_2_
  81.7 1.8 %merge_and_project.2 = (bf16[128,1536]{1,0:T(8,128)(2,1)S(1)}, bf16[128,1536]{1,0:T(8,128)(2,1)S(1)}) custom-call(s32[3]{0:T(128)S(1)} %pad_add_fusion.pos, bf16[400,128]{1,0:T(8,128)(2,1)S(1)} %get-tuple-element.190.refs_0_, bf16[400,128]{1,0:T(8,128)(2,1)S(1)} %collective-permute-done.18.refs_1_, bf16[400,128]{1,0:T(8,128)(2,1)S(1)} %collective-permute-done.19.refs_2_, ...), custom_call_target="tpu_custom_call" | custom-call | flops 10000000000 | bytes 100000000 | tf_op jit(solution)/shard_map/merge_and_project/pallas_call | solution.py:398
  83.5 1.6 %collective-permute-start.25 = (bf16[128,1536]{1,0:T(8,128)(2,1)S(1)}, bf16[128,1536]{1,0:T(8,128)(2,1)S(1)}, u32[]{:S(2)}, u32[]{:S(2)}) collective-permute-start(bf16[128,1536]{1,0:T(8,128)(2,1)S(1)} %get-tuple-element.194), channel_id=1, source_target_pairs={{0,1},{1,0},{2,3},{3,2},{4,5},{5,4},{6,7},{7,6},{8,9},{9,8},{10,11... | collective-permute-start | bytes 1179656 | tf_op jit(solution)/shard_map/ppermute | solution.py:545
  85.1 1.8 %collective-permute-done.22.refs_2_ = bf16[400,128]{1,0:T(8,128)(2,1)S(1)} collective-permute-done((bf16[400,128]{1,0:T(8,128)(2,1)S(1)}, bf16[400,128]{1,0:T(8,128)(2,1)S(1)}, u32[]{:S(2)}, u32[]{:S(2)}) %collective-permute-start.22) | collective-permute-done | bytes 102432 | tf_op jit(solution)/shard_map/ppermute | solution.py:482
  86.9 3.3 %collective-permute-done.23.refs_3_ = bf16[400,128]{1,0:T(8,128)(2,1)S(1)} collective-permute-done((bf16[400,128]{1,0:T(8,128)(2,1)S(1)}, bf16[400,128]{1,0:T(8,128)(2,1)S(1)}, u32[]{:S(2)}, u32[]{:S(2)}) %collective-permute-start.23) | collective-permute-done | bytes 102432 | tf_op jit(solution)/shard_map/ppermute | solution.py:482
  90.2 1.8 %merge_and_project.3 = (bf16[128,1536]{1,0:T(8,128)(2,1)S(1)}, bf16[128,1536]{1,0:T(8,128)(2,1)S(1)}) custom-call(s32[3]{0:T(128)S(1)} %pad_add_fusion.pos, bf16[400,128]{1,0:T(8,128)(2,1)S(1)} %get-tuple-element.195.refs_0_, bf16[400,128]{1,0:T(8,128)(2,1)S(1)} %collective-permute-done.21.refs_1_, bf16[400,128]{1,0:T(8,128)(2,1)S(1)} %collective-permute-done.22.refs_2_, ...), custom_call_target="tpu_custom_call" | custom-call | flops 10000000000 | bytes 100000000 | tf_op jit(solution)/shard_map/merge_and_project/pallas_call | solution.py:398
  92.0 1.6 %collective-permute-start.24 = (bf16[128,1536]{1,0:T(8,128)(2,1)S(1)}, bf16[128,1536]{1,0:T(8,128)(2,1)S(1)}, u32[]{:S(2)}, u32[]{:S(2)}) collective-permute-start(bf16[128,1536]{1,0:T(8,128)(2,1)S(1)} %get-tuple-element.197), channel_id=1, source_target_pairs={{0,1},{1,0},{2,3},{3,2},{4,5},{5,4},{6,7},{7,6},{8,9},{9,8},{10,11... | collective-permute-start | bytes 1179656 | tf_op jit(solution)/shard_map/ppermute | solution.py:549
  93.6 1.4 %project_kept.3.keep = f32[128,1536]{1,0:T(8,128)S(1)} custom-call(s32[3]{0:T(128)S(1)} %pad_add_fusion.pos, bf16[128,1536]{1,0:T(8,128)(2,1)S(1)} %get-tuple-element.199.attended, bf16[1536,3072]{1,0:T(8,128)(2,1)S(1)} %bitcast.7), custom_call_target="tpu_custom_call" | custom-call | flops 1000 | bytes 1000 | tf_op jit(solution)/shard_map/project_kept/pallas_call | solution.py:414
  95.0 0.7 gate_and_add.2
  95.7 0.1 collective-permute-start.26
  95.7 1.4 %project_kept.2.keep = f32[128,1536]{1,0:T(8,128)S(1)} custom-call(s32[3]{0:T(128)S(1)} %pad_add_fusion.pos, bf16[128,1536]{1,0:T(8,128)(2,1)S(1)} %get-tuple-element.196.attended, bf16[1536,3072]{1,0:T(8,128)(2,1)S(1)} %bitcast.7), custom_call_target="tpu_custom_call" | custom-call | flops 1000 | bytes 1000 | tf_op jit(solution)/shard_map/project_kept/pallas_call | solution.py:414
  97.1 0.0 copy-start.1
  97.1 1.7 %place_fresh.1 = bf16[2,2,128,1536]{3,2,1,0:T(8,128)(2,1)} custom-call(s32[3]{0:T(128)S(1)} %pad_add_fusion.pos, bf16[2,128,1536]{2,1,0:T(8,128)(2,1)S(1)} %get-tuple-element.200.mine, bf16[2,128,1536]{2,1,0:T(8,128)(2,1)S(1)} %collective-permute-done.27.got), custom_call_target="tpu_custom_call" | custom-call | tf_op jit(solution)/shard_map/place_fresh/pallas_call | solution.py:244
  98.9 3.7 %collective-permute-done.24.got = bf16[128,1536]{1,0:T(8,128)(2,1)S(1)} collective-permute-done((bf16[128,1536]{1,0:T(8,128)(2,1)S(1)}, bf16[128,1536]{1,0:T(8,128)(2,1)S(1)}, u32[]{:S(2)}, u32[]{:S(2)}) %collective-permute-start.24) | collective-permute-done | bytes 393248 | tf_op jit(solution)/shard_map/ppermute | solution.py:549
  102.5 1.4 %gate_and_add.3 = bf16[2,128,1536]{2,1,0:T(8,128)(2,1)} custom-call(s32[3]{0:T(128)S(1)} %pad_add_fusion.pos, bf16[2,128,3072]{2,1,0:T(8,128)(2,1)S(1)} %copy-done.1, f32[3,2,3072]{2,1,0:T(2,128)S(1)} %copy-done.2, f32[128,1536]{1,0:T(8,128)S(1)} %project_kept.2.keep, bf16[128,1536]{1,0:T(8,128)(2,1)S(1)} %collective-permute-done.24.got, ...), custom_call_target="tpu_custom_call" | custom-call | flops 1000 | bytes 1000 | tf_op jit(solution)/shard_map/gate_and_add/pallas_call | solution.py:459
  (27 shorter events, 0.1 us)
Async XLA Ops:
  0.6 2.1 %copy-start = (bf16[2,128,3072]{2,1,0:T(8,128)(2,1)S(1)}, bf16[2,128,3072]{2,1,0:T(8,128)(2,1)}, u32[]{:S(2)}) copy-start(bf16[2,128,3072]{2,1,0:T(8,128)(2,1)} %hidden.3) | copy-start | bytes 4718596
  0.7 9.3 %copy-start.2 = (f32[3,2,3072]{2,1,0:T(2,128)S(1)}, f32[3,2,3072]{2,1,0:T(2,128)}, u32[]{:S(2)}) copy-start(f32[3,2,3072]{2,1,0:T(2,128)} %mod.5) | copy-start | bytes 221188
  0.7 9.3 %copy-start.3 = (f32[2,128]{1,0:T(2,128)S(1)}, f32[2,128]{1,0:T(2,128)}, u32[]{:S(2)}) copy-start(f32[2,128]{1,0:T(2,128)} %gain.5) | copy-start | bytes 3076
  2.8 7.3 %collective-permute-start = (bf16[128,3072]{1,0:T(8,128)(2,1)S(1)}, bf16[128,3072]{1,0:T(8,128)(2,1)S(1)}, u32[]{:S(2)}, u32[]{:S(2)}) collective-permute-start(bf16[128,3072]{1,0:T(8,128)(2,1)S(1)} %dynamic-slice_bitcast_fusion), channel_id=1, source_target_pairs={{0,2},{2,0},{4,6},{6,4},{8,10},{10,8},{12,14},{14,12},{16,18},{18,... | collective-permute-start | bytes 2359304 | tf_op jit(solution)/shard_map/ppermute | solution.py:482
  3.3 19.5 %collective-permute-start.1 = (bf16[2,2,128,384]{3,2,1,0:T(8,128)(2,1)S(1)}, bf16[2,2,128,384]{3,2,1,0:T(8,128)(2,1)S(1)}, u32[]{:S(2)}, u32[]{:S(2)}) collective-permute-start(bf16[2,2,128,384]{3,2,1,0:T(8,128)(2,1)S(1)} %get-tuple-element.103), channel_id=1, source_target_pairs={{0,8},{2,10},{4,12},{6,14},{8,0},{10,2},{12,4},{14,6},{16,24},{18,... | collective-permute-start | bytes 1179656 | tf_op jit(solution)/shard_map/ppermute | solution.py:482
  6.0 16.8 %collective-permute-start.2 = (bf16[2,2,128,384]{3,2,1,0:T(8,128)(2,1)S(1)}, bf16[2,2,128,384]{3,2,1,0:T(8,128)(2,1)S(1)}, u32[]{:S(2)}, u32[]{:S(2)}) collective-permute-start(bf16[2,2,128,384]{3,2,1,0:T(8,128)(2,1)S(1)} %get-tuple-element.150.refs_0_.refs_4_), channel_id=1, source_target_pairs={{0,4},{2,6},{4,0},{6,2},{8,12},{10,14},{12,8},{14,10},{16,20},{18,... | collective-permute-start | bytes 1179656 | tf_op jit(solution)/shard_map/ppermute | solution.py:482
  7.5 26.1 %collective-permute-start.4 = (bf16[2,2,128,384]{3,2,1,0:T(8,128)(2,1)S(1)}, bf16[2,2,128,384]{3,2,1,0:T(8,128)(2,1)S(1)}, u32[]{:S(2)}, u32[]{:S(2)}) collective-permute-start(bf16[2,2,128,384]{3,2,1,0:T(8,128)(2,1)S(1)} %get-tuple-element.104), channel_id=1, source_target_pairs={{0,16},{2,18},{4,20},{6,22},{8,24},{10,26},{12,28},{14,30},{16,0},... | collective-permute-start | bytes 1179656 | tf_op jit(solution)/shard_map/ppermute | solution.py:482
  22.8 10.8 %collective-permute-start.5 = (bf16[2,128,384]{2,1,0:T(8,128)(2,1)S(1)}, bf16[2,128,384]{2,1,0:T(8,128)(2,1)S(1)}, u32[]{:S(2)}, u32[]{:S(2)}) collective-permute-start(bf16[2,128,384]{2,1,0:T(8,128)(2,1)S(1)} %get-tuple-element.117), channel_id=1, source_target_pairs={{0,4},{2,6},{4,0},{6,2},{8,12},{10,14},{12,8},{14,10},{16,20},{18,... | collective-permute-start | bytes 589832 | tf_op jit(solution)/shard_map/ppermute | solution.py:482
  25.5 8.9 %collective-permute-start.6 = (bf16[2,128,384]{2,1,0:T(8,128)(2,1)S(1)}, bf16[2,128,384]{2,1,0:T(8,128)(2,1)S(1)}, u32[]{:S(2)}, u32[]{:S(2)}) collective-permute-start(bf16[2,128,384]{2,1,0:T(8,128)(2,1)S(1)} %get-tuple-element.118), channel_id=1, source_target_pairs={{0,4},{2,6},{4,0},{6,2},{8,12},{10,14},{12,8},{14,10},{16,20},{18,... | collective-permute-start | bytes 589832 | tf_op jit(solution)/shard_map/ppermute | solution.py:482
  25.6 17.0 %collective-permute-start.3 = (bf16[2,2,128,384]{3,2,1,0:T(8,128)(2,1)S(1)}, bf16[2,2,128,384]{3,2,1,0:T(8,128)(2,1)S(1)}, u32[]{:S(2)}, u32[]{:S(2)}) collective-permute-start(bf16[2,2,128,384]{3,2,1,0:T(8,128)(2,1)S(1)} %get-tuple-element.115), channel_id=1, source_target_pairs={{0,24},{2,26},{4,28},{6,30},{8,16},{10,18},{12,20},{14,22},{16,8},... | collective-permute-start | bytes 1179656 | tf_op jit(solution)/shard_map/ppermute | solution.py:482
  34.5 8.1 %collective-permute-start.9 = (bf16[256,384]{1,0:T(8,128)(2,1)S(1)}, bf16[256,384]{1,0:T(8,128)(2,1)S(1)}, u32[]{:S(2)}, u32[]{:S(2)}) collective-permute-start(bf16[256,384]{1,0:T(8,128)(2,1)S(1)} %get-tuple-element.134), channel_id=1, source_target_pairs={{0,8},{2,10},{4,12},{6,14},{8,0},{10,2},{12,4},{14,6},{16,24},{18,... | collective-permute-start | bytes 589832 | tf_op jit(solution)/shard_map/ppermute | solution.py:482
  34.6 8.0 %collective-permute-start.7 = (bf16[2,128,384]{2,1,0:T(8,128)(2,1)S(1)}, bf16[2,128,384]{2,1,0:T(8,128)(2,1)S(1)}, u32[]{:S(2)}, u32[]{:S(2)}) collective-permute-start(bf16[2,128,384]{2,1,0:T(8,128)(2,1)S(1)} %get-tuple-element.130), channel_id=1, source_target_pairs={{0,4},{2,6},{4,0},{6,2},{8,12},{10,14},{12,8},{14,10},{16,20},{18,... | collective-permute-start | bytes 589832 | tf_op jit(solution)/shard_map/ppermute | solution.py:482
  36.4 8.4 %collective-permute-start.8 = (bf16[2,128,384]{2,1,0:T(8,128)(2,1)S(1)}, bf16[2,128,384]{2,1,0:T(8,128)(2,1)S(1)}, u32[]{:S(2)}, u32[]{:S(2)}) collective-permute-start(bf16[2,128,384]{2,1,0:T(8,128)(2,1)S(1)} %get-tuple-element.131), channel_id=1, source_target_pairs={{0,4},{2,6},{4,0},{6,2},{8,12},{10,14},{12,8},{14,10},{16,20},{18,... | collective-permute-start | bytes 589832 | tf_op jit(solution)/shard_map/ppermute | solution.py:482
  37.3 20.4 %collective-permute-start.13 = (bf16[4,2,128,384]{3,2,1,0:T(8,128)(2,1)S(1)}, bf16[4,2,128,384]{3,2,1,0:T(8,128)(2,1)S(1)}, u32[]{:S(2)}, u32[]{:S(2)}) collective-permute-start(bf16[4,2,128,384]{3,2,1,0:T(8,128)(2,1)S(1)} %pack.2), channel_id=1, source_target_pairs={{0,2},{2,0},{4,6},{6,4},{8,10},{10,8},{12,14},{14,12},{16,18},{18,... | collective-permute-start | bytes 2359304 | tf_op jit(solution)/shard_map/ppermute | solution.py:482
  45.3 12.3 %collective-permute-start.14 = (bf16[3,2,128,384]{3,2,1,0:T(8,128)(2,1)S(1)}, bf16[3,2,128,384]{3,2,1,0:T(8,128)(2,1)S(1)}, u32[]{:S(2)}, u32[]{:S(2)}) collective-permute-start(bf16[3,2,128,384]{3,2,1,0:T(8,128)(2,1)S(1)} %pack.3), channel_id=1, source_target_pairs={{0,2},{2,0},{4,6},{6,4},{8,10},{10,8},{12,14},{14,12},{16,18},{18,... | collective-permute-start | bytes 1769480 | tf_op jit(solution)/shard_map/ppermute | solution.py:482
  45.4 12.2 %collective-permute-start.10 = (bf16[2,2,128,384]{3,2,1,0:T(8,128)(2,1)S(1)}, bf16[2,2,128,384]{3,2,1,0:T(8,128)(2,1)S(1)}, u32[]{:S(2)}, u32[]{:S(2)}) collective-permute-start(bf16[2,2,128,384]{3,2,1,0:T(8,128)(2,1)S(1)} %collective-permute-done.3.refs_3_.refs_18_), channel_id=1, source_target_pairs={{0,4},{2,6},{4,0},{6,2},{8,12},{10,14},{12,8},{14,10},{16,20},{18,... | collective-permute-start | bytes 1179656 | tf_op jit(solution)/shard_map/ppermute | solution.py:482
  46.9 10.7 %collective-permute-start.11 = (bf16[128,384]{1,0:T(8,128)(2,1)S(1)}, bf16[128,384]{1,0:T(8,128)(2,1)S(1)}, u32[]{:S(2)}, u32[]{:S(2)}) collective-permute-start(bf16[128,384]{1,0:T(8,128)(2,1)S(1)} %get-tuple-element.146), channel_id=1, source_target_pairs={{0,16},{2,18},{4,20},{6,22},{8,24},{10,26},{12,28},{14,30},{16,0},... | collective-permute-start | bytes 294920 | tf_op jit(solution)/shard_map/ppermute | solution.py:482
  49.6 8.1 %collective-permute-start.12 = (bf16[128,384]{1,0:T(8,128)(2,1)S(1)}, bf16[128,384]{1,0:T(8,128)(2,1)S(1)}, u32[]{:S(2)}, u32[]{:S(2)}) collective-permute-start(bf16[128,384]{1,0:T(8,128)(2,1)S(1)} %get-tuple-element.147), channel_id=1, source_target_pairs={{0,24},{2,26},{4,28},{6,30},{8,16},{10,18},{12,20},{14,22},{16,8},... | collective-permute-start | bytes 294920 | tf_op jit(solution)/shard_map/ppermute | solution.py:482
  57.7 4.4 %collective-permute-start.15 = (bf16[2,2,128,384]{3,2,1,0:T(8,128)(2,1)S(1)}, bf16[2,2,128,384]{3,2,1,0:T(8,128)(2,1)S(1)}, u32[]{:S(2)}, u32[]{:S(2)}) collective-permute-start(bf16[2,2,128,384]{3,2,1,0:T(8,128)(2,1)S(1)} %collective-permute-done.10.refs_20_), channel_id=1, source_target_pairs={{0,2},{2,0},{4,6},{6,4},{8,10},{10,8},{12,14},{14,12},{16,18},{18,... | collective-permute-start | bytes 1179656 | tf_op jit(solution)/shard_map/ppermute | solution.py:482
  57.8 10.8 %collective-permute-start.16 = (bf16[128,384]{1,0:T(8,128)(2,1)S(1)}, bf16[128,384]{1,0:T(8,128)(2,1)S(1)}, u32[]{:S(2)}, u32[]{:S(2)}) collective-permute-start(bf16[128,384]{1,0:T(8,128)(2,1)S(1)} %get-tuple-element.175), channel_id=1, source_target_pairs={{0,16},{2,18},{4,20},{6,22},{8,24},{10,26},{12,28},{14,30},{16,0},... | collective-permute-start | bytes 294920 | tf_op jit(solution)/shard_map/ppermute | solution.py:482
  60.7 7.9 %collective-permute-start.17 = (bf16[128,384]{1,0:T(8,128)(2,1)S(1)}, bf16[128,384]{1,0:T(8,128)(2,1)S(1)}, u32[]{:S(2)}, u32[]{:S(2)}) collective-permute-start(bf16[128,384]{1,0:T(8,128)(2,1)S(1)} %get-tuple-element.176), channel_id=1, source_target_pairs={{0,24},{2,26},{4,28},{6,30},{8,16},{10,18},{12,20},{14,22},{16,8},... | collective-permute-start | bytes 294920 | tf_op jit(solution)/shard_map/ppermute | solution.py:482
  62.1 19.6 %slice-start = ((s8[9437184]{0:T(1024)(128)(4,1)}), s8[4194304]{0:T(1024)(128)(4,1)S(1)}, s32[]{:S(2)}) async-start(s8[9437184]{0:T(1024)(128)(4,1)} %bitcast.6), calls=%async_computation | async-start | bytes 8388608
  62.1 19.6 %slice-start.1 = ((s8[9437184]{0:T(1024)(128)(4,1)}), s8[4194304]{0:T(1024)(128)(4,1)S(1)}, s32[]{:S(2)}) async-start(s8[9437184]{0:T(1024)(128)(4,1)} %bitcast.6), calls=%async_computation.1 | async-start | bytes 8388608
  68.6 13.1 %slice-start.2 = ((s8[9437184]{0:T(1024)(128)(4,1)}), s8[1048576]{0:T(1024)(128)(4,1)S(1)}, s32[]{:S(2)}) async-start(s8[9437184]{0:T(1024)(128)(4,1)} %bitcast.6), calls=%async_computation.2 | async-start | bytes 2097152
  68.6 13.0 %collective-permute-start.18 = (bf16[400,128]{1,0:T(8,128)(2,1)S(1)}, bf16[400,128]{1,0:T(8,128)(2,1)S(1)}, u32[]{:S(2)}, u32[]{:S(2)}) collective-permute-start(bf16[400,128]{1,0:T(8,128)(2,1)S(1)} %get-tuple-element.179), channel_id=1, source_target_pairs={{0,24},{2,26},{4,28},{6,30},{8,16},{10,18},{12,20},{14,22},{16,8},... | collective-permute-start | bytes 307208 | tf_op jit(solution)/shard_map/ppermute | solution.py:482
  71.0 10.7 %collective-permute-start.19 = (bf16[400,128]{1,0:T(8,128)(2,1)S(1)}, bf16[400,128]{1,0:T(8,128)(2,1)S(1)}, u32[]{:S(2)}, u32[]{:S(2)}) collective-permute-start(bf16[400,128]{1,0:T(8,128)(2,1)S(1)} %get-tuple-element.180), channel_id=1, source_target_pairs={{0,16},{2,18},{4,20},{6,22},{8,24},{10,26},{12,28},{14,30},{16,0},... | collective-permute-start | bytes 307208 | tf_op jit(solution)/shard_map/ppermute | solution.py:482
  72.5 9.2 %collective-permute-start.20 = (bf16[400,128]{1,0:T(8,128)(2,1)S(1)}, bf16[400,128]{1,0:T(8,128)(2,1)S(1)}, u32[]{:S(2)}, u32[]{:S(2)}) collective-permute-start(bf16[400,128]{1,0:T(8,128)(2,1)S(1)} %get-tuple-element.181), channel_id=1, source_target_pairs={{0,8},{2,10},{4,12},{6,14},{8,0},{10,2},{12,4},{14,6},{16,24},{18,... | collective-permute-start | bytes 307208 | tf_op jit(solution)/shard_map/ppermute | solution.py:482
  77.9 7.2 %collective-permute-start.21 = (bf16[400,128]{1,0:T(8,128)(2,1)S(1)}, bf16[400,128]{1,0:T(8,128)(2,1)S(1)}, u32[]{:S(2)}, u32[]{:S(2)}) collective-permute-start(bf16[400,128]{1,0:T(8,128)(2,1)S(1)} %get-tuple-element.187), channel_id=1, source_target_pairs={{0,8},{2,10},{4,12},{6,14},{8,0},{10,2},{12,4},{14,6},{16,24},{18,... | collective-permute-start | bytes 307208 | tf_op jit(solution)/shard_map/ppermute | solution.py:482
  79.4 7.5 %collective-permute-start.22 = (bf16[400,128]{1,0:T(8,128)(2,1)S(1)}, bf16[400,128]{1,0:T(8,128)(2,1)S(1)}, u32[]{:S(2)}, u32[]{:S(2)}) collective-permute-start(bf16[400,128]{1,0:T(8,128)(2,1)S(1)} %get-tuple-element.188), channel_id=1, source_target_pairs={{0,24},{2,26},{4,28},{6,30},{8,16},{10,18},{12,20},{14,22},{16,8},... | collective-permute-start | bytes 307208 | tf_op jit(solution)/shard_map/ppermute | solution.py:482
  81.6 8.5 %collective-permute-start.23 = (bf16[400,128]{1,0:T(8,128)(2,1)S(1)}, bf16[400,128]{1,0:T(8,128)(2,1)S(1)}, u32[]{:S(2)}, u32[]{:S(2)}) collective-permute-start(bf16[400,128]{1,0:T(8,128)(2,1)S(1)} %get-tuple-element.189), channel_id=1, source_target_pairs={{0,16},{2,18},{4,20},{6,22},{8,24},{10,26},{12,28},{14,30},{16,0},... | collective-permute-start | bytes 307208 | tf_op jit(solution)/shard_map/ppermute | solution.py:482
  83.5 11.4 %collective-permute-start.25 = (bf16[128,1536]{1,0:T(8,128)(2,1)S(1)}, bf16[128,1536]{1,0:T(8,128)(2,1)S(1)}, u32[]{:S(2)}, u32[]{:S(2)}) collective-permute-start(bf16[128,1536]{1,0:T(8,128)(2,1)S(1)} %get-tuple-element.194), channel_id=1, source_target_pairs={{0,1},{1,0},{2,3},{3,2},{4,5},{5,4},{6,7},{7,6},{8,9},{9,8},{10,11... | collective-permute-start | bytes 1179656 | tf_op jit(solution)/shard_map/ppermute | solution.py:545
  85.1 12.0 %collective-permute-start.27 = (bf16[2,128,1536]{2,1,0:T(8,128)(2,1)S(1)}, bf16[2,128,1536]{2,1,0:T(8,128)(2,1)S(1)}, u32[]{:S(2)}, u32[]{:S(2)}) collective-permute-start(bf16[2,128,1536]{2,1,0:T(8,128)(2,1)S(1)} %get-tuple-element.201.other), channel_id=1, source_target_pairs={{0,2},{2,0},{4,6},{6,4},{8,10},{10,8},{12,14},{14,12},{16,18},{18,... | collective-permute-start | bytes 2359304 | tf_op jit(solution)/shard_map/ppermute | solution.py:482
  92.0 10.5 %collective-permute-start.24 = (bf16[128,1536]{1,0:T(8,128)(2,1)S(1)}, bf16[128,1536]{1,0:T(8,128)(2,1)S(1)}, u32[]{:S(2)}, u32[]{:S(2)}) collective-permute-start(bf16[128,1536]{1,0:T(8,128)(2,1)S(1)} %get-tuple-element.197), channel_id=1, source_target_pairs={{0,1},{1,0},{2,3},{3,2},{4,5},{5,4},{6,7},{7,6},{8,9},{9,8},{10,11... | collective-permute-start | bytes 1179656 | tf_op jit(solution)/shard_map/ppermute | solution.py:549
  95.7 6.9 %collective-permute-start.26 = (bf16[128,1536]{1,0:T(8,128)(2,1)S(1)}, bf16[128,1536]{1,0:T(8,128)(2,1)S(1)}, u32[]{:S(2)}, u32[]{:S(2)}) collective-permute-start(bf16[128,1536]{1,0:T(8,128)(2,1)S(1)} %gate_and_add.2), channel_id=1, source_target_pairs={{0,2},{2,0},{4,6},{6,4},{8,10},{10,8},{12,14},{14,12},{16,18},{18,... | collective-permute-start | bytes 1179656 | tf_op jit(solution)/shard_map/ppermute | solution.py:482
  97.1 5.4 %copy-start.1 = (bf16[2,128,3072]{2,1,0:T(8,128)(2,1)S(1)}, bf16[2,128,3072]{2,1,0:T(8,128)(2,1)}, u32[]{:S(2)}) copy-start(bf16[2,128,3072]{2,1,0:T(8,128)(2,1)} %hidden.3) | copy-start | bytes 4718596
